TPU v7x, 128 devices: a whole 4x4x4 slice. The times are simulated.
128 devices in a mesh: wide: 32 (over z, x, y_hi), narrow: 4 (over y_lo, core).
Axes of the slice: x: 4, y: 4 (y_hi: 2, y_lo: 2; y = y_hi * 2 + y_lo), z: 4, core: 2. Of those that a mesh axis runs over, the one named last changes fastest.
Arguments:
- displacement: float32 [3, 3, 512, 128, 384], P(None, None, 'wide', 'narrow'), may hold values from -6 to 6
- material: int32 [512, 128, 24], P('wide', 'narrow'), may hold values 0 or 1
- level_set: float32 [384, 128, 512], P('wide', 'narrow'), may hold values from -6 to 6
Outputs:
- level_next: float32 [384, 128, 512], P('wide', 'narrow')
- speed: float32 [384, 128, 512], P('wide', 'narrow')
All inputs are finite; a program needn't handle non-finite values. No bound on the sum of `material` on one device may be relied on, other than what follows from the above.
Results may differ from a plain program's by a relative error of at most 0.00002.
Values sent between devices are 32-bit elements; how exact they have to be, the bound alone decides.
No kernel may reach another device: no remote copies, remote signals or barrier semaphores. Data moves between devices by JAX's collectives and lax.ppermute only.
A program may use at most 192 MiB of HBM per device.

v0:
```python
import jax
import jax.numpy as jnp
from jax import lax
from jax.sharding import PartitionSpec as P

BZ = 16
EXT_PASSES = 4
HJ_STEPS = 3


SHEAR = 0.384615
LAME = 0.576923
WENO_EPS = 1e-06
TIME_STEP = 0.3
VAL_TAPS = (1.0 / 48.0, 23.0 / 48.0, 23.0 / 48.0, 1.0 / 48.0)
DER_TAPS = (-1.0 / 8.0, -5.0 / 8.0, 5.0 / 8.0, 1.0 / 8.0)


def with_halo(block, sides, width):
    for axis, dim in sides:
        count = lax.axis_size(axis)
        forward = [(i, i + 1) for i in range(count - 1)]
        backward = [(target, source) for source, target in forward]
        low = lax.ppermute(
            lax.slice_in_dim(block, block.shape[dim] - width, None, axis=dim), axis, forward
        )
        high = lax.ppermute(lax.slice_in_dim(block, 0, width, axis=dim), axis, backward)
        block = jnp.concatenate([low, block, high], axis=dim)
    return block


def apply_taps(padded, taps, axis, count):
    total = taps[0] * lax.slice_in_dim(padded, 1, 1 + count, axis=axis)
    for k in range(1, 4):
        total = total + taps[k] * lax.slice_in_dim(padded, 1 + k, 1 + k + count, axis=axis)
    return total


def strain_energy(grad_x, grad_y, grad_z, stiffness):
    exx = grad_x[:, 0]
    eyy = grad_y[:, 1]
    ezz = grad_z[:, 2]
    exy = 0.5 * (grad_y[:, 0] + grad_x[:, 1])
    exz = 0.5 * (grad_z[:, 0] + grad_x[:, 2])
    eyz = 0.5 * (grad_z[:, 1] + grad_y[:, 2])
    trace = exx + eyy + ezz
    square = exx * exx + eyy * eyy + ezz * ezz + 2.0 * (exy * exy + exz * exz + eyz * eyz)
    density = SHEAR * square + 0.5 * LAME * trace * trace
    return stiffness * jnp.sum(density, axis=0)


def neighbour_mean(padded):
    wider = jnp.pad(padded, ((0, 0), (0, 0), (1, 1)))
    total = wider[2:, 1:-1, 1:-1] + wider[:-2, 1:-1, 1:-1]
    total = total + wider[1:-1, 2:, 1:-1] + wider[1:-1, :-2, 1:-1]
    total = total + wider[1:-1, 1:-1, 2:] + wider[1:-1, 1:-1, :-2]
    return total * (1.0 / 6.0)


def weno_side(v1, v2, v3, v4, v5):
    p_one = v1 / 3.0 - 7.0 * v2 / 6.0 + 11.0 * v3 / 6.0
    p_two = -v2 / 6.0 + 5.0 * v3 / 6.0 + v4 / 3.0
    p_three = v3 / 3.0 + 5.0 * v4 / 6.0 - v5 / 6.0
    b_one = 13.0 / 12.0 * (v1 - 2.0 * v2 + v3) ** 2 + 0.25 * (v1 - 4.0 * v2 + 3.0 * v3) ** 2
    b_two = 13.0 / 12.0 * (v2 - 2.0 * v3 + v4) ** 2 + 0.25 * (v2 - v4) ** 2
    b_three = 13.0 / 12.0 * (v3 - 2.0 * v4 + v5) ** 2 + 0.25 * (3.0 * v3 - 4.0 * v4 + v5) ** 2
    a_one = 0.1 / (WENO_EPS + b_one) ** 2
    a_two = 0.6 / (WENO_EPS + b_two) ** 2
    a_three = 0.3 / (WENO_EPS + b_three) ** 2
    return (a_one * p_one + a_two * p_two + a_three * p_three) / (a_one + a_two + a_three)


def march_step(padded, speed):
    wider = jnp.pad(padded, ((0, 0), (0, 0), (3, 3)), constant_values=1.0)
    size_z = padded.shape[0] - 6
    size_y = padded.shape[1] - 6
    size_x = padded.shape[2]
    centre = wider[3 : 3 + size_z, 3 : 3 + size_y, 3 : 3 + size_x]
    lines = (
        wider[:, 3 : 3 + size_y, 3 : 3 + size_x],
        wider[3 : 3 + size_z, :, 3 : 3 + size_x],
        wider[3 : 3 + size_z, 3 : 3 + size_y, :],
    )
    grow_plus = None
    grow_minus = None
    for axis in range(3):
        line = lines[axis]
        count = centre.shape[axis]
        diffs = lax.slice_in_dim(line, 1, count + 6, axis=axis) - lax.slice_in_dim(
            line, 0, count + 5, axis=axis
        )
        parts = [lax.slice_in_dim(diffs, k, k + count, axis=axis) for k in range(6)]
        minus = weno_side(parts[0], parts[1], parts[2], parts[3], parts[4])
        plus = weno_side(parts[5], parts[4], parts[3], parts[2], parts[1])
        term_p = jnp.maximum(jnp.maximum(minus, 0.0) ** 2, jnp.minimum(plus, 0.0) ** 2)
        term_m = jnp.maximum(jnp.minimum(minus, 0.0) ** 2, jnp.maximum(plus, 0.0) ** 2)
        grow_plus = term_p if grow_plus is None else grow_plus + term_p
        grow_minus = term_m if grow_minus is None else grow_minus + term_m
    return centre - TIME_STEP * (
        jnp.maximum(speed, 0.0) * jnp.sqrt(grow_plus)
        + jnp.minimum(speed, 0.0) * jnp.sqrt(grow_minus)
    )


def ghost_fill(array, margin, value):
    own_z = array.shape[0] - 2 * margin
    own_y = array.shape[1] - 2 * margin
    pos_z = lax.axis_index("wide") * own_z - margin + jnp.arange(array.shape[0], dtype=jnp.int32)
    pos_y = lax.axis_index("narrow") * own_y - margin + jnp.arange(array.shape[1], dtype=jnp.int32)
    valid_z = (pos_z >= 0) & (pos_z < own_z * lax.axis_size("wide"))
    valid_y = (pos_y >= 0) & (pos_y < own_y * lax.axis_size("narrow"))
    inside = valid_z[:, None, None] & valid_y[None, :, None]
    return jnp.where(inside, array, value)


def per_device(displacement, material, level_set):
    size_x = displacement.shape[2]
    size_y = displacement.shape[3]
    size_z = displacement.shape[4]
    padded = with_halo(displacement, (("wide", 2), ("narrow", 3)), 2)
    padded = jnp.pad(padded, ((0, 0), (0, 0), (0, 0), (0, 0), (2, 2)))
    val_z = apply_taps(padded, VAL_TAPS, 4, size_z)
    der_z = apply_taps(padded, DER_TAPS, 4, size_z)
    vv = apply_taps(val_z, VAL_TAPS, 3, size_y)
    vd = apply_taps(val_z, DER_TAPS, 3, size_y)
    dv = apply_taps(der_z, VAL_TAPS, 3, size_y)
    grad_x = apply_taps(vv, DER_TAPS, 2, size_x)
    grad_y = apply_taps(vd, VAL_TAPS, 2, size_x)
    grad_z = apply_taps(dv, VAL_TAPS, 2, size_x)
    stiffness = 0.2 + 0.8 * jnp.repeat(material.astype(jnp.float32), BZ, axis=2)
    energy = strain_energy(grad_x, grad_y, grad_z, stiffness)
    peak = lax.pmax(jnp.max(energy), ("wide", "narrow"))
    slab_velocity = jnp.transpose(energy / (peak + 1e-06) - 0.5, (2, 1, 0))
    velocity = lax.all_to_all(slab_velocity, "wide", split_axis=0, concat_axis=2, tiled=True)
    weight = 1.0 / (1.0 + 4.0 * level_set * level_set)
    speed = velocity
    for step in range(EXT_PASSES):
        beside_all = with_halo(speed, (("wide", 0), ("narrow", 1)), 1)
        speed = weight * velocity + (1.0 - weight) * neighbour_mean(beside_all)
    phi = level_set
    for step in range(HJ_STEPS):
        beside_all = with_halo(phi, (("wide", 0), ("narrow", 1)), 3)
        phi = march_step(ghost_fill(beside_all, 3, 1.0), speed)
    return (phi, speed)


def solution(mesh):
    return jax.shard_map(
        per_device,
        mesh=mesh,
        in_specs=(
            P(None, None, "wide", "narrow", None),
            P("wide", "narrow", None),
            P("wide", "narrow", None),
        ),
        out_specs=(P("wide", "narrow", None), P("wide", "narrow", None)),
        check_vma=False,
    )
```

profile of v0, /device:TPU:23, one launch (start us, length us, event | category | flops | bytes accessed | tf_op | source)
XLA Modules:
  0.0 537.1 jit_solution(10497317140934594762)
XLA Ops:
  2.2 3.4 collective-permute-start.4
  5.6 3.6 collective-permute-start.5
  9.2 17.1 %collective-permute-done.4 = f32[3,3,2,32,384]{4,3,2,1,0:T(8,128)S(1)} collective-permute-done((f32[3,3,2,32,384]{4,3,2,1,0:T(8,128)S(1)}, f32[3,3,2,32,384]{4,3,2,1,0:T(8,128)S(1)}, u32[]{:S(2)}, u32[]{:S(2)}) %collective-permute-start.4) | collective-permute-done | bytes 884768 | tf_op jit(solution)/shard_map/ppermute | solution.py:24
  26.3 17.3 %collective-permute-done.5 = f32[3,3,2,32,384]{4,3,2,1,0:T(8,128)S(1)} collective-permute-done((f32[3,3,2,32,384]{4,3,2,1,0:T(8,128)S(1)}, f32[3,3,2,32,384]{4,3,2,1,0:T(8,128)S(1)}, u32[]{:S(2)}, u32[]{:S(2)}) %collective-permute-start.5) | collective-permute-done | bytes 884768 | tf_op jit(solution)/shard_map/ppermute | solution.py:27
  43.5 2.7 fusion.65
  47.2 4.2 collective-permute-start.6
  52.3 1.9 collective-permute-start.7
  54.5 1.9 copy.426
  56.4 2.9 collective-permute-done.6
  60.7 3.9 collective-permute-done.7
  66.0 10.4 %broadcast_multiply_fusion = (f32[3,3,20,36,384]{4,3,2,0,1:T(8,128)}, f32[3,3,20,36,384]{4,3,2,0,1:T(8,128)}) fusion(f32[3,3,20,2,384]{4,3,2,0,1:T(2,128)S(1)} %copy.402, f32[3,3,20,2,384]{4,3,2,0,1:T(2,128)S(1)} %copy.401, f32[3,3,2,32,384]{4,3,2,1,0:T(8,128)} %copy-done.4, f32[3,3,16,32,384]{4,3,2,1,0:T(8,128)} %param.3, f32[3,3,2,32,384]{4,3,2,1,0:T(8,128)} %copy-done.3), kind=kLoop, calls=%fused_computation.42 | loop fusion | flops 11888640 | bytes 29859840 | tf_op jit(solution)/shard_map/mul | solution.py:35
  76.3 43.4 %pad_slice_fusion.2 = (f32[3,3,20,36,384]{4,3,2,0,1:T(8,128)}, f32[3,3,20,36,384]{4,3,2,0,1:T(8,128)}, f32[3,3,20,36,384]{4,3,2,0,1:T(8,128)}, f32[3,3,20,36,384]{4,3,2,0,1:T(8,128)}) fusion(f32[3,3,20,36,384]{4,3,2,0,1:T(8,128)} %get-tuple-element.24), kind=kLoop, calls=%fused_computation.2 | loop fusion | flops 22394880 | bytes 49766400 | tf_op jit(solution)/shard_map/slice | solution.py:33
  119.8 18.9 %copy_add_fusion = f32[3,3,20,36,384]{4,3,2,1,0:T(8,128)} fusion(f32[3,3,20,36,384]{4,3,2,0,1:T(8,128)} %get-tuple-element.20, f32[3,3,20,36,384]{4,3,2,0,1:T(8,128)} %get-tuple-element.21, f32[3,3,20,36,384]{4,3,2,0,1:T(8,128)} %get-tuple-element.23, f32[3,3,20,36,384]{4,3,2,0,1:T(8,128)} %get-tuple-element.19), kind=kLoop, calls=%fused_computation.4 | loop fusion | flops 9953280 | bytes 49766400 | tf_op jit(solution)/shard_map/add | solution.py:35
  138.7 21.1 %fusion.63 = (f32[3,3,20,32,384]{4,3,2,1,0:T(8,128)}, f32[3,3,20,32,384]{4,3,2,1,0:T(8,128)}, f32[3,3,20,32,384]{4,3,2,1,0:T(8,128)}) fusion(f32[3,3,20,36,384]{4,3,2,1,0:T(8,128)} %copy_add_fusion), kind=kLoop, calls=%fused_computation.200 | loop fusion | bytes 53084160 | tf_op jit(solution)/shard_map/slice | solution.py:33
  159.7 17.0 %fusion.2 = f32[3,3,20,32,384]{4,3,2,1,0:T(8,128)} fusion(f32[3,3,20,36,384]{4,3,2,1,0:T(8,128)} %copy_add_fusion, f32[3,3,20,32,384]{4,3,2,1,0:T(8,128)} %get-tuple-element.18, f32[3,3,20,32,384]{4,3,2,1,0:T(8,128)} %get-tuple-element.17, f32[3,3,20,32,384]{4,3,2,1,0:T(8,128)} %get-tuple-element.16), kind=kLoop, calls=%fused_computation.12 | loop fusion | flops 15482880 | bytes 44236800 | tf_op jit(solution)/shard_map/add | solution.py:35
  176.7 13.6 %fusion.64 = (f32[3,3,16,32,384]{4,3,2,1,0:T(8,128)}, f32[3,3,16,32,384]{4,3,2,1,0:T(8,128)}, f32[3,3,16,32,384]{4,3,2,1,0:T(8,128)}) fusion(f32[3,3,20,32,384]{4,3,2,1,0:T(8,128)} %fusion.2), kind=kLoop, calls=%fused_computation.201 | loop fusion | bytes 42467328 | tf_op jit(solution)/shard_map/slice | solution.py:33
  190.4 9.7 %multiply_add_fusion.2 = (f32[3,3,20,32,384]{4,3,2,0,1:T(8,128)}, f32[3,3,20,32,384]{4,3,2,0,1:T(8,128)}) fusion(f32[3,3,20,36,384]{4,3,2,0,1:T(8,128)S(1)} %bitcast.54), kind=kLoop, calls=%fused_computation.20 | loop fusion | flops 30965760 | bytes 53084160 | tf_op jit(solution)/shard_map/add | solution.py:35
  200.1 22.8 %fusion.6 = (f32[3,3,16,32,384]{4,3,2,0,1:T(8,128)S(1)}, f32[3,3,16,32,384]{4,3,2,0,1:T(8,128)}) fusion(f32[3,3,20,32,384]{4,3,2,0,1:T(8,128)} %get-tuple-element.15, f32[3,3,20,32,384]{4,3,2,0,1:T(8,128)} %get-tuple-element.14), kind=kLoop, calls=%fused_computation.24 | loop fusion | flops 24772608 | bytes 70778880 | tf_op jit(solution)/shard_map/add | solution.py:35
  222.9 14.1 %fusion.5 = f32[3,3,16,32,384]{4,3,2,1,0:T(8,128)} fusion(f32[3,3,20,32,384]{4,3,2,1,0:T(8,128)} %fusion.2, f32[3,3,16,32,384]{4,3,2,1,0:T(8,128)} %get-tuple-element.27, f32[3,3,16,32,384]{4,3,2,1,0:T(8,128)} %get-tuple-element.26, f32[3,3,16,32,384]{4,3,2,1,0:T(8,128)} %get-tuple-element.25), kind=kLoop, calls=%fused_computation.22 | loop fusion | flops 12386304 | bytes 35389440 | tf_op jit(solution)/shard_map/add | solution.py:35
  237.0 4.9 fusion.15
  242.7 67.4 %pmax.7 = f32[]{:T(128)} all-reduce(f32[]{:T(128)} %get-tuple-element.12), channel_id=1, replica_groups=mesh['wide'=32,'narrow'=4] {'wide','narrow'}, use_global_device_ids=true, to_apply=%region_2.3 | all-reduce | flops 1 | bytes 8 | tf_op jit(solution)/shard_map/pmax | solution.py:132
  311.8 2.2 copy.427
  314.0 2.3 reshape.87
  316.3 18.6 %all_to_all.18 = f32[32,1,6144]{2,1,0:T(1,128)S(1)} all-to-all(f32[32,1,6144]{2,1,0:T(1,128)} %reshape.87), channel_id=1, replica_groups=mesh['wide'=32,'narrow'=4] {'wide'}, dimensions={0} | all-to-all | bytes 1572864 | tf_op jit(solution)/shard_map/all_to_all | solution.py:134
  335.4 2.5 reduce.4
  337.9 2.7 reshape.88
  341.8 2.3 collective-permute-start.8
  344.3 7.5 %collective-permute-start.9 = (f32[1,32,512]{2,1,0:T(8,128)S(1)}, f32[1,32,512]{2,1,0:T(8,128)S(1)}, u32[]{:S(2)}, u32[]{:S(2)}) collective-permute-start(f32[1,32,512]{2,1,0:T(8,128)S(1)} %copy.432), channel_id=1, source_target_pairs={{0,4},{4,8},{8,12},{12,16},{16,20},{20,24},{24,28},{28,32},{32,36}... | collective-permute-start | bytes 196616 | tf_op jit(solution)/shard_map/ppermute | solution.py:24
  351.7 3.9 copy.428
  355.6 2.3 copy.429
  358.0 4.6 collective-permute-start.10
  362.6 2.8 collective-permute-start.11
  365.4 3.6 collective-permute-start
  369.0 3.2 collective-permute-start.1
  373.6 1.9 collective-permute-start.12
  375.6 7.9 %collective-permute-start.13 = (f32[1,32,512]{2,1,0:T(8,128)S(1)}, f32[1,32,512]{2,1,0:T(8,128)S(1)}, u32[]{:S(2)}, u32[]{:S(2)}) collective-permute-start(f32[1,32,512]{2,1,0:T(8,128)S(1)} %get-tuple-element.58), channel_id=1, source_target_pairs={{0,4},{4,8},{8,12},{12,16},{16,20},{20,24},{24,28},{28,32},{32,36}... | collective-permute-start | bytes 196616 | tf_op jit(solution)/shard_map/ppermute | solution.py:24
  384.8 3.2 collective-permute-start.14
  388.0 2.8 collective-permute-start.15
  393.2 1.9 collective-permute-start.16
  395.1 7.9 %collective-permute-start.17 = (f32[1,32,512]{2,1,0:T(8,128)S(1)}, f32[1,32,512]{2,1,0:T(8,128)S(1)}, u32[]{:S(2)}, u32[]{:S(2)}) collective-permute-start(f32[1,32,512]{2,1,0:T(8,128)S(1)} %get-tuple-element.56), channel_id=1, source_target_pairs={{0,4},{4,8},{8,12},{12,16},{16,20},{20,24},{24,28},{28,32},{32,36}... | collective-permute-start | bytes 196616 | tf_op jit(solution)/shard_map/ppermute | solution.py:24
  404.4 2.9 collective-permute-start.18
  407.3 4.7 collective-permute-start.19
  414.4 1.9 collective-permute-start.20
  416.3 7.9 %collective-permute-start.21 = (f32[1,32,512]{2,1,0:T(8,128)S(1)}, f32[1,32,512]{2,1,0:T(8,128)S(1)}, u32[]{:S(2)}, u32[]{:S(2)}) collective-permute-start(f32[1,32,512]{2,1,0:T(8,128)S(1)} %get-tuple-element.52), channel_id=1, source_target_pairs={{0,4},{4,8},{8,12},{12,16},{16,20},{20,24},{24,28},{28,32},{32,36}... | collective-permute-start | bytes 196616 | tf_op jit(solution)/shard_map/ppermute | solution.py:24
  425.6 1.9 collective-permute-start.22
  427.5 5.7 %collective-permute-start.23 = (f32[14,1,512]{2,1,0:T(1,128)S(1)}, f32[14,1,512]{2,1,0:T(1,128)S(1)}, u32[]{:S(2)}, u32[]{:S(2)}) collective-permute-start(f32[14,1,512]{2,1,0:T(1,128)S(1)} %get-tuple-element.40), channel_id=1, source_target_pairs={{0,1},{1,2},{2,3},{4,5},{5,6},{6,7},{8,9},{9,10},{10,11},{12,13},{... | collective-permute-start | bytes 86024 | tf_op jit(solution)/shard_map/ppermute | solution.py:24
  433.3 2.4 collective-permute-start.2
  435.8 1.9 collective-permute-start.3
  438.5 3.8 collective-permute-done.3
  443.6 14.0 %slice_subtract_fusion.8 = (f32[12,32,512]{2,1,0:T(8,128)S(1)}, f32[12,32,512]{2,1,0:T(8,128)S(1)}) fusion(f32[18,38,512]{2,1,0:T(8,128)S(1)} %maximum_select_fusion, f32[12,32,517]{2,1,0:T(8,128)S(1)} %fusion.31, f32[12,37,512]{2,1,0:T(8,128)S(1)} %slice_subtract_fusion.5, f32[17,32,512]{2,1,0:T(8,128)S(1)} %slice_subtract_fusion.2, ...), kind=kLoop, calls=%fused_computation.171 | loop fusion | flops 85524480 | bytes 20635648 | tf_op jit(solution)/shard_map/sub | solution.py:99
  457.6 7.9 %collective-permute-start.24 = (f32[3,32,512]{2,1,0:T(8,128)S(1)}, f32[3,32,512]{2,1,0:T(8,128)S(1)}, u32[]{:S(2)}, u32[]{:S(2)}) collective-permute-start(f32[3,32,512]{2,1,0:T(8,128)S(1)} %get-tuple-element.50), channel_id=1, source_target_pairs={{0,4},{4,8},{8,12},{12,16},{16,20},{20,24},{24,28},{28,32},{32,36}... | collective-permute-start | bytes 589832 | tf_op jit(solution)/shard_map/ppermute | solution.py:24
  465.5 1.9 collective-permute-start.25
  468.1 8.3 %collective-permute-done.25 = f32[3,32,512]{2,1,0:T(8,128)S(1)} collective-permute-done((f32[3,32,512]{2,1,0:T(8,128)S(1)}, f32[3,32,512]{2,1,0:T(8,128)S(1)}, u32[]{:S(2)}, u32[]{:S(2)}) %collective-permute-start.25) | collective-permute-done | bytes 196640 | tf_op jit(solution)/shard_map/ppermute | solution.py:27
  476.5 3.8 collective-permute-start.26
  480.4 1.9 collective-permute-start.27
  482.5 4.3 collective-permute-done.27
  488.2 12.1 %slice_subtract_fusion.7 = f32[12,32,512]{2,1,0:T(8,128)S(1)} fusion(f32[18,38,512]{2,1,0:T(8,128)S(1)} %maximum_select_fusion.1, f32[12,32,517]{2,1,0:T(8,128)S(1)} %fusion.32, f32[12,37,512]{2,1,0:T(8,128)S(1)} %slice_subtract_fusion.4, f32[17,32,512]{2,1,0:T(8,128)S(1)} %slice_subtract_fusion.1, f32[12,32,512]{2,1,0:T(8,128)S(1)} %get-tuple-element.11), kind=kLoop, calls=%fused_computation.106 | loop fusion | flops 81199104 | bytes 16515072 | tf_op jit(solution)/shard_map/sub | solution.py:99
  500.3 1.9 collective-permute-start.28
  502.3 4.9 collective-permute-start.29
  508.3 4.9 collective-permute-done.29
  513.3 2.9 collective-permute-start.30
  516.3 1.9 collective-permute-start.31
  518.4 4.3 collective-permute-done.31
  524.0 12.8 %slice_subtract_fusion.6 = f32[12,32,512]{2,1,0:T(8,128)} fusion(f32[18,38,512]{2,1,0:T(8,128)S(1)} %maximum_select_fusion.2, f32[12,32,517]{2,1,0:T(8,128)S(1)} %fusion.33, f32[12,37,512]{2,1,0:T(8,128)S(1)} %slice_subtract_fusion.3, f32[17,32,512]{2,1,0:T(8,128)S(1)} %slice_subtract_fusion, f32[12,32,512]{2,1,0:T(8,128)S(1)} %get-tuple-element.11), kind=kLoop, calls=%fused_computation.105 | loop fusion | flops 81199104 | bytes 16515072 | tf_op jit(solution)/shard_map/sub | solution.py:99
  (106 shorter events, 27.5 us)
Async XLA Ops:
  2.2 52.0 %copy-start.6 = (s32[16,32,24]{1,2,0:T(8,128)S(1)}, s32[16,32,24]{1,2,0:T(8,128)}, u32[]{:S(2)}) copy-start(s32[16,32,24]{1,2,0:T(8,128)} %param.4) | copy-start | bytes 147460
  2.2 24.0 %collective-permute-start.4 = (f32[3,3,2,32,384]{4,3,2,1,0:T(8,128)S(1)}, f32[3,3,2,32,384]{4,3,2,1,0:T(8,128)S(1)}, u32[]{:S(2)}, u32[]{:S(2)}) collective-permute-start(f32[3,3,2,32,384]{4,3,2,1,0:T(8,128)S(1)} %get-tuple-element.30), channel_id=1, source_target_pairs={{0,4},{4,8},{8,12},{12,16},{16,20},{20,24},{24,28},{28,32},{32,36}... | collective-permute-start | bytes 2654216 | tf_op jit(solution)/shard_map/ppermute | solution.py:24
  5.6 37.9 %collective-permute-start.5 = (f32[3,3,2,32,384]{4,3,2,1,0:T(8,128)S(1)}, f32[3,3,2,32,384]{4,3,2,1,0:T(8,128)S(1)}, u32[]{:S(2)}, u32[]{:S(2)}) collective-permute-start(f32[3,3,2,32,384]{4,3,2,1,0:T(8,128)S(1)} %get-tuple-element.31), channel_id=1, source_target_pairs={{4,0},{8,4},{12,8},{16,12},{20,16},{24,20},{28,24},{32,28},{36,32}... | collective-permute-start | bytes 2654216 | tf_op jit(solution)/shard_map/ppermute | solution.py:27
  26.3 28.2 %copy-start.3 = (f32[3,3,2,32,384]{4,3,2,1,0:T(8,128)}, f32[3,3,2,32,384]{4,3,2,1,0:T(8,128)S(1)}, u32[]{:S(2)}) copy-start(f32[3,3,2,32,384]{4,3,2,1,0:T(8,128)S(1)} %collective-permute-done.4) | copy-start | bytes 2654212
  43.5 10.9 %copy-start.4 = (f32[3,3,2,32,384]{4,3,2,1,0:T(8,128)}, f32[3,3,2,32,384]{4,3,2,1,0:T(8,128)S(1)}, u32[]{:S(2)}) copy-start(f32[3,3,2,32,384]{4,3,2,1,0:T(8,128)S(1)} %collective-permute-done.5) | copy-start | bytes 2654212
  47.2 12.1 %collective-permute-start.6 = (f32[3,3,20,2,384]{4,2,3,1,0:T(8,128)}, f32[3,3,20,2,384]{4,2,3,1,0:T(8,128)}, u32[]{:S(2)}, u32[]{:S(2)}) collective-permute-start(f32[3,3,20,2,384]{4,2,3,1,0:T(8,128)} %copy.399), channel_id=1, source_target_pairs={{0,1},{1,2},{2,3},{4,5},{5,6},{6,7},{8,9},{9,10},{10,11},{12,13},{... | collective-permute-start | bytes 1658888 | tf_op jit(solution)/shard_map/ppermute | solution.py:24
  52.3 12.3 %collective-permute-start.7 = (f32[3,3,20,2,384]{4,2,3,1,0:T(8,128)}, f32[3,3,20,2,384]{4,2,3,1,0:T(8,128)}, u32[]{:S(2)}, u32[]{:S(2)}) collective-permute-start(f32[3,3,20,2,384]{4,2,3,1,0:T(8,128)} %copy.400), channel_id=1, source_target_pairs={{1,0},{2,1},{3,2},{5,4},{6,5},{7,6},{9,8},{10,9},{11,10},{13,12},{... | collective-permute-start | bytes 1658888 | tf_op jit(solution)/shard_map/ppermute | solution.py:27
  159.7 30.6 %slice-start = ((s8[11059200]{0:T(1024)(128)(4,1)}), s8[4194304]{0:T(1024)(128)(4,1)S(1)}, s32[]{:S(2)}) async-start(s8[11059200]{0:T(1024)(128)(4,1)} %bitcast.53), calls=%async_computation.1 | async-start | bytes 8388608
  159.7 30.6 %slice-start.1 = ((s8[11059200]{0:T(1024)(128)(4,1)}), s8[4194304]{0:T(1024)(128)(4,1)S(1)}, s32[]{:S(2)}) async-start(s8[11059200]{0:T(1024)(128)(4,1)} %bitcast.53), calls=%async_computation.2 | async-start | bytes 8388608
  176.7 13.6 %slice-start.2 = ((s8[11059200]{0:T(1024)(128)(4,1)}), s8[2670592]{0:T(1024)(128)(4,1)S(1)}, s32[]{:S(2)}) async-start(s8[11059200]{0:T(1024)(128)(4,1)} %bitcast.53), calls=%async_computation.3 | async-start | bytes 5341184
  222.9 14.1 %copy-start = (f32[3,3,16,32,384]{4,3,2,0,1:T(8,128)S(1)}, f32[3,3,16,32,384]{4,3,2,0,1:T(8,128)}, u32[]{:S(2)}) copy-start(f32[3,3,16,32,384]{4,3,2,0,1:T(8,128)} %get-tuple-element.63) | copy-start | bytes 21233668
  237.0 4.9 copy-start.5
  340.6 24.8 %copy-start.1 = (f32[12,32,512]{2,1,0:T(8,128)S(1)}, f32[12,32,512]{2,1,0:T(8,128)}, u32[]{:S(2)}) copy-start(f32[12,32,512]{2,1,0:T(8,128)} %param.5) | copy-start | bytes 2359300
  341.8 16.1 %collective-permute-start.8 = (f32[1,32,512]{2,1,0:T(8,128)S(1)}, f32[1,32,512]{2,1,0:T(8,128)S(1)}, u32[]{:S(2)}, u32[]{:S(2)}) collective-permute-start(f32[1,32,512]{2,1,0:T(8,128)S(1)} %copy.430), channel_id=1, source_target_pairs={{4,0},{8,4},{12,8},{16,12},{20,16},{24,20},{28,24},{32,28},{36,32}... | collective-permute-start | bytes 196616 | tf_op jit(solution)/shard_map/ppermute | solution.py:27
  344.3 13.7 %collective-permute-start.9 = (f32[1,32,512]{2,1,0:T(8,128)S(1)}, f32[1,32,512]{2,1,0:T(8,128)S(1)}, u32[]{:S(2)}, u32[]{:S(2)}) collective-permute-start(f32[1,32,512]{2,1,0:T(8,128)S(1)} %copy.432), channel_id=1, source_target_pairs={{0,4},{4,8},{8,12},{12,16},{16,20},{20,24},{24,28},{28,32},{32,36}... | collective-permute-start | bytes 196616 | tf_op jit(solution)/shard_map/ppermute | solution.py:24
  358.0 14.2 %collective-permute-start.10 = (f32[14,1,512]{2,1,0:T(1,128)S(1)}, f32[14,1,512]{2,1,0:T(1,128)S(1)}, u32[]{:S(2)}, u32[]{:S(2)}) collective-permute-start(f32[14,1,512]{2,1,0:T(1,128)S(1)} %get-tuple-element.47), channel_id=1, source_target_pairs={{1,0},{2,1},{3,2},{5,4},{6,5},{7,6},{9,8},{10,9},{11,10},{13,12},{... | collective-permute-start | bytes 86024 | tf_op jit(solution)/shard_map/ppermute | solution.py:27
  362.6 9.7 %collective-permute-start.11 = (f32[14,1,512]{2,1,0:T(1,128)S(1)}, f32[14,1,512]{2,1,0:T(1,128)S(1)}, u32[]{:S(2)}, u32[]{:S(2)}) collective-permute-start(f32[14,1,512]{2,1,0:T(1,128)S(1)} %get-tuple-element.46), channel_id=1, source_target_pairs={{0,1},{1,2},{2,3},{4,5},{5,6},{6,7},{8,9},{9,10},{10,11},{12,13},{... | collective-permute-start | bytes 86024 | tf_op jit(solution)/shard_map/ppermute | solution.py:24
  365.4 46.6 %collective-permute-start = (f32[3,32,512]{2,1,0:T(8,128)S(1)}, f32[3,32,512]{2,1,0:T(8,128)S(1)}, u32[]{:S(2)}, u32[]{:S(2)}) collective-permute-start(f32[3,32,512]{2,1,0:T(8,128)S(1)} %get-tuple-element.61), channel_id=1, source_target_pairs={{0,4},{4,8},{8,12},{12,16},{16,20},{20,24},{24,28},{28,32},{32,36}... | collective-permute-start | bytes 589832 | tf_op jit(solution)/shard_map/ppermute | solution.py:24
  369.0 55.2 %collective-permute-start.1 = (f32[3,32,512]{2,1,0:T(8,128)S(1)}, f32[3,32,512]{2,1,0:T(8,128)S(1)}, u32[]{:S(2)}, u32[]{:S(2)}) collective-permute-start(f32[3,32,512]{2,1,0:T(8,128)S(1)} %get-tuple-element.60), channel_id=1, source_target_pairs={{4,0},{8,4},{12,8},{16,12},{20,16},{24,20},{28,24},{32,28},{36,32}... | collective-permute-start | bytes 589832 | tf_op jit(solution)/shard_map/ppermute | solution.py:27
  373.6 9.9 %collective-permute-start.12 = (f32[1,32,512]{2,1,0:T(8,128)S(1)}, f32[1,32,512]{2,1,0:T(8,128)S(1)}, u32[]{:S(2)}, u32[]{:S(2)}) collective-permute-start(f32[1,32,512]{2,1,0:T(8,128)S(1)} %get-tuple-element.59), channel_id=1, source_target_pairs={{4,0},{8,4},{12,8},{16,12},{20,16},{24,20},{28,24},{32,28},{36,32}... | collective-permute-start | bytes 196616 | tf_op jit(solution)/shard_map/ppermute | solution.py:27
  375.6 9.2 %collective-permute-start.13 = (f32[1,32,512]{2,1,0:T(8,128)S(1)}, f32[1,32,512]{2,1,0:T(8,128)S(1)}, u32[]{:S(2)}, u32[]{:S(2)}) collective-permute-start(f32[1,32,512]{2,1,0:T(8,128)S(1)} %get-tuple-element.58), channel_id=1, source_target_pairs={{0,4},{4,8},{8,12},{12,16},{16,20},{20,24},{24,28},{28,32},{32,36}... | collective-permute-start | bytes 196616 | tf_op jit(solution)/shard_map/ppermute | solution.py:24
  384.8 6.0 %collective-permute-start.14 = (f32[14,1,512]{2,1,0:T(1,128)S(1)}, f32[14,1,512]{2,1,0:T(1,128)S(1)}, u32[]{:S(2)}, u32[]{:S(2)}) collective-permute-start(f32[14,1,512]{2,1,0:T(1,128)S(1)} %get-tuple-element.45), channel_id=1, source_target_pairs={{1,0},{2,1},{3,2},{5,4},{6,5},{7,6},{9,8},{10,9},{11,10},{13,12},{... | collective-permute-start | bytes 86024 | tf_op jit(solution)/shard_map/ppermute | solution.py:27
  388.0 3.8 collective-permute-start.15
  393.2 10.3 %collective-permute-start.16 = (f32[1,32,512]{2,1,0:T(8,128)S(1)}, f32[1,32,512]{2,1,0:T(8,128)S(1)}, u32[]{:S(2)}, u32[]{:S(2)}) collective-permute-start(f32[1,32,512]{2,1,0:T(8,128)S(1)} %get-tuple-element.57), channel_id=1, source_target_pairs={{4,0},{8,4},{12,8},{16,12},{20,16},{24,20},{28,24},{32,28},{36,32}... | collective-permute-start | bytes 196616 | tf_op jit(solution)/shard_map/ppermute | solution.py:27
  395.1 9.2 %collective-permute-start.17 = (f32[1,32,512]{2,1,0:T(8,128)S(1)}, f32[1,32,512]{2,1,0:T(8,128)S(1)}, u32[]{:S(2)}, u32[]{:S(2)}) collective-permute-start(f32[1,32,512]{2,1,0:T(8,128)S(1)} %get-tuple-element.56), channel_id=1, source_target_pairs={{0,4},{4,8},{8,12},{12,16},{16,20},{20,24},{24,28},{28,32},{32,36}... | collective-permute-start | bytes 196616 | tf_op jit(solution)/shard_map/ppermute | solution.py:24
  404.4 7.6 %collective-permute-start.18 = (f32[14,1,512]{2,1,0:T(1,128)S(1)}, f32[14,1,512]{2,1,0:T(1,128)S(1)}, u32[]{:S(2)}, u32[]{:S(2)}) collective-permute-start(f32[14,1,512]{2,1,0:T(1,128)S(1)} %get-tuple-element.43), channel_id=1, source_target_pairs={{1,0},{2,1},{3,2},{5,4},{6,5},{7,6},{9,8},{10,9},{11,10},{13,12},{... | collective-permute-start | bytes 86024 | tf_op jit(solution)/shard_map/ppermute | solution.py:27
  407.3 5.7 %collective-permute-start.19 = (f32[14,1,512]{2,1,0:T(1,128)S(1)}, f32[14,1,512]{2,1,0:T(1,128)S(1)}, u32[]{:S(2)}, u32[]{:S(2)}) collective-permute-start(f32[14,1,512]{2,1,0:T(1,128)S(1)} %get-tuple-element.42), channel_id=1, source_target_pairs={{0,1},{1,2},{2,3},{4,5},{5,6},{6,7},{8,9},{9,10},{10,11},{12,13},{... | collective-permute-start | bytes 86024 | tf_op jit(solution)/shard_map/ppermute | solution.py:24
  414.4 9.9 %collective-permute-start.20 = (f32[1,32,512]{2,1,0:T(8,128)S(1)}, f32[1,32,512]{2,1,0:T(8,128)S(1)}, u32[]{:S(2)}, u32[]{:S(2)}) collective-permute-start(f32[1,32,512]{2,1,0:T(8,128)S(1)} %get-tuple-element.53), channel_id=1, source_target_pairs={{4,0},{8,4},{12,8},{16,12},{20,16},{24,20},{28,24},{32,28},{36,32}... | collective-permute-start | bytes 196616 | tf_op jit(solution)/shard_map/ppermute | solution.py:27
  416.3 9.2 %collective-permute-start.21 = (f32[1,32,512]{2,1,0:T(8,128)S(1)}, f32[1,32,512]{2,1,0:T(8,128)S(1)}, u32[]{:S(2)}, u32[]{:S(2)}) collective-permute-start(f32[1,32,512]{2,1,0:T(8,128)S(1)} %get-tuple-element.52), channel_id=1, source_target_pairs={{0,4},{4,8},{8,12},{12,16},{16,20},{20,24},{24,28},{28,32},{32,36}... | collective-permute-start | bytes 196616 | tf_op jit(solution)/shard_map/ppermute | solution.py:24
  425.6 12.1 %collective-permute-start.22 = (f32[14,1,512]{2,1,0:T(1,128)S(1)}, f32[14,1,512]{2,1,0:T(1,128)S(1)}, u32[]{:S(2)}, u32[]{:S(2)}) collective-permute-start(f32[14,1,512]{2,1,0:T(1,128)S(1)} %get-tuple-element.41), channel_id=1, source_target_pairs={{1,0},{2,1},{3,2},{5,4},{6,5},{7,6},{9,8},{10,9},{11,10},{13,12},{... | collective-permute-start | bytes 86024 | tf_op jit(solution)/shard_map/ppermute | solution.py:27
  427.5 10.2 %collective-permute-start.23 = (f32[14,1,512]{2,1,0:T(1,128)S(1)}, f32[14,1,512]{2,1,0:T(1,128)S(1)}, u32[]{:S(2)}, u32[]{:S(2)}) collective-permute-start(f32[14,1,512]{2,1,0:T(1,128)S(1)} %get-tuple-element.40), channel_id=1, source_target_pairs={{0,1},{1,2},{2,3},{4,5},{5,6},{6,7},{8,9},{9,10},{10,11},{12,13},{... | collective-permute-start | bytes 86024 | tf_op jit(solution)/shard_map/ppermute | solution.py:24
  433.3 5.1 collective-permute-start.2
  435.8 6.5 %collective-permute-start.3 = (f32[18,3,512]{2,0,1:T(8,128)S(1)}, f32[18,3,512]{2,0,1:T(8,128)S(1)}, u32[]{:S(2)}, u32[]{:S(2)}) collective-permute-start(f32[18,3,512]{2,0,1:T(8,128)S(1)} %copy.445), channel_id=1, source_target_pairs={{1,0},{2,1},{3,2},{5,4},{6,5},{7,6},{9,8},{10,9},{11,10},{13,12},{... | collective-permute-start | bytes 331784 | tf_op jit(solution)/shard_map/ppermute | solution.py:27
  457.5 66.5 %copy-start.2 = (f32[12,32,512]{2,1,0:T(8,128)}, f32[12,32,512]{2,1,0:T(8,128)S(1)}, u32[]{:S(2)}) copy-start(f32[12,32,512]{2,1,0:T(8,128)S(1)} %get-tuple-element.11) | copy-start | bytes 2359300
  457.6 10.5 %collective-permute-start.24 = (f32[3,32,512]{2,1,0:T(8,128)S(1)}, f32[3,32,512]{2,1,0:T(8,128)S(1)}, u32[]{:S(2)}, u32[]{:S(2)}) collective-permute-start(f32[3,32,512]{2,1,0:T(8,128)S(1)} %get-tuple-element.50), channel_id=1, source_target_pairs={{0,4},{4,8},{8,12},{12,16},{16,20},{20,24},{24,28},{28,32},{32,36}... | collective-permute-start | bytes 589832 | tf_op jit(solution)/shard_map/ppermute | solution.py:24
  465.5 10.9 %collective-permute-start.25 = (f32[3,32,512]{2,1,0:T(8,128)S(1)}, f32[3,32,512]{2,1,0:T(8,128)S(1)}, u32[]{:S(2)}, u32[]{:S(2)}) collective-permute-start(f32[3,32,512]{2,1,0:T(8,128)S(1)} %get-tuple-element.51), channel_id=1, source_target_pairs={{4,0},{8,4},{12,8},{16,12},{20,16},{24,20},{28,24},{32,28},{36,32}... | collective-permute-start | bytes 589832 | tf_op jit(solution)/shard_map/ppermute | solution.py:27
  476.5 5.9 %collective-permute-start.26 = (f32[18,3,512]{2,0,1:T(8,128)S(1)}, f32[18,3,512]{2,0,1:T(8,128)S(1)}, u32[]{:S(2)}, u32[]{:S(2)}) collective-permute-start(f32[18,3,512]{2,0,1:T(8,128)S(1)} %copy.435), channel_id=1, source_target_pairs={{0,1},{1,2},{2,3},{4,5},{5,6},{6,7},{8,9},{9,10},{10,11},{12,13},{... | collective-permute-start | bytes 331784 | tf_op jit(solution)/shard_map/ppermute | solution.py:24
  480.4 6.5 %collective-permute-start.27 = (f32[18,3,512]{2,0,1:T(8,128)S(1)}, f32[18,3,512]{2,0,1:T(8,128)S(1)}, u32[]{:S(2)}, u32[]{:S(2)}) collective-permute-start(f32[18,3,512]{2,0,1:T(8,128)S(1)} %copy.436), channel_id=1, source_target_pairs={{1,0},{2,1},{3,2},{5,4},{6,5},{7,6},{9,8},{10,9},{11,10},{13,12},{... | collective-permute-start | bytes 331784 | tf_op jit(solution)/shard_map/ppermute | solution.py:27
  500.3 7.9 %collective-permute-start.28 = (f32[3,32,512]{2,1,0:T(8,128)S(1)}, f32[3,32,512]{2,1,0:T(8,128)S(1)}, u32[]{:S(2)}, u32[]{:S(2)}) collective-permute-start(f32[3,32,512]{2,1,0:T(8,128)S(1)} %get-tuple-element.48), channel_id=1, source_target_pairs={{0,4},{4,8},{8,12},{12,16},{16,20},{20,24},{24,28},{28,32},{32,36}... | collective-permute-start | bytes 589832 | tf_op jit(solution)/shard_map/ppermute | solution.py:24
  502.3 10.9 %collective-permute-start.29 = (f32[3,32,512]{2,1,0:T(8,128)S(1)}, f32[3,32,512]{2,1,0:T(8,128)S(1)}, u32[]{:S(2)}, u32[]{:S(2)}) collective-permute-start(f32[3,32,512]{2,1,0:T(8,128)S(1)} %get-tuple-element.49), channel_id=1, source_target_pairs={{4,0},{8,4},{12,8},{16,12},{20,16},{24,20},{28,24},{32,28},{36,32}... | collective-permute-start | bytes 589832 | tf_op jit(solution)/shard_map/ppermute | solution.py:27
  513.3 5.0 collective-permute-start.30
  516.3 6.5 %collective-permute-start.31 = (f32[18,3,512]{2,0,1:T(8,128)S(1)}, f32[18,3,512]{2,0,1:T(8,128)S(1)}, u32[]{:S(2)}, u32[]{:S(2)}) collective-permute-start(f32[18,3,512]{2,0,1:T(8,128)S(1)} %copy.440), channel_id=1, source_target_pairs={{1,0},{2,1},{3,2},{5,4},{6,5},{7,6},{9,8},{10,9},{11,10},{13,12},{... | collective-permute-start | bytes 331784 | tf_op jit(solution)/shard_map/ppermute | solution.py:27
where the time goes:
time: 547 us; the launch traced here: 537 us
  other arithmetic  196 us (36%)
  starting transfers between devices  119 us (22%)
  blocking collectives  86 us (16%)
  waiting for transfers between devices  74.6 us (14%)
  local copies, waits for them, and re-layouts  59.1 us (11%)
    add x5, other arithmetic, apply_taps(): total + taps[k] * lax.slice_in_dim(padded, 1 + k, 1 + k + count, axis=axis)  82.5 us
    ppermute x16, starting transfers between devices, with_halo(): lax.ppermute(lax.slice_in_dim(block, block.shape[dim] - width, None, axis...  77.1 us
    pmax x1, blocking collectives, per_device(): peak = lax.pmax(jnp.max(energy), ('wide', 'narrow'))  67.4 us
    ppermute x16, waiting for transfers between devices, with_halo(): lax.ppermute(lax.slice_in_dim(block, 0, width, axis=dim), axis, backward)  47.3 us
    slice x1, other arithmetic, apply_taps(): total = taps[0] * lax.slice_in_dim(padded, 1, 1 + count, axis=axis)  43.4 us
    ppermute x16, starting transfers between devices, with_halo(): lax.ppermute(lax.slice_in_dim(block, 0, width, axis=dim), axis, backward)  41.9 us
    sub x3, other arithmetic, march_step(): centre - TIME_STEP * (jnp.maximum(speed, 0.0) * jnp.sqrt(grow_plus) + jnp...  38.9 us
    slice x2, local copies, waits for them, and re-layouts, apply_taps(): total = taps[0] * lax.slice_in_dim(padded, 1, 1 + count, axis=axis)  34.7 us
  transfers between devices with their start and end apart: 32, of which 20 were waited for; matrix products, arithmetic and copies ran while one was open for 3% of the time, Pallas kernels for 0%

commit v1 on v0

--- a/solution.py
+++ b/solution.py
@@ -1,19 +1,253 @@
+import functools
 import jax
 import jax.numpy as jnp
 from jax import lax
+from jax.experimental import pallas as pl
+from jax.experimental.pallas import tpu as pltpu
 from jax.sharding import PartitionSpec as P
 
 BZ = 16
 EXT_PASSES = 4
 HJ_STEPS = 3
-
-
 SHEAR = 0.384615
 LAME = 0.576923
 WENO_EPS = 1e-06
 TIME_STEP = 0.3
-VAL_TAPS = (1.0 / 48.0, 23.0 / 48.0, 23.0 / 48.0, 1.0 / 48.0)
-DER_TAPS = (-1.0 / 8.0, -5.0 / 8.0, 5.0 / 8.0, 1.0 / 8.0)
+HALO = EXT_PASSES
+GRAD_SCALE = 1.0 / (8.0 * 48.0 * 48.0)
+
+
+def lane_shifts(value):
+    blocks = [value[:, 128 * b : 128 * (b + 1)] for b in range(value.shape[1] // 128)]
+    lane = lax.broadcasted_iota(jnp.int32, blocks[0].shape, 1)
+    zero = jnp.zeros_like(blocks[0])
+    outs = []
+    for step in (-1, 1, 2):
+        turned = [pltpu.roll(b, (-step) % 128, 1) for b in blocks]
+        if step < 0:
+            mask = lane < 1
+            parts = [jnp.where(mask, turned[i - 1] if i > 0 else zero, turned[i]) for i in range(len(blocks))]
+        else:
+            mask = lane >= 128 - step
+            parts = [
+                jnp.where(mask, turned[i + 1] if i + 1 < len(blocks) else zero, turned[i])
+                for i in range(len(blocks))
+            ]
+        outs.append(jnp.concatenate(parts, axis=1))
+    return outs
+
+
+def val4(a, b, c, d):
+    return (a + d) + 23.0 * (b + c)
+
+
+def der4(a, b, c, d):
+    return (d - a) + 5.0 * (c - b)
+
+
+def strain_kernel(last_ref, u_ref, yh_ref, xh_ref, ch_ref, stiff_ref, msg_ref, plane, filt, energy, turned):
+    load = pl.program_id(0)
+    own_x = u_ref.shape[2]
+    rows = u_ref.shape[3]
+    size_z = u_ref.shape[4]
+    tiles = rows // 8
+    keep = jnp.where(last_ref[0] == 1, 0.0, 1.0)
+
+    def filter_plane(comp, layer, get_plane, low, high0, high1):
+        plane[8 : 8 + rows, :] = get_plane
+        plane[7:8, :] = low
+        plane[8 + rows : 9 + rows, :] = high0
+        plane[9 + rows : 10 + rows, :] = high1
+        for tile in range(tiles):
+            base = 8 + 8 * tile
+            a = plane[base - 1 : base + 7, :]
+            b = plane[base : base + 8, :]
+            c = plane[base + 1 : base + 9, :]
+            d = plane[base + 2 : base + 10, :]
+            val_y = val4(a, b, c, d)
+            der_y = der4(a, b, c, d)
+            before, after, after2 = lane_shifts(val_y)
+            span = pl.ds(8 * tile, 8)
+            filt[comp, 0, layer, span, :] = val4(before, val_y, after, after2)
+            filt[comp, 2, layer, span, :] = der4(before, val_y, after, after2)
+            before, after, after2 = lane_shifts(der_y)
+            filt[comp, 1, layer, span, :] = val4(before, der_y, after, after2)
+
+    def own_layer(layer, carry):
+        for comp in range(3):
+            filter_plane(
+                comp, layer, u_ref[0, comp, layer],
+                yh_ref[0, comp, 0, pl.ds(layer, 1), :],
+                yh_ref[0, comp, 1, pl.ds(layer, 1), :],
+                yh_ref[0, comp, 2, pl.ds(layer, 1), :],
+            )
+        return carry
+
+    lax.fori_loop(0, own_x, own_layer, 0)
+    for k in range(3):
+        for comp in range(3):
+            filter_plane(
+                comp, own_x + k, xh_ref[0, comp, k],
+                ch_ref[0, comp, 0, k : k + 1, :],
+                ch_ref[0, comp, 1, k : k + 1, :],
+                ch_ref[0, comp, 2, k : k + 1, :],
+            )
+
+    def density_at(slot, masked):
+        def field(comp, which, span):
+            out = []
+            for k in range(4):
+                value = filt[comp, which, slot + k, span, :]
+                if masked[k]:
+                    value = value * keep
+                out.append(value)
+            return out
+
+        for tile in range(tiles):
+            span = pl.ds(8 * tile, 8)
+            gx = [der4(*field(comp, 0, span)) for comp in range(3)]
+            gy = [val4(*field(comp, 1, span)) for comp in range(3)]
+            gz = [val4(*field(comp, 2, span)) for comp in range(3)]
+            sxy = gy[0] + gx[1]
+            sxz = gz[0] + gx[2]
+            syz = gz[1] + gy[2]
+            trace = gx[0] + gy[1] + gz[2]
+            square = gx[0] * gx[0] + gy[1] * gy[1] + gz[2] * gz[2]
+            shear = sxy * sxy + sxz * sxz + syz * syz
+            scale = GRAD_SCALE * GRAD_SCALE
+            density = (SHEAR * scale) * (square + 0.5 * shear) + (0.5 * LAME * scale) * (trace * trace)
+
+            @pl.when(load == 0)
+            def _():
+                energy[slot, span, :] = density
+
+            @pl.when(load > 0)
+            def _():
+                energy[slot, span, :] += density
+
+    def slot_step(slot, carry):
+        density_at(slot, (False,) * 4)
+        return carry
+
+    lax.fori_loop(0, own_x - 3, slot_step, 0)
+    density_at(own_x - 3, (False, False, False, True))
+    density_at(own_x - 2, (False, False, True, True))
+    density_at(own_x - 1, (True, False, False, False))
+
+    @pl.when(load == pl.num_programs(0) - 1)
+    def _():
+        peak = jnp.zeros((8, 128), jnp.float32)
+        groups = own_x // 4
+        zeros = jnp.zeros((8, 128), jnp.float32)
+        for g in range(groups):
+            stack = []
+            for q in range(4):
+                value = energy[4 * g + q] * stiff_ref[4 * g + q]
+                stack.append(value)
+                for tile in range(tiles):
+                    for b in range(size_z // 128):
+                        peak = jnp.maximum(peak, value[8 * tile : 8 * tile + 8, 128 * b : 128 * b + 128])
+            turned[g, 0:8, :] = zeros
+            turned[g, size_z : size_z + 16, :] = jnp.zeros((16, 128), jnp.float32)
+            turned[g, HALO : HALO + size_z, :] = jnp.concatenate(stack, axis=0).T
+        peak = jnp.broadcast_to(jnp.max(peak, axis=0, keepdims=True), (8, 128))
+        peak = jnp.broadcast_to(jnp.max(peak, axis=1, keepdims=True), (8, 128))
+        parts = msg_ref.shape[0] // 88
+        own_z = size_z // parts
+        quads = (own_z + 2 * HALO) // 4
+        lane = lax.broadcasted_iota(jnp.int32, (parts, 128), 1) // rows
+        for g in range(groups):
+            for j in range(quads):
+                picked = [turned[g, pl.ds(4 * j + k, parts, stride=own_z), :] for k in range(4)]
+                for q in range(4):
+                    out = None
+                    for k in range(4):
+                        shift = (rows * (k - q)) % 128
+                        part = pltpu.roll(picked[k], shift, 1) if shift else picked[k]
+                        out = part if out is None else jnp.where(lane == k, part, out)
+                    msg_ref[pl.ds(16 * j + 4 * g + q, parts, stride=88), :] = out
+        for t in range(parts):
+            msg_ref[pl.ds(88 * t + 80, 8), :] = peak
+
+
+def strain_message(last, disp, yh, xh, ch, stiff, parts):
+    loads, comps, own_x, rows, size_z = disp.shape
+    block = lambda *shape: pl.BlockSpec((1,) + shape, lambda l: (l,) + (0,) * len(shape))
+    return pl.pallas_call(
+        strain_kernel,
+        grid=(loads,),
+        out_shape=jax.ShapeDtypeStruct((parts * 88, 128), jnp.float32),
+        in_specs=[
+            pl.BlockSpec(memory_space=pltpu.SMEM),
+            block(comps, own_x, rows, size_z),
+            block(comps, 3, own_x, size_z),
+            block(comps, 3, rows, size_z),
+            block(comps, 3, 3, size_z),
+            pl.BlockSpec((own_x, rows, size_z), lambda l: (0, 0, 0)),
+        ],
+        out_specs=pl.BlockSpec((parts * 88, 128), lambda l: (0, 0)),
+        scratch_shapes=[
+            pltpu.VMEM((rows + 16, size_z), jnp.float32),
+            pltpu.VMEM((3, 3, own_x + 3, rows, size_z), jnp.float32),
+            pltpu.VMEM((own_x, rows, size_z), jnp.float32),
+            pltpu.VMEM((own_x // 4, size_z + 16, 128), jnp.float32),
+        ],
+        compiler_params=pltpu.CompilerParams(vmem_limit_bytes=48 * 1024 * 1024),
+    )(last, disp, yh, xh, ch, stiff)
+
+
+def unpack_kernel(recv_ref, tile_ref, peak_ref):
+    parts = recv_ref.shape[0]
+    rows = tile_ref.shape[1]
+    for j in range(tile_ref.shape[0] // 4):
+        block = recv_ref[:, 16 * j : 16 * j + 16, :].reshape(parts * 16, 128)
+        wide = pltpu.roll(block.T, 1, 1)
+        for k in range(4):
+            tile_ref[4 * j + k] = wide[rows * k : rows * (k + 1), :]
+    peak = recv_ref[0, 80:88, :]
+    for s in range(1, parts):
+        peak = jnp.maximum(peak, recv_ref[s, 80:88, :])
+    peak_ref[...] = peak
+
+
+def unpack(recv, own_z, rows):
+    parts = recv.shape[0]
+    return pl.pallas_call(
+        unpack_kernel,
+        out_shape=(
+            jax.ShapeDtypeStruct((own_z + 2 * HALO, rows, parts * 16), jnp.float32),
+            jax.ShapeDtypeStruct((8, 128), jnp.float32),
+        ),
+        compiler_params=pltpu.CompilerParams(vmem_limit_bytes=48 * 1024 * 1024),
+    )(recv)
+
+
+def ring(axis, step):
+    count = lax.axis_size(axis)
+    return [(i, i + step) for i in range(count) if 0 <= i + step < count]
+
+
+def energy_message(displacement, material):
+    wide = lax.axis_size("wide")
+    backward = [(i, (i - 1) % wide) for i in range(wide)]
+    xh = lax.ppermute(displacement[:, :, :3], "wide", backward)
+    low = lax.ppermute(displacement[:, :, :, -1], "narrow", ring("narrow", 1))
+    high = lax.ppermute(
+        jnp.stack([displacement[:, :, :, 0], displacement[:, :, :, 1]], axis=2), "narrow", ring("narrow", -1)
+    )
+    yh = jnp.concatenate([low[:, :, None], high], axis=2)
+    loads, comps, own_x, rows, size_z = displacement.shape
+    blocks = material.shape[2]
+    corner = yh[:, :, :, :3].reshape(loads * comps * 3, 3, size_z)
+    first = material[0].astype(jnp.float32).reshape(-1)
+    first = jnp.pad(first, (0, 3 * size_z - first.size)).reshape(1, 3, size_z)
+    got = lax.ppermute(jnp.concatenate([corner, first], axis=0), "wide", backward)
+    ch = got[: loads * comps * 3].reshape(loads, comps, 3, 3, size_z)
+    beyond = got[loads * comps * 3].reshape(-1)[: rows * blocks].reshape(1, rows, blocks)
+    solid = jnp.concatenate([material[1:].astype(jnp.float32), beyond], axis=0)
+    stiff = 0.2 + 0.8 * jnp.repeat(solid, BZ, axis=2)
+    last = (lax.axis_index("wide") == wide - 1).astype(jnp.int32).reshape(1)
+    return strain_message(last, displacement, yh, xh, ch, stiff, wide)
 
 
 def with_halo(block, sides, width):
@@ -27,26 +261,6 @@
         high = lax.ppermute(lax.slice_in_dim(block, 0, width, axis=dim), axis, backward)
         block = jnp.concatenate([low, block, high], axis=dim)
     return block
-
-
-def apply_taps(padded, taps, axis, count):
-    total = taps[0] * lax.slice_in_dim(padded, 1, 1 + count, axis=axis)
-    for k in range(1, 4):
-        total = total + taps[k] * lax.slice_in_dim(padded, 1 + k, 1 + k + count, axis=axis)
-    return total
-
-
-def strain_energy(grad_x, grad_y, grad_z, stiffness):
-    exx = grad_x[:, 0]
-    eyy = grad_y[:, 1]
-    ezz = grad_z[:, 2]
-    exy = 0.5 * (grad_y[:, 0] + grad_x[:, 1])
-    exz = 0.5 * (grad_z[:, 0] + grad_x[:, 2])
-    eyz = 0.5 * (grad_z[:, 1] + grad_y[:, 2])
-    trace = exx + eyy + ezz
-    square = exx * exx + eyy * eyy + ezz * ezz + 2.0 * (exy * exy + exz * exz + eyz * eyz)
-    density = SHEAR * square + 0.5 * LAME * trace * trace
-    return stiffness * jnp.sum(density, axis=0)
 
 
 def neighbour_mean(padded):
@@ -114,24 +328,13 @@
 
 
 def per_device(displacement, material, level_set):
-    size_x = displacement.shape[2]
-    size_y = displacement.shape[3]
-    size_z = displacement.shape[4]
-    padded = with_halo(displacement, (("wide", 2), ("narrow", 3)), 2)
-    padded = jnp.pad(padded, ((0, 0), (0, 0), (0, 0), (0, 0), (2, 2)))
-    val_z = apply_taps(padded, VAL_TAPS, 4, size_z)
-    der_z = apply_taps(padded, DER_TAPS, 4, size_z)
-    vv = apply_taps(val_z, VAL_TAPS, 3, size_y)
-    vd = apply_taps(val_z, DER_TAPS, 3, size_y)
-    dv = apply_taps(der_z, VAL_TAPS, 3, size_y)
-    grad_x = apply_taps(vv, DER_TAPS, 2, size_x)
-    grad_y = apply_taps(vd, VAL_TAPS, 2, size_x)
-    grad_z = apply_taps(dv, VAL_TAPS, 2, size_x)
-    stiffness = 0.2 + 0.8 * jnp.repeat(material.astype(jnp.float32), BZ, axis=2)
-    energy = strain_energy(grad_x, grad_y, grad_z, stiffness)
-    peak = lax.pmax(jnp.max(energy), ("wide", "narrow"))
-    slab_velocity = jnp.transpose(energy / (peak + 1e-06) - 0.5, (2, 1, 0))
-    velocity = lax.all_to_all(slab_velocity, "wide", split_axis=0, concat_axis=2, tiled=True)
+    wide = lax.axis_size("wide")
+    own_z, rows, size_x = level_set.shape
+    message = energy_message(displacement, material).reshape(wide, 88, 128)
+    recv = lax.all_to_all(message, "wide", split_axis=0, concat_axis=0, tiled=True)
+    tile, wide_peak = unpack(recv, own_z, rows)
+    peak = jnp.max(lax.all_gather(wide_peak, "narrow"))
+    velocity = tile[HALO : HALO + own_z] / (peak + 1e-06) - 0.5
     weight = 1.0 / (1.0 + 4.0 * level_set * level_set)
     speed = velocity
     for step in range(EXT_PASSES):

time: 547 us -> 310 us (0.57); the launches traced: 537 us -> 309 us
  other arithmetic: 196 us -> 48.5 us
  blocking collectives: 86 us -> 28.8 us
  local copies, waits for them, and re-layouts: 59.1 us -> 11.1 us
  Pallas kernels: 0 us -> 31.5 us
  starting transfers between devices: 119 us -> 105 us
  waiting for transfers between devices: 74.6 us -> 82.1 us
    add x6 -> x1, other arithmetic: 82.5 us -> 0.04 us  [energy_message(): stiff = 0.2 + 0.8 * jnp.repeat(solid, BZ, axis=2)]
    pmax x1 -> x0, blocking collectives: 67.4 us -> none  [per_device(): peak = lax.pmax(jnp.max(energy), ('wide', 'narrow'))]
    slice x1 -> x0, other arithmetic: 43.4 us -> none  [apply_taps(): total = taps[0] * lax.slice_in_dim(padded, 1, 1 + count, axis=axis)]
    pallas_call x0 -> x2, Pallas kernels: none -> 31.5 us  [the longest x1 30.7 us: strain_message(): pl.pallas_call(strain_kernel, grid=(loads,), out_shape=jax.ShapeDtypeStru...]
    ppermute x0 -> x4, waiting for transfers between devices: none -> 30.2 us  [the longest x1 22.6 us: energy_message(): low = lax.ppermute(displacement[:, :, :, -1], 'narrow', ring('narrow', 1))]
    slice x2 -> x4, local copies, waits for them, and re-layouts: 34.7 us -> 5.59 us  [the longest x1 3.07 us: energy_message(): displacement[:, :, :, 0]]
    ppermute x16 -> x14, starting transfers between devices: 77.1 us -> 48.2 us  [with_halo(): lax.ppermute(lax.slice_in_dim(block, block.shape[dim] - width, None, axis...]
    ppermute x16 -> x14, waiting for transfers between devices: 27.3 us -> 2.5 us  [with_halo(): lax.ppermute(lax.slice_in_dim(block, block.shape[dim] - width, None, axis...]
  transfers between devices with their start and end apart: 32 -> 32, of which waited for: 20 -> 18; matrix products, arithmetic and copies ran while one was open for 3% -> 4% of each run, Pallas kernels for 0% -> 0%
where the time goes in v1:
time: 310 us; the launch traced here: 309 us
  starting transfers between devices  105 us (34%)
  waiting for transfers between devices  82.1 us (26%)
  other arithmetic  48.5 us (16%)
  Pallas kernels  31.5 us (10%)
  blocking collectives  28.8 us (9%)
  local copies, waits for them, and re-layouts  11.1 us (4%)
    ppermute x14, waiting for transfers between devices, with_halo(): lax.ppermute(lax.slice_in_dim(block, 0, width, axis=dim), axis, backward)  49.4 us
    ppermute x14, starting transfers between devices, with_halo(): lax.ppermute(lax.slice_in_dim(block, block.shape[dim] - width, None, axis...  48.2 us
    ppermute x14, starting transfers between devices, with_halo(): lax.ppermute(lax.slice_in_dim(block, 0, width, axis=dim), axis, backward)  42.8 us
    sub x3, other arithmetic, march_step(): centre - TIME_STEP * (jnp.maximum(speed, 0.0) * jnp.sqrt(grow_plus) + jnp...  38.8 us
    pallas_call x1, Pallas kernels, strain_message(): pl.pallas_call(strain_kernel, grid=(loads,), out_shape=jax.ShapeDtypeStru...  30.7 us
    all_to_all x1, blocking collectives, per_device(): lax.all_to_all(message, 'wide', split_axis=0, concat_axis=0, tiled=True)  23.1 us
    ppermute x1, waiting for transfers between devices, energy_message(): low = lax.ppermute(displacement[:, :, :, -1], 'narrow', ring('narrow', 1))  22.6 us
    ppermute x1, starting transfers between devices, energy_message(): lax.ppermute(jnp.concatenate([corner, first], axis=0), 'wide', backward)  7.06 us
  transfers between devices with their start and end apart: 32, of which 18 were waited for; matrix products, arithmetic and copies ran while one was open for 4% of the time, Pallas kernels for 0%

profile of v1, /device:TPU:23, one launch (start us, length us, event | category | flops | bytes accessed | tf_op | source)
XLA Modules:
  0.0 308.9 jit_solution(11895890195512160966)
XLA Ops:
  0.6 2.5 slice.498
  3.2 3.1 fusion.34
  6.3 4.8 %collective-permute-start.4 = (f32[3,3,16,384]{3,2,1,0:T(8,128)S(1)}, f32[3,3,16,384]{3,2,1,0:T(8,128)S(1)}, u32[]{:S(2)}, u32[]{:S(2)}) collective-permute-start(f32[3,3,16,384]{3,2,1,0:T(8,128)S(1)} %bitcast.19), channel_id=1, source_target_pairs={{0,1},{1,2},{2,3},{4,5},{5,6},{6,7},{8,9},{9,10},{10,11},{12,13},{... | collective-permute-start | bytes 663560 | tf_op jit(solution)/shard_map/ppermute | solution.py:234
  11.2 1.9 collective-permute-start.5
  13.3 22.6 %collective-permute-done.4 = f32[3,3,16,384]{3,2,1,0:T(8,128)S(1)} collective-permute-done((f32[3,3,16,384]{3,2,1,0:T(8,128)S(1)}, f32[3,3,16,384]{3,2,1,0:T(8,128)S(1)}, u32[]{:S(2)}, u32[]{:S(2)}) %collective-permute-start.4) | collective-permute-done | bytes 221216 | tf_op jit(solution)/shard_map/ppermute | solution.py:234
  35.9 5.3 %collective-permute-done.5 = f32[3,3,2,16,384]{4,3,2,1,0:T(8,128)S(1)} collective-permute-done((f32[3,3,2,16,384]{4,3,2,1,0:T(8,128)S(1)}, f32[3,3,2,16,384]{4,3,2,1,0:T(8,128)S(1)}, u32[]{:S(2)}, u32[]{:S(2)}) %collective-permute-start.5) | collective-permute-done | bytes 442400 | tf_op jit(solution)/shard_map/ppermute | solution.py:235
  41.3 7.1 %collective-permute-start.7 = (f32[28,3,384]{2,1,0:T(4,128)S(1)}, f32[28,3,384]{2,1,0:T(4,128)S(1)}, u32[]{:S(2)}, u32[]{:S(2)}) collective-permute-start(f32[28,3,384]{2,1,0:T(4,128)S(1)} %pad_maximum_fusion.34), channel_id=1, source_target_pairs={{0,124},{4,0},{8,4},{12,8},{16,12},{20,16},{24,20},{28,24},{32,28}... | collective-permute-start | bytes 387080 | tf_op jit(solution)/shard_map/ppermute | solution.py:244
  48.4 2.3 collective-permute-done.7
  51.0 1.9 broadcast_in_dim.35
  52.8 2.3 copy.14.stiff_ref
  55.2 30.7 %shard_map.50 = f32[2816,128]{1,0:T(8,128)S(1)} custom-call(s32[1]{0:T(128)} %bitcast.last_ref, f32[3,3,16,32,384]{4,3,2,1,0:T(8,128)} %u_ref.1, f32[3,3,3,16,384]{4,3,2,1,0:T(8,128)S(1)} %pad_maximum_fusion.yh_ref, f32[3,3,3,32,384]{4,3,2,1,0:T(8,128)S(1)} %collective-permute-done.6.xh_ref, f32[3,3,3,3,384]{4,3,2,1,0:T(4,128)S(1)} %bitcast.14, ...), custom_call_target="tpu_custom_call" | custom-call | tf_op jit(solution)/shard_map/pallas_call | solution.py:176
  85.9 23.1 %all_to_all.5.recv_ref = f32[32,88,128]{2,1,0:T(8,128)S(1)} all-to-all(f32[32,88,128]{2,1,0:T(8,128)S(1)} %bitcast.13), channel_id=1, replica_groups=mesh['wide'=32,'narrow'=4] {'wide'}, dimensions={0} | all-to-all | bytes 2883584 | tf_op jit(solution)/shard_map/all_to_all | solution.py:334
  109.0 0.8 shard_map.51
  109.8 5.7 %all-gather = f32[32,128]{1,0:T(8,128)S(1)} all-gather(f32[8,128]{1,0:T(8,128)S(1)} %get-tuple-element.5), channel_id=2, replica_groups=mesh['wide'=32,'narrow'=4] {'narrow'}, dimensions={0}, use_global_device_ids=true | all-gather | bytes 20480 | tf_op jit(solution)/shard_map/all_gather | solution.py:336
  116.8 4.1 %collective-permute-start.9 = (f32[1,32,512]{2,1,0:T(8,128)S(1)}, f32[1,32,512]{2,1,0:T(8,128)S(1)}, u32[]{:S(2)}, u32[]{:S(2)}) collective-permute-start(f32[1,32,512]{2,1,0:T(8,128)S(1)} %get-tuple-element.37), channel_id=1, source_target_pairs={{0,4},{4,8},{8,12},{12,16},{16,20},{20,24},{24,28},{28,32},{32,36}... | collective-permute-start | bytes 196616 | tf_op jit(solution)/shard_map/ppermute | solution.py:258
  120.9 2.7 collective-permute-start.8
  123.7 6.7 %collective-permute-done.8 = f32[1,32,512]{2,1,0:T(8,128)S(1)} collective-permute-done((f32[1,32,512]{2,1,0:T(8,128)S(1)}, f32[1,32,512]{2,1,0:T(8,128)S(1)}, u32[]{:S(2)}, u32[]{:S(2)}) %collective-permute-start.8) | collective-permute-done | bytes 65568 | tf_op jit(solution)/shard_map/ppermute | solution.py:261
  130.5 5.7 %collective-permute-start.11 = (f32[14,1,512]{2,1,0:T(1,128)S(1)}, f32[14,1,512]{2,1,0:T(1,128)S(1)}, u32[]{:S(2)}, u32[]{:S(2)}) collective-permute-start(f32[14,1,512]{2,1,0:T(1,128)S(1)} %get-tuple-element.23), channel_id=1, source_target_pairs={{0,1},{1,2},{2,3},{4,5},{5,6},{6,7},{8,9},{9,10},{10,11},{12,13},{... | collective-permute-start | bytes 86024 | tf_op jit(solution)/shard_map/ppermute | solution.py:258
  136.2 1.9 collective-permute-start.10
  138.1 0.8 fusion.42
  138.9 1.9 collective-permute-start.1
  140.8 7.9 %collective-permute-start = (f32[3,32,512]{2,1,0:T(8,128)}, f32[3,32,512]{2,1,0:T(8,128)S(1)}, u32[]{:S(2)}, u32[]{:S(2)}) collective-permute-start(f32[3,32,512]{2,1,0:T(8,128)} %get-tuple-element.40), channel_id=1, source_target_pairs={{0,4},{4,8},{8,12},{12,16},{16,20},{20,24},{24,28},{28,32},{32,36}... | collective-permute-start | bytes 589832 | tf_op jit(solution)/shard_map/ppermute | solution.py:258
  148.7 0.6 select_maximum_fusion.12
  149.4 0.7 fusion.26
  150.1 1.9 collective-permute-start.13
  152.0 4.9 %collective-permute-start.12 = (f32[1,32,512]{2,1,0:T(8,128)S(1)}, f32[1,32,512]{2,1,0:T(8,128)S(1)}, u32[]{:S(2)}, u32[]{:S(2)}) collective-permute-start(f32[1,32,512]{2,1,0:T(8,128)S(1)} %get-tuple-element.36), channel_id=1, source_target_pairs={{4,0},{8,4},{12,8},{16,12},{20,16},{24,20},{28,24},{32,28},{36,32}... | collective-permute-start | bytes 196616 | tf_op jit(solution)/shard_map/ppermute | solution.py:261
  156.9 4.6 %collective-permute-done.12 = f32[1,32,512]{2,1,0:T(8,128)S(1)} collective-permute-done((f32[1,32,512]{2,1,0:T(8,128)S(1)}, f32[1,32,512]{2,1,0:T(8,128)S(1)}, u32[]{:S(2)}, u32[]{:S(2)}) %collective-permute-start.12) | collective-permute-done | bytes 65568 | tf_op jit(solution)/shard_map/ppermute | solution.py:261
  161.6 5.4 %collective-permute-start.15 = (f32[14,1,512]{2,1,0:T(1,128)S(1)}, f32[14,1,512]{2,1,0:T(1,128)S(1)}, u32[]{:S(2)}, u32[]{:S(2)}) collective-permute-start(f32[14,1,512]{2,1,0:T(1,128)S(1)} %get-tuple-element.21), channel_id=1, source_target_pairs={{0,1},{1,2},{2,3},{4,5},{5,6},{6,7},{8,9},{9,10},{10,11},{12,13},{... | collective-permute-start | bytes 86024 | tf_op jit(solution)/shard_map/ppermute | solution.py:258
  167.0 1.9 collective-permute-start.14
  168.9 3.2 %collective-permute-done.14 = f32[14,1,512]{2,1,0:T(1,128)S(1)} collective-permute-done((f32[14,1,512]{2,1,0:T(1,128)S(1)}, f32[14,1,512]{2,1,0:T(1,128)S(1)}, u32[]{:S(2)}, u32[]{:S(2)}) %collective-permute-start.14) | collective-permute-done | bytes 28704 | tf_op jit(solution)/shard_map/ppermute | solution.py:261
  172.8 0.8 fusion.20
  173.6 1.9 collective-permute-start.17
  175.5 4.9 %collective-permute-start.16 = (f32[1,32,512]{2,1,0:T(8,128)S(1)}, f32[1,32,512]{2,1,0:T(8,128)S(1)}, u32[]{:S(2)}, u32[]{:S(2)}) collective-permute-start(f32[1,32,512]{2,1,0:T(8,128)S(1)} %get-tuple-element.34), channel_id=1, source_target_pairs={{4,0},{8,4},{12,8},{16,12},{20,16},{24,20},{28,24},{32,28},{36,32}... | collective-permute-start | bytes 196616 | tf_op jit(solution)/shard_map/ppermute | solution.py:261
  180.5 4.6 %collective-permute-done.16 = f32[1,32,512]{2,1,0:T(8,128)S(1)} collective-permute-done((f32[1,32,512]{2,1,0:T(8,128)S(1)}, f32[1,32,512]{2,1,0:T(8,128)S(1)}, u32[]{:S(2)}, u32[]{:S(2)}) %collective-permute-start.16) | collective-permute-done | bytes 65568 | tf_op jit(solution)/shard_map/ppermute | solution.py:261
  185.1 3.1 collective-permute-start.19
  188.2 2.1 collective-permute-start.18
  190.3 3.0 collective-permute-done.18
  194.0 0.8 fusion.14
  194.8 1.9 collective-permute-start.21
  196.7 4.9 %collective-permute-start.20 = (f32[1,32,512]{2,1,0:T(8,128)S(1)}, f32[1,32,512]{2,1,0:T(8,128)S(1)}, u32[]{:S(2)}, u32[]{:S(2)}) collective-permute-start(f32[1,32,512]{2,1,0:T(8,128)S(1)} %get-tuple-element.30), channel_id=1, source_target_pairs={{4,0},{8,4},{12,8},{16,12},{20,16},{24,20},{28,24},{32,28},{36,32}... | collective-permute-start | bytes 196616 | tf_op jit(solution)/shard_map/ppermute | solution.py:261
  201.6 4.6 %collective-permute-done.20 = f32[1,32,512]{2,1,0:T(8,128)S(1)} collective-permute-done((f32[1,32,512]{2,1,0:T(8,128)S(1)}, f32[1,32,512]{2,1,0:T(8,128)S(1)}, u32[]{:S(2)}, u32[]{:S(2)}) %collective-permute-start.20) | collective-permute-done | bytes 65568 | tf_op jit(solution)/shard_map/ppermute | solution.py:261
  206.3 3.1 collective-permute-start.23
  209.4 1.9 collective-permute-start.22
  211.4 3.6 %collective-permute-start.2 = (f32[18,3,512]{2,1,0:T(4,128)S(1)}, f32[18,3,512]{2,1,0:T(4,128)S(1)}, u32[]{:S(2)}, u32[]{:S(2)}) collective-permute-start(f32[18,3,512]{2,1,0:T(4,128)S(1)} %get-tuple-element.15), channel_id=1, source_target_pairs={{0,1},{1,2},{2,3},{4,5},{5,6},{6,7},{8,9},{9,10},{10,11},{12,13},{... | collective-permute-start | bytes 331784 | tf_op jit(solution)/shard_map/ppermute | solution.py:258
  215.0 1.9 collective-permute-start.3
  217.0 0.6 select_maximum_fusion
  217.6 3.9 %collective-permute-done.3 = f32[18,3,512]{2,1,0:T(4,128)S(1)} collective-permute-done((f32[18,3,512]{2,1,0:T(4,128)S(1)}, f32[18,3,512]{2,1,0:T(4,128)S(1)}, u32[]{:S(2)}, u32[]{:S(2)}) %collective-permute-start.3) | collective-permute-done | bytes 110624 | tf_op jit(solution)/shard_map/ppermute | solution.py:261
  222.7 13.9 %slice_subtract_fusion.8 = (f32[12,32,512]{2,1,0:T(8,128)S(1)}, f32[12,32,512]{2,1,0:T(8,128)S(1)}) fusion(f32[18,38,512]{2,1,0:T(8,128)S(1)} %maximum_select_fusion, f32[12,32,517]{2,1,0:T(8,128)S(1)} %fusion.1, f32[12,37,512]{2,1,0:T(8,128)S(1)} %slice_subtract_fusion.5, f32[17,32,512]{2,1,0:T(8,128)S(1)} %slice_subtract_fusion.2, ...), kind=kLoop, calls=%fused_computation.108 | loop fusion | flops 85917696 | bytes 20635652 | tf_op jit(solution)/shard_map/sub | solution.py:313
  236.7 1.9 collective-permute-start.24
  238.6 4.9 %collective-permute-start.25 = (f32[3,32,512]{2,1,0:T(8,128)S(1)}, f32[3,32,512]{2,1,0:T(8,128)S(1)}, u32[]{:S(2)}, u32[]{:S(2)}) collective-permute-start(f32[3,32,512]{2,1,0:T(8,128)S(1)} %get-tuple-element.28), channel_id=1, source_target_pairs={{4,0},{8,4},{12,8},{16,12},{20,16},{24,20},{28,24},{32,28},{36,32}... | collective-permute-start | bytes 589832 | tf_op jit(solution)/shard_map/ppermute | solution.py:261
  243.5 1.1 collective-permute-done.24
  244.6 5.0 %collective-permute-done.25 = f32[3,32,512]{2,1,0:T(8,128)S(1)} collective-permute-done((f32[3,32,512]{2,1,0:T(8,128)S(1)}, f32[3,32,512]{2,1,0:T(8,128)S(1)}, u32[]{:S(2)}, u32[]{:S(2)}) %collective-permute-start.25) | collective-permute-done | bytes 196640 | tf_op jit(solution)/shard_map/ppermute | solution.py:261
  249.7 2.9 collective-permute-start.26
  252.6 1.9 collective-permute-start.27
  254.7 4.4 %collective-permute-done.27 = f32[18,3,512]{2,1,0:T(4,128)S(1)} collective-permute-done((f32[18,3,512]{2,1,0:T(4,128)S(1)}, f32[18,3,512]{2,1,0:T(4,128)S(1)}, u32[]{:S(2)}, u32[]{:S(2)}) %collective-permute-start.27) | collective-permute-done | bytes 110624 | tf_op jit(solution)/shard_map/ppermute | solution.py:261
  260.3 12.1 %slice_subtract_fusion.7 = f32[12,32,512]{2,1,0:T(8,128)S(1)} fusion(f32[18,38,512]{2,1,0:T(8,128)S(1)} %maximum_select_fusion.1, f32[12,32,517]{2,1,0:T(8,128)S(1)} %fusion.2, f32[12,37,512]{2,1,0:T(8,128)S(1)} %slice_subtract_fusion.4, f32[17,32,512]{2,1,0:T(8,128)S(1)} %slice_subtract_fusion.1, f32[12,32,512]{2,1,0:T(8,128)S(1)} %get-tuple-element.7), kind=kLoop, calls=%fused_computation.43 | loop fusion | flops 81199104 | bytes 16515072 | tf_op jit(solution)/shard_map/sub | solution.py:313
  272.5 1.9 collective-permute-start.28
  274.4 4.9 %collective-permute-start.29 = (f32[3,32,512]{2,1,0:T(8,128)S(1)}, f32[3,32,512]{2,1,0:T(8,128)S(1)}, u32[]{:S(2)}, u32[]{:S(2)}) collective-permute-start(f32[3,32,512]{2,1,0:T(8,128)S(1)} %get-tuple-element.26), channel_id=1, source_target_pairs={{4,0},{8,4},{12,8},{16,12},{20,16},{24,20},{28,24},{32,28},{36,32}... | collective-permute-start | bytes 589832 | tf_op jit(solution)/shard_map/ppermute | solution.py:261
  279.3 1.1 collective-permute-done.28
  280.4 5.0 %collective-permute-done.29 = f32[3,32,512]{2,1,0:T(8,128)S(1)} collective-permute-done((f32[3,32,512]{2,1,0:T(8,128)S(1)}, f32[3,32,512]{2,1,0:T(8,128)S(1)}, u32[]{:S(2)}, u32[]{:S(2)}) %collective-permute-start.29) | collective-permute-done | bytes 196640 | tf_op jit(solution)/shard_map/ppermute | solution.py:261
  285.5 2.9 collective-permute-start.30
  288.4 2.1 collective-permute-start.31
  290.5 4.3 %collective-permute-done.31 = f32[18,3,512]{2,1,0:T(4,128)S(1)} collective-permute-done((f32[18,3,512]{2,1,0:T(4,128)S(1)}, f32[18,3,512]{2,1,0:T(4,128)S(1)}, u32[]{:S(2)}, u32[]{:S(2)}) %collective-permute-start.31) | collective-permute-done | bytes 110624 | tf_op jit(solution)/shard_map/ppermute | solution.py:261
  296.1 12.8 %slice_subtract_fusion.6 = f32[12,32,512]{2,1,0:T(8,128)} fusion(f32[18,38,512]{2,1,0:T(8,128)S(1)} %maximum_select_fusion.2, f32[12,32,517]{2,1,0:T(8,128)S(1)} %fusion.3, f32[12,37,512]{2,1,0:T(8,128)S(1)} %slice_subtract_fusion.3, f32[17,32,512]{2,1,0:T(8,128)S(1)} %slice_subtract_fusion, f32[12,32,512]{2,1,0:T(8,128)S(1)} %get-tuple-element.7), kind=kLoop, calls=%fused_computation.42 | loop fusion | flops 81199104 | bytes 16515072 | tf_op jit(solution)/shard_map/sub | solution.py:313
  (74 shorter events, 7.2 us)
Async XLA Ops:
  3.1 52.1 %collective-permute-start.6 = (f32[3,3,3,32,384]{4,3,2,1,0:T(8,128)}, f32[3,3,3,32,384]{4,3,2,1,0:T(8,128)S(1)}, u32[]{:S(2)}, u32[]{:S(2)}) collective-permute-start(f32[3,3,3,32,384]{4,3,2,1,0:T(8,128)} %slice.498), channel_id=1, source_target_pairs={{0,124},{4,0},{8,4},{12,8},{16,12},{20,16},{24,20},{28,24},{32,28}... | collective-permute-start | bytes 3981320 | tf_op jit(solution)/shard_map/ppermute | solution.py:233
  6.2 6.9 %copy-start.2 = (s32[16,32,24]{1,2,0:T(8,128)S(1)}, s32[16,32,24]{1,2,0:T(8,128)}, u32[]{:S(2)}) copy-start(s32[16,32,24]{1,2,0:T(8,128)} %param.4) | copy-start | bytes 147460
  6.3 29.6 %collective-permute-start.4 = (f32[3,3,16,384]{3,2,1,0:T(8,128)S(1)}, f32[3,3,16,384]{3,2,1,0:T(8,128)S(1)}, u32[]{:S(2)}, u32[]{:S(2)}) collective-permute-start(f32[3,3,16,384]{3,2,1,0:T(8,128)S(1)} %bitcast.19), channel_id=1, source_target_pairs={{0,1},{1,2},{2,3},{4,5},{5,6},{6,7},{8,9},{9,10},{10,11},{12,13},{... | collective-permute-start | bytes 663560 | tf_op jit(solution)/shard_map/ppermute | solution.py:234
  11.2 30.1 %collective-permute-start.5 = (f32[3,3,2,16,384]{4,3,2,1,0:T(8,128)S(1)}, f32[3,3,2,16,384]{4,3,2,1,0:T(8,128)S(1)}, u32[]{:S(2)}, u32[]{:S(2)}) collective-permute-start(f32[3,3,2,16,384]{4,3,2,1,0:T(8,128)S(1)} %pad_maximum_fusion.33), channel_id=1, source_target_pairs={{1,0},{2,1},{3,2},{5,4},{6,5},{7,6},{9,8},{10,9},{11,10},{13,12},{... | collective-permute-start | bytes 1327112 | tf_op jit(solution)/shard_map/ppermute | solution.py:235
  41.3 9.4 %collective-permute-start.7 = (f32[28,3,384]{2,1,0:T(4,128)S(1)}, f32[28,3,384]{2,1,0:T(4,128)S(1)}, u32[]{:S(2)}, u32[]{:S(2)}) collective-permute-start(f32[28,3,384]{2,1,0:T(4,128)S(1)} %pad_maximum_fusion.34), channel_id=1, source_target_pairs={{0,124},{4,0},{8,4},{12,8},{16,12},{20,16},{24,20},{28,24},{32,28}... | collective-permute-start | bytes 387080 | tf_op jit(solution)/shard_map/ppermute | solution.py:244
  109.8 28.4 %copy-start = (f32[12,32,512]{2,1,0:T(8,128)S(1)}, f32[12,32,512]{2,1,0:T(8,128)}, u32[]{:S(2)}) copy-start(f32[12,32,512]{2,1,0:T(8,128)} %param.5) | copy-start | bytes 2359300
  116.8 6.9 %collective-permute-start.9 = (f32[1,32,512]{2,1,0:T(8,128)S(1)}, f32[1,32,512]{2,1,0:T(8,128)S(1)}, u32[]{:S(2)}, u32[]{:S(2)}) collective-permute-start(f32[1,32,512]{2,1,0:T(8,128)S(1)} %get-tuple-element.37), channel_id=1, source_target_pairs={{0,4},{4,8},{8,12},{12,16},{16,20},{20,24},{24,28},{28,32},{32,36}... | collective-permute-start | bytes 196616 | tf_op jit(solution)/shard_map/ppermute | solution.py:258
  120.9 9.5 %collective-permute-start.8 = (f32[1,32,512]{2,1,0:T(8,128)S(1)}, f32[1,32,512]{2,1,0:T(8,128)S(1)}, u32[]{:S(2)}, u32[]{:S(2)}) collective-permute-start(f32[1,32,512]{2,1,0:T(8,128)S(1)} %get-tuple-element.38), channel_id=1, source_target_pairs={{4,0},{8,4},{12,8},{16,12},{20,16},{24,20},{28,24},{32,28},{36,32}... | collective-permute-start | bytes 196616 | tf_op jit(solution)/shard_map/ppermute | solution.py:261
  130.5 18.2 %collective-permute-start.11 = (f32[14,1,512]{2,1,0:T(1,128)S(1)}, f32[14,1,512]{2,1,0:T(1,128)S(1)}, u32[]{:S(2)}, u32[]{:S(2)}) collective-permute-start(f32[14,1,512]{2,1,0:T(1,128)S(1)} %get-tuple-element.23), channel_id=1, source_target_pairs={{0,1},{1,2},{2,3},{4,5},{5,6},{6,7},{8,9},{9,10},{10,11},{12,13},{... | collective-permute-start | bytes 86024 | tf_op jit(solution)/shard_map/ppermute | solution.py:258
  136.2 12.5 %collective-permute-start.10 = (f32[14,1,512]{2,1,0:T(1,128)S(1)}, f32[14,1,512]{2,1,0:T(1,128)S(1)}, u32[]{:S(2)}, u32[]{:S(2)}) collective-permute-start(f32[14,1,512]{2,1,0:T(1,128)S(1)} %get-tuple-element.24), channel_id=1, source_target_pairs={{1,0},{2,1},{3,2},{5,4},{6,5},{7,6},{9,8},{10,9},{11,10},{13,12},{... | collective-permute-start | bytes 86024 | tf_op jit(solution)/shard_map/ppermute | solution.py:261
  138.9 62.7 %collective-permute-start.1 = (f32[3,32,512]{2,1,0:T(8,128)}, f32[3,32,512]{2,1,0:T(8,128)S(1)}, u32[]{:S(2)}, u32[]{:S(2)}) collective-permute-start(f32[3,32,512]{2,1,0:T(8,128)} %get-tuple-element.39), channel_id=1, source_target_pairs={{4,0},{8,4},{12,8},{16,12},{20,16},{24,20},{28,24},{32,28},{36,32}... | collective-permute-start | bytes 589832 | tf_op jit(solution)/shard_map/ppermute | solution.py:261
  140.8 49.4 %collective-permute-start = (f32[3,32,512]{2,1,0:T(8,128)}, f32[3,32,512]{2,1,0:T(8,128)S(1)}, u32[]{:S(2)}, u32[]{:S(2)}) collective-permute-start(f32[3,32,512]{2,1,0:T(8,128)} %get-tuple-element.40), channel_id=1, source_target_pairs={{0,4},{4,8},{8,12},{12,16},{16,20},{20,24},{24,28},{28,32},{32,36}... | collective-permute-start | bytes 589832 | tf_op jit(solution)/shard_map/ppermute | solution.py:258
  150.1 6.8 %collective-permute-start.13 = (f32[1,32,512]{2,1,0:T(8,128)S(1)}, f32[1,32,512]{2,1,0:T(8,128)S(1)}, u32[]{:S(2)}, u32[]{:S(2)}) collective-permute-start(f32[1,32,512]{2,1,0:T(8,128)S(1)} %get-tuple-element.35), channel_id=1, source_target_pairs={{0,4},{4,8},{8,12},{12,16},{16,20},{20,24},{24,28},{28,32},{32,36}... | collective-permute-start | bytes 196616 | tf_op jit(solution)/shard_map/ppermute | solution.py:258
  152.0 9.5 %collective-permute-start.12 = (f32[1,32,512]{2,1,0:T(8,128)S(1)}, f32[1,32,512]{2,1,0:T(8,128)S(1)}, u32[]{:S(2)}, u32[]{:S(2)}) collective-permute-start(f32[1,32,512]{2,1,0:T(8,128)S(1)} %get-tuple-element.36), channel_id=1, source_target_pairs={{4,0},{8,4},{12,8},{16,12},{20,16},{24,20},{28,24},{32,28},{36,32}... | collective-permute-start | bytes 196616 | tf_op jit(solution)/shard_map/ppermute | solution.py:261
  161.6 7.3 %collective-permute-start.15 = (f32[14,1,512]{2,1,0:T(1,128)S(1)}, f32[14,1,512]{2,1,0:T(1,128)S(1)}, u32[]{:S(2)}, u32[]{:S(2)}) collective-permute-start(f32[14,1,512]{2,1,0:T(1,128)S(1)} %get-tuple-element.21), channel_id=1, source_target_pairs={{0,1},{1,2},{2,3},{4,5},{5,6},{6,7},{8,9},{9,10},{10,11},{12,13},{... | collective-permute-start | bytes 86024 | tf_op jit(solution)/shard_map/ppermute | solution.py:258
  167.0 5.2 %collective-permute-start.14 = (f32[14,1,512]{2,1,0:T(1,128)S(1)}, f32[14,1,512]{2,1,0:T(1,128)S(1)}, u32[]{:S(2)}, u32[]{:S(2)}) collective-permute-start(f32[14,1,512]{2,1,0:T(1,128)S(1)} %get-tuple-element.22), channel_id=1, source_target_pairs={{1,0},{2,1},{3,2},{5,4},{6,5},{7,6},{9,8},{10,9},{11,10},{13,12},{... | collective-permute-start | bytes 86024 | tf_op jit(solution)/shard_map/ppermute | solution.py:261
  173.6 6.9 %collective-permute-start.17 = (f32[1,32,512]{2,1,0:T(8,128)S(1)}, f32[1,32,512]{2,1,0:T(8,128)S(1)}, u32[]{:S(2)}, u32[]{:S(2)}) collective-permute-start(f32[1,32,512]{2,1,0:T(8,128)S(1)} %get-tuple-element.33), channel_id=1, source_target_pairs={{0,4},{4,8},{8,12},{12,16},{16,20},{20,24},{24,28},{28,32},{32,36}... | collective-permute-start | bytes 196616 | tf_op jit(solution)/shard_map/ppermute | solution.py:258
  175.5 9.5 %collective-permute-start.16 = (f32[1,32,512]{2,1,0:T(8,128)S(1)}, f32[1,32,512]{2,1,0:T(8,128)S(1)}, u32[]{:S(2)}, u32[]{:S(2)}) collective-permute-start(f32[1,32,512]{2,1,0:T(8,128)S(1)} %get-tuple-element.34), channel_id=1, source_target_pairs={{4,0},{8,4},{12,8},{16,12},{20,16},{24,20},{28,24},{32,28},{36,32}... | collective-permute-start | bytes 196616 | tf_op jit(solution)/shard_map/ppermute | solution.py:261
  185.1 5.2 %collective-permute-start.19 = (f32[14,1,512]{2,1,0:T(1,128)S(1)}, f32[14,1,512]{2,1,0:T(1,128)S(1)}, u32[]{:S(2)}, u32[]{:S(2)}) collective-permute-start(f32[14,1,512]{2,1,0:T(1,128)S(1)} %get-tuple-element.19), channel_id=1, source_target_pairs={{0,1},{1,2},{2,3},{4,5},{5,6},{6,7},{8,9},{9,10},{10,11},{12,13},{... | collective-permute-start | bytes 86024 | tf_op jit(solution)/shard_map/ppermute | solution.py:258
  188.2 5.2 %collective-permute-start.18 = (f32[14,1,512]{2,1,0:T(1,128)S(1)}, f32[14,1,512]{2,1,0:T(1,128)S(1)}, u32[]{:S(2)}, u32[]{:S(2)}) collective-permute-start(f32[14,1,512]{2,1,0:T(1,128)S(1)} %get-tuple-element.20), channel_id=1, source_target_pairs={{1,0},{2,1},{3,2},{5,4},{6,5},{7,6},{9,8},{10,9},{11,10},{13,12},{... | collective-permute-start | bytes 86024 | tf_op jit(solution)/shard_map/ppermute | solution.py:261
  194.8 6.8 %collective-permute-start.21 = (f32[1,32,512]{2,1,0:T(8,128)S(1)}, f32[1,32,512]{2,1,0:T(8,128)S(1)}, u32[]{:S(2)}, u32[]{:S(2)}) collective-permute-start(f32[1,32,512]{2,1,0:T(8,128)S(1)} %get-tuple-element.29), channel_id=1, source_target_pairs={{0,4},{4,8},{8,12},{12,16},{16,20},{20,24},{24,28},{28,32},{32,36}... | collective-permute-start | bytes 196616 | tf_op jit(solution)/shard_map/ppermute | solution.py:258
  196.7 9.5 %collective-permute-start.20 = (f32[1,32,512]{2,1,0:T(8,128)S(1)}, f32[1,32,512]{2,1,0:T(8,128)S(1)}, u32[]{:S(2)}, u32[]{:S(2)}) collective-permute-start(f32[1,32,512]{2,1,0:T(8,128)S(1)} %get-tuple-element.30), channel_id=1, source_target_pairs={{4,0},{8,4},{12,8},{16,12},{20,16},{24,20},{28,24},{32,28},{36,32}... | collective-permute-start | bytes 196616 | tf_op jit(solution)/shard_map/ppermute | solution.py:261
  206.3 10.7 %collective-permute-start.23 = (f32[14,1,512]{2,1,0:T(1,128)S(1)}, f32[14,1,512]{2,1,0:T(1,128)S(1)}, u32[]{:S(2)}, u32[]{:S(2)}) collective-permute-start(f32[14,1,512]{2,1,0:T(1,128)S(1)} %get-tuple-element.17), channel_id=1, source_target_pairs={{0,1},{1,2},{2,3},{4,5},{5,6},{6,7},{8,9},{9,10},{10,11},{12,13},{... | collective-permute-start | bytes 86024 | tf_op jit(solution)/shard_map/ppermute | solution.py:258
  209.4 7.6 %collective-permute-start.22 = (f32[14,1,512]{2,1,0:T(1,128)S(1)}, f32[14,1,512]{2,1,0:T(1,128)S(1)}, u32[]{:S(2)}, u32[]{:S(2)}) collective-permute-start(f32[14,1,512]{2,1,0:T(1,128)S(1)} %get-tuple-element.18), channel_id=1, source_target_pairs={{1,0},{2,1},{3,2},{5,4},{6,5},{7,6},{9,8},{10,9},{11,10},{13,12},{... | collective-permute-start | bytes 86024 | tf_op jit(solution)/shard_map/ppermute | solution.py:261
  211.4 6.3 %collective-permute-start.2 = (f32[18,3,512]{2,1,0:T(4,128)S(1)}, f32[18,3,512]{2,1,0:T(4,128)S(1)}, u32[]{:S(2)}, u32[]{:S(2)}) collective-permute-start(f32[18,3,512]{2,1,0:T(4,128)S(1)} %get-tuple-element.15), channel_id=1, source_target_pairs={{0,1},{1,2},{2,3},{4,5},{5,6},{6,7},{8,9},{9,10},{10,11},{12,13},{... | collective-permute-start | bytes 331784 | tf_op jit(solution)/shard_map/ppermute | solution.py:258
  215.0 6.5 %collective-permute-start.3 = (f32[18,3,512]{2,1,0:T(4,128)S(1)}, f32[18,3,512]{2,1,0:T(4,128)S(1)}, u32[]{:S(2)}, u32[]{:S(2)}) collective-permute-start(f32[18,3,512]{2,1,0:T(4,128)S(1)} %get-tuple-element.16), channel_id=1, source_target_pairs={{1,0},{2,1},{3,2},{5,4},{6,5},{7,6},{9,8},{10,9},{11,10},{13,12},{... | collective-permute-start | bytes 331784 | tf_op jit(solution)/shard_map/ppermute | solution.py:261
  236.6 59.5 %copy-start.1 = (f32[12,32,512]{2,1,0:T(8,128)}, f32[12,32,512]{2,1,0:T(8,128)S(1)}, u32[]{:S(2)}) copy-start(f32[12,32,512]{2,1,0:T(8,128)S(1)} %get-tuple-element.7) | copy-start | bytes 2359300
  236.7 7.9 %collective-permute-start.24 = (f32[3,32,512]{2,1,0:T(8,128)S(1)}, f32[3,32,512]{2,1,0:T(8,128)S(1)}, u32[]{:S(2)}, u32[]{:S(2)}) collective-permute-start(f32[3,32,512]{2,1,0:T(8,128)S(1)} %get-tuple-element.27), channel_id=1, source_target_pairs={{0,4},{4,8},{8,12},{12,16},{16,20},{20,24},{24,28},{28,32},{32,36}... | collective-permute-start | bytes 589832 | tf_op jit(solution)/shard_map/ppermute | solution.py:258
  238.6 11.0 %collective-permute-start.25 = (f32[3,32,512]{2,1,0:T(8,128)S(1)}, f32[3,32,512]{2,1,0:T(8,128)S(1)}, u32[]{:S(2)}, u32[]{:S(2)}) collective-permute-start(f32[3,32,512]{2,1,0:T(8,128)S(1)} %get-tuple-element.28), channel_id=1, source_target_pairs={{4,0},{8,4},{12,8},{16,12},{20,16},{24,20},{28,24},{32,28},{36,32}... | collective-permute-start | bytes 589832 | tf_op jit(solution)/shard_map/ppermute | solution.py:261
  249.7 5.0 %collective-permute-start.26 = (f32[18,3,512]{2,1,0:T(4,128)S(1)}, f32[18,3,512]{2,1,0:T(4,128)S(1)}, u32[]{:S(2)}, u32[]{:S(2)}) collective-permute-start(f32[18,3,512]{2,1,0:T(4,128)S(1)} %get-tuple-element.13), channel_id=1, source_target_pairs={{0,1},{1,2},{2,3},{4,5},{5,6},{6,7},{8,9},{9,10},{10,11},{12,13},{... | collective-permute-start | bytes 331784 | tf_op jit(solution)/shard_map/ppermute | solution.py:258
  252.6 6.5 %collective-permute-start.27 = (f32[18,3,512]{2,1,0:T(4,128)S(1)}, f32[18,3,512]{2,1,0:T(4,128)S(1)}, u32[]{:S(2)}, u32[]{:S(2)}) collective-permute-start(f32[18,3,512]{2,1,0:T(4,128)S(1)} %get-tuple-element.14), channel_id=1, source_target_pairs={{1,0},{2,1},{3,2},{5,4},{6,5},{7,6},{9,8},{10,9},{11,10},{13,12},{... | collective-permute-start | bytes 331784 | tf_op jit(solution)/shard_map/ppermute | solution.py:261
  272.5 7.9 %collective-permute-start.28 = (f32[3,32,512]{2,1,0:T(8,128)S(1)}, f32[3,32,512]{2,1,0:T(8,128)S(1)}, u32[]{:S(2)}, u32[]{:S(2)}) collective-permute-start(f32[3,32,512]{2,1,0:T(8,128)S(1)} %get-tuple-element.25), channel_id=1, source_target_pairs={{0,4},{4,8},{8,12},{12,16},{16,20},{20,24},{24,28},{28,32},{32,36}... | collective-permute-start | bytes 589832 | tf_op jit(solution)/shard_map/ppermute | solution.py:258
  274.4 11.0 %collective-permute-start.29 = (f32[3,32,512]{2,1,0:T(8,128)S(1)}, f32[3,32,512]{2,1,0:T(8,128)S(1)}, u32[]{:S(2)}, u32[]{:S(2)}) collective-permute-start(f32[3,32,512]{2,1,0:T(8,128)S(1)} %get-tuple-element.26), channel_id=1, source_target_pairs={{4,0},{8,4},{12,8},{16,12},{20,16},{24,20},{28,24},{32,28},{36,32}... | collective-permute-start | bytes 589832 | tf_op jit(solution)/shard_map/ppermute | solution.py:261
  285.5 5.1 %collective-permute-start.30 = (f32[18,3,512]{2,1,0:T(4,128)S(1)}, f32[18,3,512]{2,1,0:T(4,128)S(1)}, u32[]{:S(2)}, u32[]{:S(2)}) collective-permute-start(f32[18,3,512]{2,1,0:T(4,128)S(1)} %get-tuple-element.11), channel_id=1, source_target_pairs={{0,1},{1,2},{2,3},{4,5},{5,6},{6,7},{8,9},{9,10},{10,11},{12,13},{... | collective-permute-start | bytes 331784 | tf_op jit(solution)/shard_map/ppermute | solution.py:258
  288.4 6.5 %collective-permute-start.31 = (f32[18,3,512]{2,1,0:T(4,128)S(1)}, f32[18,3,512]{2,1,0:T(4,128)S(1)}, u32[]{:S(2)}, u32[]{:S(2)}) collective-permute-start(f32[18,3,512]{2,1,0:T(4,128)S(1)} %get-tuple-element.12), channel_id=1, source_target_pairs={{1,0},{2,1},{3,2},{5,4},{6,5},{7,6},{9,8},{10,9},{11,10},{13,12},{... | collective-permute-start | bytes 331784 | tf_op jit(solution)/shard_map/ppermute | solution.py:261

commit v2 on v1

--- a/solution.py
+++ b/solution.py
@@ -196,32 +196,6 @@
     )(last, disp, yh, xh, ch, stiff)
 
 
-def unpack_kernel(recv_ref, tile_ref, peak_ref):
-    parts = recv_ref.shape[0]
-    rows = tile_ref.shape[1]
-    for j in range(tile_ref.shape[0] // 4):
-        block = recv_ref[:, 16 * j : 16 * j + 16, :].reshape(parts * 16, 128)
-        wide = pltpu.roll(block.T, 1, 1)
-        for k in range(4):
-            tile_ref[4 * j + k] = wide[rows * k : rows * (k + 1), :]
-    peak = recv_ref[0, 80:88, :]
-    for s in range(1, parts):
-        peak = jnp.maximum(peak, recv_ref[s, 80:88, :])
-    peak_ref[...] = peak
-
-
-def unpack(recv, own_z, rows):
-    parts = recv.shape[0]
-    return pl.pallas_call(
-        unpack_kernel,
-        out_shape=(
-            jax.ShapeDtypeStruct((own_z + 2 * HALO, rows, parts * 16), jnp.float32),
-            jax.ShapeDtypeStruct((8, 128), jnp.float32),
-        ),
-        compiler_params=pltpu.CompilerParams(vmem_limit_bytes=48 * 1024 * 1024),
-    )(recv)
-
-
 def ring(axis, step):
     count = lax.axis_size(axis)
     return [(i, i + step) for i in range(count) if 0 <= i + step < count]
@@ -250,101 +224,461 @@
     return strain_message(last, displacement, yh, xh, ch, stiff, wide)
 
 
-def with_halo(block, sides, width):
-    for axis, dim in sides:
-        count = lax.axis_size(axis)
-        forward = [(i, i + 1) for i in range(count - 1)]
-        backward = [(target, source) for source, target in forward]
-        low = lax.ppermute(
-            lax.slice_in_dim(block, block.shape[dim] - width, None, axis=dim), axis, forward
-        )
-        high = lax.ppermute(lax.slice_in_dim(block, 0, width, axis=dim), axis, backward)
-        block = jnp.concatenate([low, block, high], axis=dim)
-    return block
-
-
-def neighbour_mean(padded):
-    wider = jnp.pad(padded, ((0, 0), (0, 0), (1, 1)))
-    total = wider[2:, 1:-1, 1:-1] + wider[:-2, 1:-1, 1:-1]
-    total = total + wider[1:-1, 2:, 1:-1] + wider[1:-1, :-2, 1:-1]
-    total = total + wider[1:-1, 1:-1, 2:] + wider[1:-1, 1:-1, :-2]
-    return total * (1.0 / 6.0)
-
-
-def weno_side(v1, v2, v3, v4, v5):
-    p_one = v1 / 3.0 - 7.0 * v2 / 6.0 + 11.0 * v3 / 6.0
-    p_two = -v2 / 6.0 + 5.0 * v3 / 6.0 + v4 / 3.0
-    p_three = v3 / 3.0 + 5.0 * v4 / 6.0 - v5 / 6.0
-    b_one = 13.0 / 12.0 * (v1 - 2.0 * v2 + v3) ** 2 + 0.25 * (v1 - 4.0 * v2 + 3.0 * v3) ** 2
-    b_two = 13.0 / 12.0 * (v2 - 2.0 * v3 + v4) ** 2 + 0.25 * (v2 - v4) ** 2
-    b_three = 13.0 / 12.0 * (v3 - 2.0 * v4 + v5) ** 2 + 0.25 * (3.0 * v3 - 4.0 * v4 + v5) ** 2
-    a_one = 0.1 / (WENO_EPS + b_one) ** 2
-    a_two = 0.6 / (WENO_EPS + b_two) ** 2
-    a_three = 0.3 / (WENO_EPS + b_three) ** 2
-    return (a_one * p_one + a_two * p_two + a_three * p_three) / (a_one + a_two + a_three)
-
-
-def march_step(padded, speed):
-    wider = jnp.pad(padded, ((0, 0), (0, 0), (3, 3)), constant_values=1.0)
-    size_z = padded.shape[0] - 6
-    size_y = padded.shape[1] - 6
-    size_x = padded.shape[2]
-    centre = wider[3 : 3 + size_z, 3 : 3 + size_y, 3 : 3 + size_x]
-    lines = (
-        wider[:, 3 : 3 + size_y, 3 : 3 + size_x],
-        wider[3 : 3 + size_z, :, 3 : 3 + size_x],
-        wider[3 : 3 + size_z, 3 : 3 + size_y, :],
-    )
-    grow_plus = None
-    grow_minus = None
-    for axis in range(3):
-        line = lines[axis]
-        count = centre.shape[axis]
-        diffs = lax.slice_in_dim(line, 1, count + 6, axis=axis) - lax.slice_in_dim(
-            line, 0, count + 5, axis=axis
-        )
-        parts = [lax.slice_in_dim(diffs, k, k + count, axis=axis) for k in range(6)]
-        minus = weno_side(parts[0], parts[1], parts[2], parts[3], parts[4])
-        plus = weno_side(parts[5], parts[4], parts[3], parts[2], parts[1])
-        term_p = jnp.maximum(jnp.maximum(minus, 0.0) ** 2, jnp.minimum(plus, 0.0) ** 2)
-        term_m = jnp.maximum(jnp.minimum(minus, 0.0) ** 2, jnp.maximum(plus, 0.0) ** 2)
-        grow_plus = term_p if grow_plus is None else grow_plus + term_p
-        grow_minus = term_m if grow_minus is None else grow_minus + term_m
-    return centre - TIME_STEP * (
-        jnp.maximum(speed, 0.0) * jnp.sqrt(grow_plus)
-        + jnp.minimum(speed, 0.0) * jnp.sqrt(grow_minus)
-    )
-
-
-def ghost_fill(array, margin, value):
-    own_z = array.shape[0] - 2 * margin
-    own_y = array.shape[1] - 2 * margin
-    pos_z = lax.axis_index("wide") * own_z - margin + jnp.arange(array.shape[0], dtype=jnp.int32)
-    pos_y = lax.axis_index("narrow") * own_y - margin + jnp.arange(array.shape[1], dtype=jnp.int32)
-    valid_z = (pos_z >= 0) & (pos_z < own_z * lax.axis_size("wide"))
-    valid_y = (pos_y >= 0) & (pos_y < own_y * lax.axis_size("narrow"))
-    inside = valid_z[:, None, None] & valid_y[None, :, None]
-    return jnp.where(inside, array, value)
+YE = 10
+Y1 = 6
+Y2 = 3
+VMEM_LIMIT = 48 * 1024 * 1024
+
+
+def newton_reciprocal(x):
+    r = pl.reciprocal(x, approx=True)
+    return r * (2.0 - x * r)
+
+
+def weno_cell(d, e0, e1, e2, e3):
+    f0 = e1 - e0
+    f1 = e2 - e1
+    f2 = e3 - e2
+    g0 = f1 - f0
+    g1 = f2 - f1
+    twice1 = e1 + e1
+    twice2 = e2 + e2
+    third = 13.0 / 3.0
+    eps = 4.0 * WENO_EPS
+    pa = twice1 + f0
+    pb = twice1 + f1
+    pc = twice2 - f2
+    a = (f0 * f0 * third + eps) + pa * pa
+    b = (f1 * f1 * third + eps) + pb * pb
+    c = (f2 * f2 * third + eps) + pc * pc
+    a = a * a
+    b = b * b * (1.0 / 6.0)
+    c = c * c
+    ac = a * c
+    ab = a * b
+    cb = c * b
+    u = cb * g0
+    v = ab * g1
+    both = u + v
+    both = both + both
+    s = e1 + e2
+    d6 = 6.0 * d
+    minus = d6 + (s + e2) - (both + v) * newton_reciprocal(ac + cb + 3.0 * ab)
+    plus = (s + e1) - d6 - (both + u) * newton_reciprocal(ac + ab + 3.0 * cb)
+    return minus, plus
+
+
+def godunov(minus, plus):
+    high = jnp.maximum(jnp.maximum(minus, plus), 0.0)
+    low = jnp.minimum(jnp.minimum(minus, plus), 0.0)
+    return high * high, low * low
+
+
+def x_terms(phi):
+    rows, size = phi.shape
+    wide = size + 128
+    phi = jnp.concatenate([phi, jnp.ones((rows, 128), jnp.float32)], axis=1)
+    d = pltpu.roll(phi, wide - 1, 1) - phi
+    e = pltpu.roll(d, wide - 1, 1) - d
+    minus, plus = weno_cell(
+        d, pltpu.roll(e, 2, 1), pltpu.roll(e, 1, 1), e, pltpu.roll(e, wide - 1, 1)
+    )
+    return godunov(pltpu.roll(minus, 1, 1)[:, :size], plus[:, :size])
+
+
+def y_cells(ref, layer, row):
+    p = [ref[layer, row + k : row + k + 8, :] for k in range(6)]
+    d = [p[k + 1] - p[k] for k in range(5)]
+    e = [d[k + 1] - d[k] for k in range(4)]
+    return weno_cell(d[2], *e)
+
+
+def xy_stage(phi_ref, offset, layer0, layers, gp_ref, gm_ref, exact=False):
+    rows = gp_ref.shape[1]
+    tiles = rows // 8
+
+    def layer_step(z, carry):
+        cells = [y_cells(phi_ref, z + layer0, 8 * t + offset - 3) for t in range(tiles)]
+        turned = [pltpu.roll(c[1], 7, 0) for c in cells]
+        if exact:
+            start = min(rows + offset - 3, phi_ref.shape[1] - 13)
+            extra = y_cells(phi_ref, z + layer0, start)[1]
+            turned.append(pltpu.roll(extra, 7 - (rows + offset - 3 - start), 0))
+        else:
+            turned.append(turned[-1])
+        row = lax.broadcasted_iota(jnp.int32, turned[0].shape, 0)
+        for t in range(tiles):
+            plus = jnp.where(row == 7, turned[t + 1], turned[t])
+            yp, ym = godunov(cells[t][0], plus)
+            xp, xm = x_terms(phi_ref[z + layer0, 8 * t + offset : 8 * t + offset + 8, :])
+            gp_ref[z, 8 * t : 8 * t + 8, :] = xp + yp
+            gm_ref[z, 8 * t : 8 * t + 8, :] = xm + ym
+        return carry
+
+    lax.fori_loop(0, layers, layer_step, 0)
+
+
+def z_stage(get_phi, layers, rows, lanes, finish):
+    def lane_step(block, carry):
+        span = pl.ds(pl.multiple_of(128 * block, 128), 128)
+        for t in range(rows // 8):
+            p = [get_phi(z, t, span) for z in range(-3, layers + 3)]
+            d = [p[k + 1] - p[k] for k in range(len(p) - 1)]
+            e = [d[k + 1] - d[k] for k in range(len(d) - 1)]
+            before = None
+            for cell in range(layers + 1):
+                minus, plus = weno_cell(d[cell + 2], e[cell], e[cell + 1], e[cell + 2], e[cell + 3])
+                if before is not None:
+                    finish(cell - 1, t, span, *godunov(before, plus))
+                before = minus
+        return carry
+
+    lax.fori_loop(0, lanes // 128, lane_step, 0)
+
+
+def first_gradient_kernel(ls_ref, sp_ref, sm_ref):
+    layers, rows, lanes = sp_ref.shape
+    offset = YE - Y1
+    xy_stage(ls_ref, offset, 3, layers, sp_ref, sm_ref)
+
+    def finish(z, t, span, gp, gm):
+        where = pl.ds(8 * t, 8)
+        scale = TIME_STEP / 6.0
+        sp_ref[z, where, span] = scale * jnp.sqrt(sp_ref[z, where, span] + gp)
+        sm_ref[z, where, span] = scale * jnp.sqrt(sm_ref[z, where, span] + gm)
+
+    z_stage(
+        lambda z, t, span: ls_ref[z + 3, 8 * t + offset : 8 * t + offset + 8, span], layers, rows, lanes, finish
+    )
+
+
+def vmem_call(kernel, outs, args, scratch=(), cycles=0):
+    specs = []
+    for arg in args:
+        space = pltpu.SMEM if arg.dtype == jnp.int32 else pltpu.VMEM
+        specs.append(pl.BlockSpec(memory_space=space))
+    return pl.pallas_call(
+        kernel,
+        out_shape=tuple(jax.ShapeDtypeStruct(shape, jnp.float32) for shape in outs),
+        in_specs=specs,
+        out_specs=tuple(pl.BlockSpec(memory_space=pltpu.VMEM) for _ in outs),
+        scratch_shapes=[pltpu.VMEM(shape, jnp.float32) for shape in scratch],
+        compiler_params=pltpu.CompilerParams(vmem_limit_bytes=VMEM_LIMIT),
+        cost_estimate=pl.CostEstimate(flops=cycles * 4096, bytes_accessed=1 << 20, transcendentals=0),
+    )(*args)
+
+
+def place_flags():
+    wide, narrow = lax.axis_index("wide"), lax.axis_index("narrow")
+    flags = [
+        1 - wide % 2, wide == 0, wide == lax.axis_size("wide") - 1,
+        1 - narrow % 2, narrow == 0, narrow == lax.axis_size("narrow") - 1,
+    ]
+    return jnp.stack([jnp.asarray(f).astype(jnp.int32) for f in flags])
+
+
+def y_inside(place_ref, base, first_row, shape, rows):
+    row = lax.broadcasted_iota(jnp.int32, shape, 0) + (first_row - base)
+    inside = (row >= 0) | (place_ref[4] == 0)
+    return inside & ((row < rows) | (place_ref[5] == 0))
+
+
+def extend_kernel(
+    place_ref, tile_ref, ra_ref, rb_ref, pa_ref, pb_ref, pc_ref, po_ref, ls_ref, sp_ref, sm_ref,
+    speed_ref, speed6_ref, phi_ref, ma_ref, mb_ref, one, two, keep, pull,
+):
+    depth, rows, lanes = tile_ref.shape
+    layers = depth - 2 * HALO
+    tall = ls_ref.shape[1]
+    margin = 8
+    base = margin + YE
+    peak = jnp.maximum(jnp.maximum(pa_ref[...], pb_ref[...]), jnp.maximum(pc_ref[...], po_ref[...]))
+    scale = 1.0 / (peak[0:1, 0:1] + 1e-06)
+
+    def assemble(z, carry):
+        one[z, base : base + rows, :] = tile_ref[z]
+        return carry
+
+    lax.fori_loop(0, depth, assemble, 0)
+
+    def below(ref):
+        for z in range(depth):
+            one[z, base - 8 : base, :] = ref[z]
+            one[z, base - 10 : base - 8, :] = ref[depth + z // 4, 2 * (z % 4) : 2 * (z % 4) + 2, :]
+
+    def above(ref):
+        for z in range(depth):
+            one[z, base + rows : base + rows + 8, :] = ref[z]
+            one[z, base + rows + 8 : base + rows + 10, :] = ref[depth + z // 4, 2 * (z % 4) : 2 * (z % 4) + 2, :]
+
+    @pl.when(place_ref[3] == 1)
+    def _():
+        above(ra_ref)
+        below(rb_ref)
+
+    @pl.when(place_ref[3] == 0)
+    def _():
+        below(ra_ref)
+        above(rb_ref)
+
+    def normalise(z, carry):
+        outside = ((z < HALO) & (place_ref[1] == 1)) | ((z >= depth - HALO) & (place_ref[2] == 1))
+        for t in range(tall // 8):
+            at = slice(margin + 8 * t, margin + 8 * t + 8)
+            ok = y_inside(place_ref, YE, 8 * t, (8, lanes), rows) & jnp.logical_not(outside)
+            velocity = jnp.where(ok, one[z, at, :] * scale - 0.5, 0.0)
+            one[z, at, :] = velocity
+
+            @pl.when((z >= 1) & (z < depth - 1))
+            def _():
+                ls = ls_ref[z - 1, 8 * t : 8 * t + 8, :]
+                weight = 1.0 / (1.0 + 4.0 * ls * ls)
+                keep[z, 8 * t : 8 * t + 8, :] = weight * velocity
+                pull[z, 8 * t : 8 * t + 8, :] = jnp.where(ok, (1.0 - weight) * (1.0 / 6.0), 0.0)
+
+        return carry
+
+    lax.fori_loop(0, depth, normalise, 0)
+    for step in range(EXT_PASSES):
+        source, target = (one, two) if step % 2 == 0 else (two, one)
+
+        def extend(z, carry):
+            for t in range(tall // 8):
+                at = margin + 8 * t
+                centre = source[z, at : at + 8, :]
+                lane = lax.broadcasted_iota(jnp.int32, centre.shape, 1)
+                total = source[z - 1, at : at + 8, :] + source[z + 1, at : at + 8, :]
+                total = total + (source[z, at - 1 : at + 7, :] + source[z, at + 1 : at + 9, :])
+                total = total + jnp.where(lane == 0, 0.0, pltpu.roll(centre, 1, 1))
+                total = total + jnp.where(lane == lanes - 1, 0.0, pltpu.roll(centre, lanes - 1, 1))
+                span = slice(8 * t, 8 * t + 8)
+                target[z, at : at + 8, :] = keep[z, span, :] + pull[z, span, :] * total
+            return carry
+
+        lax.fori_loop(step + 1, depth - 1 - step, extend, 0)
+
+    final = one if EXT_PASSES % 2 == 0 else two
+
+    def march(z, carry):
+        speed_ref[z] = final[z + HALO, base : base + rows, :]
+        shift = YE - Y1
+        for t in range(speed6_ref.shape[1] // 8):
+            span = slice(8 * t, 8 * t + 8)
+            speed = final[z + HALO, margin + shift + 8 * t : margin + shift + 8 * t + 8, :]
+            speed6_ref[z, span, :] = speed
+            change = jnp.maximum(speed, 0.0) * sp_ref[z, span, :] + jnp.minimum(speed, 0.0) * sm_ref[z, span, :]
+            phi = ls_ref[z + 3, shift + 8 * t : shift + 8 * t + 8, :] - change
+            phi_ref[z, span, :] = jnp.where(y_inside(place_ref, Y1, 8 * t, phi.shape, rows), phi, 1.0)
+        return carry
+
+    lax.fori_loop(0, layers, march, 0)
+    send_edges(place_ref, phi_ref, Y1 - Y2, ma_ref, mb_ref)
+
+
+def send_edges(place_ref, phi_ref, offset, ma_ref, mb_ref):
+    layers = phi_ref.shape[0]
+    count = ma_ref.shape[1]
+    upper = place_ref[0] * (layers - 3)
+    lower = (1 - place_ref[0]) * (layers - 3)
+    for k in range(3):
+        ma_ref[k] = phi_ref[upper + k, offset : offset + count, :]
+        mb_ref[k] = phi_ref[lower + k, offset : offset + count, :]
+
+
+def take_edges(place_ref, ra_ref, rb_ref, edges):
+    upper = 3 * place_ref[0]
+    lower = 3 - upper
+    for k in range(3):
+        edges[upper + k] = ra_ref[k]
+        edges[lower + k] = rb_ref[k]
+
+    @pl.when(place_ref[1] == 1)
+    def _():
+        edges[0:3] = jnp.ones((3,) + tuple(edges.shape[1:]), jnp.float32)
+
+    @pl.when(place_ref[2] == 1)
+    def _():
+        edges[3:6] = jnp.ones((3,) + tuple(edges.shape[1:]), jnp.float32)
+
+
+def plane_kernel(offset, exact, phi_ref, gp_ref, gm_ref):
+    xy_stage(phi_ref, offset, 0, gp_ref.shape[0], gp_ref, gm_ref, exact)
+
+
+def finish_kernel(
+    offset, rows, place_ref, phi_ref, ra_ref, rb_ref, gp_ref, gm_ref, speed_ref, *rest
+):
+    out_ref, edges = rest[0], rest[-1]
+    layers, count, lanes = out_ref.shape
+    base = Y2 if count > rows else 0
+    speed_offset = offset if count > rows else 0
+    take_edges(place_ref, ra_ref, rb_ref, edges)
+
+    def get_phi(z, t, span):
+        if z < 0:
+            return edges[z + 3, 8 * t : 8 * t + 8, span]
+        if z >= layers:
+            return edges[z - layers + 3, 8 * t : 8 * t + 8, span]
+        return phi_ref[z, 8 * t + offset : 8 * t + offset + 8, span]
+
+    def finish(z, t, span, gp, gm):
+        where = pl.ds(8 * t, 8)
+        speed = speed_ref[z, 8 * t + speed_offset : 8 * t + speed_offset + 8, span]
+        total = jnp.where(speed > 0.0, gp_ref[z, where, span] + gp, gm_ref[z, where, span] + gm)
+        phi = get_phi(z, t, span) - (TIME_STEP / 6.0) * speed * jnp.sqrt(total)
+        if count > rows:
+            phi = jnp.where(y_inside(place_ref, base, 8 * t, phi.shape, rows), phi, 1.0)
+        out_ref[z, where, span] = phi
+
+    z_stage(get_phi, layers, count, lanes, finish)
+    if len(rest) > 2:
+        send_edges(place_ref, out_ref, Y2, rest[1], rest[2])
+
+
+def swaps(axis):
+    count = lax.axis_size(axis)
+    first, second = [], []
+    for i in range(0, count, 2):
+        first += [(i, i + 1), (i + 1, i)]
+        j = (i + 2) % count
+        second += [(i + 1, j), (j, i + 1)]
+    return first, second
+
+
+def level_halo(level_set, place):
+    first, second = swaps("wide")
+    layers, rows, lanes = level_set.shape
+    even = place[0] == 1
+    low, high = level_set[:3], level_set[layers - 3 :]
+    got_a = lax.ppermute(jnp.where(even, high, low), "wide", first)
+    got_b = lax.ppermute(jnp.where(even, low, high), "wide", second)
+    below = jnp.where(even, got_b, got_a)
+    above = jnp.where(even, got_a, got_b)
+    below = jnp.where(place[1] == 1, 1.0, below)
+    above = jnp.where(place[2] == 1, 1.0, above)
+    tall = jnp.concatenate([below, level_set, above], axis=0)
+    low = lax.ppermute(tall[:, rows - 9 :], "narrow", ring("narrow", 1))
+    high = lax.ppermute(tall[:, :9], "narrow", ring("narrow", -1))
+    low = jnp.where(place[4] == 1, 1.0, low)
+    high = jnp.where(place[5] == 1, 1.0, high)
+    total = -(-(rows + 2 * YE) // 8) * 8
+    left = jnp.ones((layers + 6, YE - 9, lanes), jnp.float32)
+    right = jnp.ones((layers + 6, total - rows - 9 - YE, lanes), jnp.float32)
+    return jnp.concatenate([left, low, tall, high, right], axis=1)
+
+
+def level_part(place, tile, ma, mb, wide_peak, level_set, ls, sp, sm):
+    layers, rows, lanes = level_set.shape
+    nfirst, nsecond = swaps("narrow")
+    wfirst, wsecond = swaps("wide")
+    count = lax.axis_size("narrow")
+    across = [(i, (i + count // 2) % count) for i in range(count)]
+    ra = lax.ppermute(ma, "narrow", nfirst)
+    rb = lax.ppermute(mb, "narrow", nsecond)
+    pc = lax.ppermute(wide_peak, "narrow", across)
+    pa, pb = ra[-1, :, :128], rb[-1, :, :128]
+    tall = ls.shape[1]
+    rows1 = -(-(rows + 2 * Y1) // 8) * 8
+    rows2 = -(-(rows + 2 * Y2) // 8) * 8
+    depth = layers + 2 * HALO
+    speed, speed6, phi, sa, sb = vmem_call(
+        extend_kernel,
+        [(layers, rows, lanes), (layers, rows1, lanes), (layers, rows1, lanes), (3, rows2, lanes), (3, rows2, lanes)],
+        (place, tile, ra, rb, pa, pb, pc, wide_peak, ls, sp, sm),
+        [(depth, tall + 16, lanes)] * 2 + [(depth, tall, lanes)] * 2,
+        8000,
+    )
+    ga = lax.ppermute(sa, "wide", wfirst)
+    gb = lax.ppermute(sb, "wide", wsecond)
+    gp, gm = vmem_call(functools.partial(plane_kernel, Y1 - Y2, False), [(layers, rows2, lanes)] * 2, (phi,), (), 12000)
+    phi, sa, sb = vmem_call(
+        functools.partial(finish_kernel, Y1 - Y2, rows),
+        [(layers, rows2, lanes), (3, rows, lanes), (3, rows, lanes)],
+        (place, phi, ga, gb, gp, gm, speed6),
+        [(6, rows2, lanes)],
+        5000,
+    )
+    ga = lax.ppermute(sa, "wide", wfirst)
+    gb = lax.ppermute(sb, "wide", wsecond)
+    gp, gm = vmem_call(functools.partial(plane_kernel, Y2, True), [(layers, rows, lanes)] * 2, (phi,), (), 12000)
+    (phi,) = vmem_call(
+        functools.partial(finish_kernel, Y2, rows),
+        [(layers, rows, lanes)],
+        (place, phi, ga, gb, gp, gm, speed),
+        [(6, rows, lanes)],
+        5000,
+    )
+    return phi, speed
+
+
+def first_gradient(ls, layers, rows):
+    rows1 = -(-(rows + 2 * Y1) // 8) * 8
+    return vmem_call(first_gradient_kernel, [(layers, rows1, ls.shape[2])] * 2, (ls,), (), 25000)
+
+
+def unpack_kernel(place_ref, recv_ref, tile_ref, peak_ref, ma_ref, mb_ref):
+    parts = recv_ref.shape[0]
+    depth, rows, lanes = tile_ref.shape
+    for j in range(depth // 4):
+        block = recv_ref[:, 16 * j : 16 * j + 16, :].reshape(parts * 16, 128)
+        wide = pltpu.roll(block.T, 1, 1)
+        for k in range(4):
+            tile_ref[4 * j + k] = wide[rows * k : rows * (k + 1), :]
+    peak = recv_ref[0, 80:88, :]
+    for s in range(1, parts):
+        peak = jnp.maximum(peak, recv_ref[s, 80:88, :])
+    peak_ref[...] = peak
+    fill_edges(place_ref, tile_ref, peak, ma_ref, mb_ref)
+
+
+def fill_edges(place_ref, tile_ref, peak, ma_ref, mb_ref):
+    depth, rows, lanes = tile_ref.shape
+
+    def upper(ref):
+        for z in range(depth):
+            ref[z] = tile_ref[z, rows - 8 : rows, :]
+            ref[depth + z // 4, 2 * (z % 4) : 2 * (z % 4) + 2, :] = tile_ref[z, rows - 10 : rows - 8, :]
+
+    def lower(ref):
+        for z in range(depth):
+            ref[z] = tile_ref[z, 0:8, :]
+            ref[depth + z // 4, 2 * (z % 4) : 2 * (z % 4) + 2, :] = tile_ref[z, 8:10, :]
+
+    last = ma_ref.shape[0] - 1
+    ma_ref[last, :, 0:128] = peak
+    mb_ref[last, :, 0:128] = peak
+
+    @pl.when(place_ref[3] == 1)
+    def _():
+        upper(ma_ref)
+        lower(mb_ref)
+
+    @pl.when(place_ref[3] == 0)
+    def _():
+        lower(ma_ref)
+        upper(mb_ref)
+
+
+def unpack(place, recv, own_z, rows):
+    parts = recv.shape[0]
+    lanes = parts * 16
+    depth = own_z + 2 * HALO
+    edge = (depth + depth // 4 + 1, 8, lanes)
+    return vmem_call(
+        unpack_kernel, [(depth, rows, lanes), (8, 128), edge, edge], (place, recv), (), 1500
+    )
 
 
 def per_device(displacement, material, level_set):
     wide = lax.axis_size("wide")
     own_z, rows, size_x = level_set.shape
+    place = place_flags()
     message = energy_message(displacement, material).reshape(wide, 88, 128)
+    ls = level_halo(level_set, place)
+    sp, sm = first_gradient(ls, own_z, rows)
     recv = lax.all_to_all(message, "wide", split_axis=0, concat_axis=0, tiled=True)
-    tile, wide_peak = unpack(recv, own_z, rows)
-    peak = jnp.max(lax.all_gather(wide_peak, "narrow"))
-    velocity = tile[HALO : HALO + own_z] / (peak + 1e-06) - 0.5
-    weight = 1.0 / (1.0 + 4.0 * level_set * level_set)
-    speed = velocity
-    for step in range(EXT_PASSES):
-        beside_all = with_halo(speed, (("wide", 0), ("narrow", 1)), 1)
-        speed = weight * velocity + (1.0 - weight) * neighbour_mean(beside_all)
-    phi = level_set
-    for step in range(HJ_STEPS):
-        beside_all = with_halo(phi, (("wide", 0), ("narrow", 1)), 3)
-        phi = march_step(ghost_fill(beside_all, 3, 1.0), speed)
-    return (phi, speed)
+    tile, wide_peak, ma, mb = unpack(place, recv, own_z, rows)
+    return level_part(place, tile, ma, mb, wide_peak, level_set, ls, sp, sm)
 
 
 def solution(mesh):

time: 310 us -> 242 us (0.78)
  the two profiles are of different devices: /device:TPU:23 before, /device:TPU:2 now
where the time goes in v2:
time: 242 us; the launch traced here: 241 us
  Pallas kernels  108 us (45%)
  starting transfers between devices  51.8 us (21%)
  waiting for transfers between devices  47.9 us (20%)
  local copies, waits for them, and re-layouts  28.4 us (12%)
  other arithmetic  3.71 us (2%)
    pallas_call x7, Pallas kernels, vmem_call(): pl.pallas_call(kernel, out_shape=tuple((jax.ShapeDtypeStruct(shape, jnp.f...  76.2 us
    pallas_call x1, Pallas kernels, strain_message(): pl.pallas_call(strain_kernel, grid=(loads,), out_shape=jax.ShapeDtypeStru...  31.8 us
    ppermute x1, waiting for transfers between devices, energy_message(): lax.ppermute(jnp.concatenate([corner, first], axis=0), 'wide', backward)  24.6 us
    concatenate x1, local copies, waits for them, and re-layouts, level_halo(): return jnp.concatenate([left, low, tall, high, right], axis=1)  14.3 us
    all_to_all x1, starting transfers between devices, per_device(): lax.all_to_all(message, 'wide', split_axis=0, concat_axis=0, tiled=True)  12.9 us
    ppermute x1, waiting for transfers between devices, level_halo(): got_b = lax.ppermute(jnp.where(even, low, high), 'wide', second)  12.6 us
    ppermute x2, starting transfers between devices, level_part(): gb = lax.ppermute(sb, 'wide', wsecond)  10.5 us
    ppermute x1, waiting for transfers between devices, level_halo(): got_a = lax.ppermute(jnp.where(even, high, low), 'wide', first)  8.38 us
  transfers between devices with their start and end apart: 16, of which 5 were waited for; matrix products, arithmetic and copies ran while one was open for 12% of the time, Pallas kernels for 21%

profile of v2, /device:TPU:2, one launch (start us, length us, event | category | flops | bytes accessed | tf_op | source)
XLA Modules:
  0.0 240.8 jit_solution(11423931590380278777)
XLA Ops:
  0.6 2.5 %slice.51 = f32[3,3,3,32,384]{4,3,2,1,0:T(8,128)} slice(f32[3,3,16,32,384]{4,3,2,1,0:T(8,128)} %u_ref.1), slice={[0:3], [0:3], [0:3], [0:32], [0:384]} | slice | bytes 2654208 | tf_op jit(solution)/shard_map/slice | solution.py:207
  3.1 3.2 %collective-permute-start.2 = (f32[3,3,3,32,384]{4,3,2,1,0:T(8,128)}, f32[3,3,3,32,384]{4,3,2,1,0:T(8,128)S(1)}, u32[]{:S(2)}, u32[]{:S(2)}) collective-permute-start(f32[3,3,3,32,384]{4,3,2,1,0:T(8,128)} %slice.51), channel_id=1, source_target_pairs={{0,124},{4,0},{8,4},{12,8},{16,12},{20,16},{24,20},{28,24},{32,28}... | collective-permute-start | bytes 3981320 | tf_op jit(solution)/shard_map/ppermute | solution.py:207
  6.3 3.1 %fusion.2 = (f32[3,3,16,1,384]{4,3,2,1,0:T(1,128)S(1)}, f32[3,3,16,1,384]{4,3,2,1,0:T(1,128)S(1)}, f32[3,3,16,1,384]{4,3,2,1,0:T(1,128)S(1)}) fusion(f32[3,3,16,32,384]{4,3,2,1,0:T(8,128)} %u_ref.1), kind=kLoop, calls=%fused_computation.22 | loop fusion | bytes 1327104 | tf_op jit(solution)/shard_map/slice | solution.py:210
  9.3 0.0 copy-start.5
  9.4 0.1 copy_bitcast_fusion
  9.4 0.1 pad_maximum_fusion.2
  9.5 1.3 collective-permute-start.1
  10.8 3.0 %collective-permute-start = (f32[3,3,16,384]{3,2,1,0:T(8,128)S(1)}, f32[3,3,16,384]{3,2,1,0:T(8,128)S(1)}, u32[]{:S(2)}, u32[]{:S(2)}) collective-permute-start(f32[3,3,16,384]{3,2,1,0:T(8,128)S(1)} %bitcast.27), channel_id=1, source_target_pairs={{0,1},{1,2},{2,3},{4,5},{5,6},{6,7},{8,9},{9,10},{10,11},{12,13},{... | collective-permute-start | bytes 663560 | tf_op jit(solution)/shard_map/ppermute | solution.py:208
  13.8 0.0 copy-done.5
  13.9 0.1 copy.18
  13.9 0.1 convert_element_type.30
  14.1 0.8 collective-permute-done
  14.9 0.0 collective-permute-done.1
  15.0 0.3 collective-permute-start.3
  15.4 24.6 %collective-permute-done.3 = f32[28,3,384]{2,1,0:T(4,128)S(1)} collective-permute-done((f32[28,3,384]{2,1,0:T(4,128)S(1)}, f32[28,3,384]{2,1,0:T(4,128)S(1)}, u32[]{:S(2)}, u32[]{:S(2)}) %collective-permute-start.3) | collective-permute-done | bytes 129056 | tf_op jit(solution)/shard_map/ppermute | solution.py:218
  39.9 0.1 reshape.33
  40.0 0.1 copy.19
  40.1 1.9 broadcast_in_dim.23
  42.0 2.3 copy.20.stiff_ref
  44.4 0.0 collective-permute-done.2.xh_ref
  44.4 31.8 %shard_map.50 = f32[2816,128]{1,0:T(8,128)} custom-call(s32[1]{0:T(128)} %bitcast.2.last_ref, f32[3,3,16,32,384]{4,3,2,1,0:T(8,128)} %u_ref.1, f32[3,3,3,16,384]{4,3,2,1,0:T(8,128)S(1)} %pad_maximum_fusion.1.yh_ref, f32[3,3,3,32,384]{4,3,2,1,0:T(8,128)S(1)} %collective-permute-done.2.xh_ref, f32[3,3,3,3,384]{4,3,2,1,0:T(4,128)S(1)} %bitcast.22, ...), custom_call_target="tpu_custom_call" | custom-call | tf_op jit(solution)/shard_map/pallas_call | solution.py:176
  76.2 12.9 %all-to-all-start = ((f32[32,88,128]{2,1,0:T(8,128)}), f32[32,88,128]{2,1,0:T(8,128)S(1)}, u32[]{:S(2)}, u32[]{:S(2)}) async-start(f32[32,88,128]{2,1,0:T(8,128)} %bitcast.13), calls=%async_computation | async-start | bytes 2883584 | tf_op jit(solution)/shard_map/all_to_all | solution.py:679
  89.1 0.0 copy-done.4
  89.2 3.0 %collective-permute-start.7 = (f32[3,32,512]{2,1,0:T(8,128)S(1)}, f32[3,32,512]{2,1,0:T(8,128)S(1)}, u32[]{:S(2)}, u32[]{:S(2)}) collective-permute-start(f32[3,32,512]{2,1,0:T(8,128)S(1)} %get-tuple-element.43), channel_id=1, source_target_pairs={{4,8},{8,4},{12,16},{16,12},{20,24},{24,20},{28,32},{32,28},{36,40... | collective-permute-start | bytes 589832 | tf_op jit(solution)/shard_map/ppermute | solution.py:554
  92.2 1.5 collective-permute-start.8
  93.7 12.6 %collective-permute-done.7 = f32[3,32,512]{2,1,0:T(8,128)S(1)} collective-permute-done((f32[3,32,512]{2,1,0:T(8,128)S(1)}, f32[3,32,512]{2,1,0:T(8,128)S(1)}, u32[]{:S(2)}, u32[]{:S(2)}) %collective-permute-start.7) | collective-permute-done | bytes 196640 | tf_op jit(solution)/shard_map/ppermute | solution.py:554
  106.2 8.4 %collective-permute-done.8 = f32[3,32,512]{2,1,0:T(8,128)S(1)} collective-permute-done((f32[3,32,512]{2,1,0:T(8,128)S(1)}, f32[3,32,512]{2,1,0:T(8,128)S(1)}, u32[]{:S(2)}, u32[]{:S(2)}) %collective-permute-start.8) | collective-permute-done | bytes 196640 | tf_op jit(solution)/shard_map/ppermute | solution.py:553
  114.7 0.1 pad_maximum_fusion
  114.8 1.0 copy-done.3
  115.8 0.1 fusion.3
  116.0 1.0 copy.23
  116.9 1.3 collective-permute-start.10
  118.2 1.0 copy.21
  119.2 5.4 %collective-permute-start.9 = (f32[18,9,512]{2,0,1:T(8,128)}, f32[18,9,512]{2,0,1:T(8,128)S(1)}, u32[]{:S(2)}, u32[]{:S(2)}) collective-permute-start(f32[18,9,512]{2,0,1:T(8,128)} %copy.21), channel_id=1, source_target_pairs={{0,1},{1,2},{2,3},{4,5},{5,6},{6,7},{8,9},{9,10},{10,11},{12,13},{... | collective-permute-start | bytes 995336 | tf_op jit(solution)/shard_map/ppermute | solution.py:560
  124.6 0.1 stack.30.place_ref
  124.6 0.0 all-to-all-done.recv_ref
  124.6 2.2 shard_map.51
  126.8 0.3 collective-permute-start.5
  127.1 0.0 collective-permute-done.10
  127.1 2.3 copy_select_fusion
  129.3 2.4 collective-permute-start.4
  131.7 0.0 collective-permute-done.9
  131.7 1.0 copy_select_fusion.1
  132.8 0.7 broadcast_in_dim.27
  133.5 14.3 %concatenate.19.ls_ref = f32[18,56,512]{2,1,0:T(8,128)S(1)} concatenate(f32[18,1,512]{2,1,0:T(1,128)S(1)} %broadcast_in_dim.24, f32[18,9,512]{2,1,0:T(8,128)} %copy_select_fusion.1, f32[18,32,512]{2,1,0:T(8,128)} %copy-done.3, f32[18,9,512]{2,1,0:T(8,128)} %copy_select_fusion, f32[18,5,512]{2,1,0:T(8,128)} %broadcast_in_dim.27), dimensions={1} | concatenate | bytes 4128768 | tf_op jit(solution)/shard_map/concatenate | solution.py:567
  147.8 21.7 %shard_map.52 = (f32[12,48,512]{2,1,0:T(8,128)S(1)}, f32[12,48,512]{2,1,0:T(8,128)S(1)}) custom-call(f32[18,56,512]{2,1,0:T(8,128)S(1)} %concatenate.19.ls_ref), custom_call_target="tpu_custom_call" | custom-call | flops 102400000 | bytes 1048576 | tf_op jit(solution)/shard_map/pallas_call | solution.py:360
  169.6 5.5 %collective-permute-start.6 = (f32[8,128]{1,0:T(8,128)S(1)}, f32[8,128]{1,0:T(8,128)S(1)}, u32[]{:S(2)}, u32[]{:S(2)}) collective-permute-start(f32[8,128]{1,0:T(8,128)S(1)} %get-tuple-element.23.po_ref), channel_id=1, source_target_pairs={{0,2},{1,3},{2,0},{3,1},{4,6},{5,7},{6,4},{7,5},{8,10},{9,11},{10,... | collective-permute-start | bytes 12296 | tf_op jit(solution)/shard_map/ppermute | solution.py:578
  175.1 0.0 collective-permute-done.5.rb_ref
  175.1 0.0 collective-permute-done.4.ra_ref
  175.1 1.6 collective-permute-done.6.pc_ref
  176.7 14.6 %shard_map.53 = (f32[12,32,512]{2,1,0:T(8,128)}, f32[12,48,512]{2,1,0:T(8,128)S(1)}, f32[12,48,512]{2,1,0:T(8,128)S(1)}, f32[3,40,512]{2,1,0:T(8,128)S(1)}, f32[3,40,512]{2,1,0:T(8,128)S(1)}) custom-call(s32[6]{0:T(128)S(1)} %stack.30.place_ref, f32[20,32,512]{2,1,0:T(8,128)} %copy-done.1, f32[26,8,512]{2,1,0:T(8,128)S(1)} %collective-permute-done.4.ra_ref, ...), custom_call_target="tpu_custom_call" | custom-call | flops 32768000 | bytes 1048576 | tf_op jit(solution)/shard_map/pallas_call | solution.py:360
  191.3 0.5 collective-permute-start.11
  191.9 4.3 %collective-permute-start.12 = (f32[3,40,512]{2,1,0:T(8,128)S(1)}, f32[3,40,512]{2,1,0:T(8,128)S(1)}, u32[]{:S(2)}, u32[]{:S(2)}) collective-permute-start(f32[3,40,512]{2,1,0:T(8,128)S(1)} %get-tuple-element.28), channel_id=1, source_target_pairs={{4,8},{8,4},{12,16},{16,12},{20,24},{24,20},{28,32},{32,28},{36,40... | collective-permute-start | bytes 737288 | tf_op jit(solution)/shard_map/ppermute | solution.py:592
  196.2 13.7 %shard_map.54 = (f32[12,40,512]{2,1,0:T(8,128)S(1)}, f32[12,40,512]{2,1,0:T(8,128)S(1)}) custom-call(f32[12,48,512]{2,1,0:T(8,128)S(1)} %get-tuple-element.26.phi_ref), custom_call_target="tpu_custom_call" | custom-call | flops 49152000 | bytes 1048576 | tf_op jit(solution)/shard_map/pallas_call | solution.py:360
  209.9 0.0 collective-permute-done.11.ra_ref
  209.9 0.0 collective-permute-done.12.rb_ref
  209.9 5.9 %shard_map.55 = (f32[12,40,512]{2,1,0:T(8,128)S(1)}, f32[3,32,512]{2,1,0:T(8,128)S(1)}, f32[3,32,512]{2,1,0:T(8,128)S(1)}) custom-call(s32[6]{0:T(128)S(1)} %stack.30.place_ref, f32[12,48,512]{2,1,0:T(8,128)S(1)} %get-tuple-element.26.phi_ref, f32[3,40,512]{2,1,0:T(8,128)S(1)} %collective-permute-done.11.ra_ref, ...), custom_call_target="tpu_custom_call" | custom-call | flops 20480000 | bytes 1048576 | tf_op jit(solution)/shard_map/pallas_call | solution.py:360
  215.9 0.0 copy-start.2
  215.9 0.7 collective-permute-start.13
  216.6 6.2 %collective-permute-start.14 = (f32[3,32,512]{2,1,0:T(8,128)S(1)}, f32[3,32,512]{2,1,0:T(8,128)S(1)}, u32[]{:S(2)}, u32[]{:S(2)}) collective-permute-start(f32[3,32,512]{2,1,0:T(8,128)S(1)} %get-tuple-element.34), channel_id=1, source_target_pairs={{4,8},{8,4},{12,16},{16,12},{20,24},{24,20},{28,32},{32,28},{36,40... | collective-permute-start | bytes 589832 | tf_op jit(solution)/shard_map/ppermute | solution.py:602
  222.7 12.6 %shard_map.56 = (f32[12,32,512]{2,1,0:T(8,128)S(1)}, f32[12,32,512]{2,1,0:T(8,128)S(1)}) custom-call(f32[12,40,512]{2,1,0:T(8,128)S(1)} %get-tuple-element.32.phi_ref), custom_call_target="tpu_custom_call" | custom-call | flops 49152000 | bytes 1048576 | tf_op jit(solution)/shard_map/pallas_call | solution.py:360
  235.4 0.0 collective-permute-done.13.ra_ref
  235.4 0.0 collective-permute-done.14.rb_ref
  235.4 5.4 %shard_map.57 = f32[12,32,512]{2,1,0:T(8,128)} custom-call(s32[6]{0:T(128)S(1)} %stack.30.place_ref, f32[12,40,512]{2,1,0:T(8,128)S(1)} %get-tuple-element.32.phi_ref, f32[3,32,512]{2,1,0:T(8,128)S(1)} %collective-permute-done.13.ra_ref, f32[3,32,512]{2,1,0:T(8,128)S(1)} %collective-permute-done.14.rb_ref, f32[12,32,512]{2,1,0:T(8,128)S(1)} %get-tuple-element.35.gp_ref, ...), custom_call_target="tpu_custom_call" | custom-call | flops 20480000 | bytes 1048576 | tf_op jit(solution)/shard_map/pallas_call | solution.py:360
  (23 shorter events, 0.3 us)
Async XLA Ops:
  3.1 41.2 %collective-permute-start.2 = (f32[3,3,3,32,384]{4,3,2,1,0:T(8,128)}, f32[3,3,3,32,384]{4,3,2,1,0:T(8,128)S(1)}, u32[]{:S(2)}, u32[]{:S(2)}) collective-permute-start(f32[3,3,3,32,384]{4,3,2,1,0:T(8,128)} %slice.51), channel_id=1, source_target_pairs={{0,124},{4,0},{8,4},{12,8},{16,12},{20,16},{24,20},{28,24},{32,28}... | collective-permute-start | bytes 3981320 | tf_op jit(solution)/shard_map/ppermute | solution.py:207
  9.3 4.5 %copy-start.5 = (s32[16,32,24]{1,2,0:T(8,128)S(1)}, s32[16,32,24]{1,2,0:T(8,128)}, u32[]{:S(2)}) copy-start(s32[16,32,24]{1,2,0:T(8,128)} %param.4) | copy-start | bytes 147460
  9.5 5.4 %collective-permute-start.1 = (f32[3,3,2,16,384]{4,3,2,1,0:T(8,128)S(1)}, f32[3,3,2,16,384]{4,3,2,1,0:T(8,128)S(1)}, u32[]{:S(2)}, u32[]{:S(2)}) collective-permute-start(f32[3,3,2,16,384]{4,3,2,1,0:T(8,128)S(1)} %pad_maximum_fusion.2), channel_id=1, source_target_pairs={{1,0},{2,1},{3,2},{5,4},{6,5},{7,6},{9,8},{10,9},{11,10},{13,12},{... | collective-permute-start | bytes 1327112 | tf_op jit(solution)/shard_map/ppermute | solution.py:209
  10.8 4.1 %collective-permute-start = (f32[3,3,16,384]{3,2,1,0:T(8,128)S(1)}, f32[3,3,16,384]{3,2,1,0:T(8,128)S(1)}, u32[]{:S(2)}, u32[]{:S(2)}) collective-permute-start(f32[3,3,16,384]{3,2,1,0:T(8,128)S(1)} %bitcast.27), channel_id=1, source_target_pairs={{0,1},{1,2},{2,3},{4,5},{5,6},{6,7},{8,9},{9,10},{10,11},{12,13},{... | collective-permute-start | bytes 663560 | tf_op jit(solution)/shard_map/ppermute | solution.py:208
  15.0 24.9 %collective-permute-start.3 = (f32[28,3,384]{2,1,0:T(4,128)S(1)}, f32[28,3,384]{2,1,0:T(4,128)S(1)}, u32[]{:S(2)}, u32[]{:S(2)}) collective-permute-start(f32[28,3,384]{2,1,0:T(4,128)S(1)} %pad_maximum_fusion.3), channel_id=1, source_target_pairs={{0,124},{4,0},{8,4},{12,8},{16,12},{20,16},{24,20},{28,24},{32,28}... | collective-permute-start | bytes 387080 | tf_op jit(solution)/shard_map/ppermute | solution.py:218
  76.2 12.9 %copy-start.4 = (f32[12,32,512]{2,1,0:T(8,128)S(1)}, f32[12,32,512]{2,1,0:T(8,128)}, u32[]{:S(2)}) copy-start(f32[12,32,512]{2,1,0:T(8,128)} %param.5) | copy-start | bytes 2359300
  76.2 48.4 %all-to-all-start = ((f32[32,88,128]{2,1,0:T(8,128)}), f32[32,88,128]{2,1,0:T(8,128)S(1)}, u32[]{:S(2)}, u32[]{:S(2)}) async-start(f32[32,88,128]{2,1,0:T(8,128)} %bitcast.13), calls=%async_computation | async-start | bytes 2883584 | tf_op jit(solution)/shard_map/all_to_all | solution.py:679
  89.2 17.1 %collective-permute-start.7 = (f32[3,32,512]{2,1,0:T(8,128)S(1)}, f32[3,32,512]{2,1,0:T(8,128)S(1)}, u32[]{:S(2)}, u32[]{:S(2)}) collective-permute-start(f32[3,32,512]{2,1,0:T(8,128)S(1)} %get-tuple-element.43), channel_id=1, source_target_pairs={{4,8},{8,4},{12,16},{16,12},{20,24},{24,20},{28,32},{32,28},{36,40... | collective-permute-start | bytes 589832 | tf_op jit(solution)/shard_map/ppermute | solution.py:554
  92.2 22.4 %collective-permute-start.8 = (f32[3,32,512]{2,1,0:T(8,128)S(1)}, f32[3,32,512]{2,1,0:T(8,128)S(1)}, u32[]{:S(2)}, u32[]{:S(2)}) collective-permute-start(f32[3,32,512]{2,1,0:T(8,128)S(1)} %get-tuple-element.44), channel_id=1, source_target_pairs={{0,4},{4,0},{8,12},{12,8},{16,20},{20,16},{24,28},{28,24},{32,36},... | collective-permute-start | bytes 589832 | tf_op jit(solution)/shard_map/ppermute | solution.py:553
  114.8 1.0 copy-start.3
  116.9 10.1 %collective-permute-start.10 = (f32[18,9,512]{2,0,1:T(8,128)}, f32[18,9,512]{2,0,1:T(8,128)}, u32[]{:S(2)}, u32[]{:S(2)}) collective-permute-start(f32[18,9,512]{2,0,1:T(8,128)} %copy.23), channel_id=1, source_target_pairs={{1,0},{2,1},{3,2},{5,4},{6,5},{7,6},{9,8},{10,9},{11,10},{13,12},{... | collective-permute-start | bytes 995336 | tf_op jit(solution)/shard_map/ppermute | solution.py:561
  119.2 12.6 %collective-permute-start.9 = (f32[18,9,512]{2,0,1:T(8,128)}, f32[18,9,512]{2,0,1:T(8,128)S(1)}, u32[]{:S(2)}, u32[]{:S(2)}) collective-permute-start(f32[18,9,512]{2,0,1:T(8,128)} %copy.21), channel_id=1, source_target_pairs={{0,1},{1,2},{2,3},{4,5},{5,6},{6,7},{8,9},{9,10},{10,11},{12,13},{... | collective-permute-start | bytes 995336 | tf_op jit(solution)/shard_map/ppermute | solution.py:560
  126.8 6.7 %copy-start.1 = (f32[20,32,512]{2,1,0:T(8,128)}, f32[20,32,512]{2,1,0:T(8,128)S(1)}, u32[]{:S(2)}) copy-start(f32[20,32,512]{2,1,0:T(8,128)S(1)} %get-tuple-element.20.tile_ref) | copy-start | bytes 3932164
  126.8 48.3 %collective-permute-start.5 = (f32[26,8,512]{2,1,0:T(8,128)}, f32[26,8,512]{2,1,0:T(8,128)S(1)}, u32[]{:S(2)}, u32[]{:S(2)}) collective-permute-start(f32[26,8,512]{2,1,0:T(8,128)} %get-tuple-element.22), channel_id=1, source_target_pairs={{1,2},{2,1},{3,0},{0,3},{5,6},{6,5},{7,4},{4,7},{9,10},{10,9},{11,... | collective-permute-start | bytes 1277960 | tf_op jit(solution)/shard_map/ppermute | solution.py:577
  129.3 45.8 %collective-permute-start.4 = (f32[26,8,512]{2,1,0:T(8,128)S(1)}, f32[26,8,512]{2,1,0:T(8,128)S(1)}, u32[]{:S(2)}, u32[]{:S(2)}) collective-permute-start(f32[26,8,512]{2,1,0:T(8,128)S(1)} %get-tuple-element.21), channel_id=1, source_target_pairs={{0,1},{1,0},{2,3},{3,2},{4,5},{5,4},{6,7},{7,6},{8,9},{9,8},{10,11... | collective-permute-start | bytes 1277960 | tf_op jit(solution)/shard_map/ppermute | solution.py:576
  147.8 28.9 %copy-start = (f32[18,56,512]{2,1,0:T(8,128)}, f32[18,56,512]{2,1,0:T(8,128)S(1)}, u32[]{:S(2)}) copy-start(f32[18,56,512]{2,1,0:T(8,128)S(1)} %concatenate.19.ls_ref) | copy-start | bytes 6193156
  169.6 7.1 %collective-permute-start.6 = (f32[8,128]{1,0:T(8,128)S(1)}, f32[8,128]{1,0:T(8,128)S(1)}, u32[]{:S(2)}, u32[]{:S(2)}) collective-permute-start(f32[8,128]{1,0:T(8,128)S(1)} %get-tuple-element.23.po_ref), channel_id=1, source_target_pairs={{0,2},{1,3},{2,0},{3,1},{4,6},{5,7},{6,4},{7,5},{8,10},{9,11},{10,... | collective-permute-start | bytes 12296 | tf_op jit(solution)/shard_map/ppermute | solution.py:578
  191.3 18.6 %collective-permute-start.11 = (f32[3,40,512]{2,1,0:T(8,128)S(1)}, f32[3,40,512]{2,1,0:T(8,128)S(1)}, u32[]{:S(2)}, u32[]{:S(2)}) collective-permute-start(f32[3,40,512]{2,1,0:T(8,128)S(1)} %get-tuple-element.27), channel_id=1, source_target_pairs={{0,4},{4,0},{8,12},{12,8},{16,20},{20,16},{24,28},{28,24},{32,36},... | collective-permute-start | bytes 737288 | tf_op jit(solution)/shard_map/ppermute | solution.py:591
  191.9 18.1 %collective-permute-start.12 = (f32[3,40,512]{2,1,0:T(8,128)S(1)}, f32[3,40,512]{2,1,0:T(8,128)S(1)}, u32[]{:S(2)}, u32[]{:S(2)}) collective-permute-start(f32[3,40,512]{2,1,0:T(8,128)S(1)} %get-tuple-element.28), channel_id=1, source_target_pairs={{4,8},{8,4},{12,16},{16,12},{20,24},{24,20},{28,32},{32,28},{36,40... | collective-permute-start | bytes 737288 | tf_op jit(solution)/shard_map/ppermute | solution.py:592
  215.9 19.6 %copy-start.2 = (f32[12,32,512]{2,1,0:T(8,128)S(1)}, f32[12,32,512]{2,1,0:T(8,128)}, u32[]{:S(2)}) copy-start(f32[12,32,512]{2,1,0:T(8,128)} %get-tuple-element.19.speed_ref) | copy-start | bytes 2359300
  215.9 19.5 %collective-permute-start.13 = (f32[3,32,512]{2,1,0:T(8,128)S(1)}, f32[3,32,512]{2,1,0:T(8,128)S(1)}, u32[]{:S(2)}, u32[]{:S(2)}) collective-permute-start(f32[3,32,512]{2,1,0:T(8,128)S(1)} %get-tuple-element.33), channel_id=1, source_target_pairs={{0,4},{4,0},{8,12},{12,8},{16,20},{20,16},{24,28},{28,24},{32,36},... | collective-permute-start | bytes 589832 | tf_op jit(solution)/shard_map/ppermute | solution.py:601
  216.6 18.8 %collective-permute-start.14 = (f32[3,32,512]{2,1,0:T(8,128)S(1)}, f32[3,32,512]{2,1,0:T(8,128)S(1)}, u32[]{:S(2)}, u32[]{:S(2)}) collective-permute-start(f32[3,32,512]{2,1,0:T(8,128)S(1)} %get-tuple-element.34), channel_id=1, source_target_pairs={{4,8},{8,4},{12,16},{16,12},{20,24},{24,20},{28,32},{32,28},{36,40... | collective-permute-start | bytes 589832 | tf_op jit(solution)/shard_map/ppermute | solution.py:602

commit v3 on v2

--- a/solution.py
+++ b/solution.py
@@ -15,6 +15,10 @@
 TIME_STEP = 0.3
 HALO = EXT_PASSES
 GRAD_SCALE = 1.0 / (8.0 * 48.0 * 48.0)
+YE = 10
+Y1 = 6
+Y2 = 3
+VMEM_LIMIT = 48 * 1024 * 1024
 
 
 def lane_shifts(value):
@@ -45,109 +49,123 @@
     return (d - a) + 5.0 * (c - b)
 
 
-def strain_kernel(last_ref, u_ref, yh_ref, xh_ref, ch_ref, stiff_ref, msg_ref, plane, filt, energy, turned):
+def filter_plane(plane, filt, comp, layer, value, low, high0, high1):
+    rows = value.shape[0]
+    plane[8 : 8 + rows, :] = value
+    plane[7:8, :] = low
+    plane[8 + rows : 9 + rows, :] = high0
+    plane[9 + rows : 10 + rows, :] = high1
+    for tile in range(rows // 8):
+        base = 8 + 8 * tile
+        a = plane[base - 1 : base + 7, :]
+        b = plane[base : base + 8, :]
+        c = plane[base + 1 : base + 9, :]
+        d = plane[base + 2 : base + 10, :]
+        val_y = val4(a, b, c, d)
+        der_y = der4(a, b, c, d)
+        before, after, after2 = lane_shifts(val_y)
+        span = pl.ds(8 * tile, 8)
+        filt[comp, 0, layer, span, :] = val4(before, val_y, after, after2)
+        filt[comp, 2, layer, span, :] = der4(before, val_y, after, after2)
+        before, after, after2 = lane_shifts(der_y)
+        filt[comp, 1, layer, span, :] = val4(before, der_y, after, after2)
+
+
+def densities(field, rows, finish):
+    for tile in range(rows // 8):
+        span = pl.ds(8 * tile, 8)
+        gx = [der4(*field(comp, 0, span)) for comp in range(3)]
+        gy = [val4(*field(comp, 1, span)) for comp in range(3)]
+        gz = [val4(*field(comp, 2, span)) for comp in range(3)]
+        sxy = gy[0] + gx[1]
+        sxz = gz[0] + gx[2]
+        syz = gz[1] + gy[2]
+        trace = gx[0] + gy[1] + gz[2]
+        square = gx[0] * gx[0] + gy[1] * gy[1] + gz[2] * gz[2]
+        shear = sxy * sxy + sxz * sxz + syz * syz
+        scale = GRAD_SCALE * GRAD_SCALE
+        finish(span, (SHEAR * scale) * (square + 0.5 * shear) + (0.5 * LAME * scale) * (trace * trace))
+
+
+def accumulate(ref, slot):
     load = pl.program_id(0)
-    own_x = u_ref.shape[2]
-    rows = u_ref.shape[3]
-    size_z = u_ref.shape[4]
-    tiles = rows // 8
-    keep = jnp.where(last_ref[0] == 1, 0.0, 1.0)
-
-    def filter_plane(comp, layer, get_plane, low, high0, high1):
-        plane[8 : 8 + rows, :] = get_plane
-        plane[7:8, :] = low
-        plane[8 + rows : 9 + rows, :] = high0
-        plane[9 + rows : 10 + rows, :] = high1
-        for tile in range(tiles):
-            base = 8 + 8 * tile
-            a = plane[base - 1 : base + 7, :]
-            b = plane[base : base + 8, :]
-            c = plane[base + 1 : base + 9, :]
-            d = plane[base + 2 : base + 10, :]
-            val_y = val4(a, b, c, d)
-            der_y = der4(a, b, c, d)
-            before, after, after2 = lane_shifts(val_y)
-            span = pl.ds(8 * tile, 8)
-            filt[comp, 0, layer, span, :] = val4(before, val_y, after, after2)
-            filt[comp, 2, layer, span, :] = der4(before, val_y, after, after2)
-            before, after, after2 = lane_shifts(der_y)
-            filt[comp, 1, layer, span, :] = val4(before, der_y, after, after2)
+
+    def finish(span, density):
+        @pl.when(load == 0)
+        def _():
+            ref[slot, span, :] = density
+
+        @pl.when(load > 0)
+        def _():
+            ref[slot, span, :] += density
+
+    return finish
+
+
+def inner_kernel(u_ref, yh_ref, energy_ref, tail_ref, plane, filt):
+    own_x, rows = u_ref.shape[2:4]
 
     def own_layer(layer, carry):
         for comp in range(3):
-            filter_plane(
-                comp, layer, u_ref[0, comp, layer],
-                yh_ref[0, comp, 0, pl.ds(layer, 1), :],
-                yh_ref[0, comp, 1, pl.ds(layer, 1), :],
-                yh_ref[0, comp, 2, pl.ds(layer, 1), :],
-            )
+            edge = [yh_ref[0, comp, k, pl.ds(layer, 1), :] for k in range(3)]
+            filter_plane(plane, filt, comp, layer, u_ref[0, comp, layer], *edge)
         return carry
 
     lax.fori_loop(0, own_x, own_layer, 0)
-    for k in range(3):
-        for comp in range(3):
-            filter_plane(
-                comp, own_x + k, xh_ref[0, comp, k],
-                ch_ref[0, comp, 0, k : k + 1, :],
-                ch_ref[0, comp, 1, k : k + 1, :],
-                ch_ref[0, comp, 2, k : k + 1, :],
-            )
+
+    def slot_step(slot, carry):
+        field = lambda comp, which, span: [filt[comp, which, slot + k, span, :] for k in range(4)]
+        densities(field, rows, accumulate(energy_ref, slot))
+        return carry
+
+    lax.fori_loop(0, own_x - 3, slot_step, 0)
+    for comp in range(3):
+        for which in range(3):
+            for k in range(3):
+                tail_ref[0, comp, which, k] = filt[comp, which, own_x - 3 + k]
+
+
+def outer_kernel(place_ref, tail_ref, xh_ref, ch_ref, inner_ref, stiff_ref, msg_ref, plane, filt, energy, turned):
+    load = pl.program_id(0)
+    rows, size_z = xh_ref.shape[3:5]
+    own_x = stiff_ref.shape[0]
+    inner = own_x - 3
+    tiles = rows // 8
+    keep = jnp.where(place_ref[2] == 1, 0.0, 1.0)
+    for comp in range(3):
+        for k in range(3):
+            edge = [ch_ref[0, comp, which, k : k + 1, :] for which in range(3)]
+            filter_plane(plane, filt, comp, k, xh_ref[0, comp, k], *edge)
 
     def density_at(slot, masked):
         def field(comp, which, span):
             out = []
             for k in range(4):
-                value = filt[comp, which, slot + k, span, :]
-                if masked[k]:
-                    value = value * keep
-                out.append(value)
+                at = slot + k
+                value = tail_ref[0, comp, which, at, span, :] if at < 3 else filt[comp, which, at - 3, span, :]
+                out.append(value * keep if masked[k] else value)
             return out
 
-        for tile in range(tiles):
-            span = pl.ds(8 * tile, 8)
-            gx = [der4(*field(comp, 0, span)) for comp in range(3)]
-            gy = [val4(*field(comp, 1, span)) for comp in range(3)]
-            gz = [val4(*field(comp, 2, span)) for comp in range(3)]
-            sxy = gy[0] + gx[1]
-            sxz = gz[0] + gx[2]
-            syz = gz[1] + gy[2]
-            trace = gx[0] + gy[1] + gz[2]
-            square = gx[0] * gx[0] + gy[1] * gy[1] + gz[2] * gz[2]
-            shear = sxy * sxy + sxz * sxz + syz * syz
-            scale = GRAD_SCALE * GRAD_SCALE
-            density = (SHEAR * scale) * (square + 0.5 * shear) + (0.5 * LAME * scale) * (trace * trace)
-
-            @pl.when(load == 0)
-            def _():
-                energy[slot, span, :] = density
-
-            @pl.when(load > 0)
-            def _():
-                energy[slot, span, :] += density
-
-    def slot_step(slot, carry):
-        density_at(slot, (False,) * 4)
-        return carry
-
-    lax.fori_loop(0, own_x - 3, slot_step, 0)
-    density_at(own_x - 3, (False, False, False, True))
-    density_at(own_x - 2, (False, False, True, True))
-    density_at(own_x - 1, (True, False, False, False))
+        densities(field, rows, accumulate(energy, slot))
+
+    density_at(0, (False, False, False, True))
+    density_at(1, (False, False, True, True))
+    density_at(2, (True, False, False, False))
 
     @pl.when(load == pl.num_programs(0) - 1)
     def _():
         peak = jnp.zeros((8, 128), jnp.float32)
         groups = own_x // 4
-        zeros = jnp.zeros((8, 128), jnp.float32)
         for g in range(groups):
             stack = []
             for q in range(4):
-                value = energy[4 * g + q] * stiff_ref[4 * g + q]
+                x = 4 * g + q
+                value = (inner_ref[x] if x < inner else energy[x - inner]) * stiff_ref[x]
                 stack.append(value)
                 for tile in range(tiles):
                     for b in range(size_z // 128):
                         peak = jnp.maximum(peak, value[8 * tile : 8 * tile + 8, 128 * b : 128 * b + 128])
-            turned[g, 0:8, :] = zeros
+            turned[g, 0:8, :] = jnp.zeros((8, 128), jnp.float32)
             turned[g, size_z : size_z + 16, :] = jnp.zeros((16, 128), jnp.float32)
             turned[g, HALO : HALO + size_z, :] = jnp.concatenate(stack, axis=0).T
         peak = jnp.broadcast_to(jnp.max(peak, axis=0, keepdims=True), (8, 128))
@@ -170,64 +188,64 @@
             msg_ref[pl.ds(88 * t + 80, 8), :] = peak
 
 
-def strain_message(last, disp, yh, xh, ch, stiff, parts):
+def load_block(*shape):
+    return pl.BlockSpec((1,) + shape, lambda l: (l,) + (0,) * len(shape))
+
+
+def fixed_block(*shape):
+    return pl.BlockSpec(shape, lambda l: (0,) * len(shape))
+
+
+def inner_strain(disp, yh):
     loads, comps, own_x, rows, size_z = disp.shape
-    block = lambda *shape: pl.BlockSpec((1,) + shape, lambda l: (l,) + (0,) * len(shape))
     return pl.pallas_call(
-        strain_kernel,
+        inner_kernel,
+        grid=(loads,),
+        out_shape=(
+            jax.ShapeDtypeStruct((own_x - 3, rows, size_z), jnp.float32),
+            jax.ShapeDtypeStruct((loads, comps, 3, 3, rows, size_z), jnp.float32),
+        ),
+        in_specs=[load_block(comps, own_x, rows, size_z), load_block(comps, 3, own_x, size_z)],
+        out_specs=(fixed_block(own_x - 3, rows, size_z), load_block(comps, 3, 3, rows, size_z)),
+        scratch_shapes=[
+            pltpu.VMEM((rows + 16, size_z), jnp.float32),
+            pltpu.VMEM((3, 3, own_x, rows, size_z), jnp.float32),
+        ],
+        compiler_params=pltpu.CompilerParams(vmem_limit_bytes=VMEM_LIMIT),
+        cost_estimate=pl.CostEstimate(flops=40000 * 4096, bytes_accessed=1 << 20, transcendentals=0),
+    )(disp, yh)
+
+
+def strain_message(place, tail, xh, ch, inner, stiff, parts):
+    loads, comps = xh.shape[:2]
+    own_x, rows, size_z = stiff.shape
+    return pl.pallas_call(
+        outer_kernel,
         grid=(loads,),
         out_shape=jax.ShapeDtypeStruct((parts * 88, 128), jnp.float32),
         in_specs=[
             pl.BlockSpec(memory_space=pltpu.SMEM),
-            block(comps, own_x, rows, size_z),
-            block(comps, 3, own_x, size_z),
-            block(comps, 3, rows, size_z),
-            block(comps, 3, 3, size_z),
-            pl.BlockSpec((own_x, rows, size_z), lambda l: (0, 0, 0)),
+            load_block(comps, 3, 3, rows, size_z),
+            load_block(comps, 3, rows, size_z),
+            load_block(comps, 3, 3, size_z),
+            fixed_block(own_x - 3, rows, size_z),
+            fixed_block(own_x, rows, size_z),
         ],
-        out_specs=pl.BlockSpec((parts * 88, 128), lambda l: (0, 0)),
+        out_specs=fixed_block(parts * 88, 128),
         scratch_shapes=[
             pltpu.VMEM((rows + 16, size_z), jnp.float32),
-            pltpu.VMEM((3, 3, own_x + 3, rows, size_z), jnp.float32),
-            pltpu.VMEM((own_x, rows, size_z), jnp.float32),
+            pltpu.VMEM((3, 3, 3, rows, size_z), jnp.float32),
+            pltpu.VMEM((3, rows, size_z), jnp.float32),
             pltpu.VMEM((own_x // 4, size_z + 16, 128), jnp.float32),
         ],
-        compiler_params=pltpu.CompilerParams(vmem_limit_bytes=48 * 1024 * 1024),
-    )(last, disp, yh, xh, ch, stiff)
+        compiler_params=pltpu.CompilerParams(vmem_limit_bytes=VMEM_LIMIT),
+        cost_estimate=pl.CostEstimate(flops=10000 * 4096, bytes_accessed=1 << 20, transcendentals=0),
+    )(place, tail, xh, ch, inner, stiff)
 
 
 def ring(axis, step):
     count = lax.axis_size(axis)
     return [(i, i + step) for i in range(count) if 0 <= i + step < count]
-
-
-def energy_message(displacement, material):
-    wide = lax.axis_size("wide")
-    backward = [(i, (i - 1) % wide) for i in range(wide)]
-    xh = lax.ppermute(displacement[:, :, :3], "wide", backward)
-    low = lax.ppermute(displacement[:, :, :, -1], "narrow", ring("narrow", 1))
-    high = lax.ppermute(
-        jnp.stack([displacement[:, :, :, 0], displacement[:, :, :, 1]], axis=2), "narrow", ring("narrow", -1)
-    )
-    yh = jnp.concatenate([low[:, :, None], high], axis=2)
-    loads, comps, own_x, rows, size_z = displacement.shape
-    blocks = material.shape[2]
-    corner = yh[:, :, :, :3].reshape(loads * comps * 3, 3, size_z)
-    first = material[0].astype(jnp.float32).reshape(-1)
-    first = jnp.pad(first, (0, 3 * size_z - first.size)).reshape(1, 3, size_z)
-    got = lax.ppermute(jnp.concatenate([corner, first], axis=0), "wide", backward)
-    ch = got[: loads * comps * 3].reshape(loads, comps, 3, 3, size_z)
-    beyond = got[loads * comps * 3].reshape(-1)[: rows * blocks].reshape(1, rows, blocks)
-    solid = jnp.concatenate([material[1:].astype(jnp.float32), beyond], axis=0)
-    stiff = 0.2 + 0.8 * jnp.repeat(solid, BZ, axis=2)
-    last = (lax.axis_index("wide") == wide - 1).astype(jnp.int32).reshape(1)
-    return strain_message(last, displacement, yh, xh, ch, stiff, wide)
-
-
-YE = 10
-Y1 = 6
-Y2 = 3
-VMEM_LIMIT = 48 * 1024 * 1024
 
 
 def newton_reciprocal(x):
@@ -336,8 +354,43 @@
     lax.fori_loop(0, lanes // 128, lane_step, 0)
 
 
-def first_gradient_kernel(ls_ref, sp_ref, sm_ref):
+def first_gradient_kernel(place_ref, tall_ref, ra_ref, rb_ref, ls_ref, sp_ref, sm_ref):
     layers, rows, lanes = sp_ref.shape
+    depth, own, _ = tall_ref.shape
+    ones = jnp.ones((8, lanes), jnp.float32)
+
+    def copy(z, carry):
+        for t in range(ls_ref.shape[1] // 8):
+            ls_ref[z, 8 * t : 8 * t + 8, :] = ones
+        ls_ref[z, YE : YE + own, :] = tall_ref[z]
+        return carry
+
+    lax.fori_loop(0, depth, copy, 0)
+
+    def below(ref):
+        @pl.when(place_ref[4] == 0)
+        def _():
+            for z in range(depth):
+                ls_ref[z, YE - 8 : YE, :] = ref[z]
+                ls_ref[z, YE - 9 : YE - 8, :] = ref[depth + z // 8, z % 8 : z % 8 + 1, :]
+
+    def above(ref):
+        @pl.when(place_ref[5] == 0)
+        def _():
+            for z in range(depth):
+                ls_ref[z, YE + own : YE + own + 8, :] = ref[z]
+                ls_ref[z, YE + own + 8 : YE + own + 9, :] = ref[depth + z // 8, z % 8 : z % 8 + 1, :]
+
+    @pl.when(place_ref[3] == 1)
+    def _():
+        above(ra_ref)
+        below(rb_ref)
+
+    @pl.when(place_ref[3] == 0)
+    def _():
+        below(ra_ref)
+        above(rb_ref)
+
     offset = YE - Y1
     xy_stage(ls_ref, offset, 3, layers, sp_ref, sm_ref)
 
@@ -545,26 +598,39 @@
     return first, second
 
 
-def level_halo(level_set, place):
-    first, second = swaps("wide")
-    layers, rows, lanes = level_set.shape
-    even = place[0] == 1
-    low, high = level_set[:3], level_set[layers - 3 :]
-    got_a = lax.ppermute(jnp.where(even, high, low), "wide", first)
-    got_b = lax.ppermute(jnp.where(even, low, high), "wide", second)
-    below = jnp.where(even, got_b, got_a)
-    above = jnp.where(even, got_a, got_b)
-    below = jnp.where(place[1] == 1, 1.0, below)
-    above = jnp.where(place[2] == 1, 1.0, above)
-    tall = jnp.concatenate([below, level_set, above], axis=0)
-    low = lax.ppermute(tall[:, rows - 9 :], "narrow", ring("narrow", 1))
-    high = lax.ppermute(tall[:, :9], "narrow", ring("narrow", -1))
-    low = jnp.where(place[4] == 1, 1.0, low)
-    high = jnp.where(place[5] == 1, 1.0, high)
-    total = -(-(rows + 2 * YE) // 8) * 8
-    left = jnp.ones((layers + 6, YE - 9, lanes), jnp.float32)
-    right = jnp.ones((layers + 6, total - rows - 9 - YE, lanes), jnp.float32)
-    return jnp.concatenate([left, low, tall, high, right], axis=1)
+def stack_kernel(place_ref, ls_ref, ra_ref, rb_ref, tall_ref, ma_ref, mb_ref, edges):
+    layers, rows = ls_ref.shape[:2]
+    take_edges(place_ref, ra_ref, rb_ref, edges)
+    for k in range(3):
+        tall_ref[k] = edges[k]
+        tall_ref[layers + 3 + k] = edges[3 + k]
+
+    def copy(z, carry):
+        tall_ref[z + 3] = ls_ref[z]
+        return carry
+
+    lax.fori_loop(0, layers, copy, 0)
+    depth = layers + 6
+
+    def upper(ref):
+        for z in range(depth):
+            ref[z] = tall_ref[z, rows - 8 : rows, :]
+            ref[depth + z // 8, z % 8 : z % 8 + 1, :] = tall_ref[z, rows - 9 : rows - 8, :]
+
+    def lower(ref):
+        for z in range(depth):
+            ref[z] = tall_ref[z, 0:8, :]
+            ref[depth + z // 8, z % 8 : z % 8 + 1, :] = tall_ref[z, 8:9, :]
+
+    @pl.when(place_ref[3] == 1)
+    def _():
+        upper(ma_ref)
+        lower(mb_ref)
+
+    @pl.when(place_ref[3] == 0)
+    def _():
+        lower(ma_ref)
+        upper(mb_ref)
 
 
 def level_part(place, tile, ma, mb, wide_peak, level_set, ls, sp, sm):
@@ -611,9 +677,22 @@
     return phi, speed
 
 
-def first_gradient(ls, layers, rows):
+def first_gradient(place, tall, ra, rb):
+    depth, rows, lanes = tall.shape
     rows1 = -(-(rows + 2 * Y1) // 8) * 8
-    return vmem_call(first_gradient_kernel, [(layers, rows1, ls.shape[2])] * 2, (ls,), (), 25000)
+    total = -(-(rows + 2 * YE) // 8) * 8
+    return vmem_call(
+        first_gradient_kernel, [(depth, total, lanes)] + [(depth - 6, rows1, lanes)] * 2, (place, tall, ra, rb), (), 35000
+    )
+
+
+def stack_level(place, level_set, ra, rb):
+    layers, rows, lanes = level_set.shape
+    depth = layers + 6
+    edge = (depth + -(-depth // 8), 8, lanes)
+    return vmem_call(
+        stack_kernel, [(depth, rows, lanes), edge, edge], (place, level_set, ra, rb), [(6, rows, lanes)], 1500
+    )
 
 
 def unpack_kernel(place_ref, recv_ref, tile_ref, peak_ref, ma_ref, mb_ref):
@@ -671,12 +750,45 @@
 
 def per_device(displacement, material, level_set):
     wide = lax.axis_size("wide")
-    own_z, rows, size_x = level_set.shape
+    loads, comps, own_x, rows, size_z = displacement.shape
+    own_z, _, size_x = level_set.shape
     place = place_flags()
-    message = energy_message(displacement, material).reshape(wide, 88, 128)
-    ls = level_halo(level_set, place)
-    sp, sm = first_gradient(ls, own_z, rows)
-    recv = lax.all_to_all(message, "wide", split_axis=0, concat_axis=0, tiled=True)
+    backward = [(i, (i - 1) % wide) for i in range(wide)]
+    wfirst, wsecond = swaps("wide")
+    nfirst, nsecond = swaps("narrow")
+
+    xh = lax.ppermute(displacement[:, :, :3], "wide", backward)
+    low = lax.ppermute(displacement[:, :, :, -1], "narrow", ring("narrow", 1))
+    high = lax.ppermute(
+        jnp.stack([displacement[:, :, :, 0], displacement[:, :, :, 1]], axis=2), "narrow", ring("narrow", -1)
+    )
+    yh = jnp.concatenate([low[:, :, None], high], axis=2)
+    blocks = material.shape[2]
+    corner = yh[:, :, :, :3].reshape(loads * comps * 3, 3, size_z)
+    first = material[0].astype(jnp.float32).reshape(-1)
+    first = jnp.pad(first, (0, 3 * size_z - first.size)).reshape(1, 3, size_z)
+    got = lax.ppermute(jnp.concatenate([corner, first], axis=0), "wide", backward)
+    ch = got[: loads * comps * 3].reshape(loads, comps, 3, 3, size_z)
+    beyond = got[loads * comps * 3].reshape(-1)[: rows * blocks].reshape(1, rows, blocks)
+    solid = jnp.concatenate([material[1:].astype(jnp.float32), beyond], axis=0)
+    stiff = 0.2 + 0.8 * jnp.repeat(solid, BZ, axis=2)
+
+    bounds = level_set[:3], level_set[own_z - 3 :]
+    even = place[0] == 1
+    la = lax.ppermute(jnp.where(even, bounds[1], bounds[0]), "wide", wfirst)
+    lb = lax.ppermute(jnp.where(even, bounds[0], bounds[1]), "wide", wsecond)
+
+    inner, tail = inner_strain(displacement, yh)
+    la, lb, inner = lax.optimization_barrier((la, lb, inner))
+    tall, ya, yb = stack_level(place, level_set, la, lb)
+    ya = lax.ppermute(ya, "narrow", nfirst)
+    yb = lax.ppermute(yb, "narrow", nsecond)
+    xh, ya, yb = lax.optimization_barrier((xh, ya, yb))
+    message = strain_message(place, tail, xh, ch, inner, stiff, wide)
+    message, tall = lax.optimization_barrier((message, tall))
+    recv = lax.all_to_all(message.reshape(wide, 88, 128), "wide", split_axis=0, concat_axis=0, tiled=True)
+    ls, sp, sm = first_gradient(place, tall, ya, yb)
+    recv, sp = lax.optimization_barrier((recv, sp))
     tile, wide_peak, ma, mb = unpack(place, recv, own_z, rows)
     return level_part(place, tile, ma, mb, wide_peak, level_set, ls, sp, sm)
 

time: 242 us -> 219 us (0.905)
  waiting for transfers between devices: 47.9 us -> 14.6 us
  starting transfers between devices: 51.8 us -> 67.8 us
  local copies, waits for them, and re-layouts: 28.4 us -> 20.9 us
  Pallas kernels: 108 us -> 112 us
    ppermute x8, waiting for transfers between devices: 46.3 us -> 4.54 us  [the longest x1 4.46 us: per_device(): yb = lax.ppermute(yb, 'narrow', nsecond)]
    ppermute x8, starting transfers between devices: 19 us -> 42.2 us  [the longest x1 24.9 us: per_device(): ya = lax.ppermute(ya, 'narrow', nfirst)]
    concatenate x1 -> x0, local copies, waits for them, and re-layouts: 14.3 us -> none  [level_halo(): return jnp.concatenate([left, low, tall, high, right], axis=1)]
    unnamed x13 -> x31, local copies, waits for them, and re-layouts: 1.07 us -> 10.5 us
    ppermute x1, waiting for transfers between devices: 0.01 us -> 9.33 us  [level_part(): rb = lax.ppermute(mb, 'narrow', nsecond)]
    ppermute x2, starting transfers between devices: 10.5 us -> 4.22 us  [level_part(): gb = lax.ppermute(sb, 'wide', wsecond)]
    ppermute x2, starting transfers between devices: 1.23 us -> 7.24 us  [level_part(): ga = lax.ppermute(sa, 'wide', wfirst)]
    ppermute x1, starting transfers between devices: 5.55 us -> 1.42 us  [level_part(): pc = lax.ppermute(wide_peak, 'narrow', across)]
  transfers between devices with their start and end apart: 16 -> 16, of which waited for: 5 -> 4; matrix products, arithmetic and copies ran while one was open for 12% -> 5% of each run, Pallas kernels for 21% -> 35%
where the time goes in v3:
time: 219 us
  Pallas kernels  112 us (51%)
  starting transfers between devices  67.8 us (31%)
  local copies, waits for them, and re-layouts  20.9 us (10%)
  waiting for transfers between devices  14.6 us (7%)
  other arithmetic  2.47 us (1%)
    pallas_call x8, Pallas kernels, vmem_call(): pl.pallas_call(kernel, out_shape=tuple((jax.ShapeDtypeStruct(shape, jnp.f...  78.4 us
    pallas_call x1, Pallas kernels, inner_strain(): pl.pallas_call(inner_kernel, grid=(loads,), out_shape=(jax.ShapeDtypeStru...  25.4 us
    ppermute x1, starting transfers between devices, per_device(): ya = lax.ppermute(ya, 'narrow', nfirst)  24.9 us
    all_to_all x1, starting transfers between devices, per_device(): lax.all_to_all(message.reshape(wide, 88, 128), 'wide', split_axis=0, conc...  12 us
    unnamed x31, local copies, waits for them, and re-layouts  10.5 us
    ppermute x1, waiting for transfers between devices, level_part(): rb = lax.ppermute(mb, 'narrow', nsecond)  9.33 us
    pallas_call x1, Pallas kernels, strain_message(): pl.pallas_call(outer_kernel, grid=(loads,), out_shape=jax.ShapeDtypeStruc...  8.11 us
    ppermute x2, starting transfers between devices, level_part(): ga = lax.ppermute(sa, 'wide', wfirst)  7.24 us
  transfers between devices with their start and end apart: 16, of which 4 were waited for; matrix products, arithmetic and copies ran while one was open for 5% of the time, Pallas kernels for 35%

profile of v3, /device:TPU:2, one launch (start us, length us, event | category | flops | bytes accessed | tf_op | source)
XLA Modules:
  0.0 218.6 jit_solution(15195082767656141151)
XLA Ops:
  0.6 2.6 %slice.45 = f32[3,3,3,32,384]{4,3,2,1,0:T(8,128)} slice(f32[3,3,16,32,384]{4,3,2,1,0:T(8,128)} %u_ref.1), slice={[0:3], [0:3], [0:3], [0:32], [0:384]} | slice | bytes 2654208 | tf_op jit(solution)/shard_map/slice | solution.py:760
  3.2 3.2 %collective-permute-start.2 = (f32[3,3,3,32,384]{4,3,2,1,0:T(8,128)}, f32[3,3,3,32,384]{4,3,2,1,0:T(8,128)S(1)}, u32[]{:S(2)}, u32[]{:S(2)}) collective-permute-start(f32[3,3,3,32,384]{4,3,2,1,0:T(8,128)} %slice.45), channel_id=1, source_target_pairs={{0,124},{4,0},{8,4},{12,8},{16,12},{20,16},{24,20},{28,24},{32,28}... | collective-permute-start | bytes 3981320 | tf_op jit(solution)/shard_map/ppermute | solution.py:760
  6.4 3.1 %fusion.2 = (f32[3,3,16,1,384]{4,3,2,1,0:T(1,128)S(1)}, f32[3,3,16,1,384]{4,3,2,1,0:T(1,128)S(1)}, f32[3,3,16,1,384]{4,3,2,1,0:T(1,128)S(1)}) fusion(f32[3,3,16,32,384]{4,3,2,1,0:T(8,128)} %u_ref.1), kind=kLoop, calls=%fused_computation.17 | loop fusion | bytes 1327104 | tf_op jit(solution)/shard_map/slice | solution.py:763
  9.4 0.1 copy_bitcast_fusion
  9.5 0.8 pad_maximum_fusion.1
  10.3 1.3 collective-permute-start.1
  11.6 0.8 slice_select_fusion
  12.4 0.3 collective-permute-start.4
  12.6 4.2 %collective-permute-start.3 = (f32[3,32,512]{2,1,0:T(8,128)}, f32[3,32,512]{2,1,0:T(8,128)S(1)}, u32[]{:S(2)}, u32[]{:S(2)}) collective-permute-start(f32[3,32,512]{2,1,0:T(8,128)} %get-tuple-element.74), channel_id=1, source_target_pairs={{0,4},{4,0},{8,12},{12,8},{16,20},{20,16},{24,28},{28,24},{32,36},... | collective-permute-start | bytes 589832 | tf_op jit(solution)/shard_map/ppermute | solution.py:778
  16.9 2.5 %collective-permute-start = (f32[3,3,16,384]{3,2,1,0:T(8,128)S(1)}, f32[3,3,16,384]{3,2,1,0:T(8,128)S(1)}, u32[]{:S(2)}, u32[]{:S(2)}) collective-permute-start(f32[3,3,16,384]{3,2,1,0:T(8,128)S(1)} %bitcast.27), channel_id=1, source_target_pairs={{0,1},{1,2},{2,3},{4,5},{5,6},{6,7},{8,9},{9,10},{10,11},{12,13},{... | collective-permute-start | bytes 663560 | tf_op jit(solution)/shard_map/ppermute | solution.py:761
  19.4 0.7 slice_convert_fusion.1
  20.1 0.1 copy.12
  20.2 0.1 convert_element_type.17
  20.3 0.1 stack.46.place_ref
  20.4 0.1 collective-permute-done
  20.4 0.0 collective-permute-done.1
  20.5 5.1 %collective-permute-start.7 = (f32[28,3,384]{2,1,0:T(4,128)S(1)}, f32[28,3,384]{2,1,0:T(4,128)S(1)}, u32[]{:S(2)}, u32[]{:S(2)}) collective-permute-start(f32[28,3,384]{2,1,0:T(4,128)S(1)} %pad_maximum_fusion.2), channel_id=1, source_target_pairs={{0,124},{4,0},{8,4},{12,8},{16,12},{20,16},{24,20},{28,24},{32,28}... | collective-permute-start | bytes 387080 | tf_op jit(solution)/shard_map/ppermute | solution.py:770
  25.7 0.0 copy-start.12
  25.7 25.4 %shard_map.50 = (f32[13,32,384]{2,1,0:T(8,128)S(1)}, f32[3,3,3,3,32,384]{5,4,3,2,1,0:T(8,128)S(1)}) custom-call(f32[3,3,16,32,384]{4,3,2,1,0:T(8,128)} %u_ref.1, f32[3,3,3,16,384]{4,3,2,1,0:T(8,128)S(1)} %pad_maximum_fusion.yh_ref), custom_call_target="tpu_custom_call" | custom-call | flops 163840000 | bytes 1048576 | tf_op jit(solution)/shard_map/pallas_call | solution.py:201
  51.1 1.9 copy-done
  53.0 0.8 copy-done.8
  53.8 0.0 collective-permute-done.4.rb_ref
  53.8 0.0 collective-permute-done.3.ra_ref
  53.8 0.7 copy-done.10
  54.5 0.9 copy-done.11
  55.4 1.6 shard_map.51
  57.0 24.9 %collective-permute-start.5 = (f32[21,8,512]{2,1,0:T(8,128)}, f32[21,8,512]{2,1,0:T(8,128)}, u32[]{:S(2)}, u32[]{:S(2)}) collective-permute-start(f32[21,8,512]{2,1,0:T(8,128)} %get-tuple-element.40), channel_id=1, source_target_pairs={{0,1},{1,0},{2,3},{3,2},{4,5},{5,4},{6,7},{7,6},{8,9},{9,8},{10,11... | collective-permute-start | bytes 1032200 | tf_op jit(solution)/shard_map/ppermute | solution.py:784
  81.9 0.8 collective-permute-start.6
  82.7 0.0 collective-permute-done.7
  82.7 0.7 copy-done.13
  83.4 0.1 reshape.32
  83.5 0.1 copy.13
  83.6 1.9 broadcast_in_dim.7
  85.5 2.4 %copy.14.stiff_ref = f32[16,32,384]{2,1,0:T(8,128)S(1)} copy(f32[16,32,384]{1,2,0:T(8,128)} %bitcast.23) | data formatting | bytes 1572864 | tf_op jit(solution)/shard_map/add | solution.py:774
  87.9 0.0 collective-permute-done.5.ra_ref
  87.9 4.5 %collective-permute-done.6.rb_ref = f32[21,8,512]{2,1,0:T(8,128)} collective-permute-done((f32[21,8,512]{2,1,0:T(8,128)}, f32[21,8,512]{2,1,0:T(8,128)}, u32[]{:S(2)}, u32[]{:S(2)}) %collective-permute-start.6) | collective-permute-done | bytes 344096 | tf_op jit(solution)/shard_map/ppermute | solution.py:785
  92.4 0.0 collective-permute-done.2.xh_ref
  92.4 1.1 copy-done.9
  93.5 8.1 %shard_map.52 = f32[2816,128]{1,0:T(8,128)} custom-call(s32[6]{0:T(128)S(1)} %stack.46.place_ref, f32[3,3,3,3,32,384]{5,4,3,2,1,0:T(8,128)} %copy-done, f32[3,3,3,32,384]{4,3,2,1,0:T(8,128)S(1)} %collective-permute-done.2.xh_ref, f32[3,3,3,3,384]{4,3,2,1,0:T(4,128)S(1)} %bitcast.22, f32[13,32,384]{2,1,0:T(8,128)S(1)} %copy-done.9, ...), custom_call_target="tpu_custom_call" | custom-call | flops 40960000 | bytes 1048576 | tf_op jit(solution)/shard_map/pallas_call | solution.py:222
  101.6 12.0 %all-to-all-start = ((f32[32,88,128]{2,1,0:T(8,128)}), f32[32,88,128]{2,1,0:T(8,128)S(1)}, u32[]{:S(2)}, u32[]{:S(2)}) async-start(f32[32,88,128]{2,1,0:T(8,128)} %bitcast.13), calls=%async_computation | async-start | bytes 2883584 | tf_op jit(solution)/shard_map/all_to_all | solution.py:789
  113.6 23.1 %shard_map.53 = (f32[18,56,512]{2,1,0:T(8,128)}, f32[12,48,512]{2,1,0:T(8,128)S(1)}, f32[12,48,512]{2,1,0:T(8,128)S(1)}) custom-call(s32[6]{0:T(128)S(1)} %stack.46.place_ref, f32[18,32,512]{2,1,0:T(8,128)S(1)} %get-tuple-element.46.tall_ref, f32[21,8,512]{2,1,0:T(8,128)} %collective-permute-done.5.ra_ref, f32[21,8,512]{2,1,0:T(8,128)} %collective-permute-done.6.rb_ref), custom_call_target="tpu_custom_call" | custom-call | flops 143360000 | bytes 1048576 | tf_op jit(solution)/shard_map/pallas_call | solution.py:413
  136.7 1.0 copy-done.3
  137.7 1.0 copy-done.5
  138.8 0.0 all-to-all-done.recv_ref
  138.8 1.4 shard_map.54
  140.2 1.1 copy-done.2
  141.2 0.0 collective-permute-start.8
  141.2 0.7 collective-permute-start.9
  142.0 1.4 collective-permute-start.10
  143.4 0.0 collective-permute-done.8.ra_ref
  143.4 9.3 %collective-permute-done.9.rb_ref = f32[26,8,512]{2,1,0:T(8,128)S(1)} collective-permute-done((f32[26,8,512]{2,1,0:T(8,128)S(1)}, f32[26,8,512]{2,1,0:T(8,128)S(1)}, u32[]{:S(2)}, u32[]{:S(2)}) %collective-permute-start.9) | collective-permute-done | bytes 426016 | tf_op jit(solution)/shard_map/ppermute | solution.py:643
  152.7 0.7 collective-permute-done.10.pc_ref
  153.4 1.3 copy-done.6
  154.7 14.6 %shard_map.55 = (f32[12,32,512]{2,1,0:T(8,128)}, f32[12,48,512]{2,1,0:T(8,128)S(1)}, f32[12,48,512]{2,1,0:T(8,128)S(1)}, f32[3,40,512]{2,1,0:T(8,128)S(1)}, f32[3,40,512]{2,1,0:T(8,128)S(1)}) custom-call(s32[6]{0:T(128)S(1)} %stack.46.place_ref, f32[20,32,512]{2,1,0:T(8,128)} %copy-done.2, f32[26,8,512]{2,1,0:T(8,128)S(1)} %collective-permute-done.8.ra_ref, ...), custom_call_target="tpu_custom_call" | custom-call | flops 32768000 | bytes 1048576 | tf_op jit(solution)/shard_map/pallas_call | solution.py:413
  169.4 3.0 %collective-permute-start.11 = (f32[3,40,512]{2,1,0:T(8,128)S(1)}, f32[3,40,512]{2,1,0:T(8,128)S(1)}, u32[]{:S(2)}, u32[]{:S(2)}) collective-permute-start(f32[3,40,512]{2,1,0:T(8,128)S(1)} %get-tuple-element.59), channel_id=1, source_target_pairs={{0,4},{4,0},{8,12},{12,8},{16,20},{20,16},{24,28},{28,24},{32,36},... | collective-permute-start | bytes 737288 | tf_op jit(solution)/shard_map/ppermute | solution.py:657
  172.3 0.2 collective-permute-start.12
  172.6 13.7 %shard_map.56 = (f32[12,40,512]{2,1,0:T(8,128)S(1)}, f32[12,40,512]{2,1,0:T(8,128)S(1)}) custom-call(f32[12,48,512]{2,1,0:T(8,128)S(1)} %get-tuple-element.58.phi_ref), custom_call_target="tpu_custom_call" | custom-call | flops 49152000 | bytes 1048576 | tf_op jit(solution)/shard_map/pallas_call | solution.py:413
  186.3 0.0 collective-permute-done.11.ra_ref
  186.3 5.9 %shard_map.57 = (f32[12,40,512]{2,1,0:T(8,128)S(1)}, f32[3,32,512]{2,1,0:T(8,128)S(1)}, f32[3,32,512]{2,1,0:T(8,128)S(1)}) custom-call(s32[6]{0:T(128)S(1)} %stack.46.place_ref, f32[12,48,512]{2,1,0:T(8,128)S(1)} %get-tuple-element.58.phi_ref, f32[3,40,512]{2,1,0:T(8,128)S(1)} %collective-permute-done.11.ra_ref, ...), custom_call_target="tpu_custom_call" | custom-call | flops 20480000 | bytes 1048576 | tf_op jit(solution)/shard_map/pallas_call | solution.py:413
  192.2 0.0 copy-start.7
  192.3 4.3 %collective-permute-start.13 = (f32[3,32,512]{2,1,0:T(8,128)S(1)}, f32[3,32,512]{2,1,0:T(8,128)S(1)}, u32[]{:S(2)}, u32[]{:S(2)}) collective-permute-start(f32[3,32,512]{2,1,0:T(8,128)S(1)} %get-tuple-element.65), channel_id=1, source_target_pairs={{0,4},{4,0},{8,12},{12,8},{16,20},{20,16},{24,28},{28,24},{32,36},... | collective-permute-start | bytes 589832 | tf_op jit(solution)/shard_map/ppermute | solution.py:667
  196.5 4.0 %collective-permute-start.14 = (f32[3,32,512]{2,1,0:T(8,128)S(1)}, f32[3,32,512]{2,1,0:T(8,128)S(1)}, u32[]{:S(2)}, u32[]{:S(2)}) collective-permute-start(f32[3,32,512]{2,1,0:T(8,128)S(1)} %get-tuple-element.66), channel_id=1, source_target_pairs={{4,8},{8,4},{12,16},{16,12},{20,24},{24,20},{28,32},{32,28},{36,40... | collective-permute-start | bytes 589832 | tf_op jit(solution)/shard_map/ppermute | solution.py:668
  200.5 12.6 %shard_map.58 = (f32[12,32,512]{2,1,0:T(8,128)S(1)}, f32[12,32,512]{2,1,0:T(8,128)S(1)}) custom-call(f32[12,40,512]{2,1,0:T(8,128)S(1)} %get-tuple-element.64.phi_ref), custom_call_target="tpu_custom_call" | custom-call | flops 49152000 | bytes 1048576 | tf_op jit(solution)/shard_map/pallas_call | solution.py:413
  213.2 5.4 %shard_map.59 = f32[12,32,512]{2,1,0:T(8,128)} custom-call(s32[6]{0:T(128)S(1)} %stack.46.place_ref, f32[12,40,512]{2,1,0:T(8,128)S(1)} %get-tuple-element.64.phi_ref, f32[3,32,512]{2,1,0:T(8,128)S(1)} %collective-permute-done.13.ra_ref, f32[3,32,512]{2,1,0:T(8,128)S(1)} %collective-permute-done.14.rb_ref, f32[12,32,512]{2,1,0:T(8,128)S(1)} %get-tuple-element.67.gp_ref, ...), custom_call_target="tpu_custom_call" | custom-call | flops 20480000 | bytes 1048576 | tf_op jit(solution)/shard_map/pallas_call | solution.py:413
  (33 shorter events, 0.3 us)
Async XLA Ops:
  3.2 8.4 %copy-start.1 = (f32[12,32,512]{2,1,0:T(8,128)S(1)}, f32[12,32,512]{2,1,0:T(8,128)}, u32[]{:S(2)}) copy-start(f32[12,32,512]{2,1,0:T(8,128)} %ls_ref.1) | copy-start | bytes 2359300
  3.2 89.2 %collective-permute-start.2 = (f32[3,3,3,32,384]{4,3,2,1,0:T(8,128)}, f32[3,3,3,32,384]{4,3,2,1,0:T(8,128)S(1)}, u32[]{:S(2)}, u32[]{:S(2)}) collective-permute-start(f32[3,3,3,32,384]{4,3,2,1,0:T(8,128)} %slice.45), channel_id=1, source_target_pairs={{0,124},{4,0},{8,4},{12,8},{16,12},{20,16},{24,20},{28,24},{32,28}... | collective-permute-start | bytes 3981320 | tf_op jit(solution)/shard_map/ppermute | solution.py:760
  10.3 10.1 %collective-permute-start.1 = (f32[3,3,2,16,384]{4,3,2,1,0:T(8,128)}, f32[3,3,2,16,384]{4,3,2,1,0:T(8,128)S(1)}, u32[]{:S(2)}, u32[]{:S(2)}) collective-permute-start(f32[3,3,2,16,384]{4,3,2,1,0:T(8,128)} %pad_maximum_fusion.1), channel_id=1, source_target_pairs={{1,0},{2,1},{3,2},{5,4},{6,5},{7,6},{9,8},{10,9},{11,10},{13,12},{... | collective-permute-start | bytes 1327112 | tf_op jit(solution)/shard_map/ppermute | solution.py:762
  12.4 41.4 %collective-permute-start.4 = (f32[3,32,512]{2,1,0:T(8,128)}, f32[3,32,512]{2,1,0:T(8,128)S(1)}, u32[]{:S(2)}, u32[]{:S(2)}) collective-permute-start(f32[3,32,512]{2,1,0:T(8,128)} %get-tuple-element.73), channel_id=1, source_target_pairs={{4,8},{8,4},{12,16},{16,12},{20,24},{24,20},{28,32},{32,28},{36,40... | collective-permute-start | bytes 589832 | tf_op jit(solution)/shard_map/ppermute | solution.py:779
  12.6 41.2 %collective-permute-start.3 = (f32[3,32,512]{2,1,0:T(8,128)}, f32[3,32,512]{2,1,0:T(8,128)S(1)}, u32[]{:S(2)}, u32[]{:S(2)}) collective-permute-start(f32[3,32,512]{2,1,0:T(8,128)} %get-tuple-element.74), channel_id=1, source_target_pairs={{0,4},{4,0},{8,12},{12,8},{16,20},{20,16},{24,28},{28,24},{32,36},... | collective-permute-start | bytes 589832 | tf_op jit(solution)/shard_map/ppermute | solution.py:778
  16.9 3.6 %collective-permute-start = (f32[3,3,16,384]{3,2,1,0:T(8,128)S(1)}, f32[3,3,16,384]{3,2,1,0:T(8,128)S(1)}, u32[]{:S(2)}, u32[]{:S(2)}) collective-permute-start(f32[3,3,16,384]{3,2,1,0:T(8,128)S(1)} %bitcast.27), channel_id=1, source_target_pairs={{0,1},{1,2},{2,3},{4,5},{5,6},{6,7},{8,9},{9,10},{10,11},{12,13},{... | collective-permute-start | bytes 663560 | tf_op jit(solution)/shard_map/ppermute | solution.py:761
  20.5 62.2 %collective-permute-start.7 = (f32[28,3,384]{2,1,0:T(4,128)S(1)}, f32[28,3,384]{2,1,0:T(4,128)S(1)}, u32[]{:S(2)}, u32[]{:S(2)}) collective-permute-start(f32[28,3,384]{2,1,0:T(4,128)S(1)} %pad_maximum_fusion.2), channel_id=1, source_target_pairs={{0,124},{4,0},{8,4},{12,8},{16,12},{20,16},{24,20},{28,24},{32,28}... | collective-permute-start | bytes 387080 | tf_op jit(solution)/shard_map/ppermute | solution.py:770
  25.7 57.0 %copy-start.12 = (s32[16,32,24]{1,2,0:T(8,128)S(1)}, s32[16,32,24]{1,2,0:T(8,128)}, u32[]{:S(2)}) copy-start(s32[16,32,24]{1,2,0:T(8,128)} %param.4) | copy-start | bytes 147460
  51.1 1.9 copy-start
  53.0 0.8 copy-start.8
  53.8 0.7 copy-start.10
  54.5 0.9 copy-start.11
  57.0 30.9 %collective-permute-start.5 = (f32[21,8,512]{2,1,0:T(8,128)}, f32[21,8,512]{2,1,0:T(8,128)}, u32[]{:S(2)}, u32[]{:S(2)}) collective-permute-start(f32[21,8,512]{2,1,0:T(8,128)} %get-tuple-element.40), channel_id=1, source_target_pairs={{0,1},{1,0},{2,3},{3,2},{4,5},{5,4},{6,7},{7,6},{8,9},{9,8},{10,11... | collective-permute-start | bytes 1032200 | tf_op jit(solution)/shard_map/ppermute | solution.py:784
  81.9 10.5 %collective-permute-start.6 = (f32[21,8,512]{2,1,0:T(8,128)}, f32[21,8,512]{2,1,0:T(8,128)}, u32[]{:S(2)}, u32[]{:S(2)}) collective-permute-start(f32[21,8,512]{2,1,0:T(8,128)} %get-tuple-element.41), channel_id=1, source_target_pairs={{1,2},{2,1},{3,0},{0,3},{5,6},{6,5},{7,4},{4,7},{9,10},{10,9},{11,... | collective-permute-start | bytes 1032200 | tf_op jit(solution)/shard_map/ppermute | solution.py:785
  82.7 0.7 copy-start.13
  85.5 2.4 %copy-start.14 = (f32[28,3,384]{2,1,0:T(4,128)S(1)}, f32[28,3,384]{2,1,0:T(4,128)}, u32[]{:S(2)}) copy-start(f32[28,3,384]{2,1,0:T(4,128)} %copy-done.13) | copy-start | bytes 387076
  92.4 1.1 copy-start.9
  101.6 37.2 %all-to-all-start = ((f32[32,88,128]{2,1,0:T(8,128)}), f32[32,88,128]{2,1,0:T(8,128)S(1)}, u32[]{:S(2)}, u32[]{:S(2)}) async-start(f32[32,88,128]{2,1,0:T(8,128)} %bitcast.13), calls=%async_computation | async-start | bytes 2883584 | tf_op jit(solution)/shard_map/all_to_all | solution.py:789
  136.7 1.1 copy-start.3
  137.7 1.0 copy-start.5
  138.8 14.7 %copy-start.4 = (f32[12,48,512]{2,1,0:T(8,128)S(1)}, f32[12,48,512]{2,1,0:T(8,128)}, u32[]{:S(2)}) copy-start(f32[12,48,512]{2,1,0:T(8,128)} %copy-done.3) | copy-start | bytes 3538948
  140.2 1.1 copy-start.2
  141.2 2.1 collective-permute-start.8
  141.2 11.5 %collective-permute-start.9 = (f32[26,8,512]{2,1,0:T(8,128)S(1)}, f32[26,8,512]{2,1,0:T(8,128)S(1)}, u32[]{:S(2)}, u32[]{:S(2)}) collective-permute-start(f32[26,8,512]{2,1,0:T(8,128)S(1)} %get-tuple-element.53), channel_id=1, source_target_pairs={{1,2},{2,1},{3,0},{0,3},{5,6},{6,5},{7,4},{4,7},{9,10},{10,9},{11,... | collective-permute-start | bytes 1277960 | tf_op jit(solution)/shard_map/ppermute | solution.py:643
  142.0 11.5 %collective-permute-start.10 = (f32[8,128]{1,0:T(8,128)S(1)}, f32[8,128]{1,0:T(8,128)S(1)}, u32[]{:S(2)}, u32[]{:S(2)}) collective-permute-start(f32[8,128]{1,0:T(8,128)S(1)} %get-tuple-element.54.po_ref), channel_id=1, source_target_pairs={{0,2},{1,3},{2,0},{3,1},{4,6},{5,7},{6,4},{7,5},{8,10},{9,11},{10,... | collective-permute-start | bytes 12296 | tf_op jit(solution)/shard_map/ppermute | solution.py:644
  153.4 1.3 copy-start.6
  169.4 16.9 %collective-permute-start.11 = (f32[3,40,512]{2,1,0:T(8,128)S(1)}, f32[3,40,512]{2,1,0:T(8,128)S(1)}, u32[]{:S(2)}, u32[]{:S(2)}) collective-permute-start(f32[3,40,512]{2,1,0:T(8,128)S(1)} %get-tuple-element.59), channel_id=1, source_target_pairs={{0,4},{4,0},{8,12},{12,8},{16,20},{20,16},{24,28},{28,24},{32,36},... | collective-permute-start | bytes 737288 | tf_op jit(solution)/shard_map/ppermute | solution.py:657
  172.3 14.0 %collective-permute-start.12 = (f32[3,40,512]{2,1,0:T(8,128)S(1)}, f32[3,40,512]{2,1,0:T(8,128)S(1)}, u32[]{:S(2)}, u32[]{:S(2)}) collective-permute-start(f32[3,40,512]{2,1,0:T(8,128)S(1)} %get-tuple-element.60), channel_id=1, source_target_pairs={{4,8},{8,4},{12,16},{16,12},{20,24},{24,20},{28,32},{32,28},{36,40... | collective-permute-start | bytes 737288 | tf_op jit(solution)/shard_map/ppermute | solution.py:658
  192.2 20.9 %copy-start.7 = (f32[12,32,512]{2,1,0:T(8,128)S(1)}, f32[12,32,512]{2,1,0:T(8,128)}, u32[]{:S(2)}) copy-start(f32[12,32,512]{2,1,0:T(8,128)} %get-tuple-element.35.speed_ref) | copy-start | bytes 2359300
  192.3 20.9 %collective-permute-start.13 = (f32[3,32,512]{2,1,0:T(8,128)S(1)}, f32[3,32,512]{2,1,0:T(8,128)S(1)}, u32[]{:S(2)}, u32[]{:S(2)}) collective-permute-start(f32[3,32,512]{2,1,0:T(8,128)S(1)} %get-tuple-element.65), channel_id=1, source_target_pairs={{0,4},{4,0},{8,12},{12,8},{16,20},{20,16},{24,28},{28,24},{32,36},... | collective-permute-start | bytes 589832 | tf_op jit(solution)/shard_map/ppermute | solution.py:667
  196.5 16.6 %collective-permute-start.14 = (f32[3,32,512]{2,1,0:T(8,128)S(1)}, f32[3,32,512]{2,1,0:T(8,128)S(1)}, u32[]{:S(2)}, u32[]{:S(2)}) collective-permute-start(f32[3,32,512]{2,1,0:T(8,128)S(1)} %get-tuple-element.66), channel_id=1, source_target_pairs={{4,8},{8,4},{12,16},{16,12},{20,24},{24,20},{28,32},{32,28},{36,40... | collective-permute-start | bytes 589832 | tf_op jit(solution)/shard_map/ppermute | solution.py:668

commit v4 on v3

--- a/solution.py
+++ b/solution.py
@@ -125,10 +125,10 @@
                 tail_ref[0, comp, which, k] = filt[comp, which, own_x - 3 + k]
 
 
-def outer_kernel(place_ref, tail_ref, xh_ref, ch_ref, inner_ref, stiff_ref, msg_ref, plane, filt, energy, turned):
+def outer_kernel(place_ref, tail_ref, xh_ref, ch_ref, inner_ref, solid_ref, msg_ref, plane, filt, energy, turned):
     load = pl.program_id(0)
     rows, size_z = xh_ref.shape[3:5]
-    own_x = stiff_ref.shape[0]
+    own_x, _, blocks = solid_ref.shape
     inner = own_x - 3
     tiles = rows // 8
     keep = jnp.where(place_ref[2] == 1, 0.0, 1.0)
@@ -156,11 +156,14 @@
     def _():
         peak = jnp.zeros((8, 128), jnp.float32)
         groups = own_x // 4
+        block_of = lax.broadcasted_iota(jnp.int32, (blocks, size_z), 1) // (size_z // blocks)
+        spread = jnp.where(block_of == lax.broadcasted_iota(jnp.int32, (blocks, size_z), 0), 1.0, 0.0)
         for g in range(groups):
             stack = []
             for q in range(4):
                 x = 4 * g + q
-                value = (inner_ref[x] if x < inner else energy[x - inner]) * stiff_ref[x]
+                solid = jnp.dot(solid_ref[x], spread, preferred_element_type=jnp.float32)
+                value = (inner_ref[x] if x < inner else energy[x - inner]) * (0.2 + 0.8 * solid)
                 stack.append(value)
                 for tile in range(tiles):
                     for b in range(size_z // 128):
@@ -216,9 +219,10 @@
     )(disp, yh)
 
 
-def strain_message(place, tail, xh, ch, inner, stiff, parts):
+def strain_message(place, tail, xh, ch, inner, solid, parts):
     loads, comps = xh.shape[:2]
-    own_x, rows, size_z = stiff.shape
+    own_x, rows, blocks = solid.shape
+    size_z = xh.shape[4]
     return pl.pallas_call(
         outer_kernel,
         grid=(loads,),
@@ -229,7 +233,7 @@
             load_block(comps, 3, rows, size_z),
             load_block(comps, 3, 3, size_z),
             fixed_block(own_x - 3, rows, size_z),
-            fixed_block(own_x, rows, size_z),
+            fixed_block(own_x, rows, blocks),
         ],
         out_specs=fixed_block(parts * 88, 128),
         scratch_shapes=[
@@ -240,7 +244,7 @@
         ],
         compiler_params=pltpu.CompilerParams(vmem_limit_bytes=VMEM_LIMIT),
         cost_estimate=pl.CostEstimate(flops=10000 * 4096, bytes_accessed=1 << 20, transcendentals=0),
-    )(place, tail, xh, ch, inner, stiff)
+    )(place, tail, xh, ch, inner, solid)
 
 
 def ring(axis, step):
@@ -757,7 +761,6 @@
     wfirst, wsecond = swaps("wide")
     nfirst, nsecond = swaps("narrow")
 
-    xh = lax.ppermute(displacement[:, :, :3], "wide", backward)
     low = lax.ppermute(displacement[:, :, :, -1], "narrow", ring("narrow", 1))
     high = lax.ppermute(
         jnp.stack([displacement[:, :, :, 0], displacement[:, :, :, 1]], axis=2), "narrow", ring("narrow", -1)
@@ -771,20 +774,21 @@
     ch = got[: loads * comps * 3].reshape(loads, comps, 3, 3, size_z)
     beyond = got[loads * comps * 3].reshape(-1)[: rows * blocks].reshape(1, rows, blocks)
     solid = jnp.concatenate([material[1:].astype(jnp.float32), beyond], axis=0)
-    stiff = 0.2 + 0.8 * jnp.repeat(solid, BZ, axis=2)
 
     bounds = level_set[:3], level_set[own_z - 3 :]
     even = place[0] == 1
     la = lax.ppermute(jnp.where(even, bounds[1], bounds[0]), "wide", wfirst)
     lb = lax.ppermute(jnp.where(even, bounds[0], bounds[1]), "wide", wsecond)
 
+    layers, yh, ch, la, lb = lax.optimization_barrier((displacement[:, :, :3], yh, ch, la, lb))
+    xh = lax.ppermute(layers, "wide", backward)
     inner, tail = inner_strain(displacement, yh)
     la, lb, inner = lax.optimization_barrier((la, lb, inner))
     tall, ya, yb = stack_level(place, level_set, la, lb)
     ya = lax.ppermute(ya, "narrow", nfirst)
     yb = lax.ppermute(yb, "narrow", nsecond)
-    xh, ya, yb = lax.optimization_barrier((xh, ya, yb))
-    message = strain_message(place, tail, xh, ch, inner, stiff, wide)
+    xh, tall = lax.optimization_barrier((xh, tall))
+    message = strain_message(place, tail, xh, ch, inner, solid, wide)
     message, tall = lax.optimization_barrier((message, tall))
     recv = lax.all_to_all(message.reshape(wide, 88, 128), "wide", split_axis=0, concat_axis=0, tiled=True)
     ls, sp, sm = first_gradient(place, tall, ya, yb)

time: 219 us -> 211 us (0.963)
  starting transfers between devices: 67.8 us -> 54 us
  waiting for transfers between devices: 14.6 us -> 25.3 us
  local copies, waits for them, and re-layouts: 20.9 us -> 16.6 us
    ppermute x1, starting transfers between devices: 24.9 us -> 6.1 us  [per_device(): ya = lax.ppermute(ya, 'narrow', nfirst)]
    ppermute x1, waiting for transfers between devices: 4.46 us -> 14.2 us  [per_device(): yb = lax.ppermute(yb, 'narrow', nsecond)]
    all_to_all x1, starting transfers between devices: 12 us -> 7.92 us  [per_device(): lax.all_to_all(message.reshape(wide, 88, 128), 'wide', split_axis=0, conc...]
    ppermute x1, starting transfers between devices: 0.25 us -> 3.25 us  [per_device(): lb = lax.ppermute(jnp.where(even, bounds[0], bounds[1]), 'wide', wsecond)]
    ppermute x1, starting transfers between devices: 4.2 us -> 1.29 us  [per_device(): la = lax.ppermute(jnp.where(even, bounds[1], bounds[0]), 'wide', wfirst)]
    ppermute x1, starting transfers between devices: 0.77 us -> 3.61 us  [per_device(): yb = lax.ppermute(yb, 'narrow', nsecond)]
    ppermute x1, starting transfers between devices: 5.15 us -> 7.98 us  [per_device(): lax.ppermute(jnp.concatenate([corner, first], axis=0), 'wide', backward)]
    add x1 -> x0, local copies, waits for them, and re-layouts: 2.36 us -> none  [per_device(): stiff = 0.2 + 0.8 * jnp.repeat(solid, BZ, axis=2)]
  transfers between devices with their start and end apart: 16 -> 16, of which waited for: 4 -> 5; matrix products, arithmetic and copies ran while one was open for 5% -> 4% of each run, Pallas kernels for 35% -> 36%
where the time goes in v4:
time: 211 us; the launch traced here: 210 us
  Pallas kernels  111 us (53%)
  starting transfers between devices  54 us (26%)
  waiting for transfers between devices  25.3 us (12%)
  local copies, waits for them, and re-layouts  16.6 us (8%)
  other arithmetic  2.58 us (1%)
    pallas_call x8, Pallas kernels, vmem_call(): pl.pallas_call(kernel, out_shape=tuple((jax.ShapeDtypeStruct(shape, jnp.f...  77 us
    pallas_call x1, Pallas kernels, inner_strain(): pl.pallas_call(inner_kernel, grid=(loads,), out_shape=(jax.ShapeDtypeStru...  25.3 us
    ppermute x1, waiting for transfers between devices, per_device(): yb = lax.ppermute(yb, 'narrow', nsecond)  14.2 us
    ppermute x1, waiting for transfers between devices, level_part(): rb = lax.ppermute(mb, 'narrow', nsecond)  10.3 us
    unnamed x34, local copies, waits for them, and re-layouts  8.86 us
    pallas_call x1, Pallas kernels, strain_message(): pl.pallas_call(outer_kernel, grid=(loads,), out_shape=jax.ShapeDtypeStruc...  8.57 us
    ppermute x2, starting transfers between devices, level_part(): ga = lax.ppermute(sa, 'wide', wfirst)  8.1 us
    ppermute x1, starting transfers between devices, per_device(): lax.ppermute(jnp.concatenate([corner, first], axis=0), 'wide', backward)  7.98 us
  transfers between devices with their start and end apart: 16, of which 5 were waited for; matrix products, arithmetic and copies ran while one was open for 4% of the time, Pallas kernels for 36%

profile of v4, /device:TPU:2, one launch (start us, length us, event | category | flops | bytes accessed | tf_op | source)
XLA Modules:
  0.0 210.3 jit_solution(14260173803820271672)
XLA Ops:
  0.6 3.1 %fusion.1 = (f32[3,3,16,1,384]{4,3,2,1,0:T(1,128)S(1)}, f32[3,3,16,1,384]{4,3,2,1,0:T(1,128)S(1)}, f32[3,3,16,1,384]{4,3,2,1,0:T(1,128)S(1)}) fusion(f32[3,3,16,32,384]{4,3,2,1,0:T(8,128)} %u_ref.1), kind=kLoop, calls=%fused_computation.15 | loop fusion | bytes 1327104 | tf_op jit(solution)/shard_map/slice | solution.py:766
  3.8 0.1 copy_bitcast_fusion
  3.8 0.1 pad_maximum_fusion.1
  3.9 1.3 collective-permute-start.1
  5.2 3.2 %collective-permute-start.4 = (f32[3,32,512]{2,1,0:T(8,128)S(1)}, f32[3,32,512]{2,1,0:T(8,128)S(1)}, u32[]{:S(2)}, u32[]{:S(2)}) collective-permute-start(f32[3,32,512]{2,1,0:T(8,128)S(1)} %get-tuple-element.81), channel_id=1, source_target_pairs={{4,8},{8,4},{12,16},{16,12},{20,24},{24,20},{28,32},{32,28},{36,40... | collective-permute-start | bytes 589832 | tf_op jit(solution)/shard_map/ppermute | solution.py:781
  8.5 1.3 collective-permute-start.3
  9.8 2.5 %collective-permute-start = (f32[3,3,16,384]{3,2,1,0:T(8,128)S(1)}, f32[3,3,16,384]{3,2,1,0:T(8,128)S(1)}, u32[]{:S(2)}, u32[]{:S(2)}) collective-permute-start(f32[3,3,16,384]{3,2,1,0:T(8,128)S(1)} %bitcast.25), channel_id=1, source_target_pairs={{0,1},{1,2},{2,3},{4,5},{5,6},{6,7},{8,9},{9,10},{10,11},{12,13},{... | collective-permute-start | bytes 663560 | tf_op jit(solution)/shard_map/ppermute | solution.py:764
  12.3 0.7 slice_convert_fusion
  13.0 0.1 copy.12
  13.1 0.1 convert_element_type.17
  13.2 0.2 collective-permute-done
  13.4 0.0 collective-permute-done.1
  13.4 8.0 %collective-permute-start.2 = (f32[28,3,384]{2,1,0:T(4,128)S(1)}, f32[28,3,384]{2,1,0:T(4,128)S(1)}, u32[]{:S(2)}, u32[]{:S(2)}) collective-permute-start(f32[28,3,384]{2,1,0:T(4,128)S(1)} %pad_maximum_fusion.3), channel_id=1, source_target_pairs={{0,124},{4,0},{8,4},{12,8},{16,12},{20,16},{24,20},{28,24},{32,28}... | collective-permute-start | bytes 387080 | tf_op jit(solution)/shard_map/ppermute | solution.py:773
  21.4 2.5 %slice.42 = f32[3,3,3,32,384]{4,3,2,1,0:T(8,128)} slice(f32[3,3,16,32,384]{4,3,2,1,0:T(8,128)} %u_ref.1), slice={[0:3], [0:3], [0:3], [0:32], [0:384]} | slice | bytes 2654208 | tf_op jit(solution)/shard_map/slice | solution.py:783
  24.0 0.4 collective-permute-done.2
  24.4 0.0 collective-permute-done.4.rb_ref
  24.4 0.0 collective-permute-done.3.ra_ref
  24.4 0.6 copy-done.15
  25.0 4.9 %collective-permute-start.5 = (f32[3,3,3,32,384]{4,3,2,1,0:T(8,128)}, f32[3,3,3,32,384]{4,3,2,1,0:T(8,128)S(1)}, u32[]{:S(2)}, u32[]{:S(2)}) collective-permute-start(f32[3,3,3,32,384]{4,3,2,1,0:T(8,128)} %slice.42), channel_id=1, source_target_pairs={{0,124},{4,0},{8,4},{12,8},{16,12},{20,16},{24,20},{28,24},{32,28}... | collective-permute-start | bytes 3981320 | tf_op jit(solution)/shard_map/ppermute | solution.py:784
  29.9 0.9 slice.51
  30.9 0.8 copy.17
  31.7 1.7 convert_element_type.18
  33.3 0.1 stack.46.place_ref
  33.4 0.7 slice.58
  34.1 0.1 reshape.27
  34.2 25.3 %shard_map.50 = (f32[13,32,384]{2,1,0:T(8,128)S(1)}, f32[3,3,3,3,32,384]{5,4,3,2,1,0:T(8,128)S(1)}) custom-call(f32[3,3,16,32,384]{4,3,2,1,0:T(8,128)} %u_ref.1, f32[3,3,3,16,384]{4,3,2,1,0:T(8,128)S(1)} %pad_maximum_fusion.yh_ref), custom_call_target="tpu_custom_call" | custom-call | flops 163840000 | bytes 1048576 | tf_op jit(solution)/shard_map/pallas_call | solution.py:204
  59.5 1.9 copy-done
  61.4 0.7 shard_map.51
  62.2 1.0 copy-done.3
  63.3 0.0 collective-permute-done.5.xh_ref
  63.3 8.6 %shard_map.52 = f32[2816,128]{1,0:T(8,128)} custom-call(s32[6]{0:T(128)S(1)} %stack.46.place_ref, f32[3,3,3,3,32,384]{5,4,3,2,1,0:T(8,128)} %copy-done, f32[3,3,3,32,384]{4,3,2,1,0:T(8,128)S(1)} %collective-permute-done.5.xh_ref, f32[3,3,3,3,384]{4,3,2,1,0:T(4,128)S(1)} %bitcast.21, f32[13,32,384]{2,1,0:T(8,128)S(1)} %get-tuple-element.51.inner_ref, ...), custom_call_target="tpu_custom_call" | custom-call | flops 40960000 | bytes 1048576 | tf_op jit(solution)/shard_map/pallas_call | solution.py:226
  71.9 0.0 copy-start.11
  71.9 7.9 %all-to-all-start = ((f32[32,88,128]{2,1,0:T(8,128)}), f32[32,88,128]{2,1,0:T(8,128)S(1)}, u32[]{:S(2)}, u32[]{:S(2)}) async-start(f32[32,88,128]{2,1,0:T(8,128)} %bitcast.12), calls=%async_computation | async-start | bytes 2883584 | tf_op jit(solution)/shard_map/all_to_all | solution.py:793
  79.8 6.1 %collective-permute-start.6 = (f32[21,8,512]{2,1,0:T(8,128)S(1)}, f32[21,8,512]{2,1,0:T(8,128)S(1)}, u32[]{:S(2)}, u32[]{:S(2)}) collective-permute-start(f32[21,8,512]{2,1,0:T(8,128)S(1)} %copy-done.13), channel_id=1, source_target_pairs={{0,1},{1,0},{2,3},{3,2},{4,5},{5,4},{6,7},{7,6},{8,9},{9,8},{10,11... | collective-permute-start | bytes 1032200 | tf_op jit(solution)/shard_map/ppermute | solution.py:788
  85.9 3.6 %collective-permute-start.7 = (f32[21,8,512]{2,1,0:T(8,128)S(1)}, f32[21,8,512]{2,1,0:T(8,128)S(1)}, u32[]{:S(2)}, u32[]{:S(2)}) collective-permute-start(f32[21,8,512]{2,1,0:T(8,128)S(1)} %copy-done.11), channel_id=1, source_target_pairs={{1,2},{2,1},{3,0},{0,3},{5,6},{6,5},{7,4},{4,7},{9,10},{10,9},{11,... | collective-permute-start | bytes 1032200 | tf_op jit(solution)/shard_map/ppermute | solution.py:789
  89.5 0.0 collective-permute-done.6.ra_ref
  89.5 14.2 %collective-permute-done.7.rb_ref = f32[21,8,512]{2,1,0:T(8,128)S(1)} collective-permute-done((f32[21,8,512]{2,1,0:T(8,128)S(1)}, f32[21,8,512]{2,1,0:T(8,128)S(1)}, u32[]{:S(2)}, u32[]{:S(2)}) %collective-permute-start.7) | collective-permute-done | bytes 344096 | tf_op jit(solution)/shard_map/ppermute | solution.py:789
  103.7 22.5 %shard_map.53 = (f32[18,56,512]{2,1,0:T(8,128)}, f32[12,48,512]{2,1,0:T(8,128)S(1)}, f32[12,48,512]{2,1,0:T(8,128)S(1)}) custom-call(s32[6]{0:T(128)S(1)} %stack.46.place_ref, f32[18,32,512]{2,1,0:T(8,128)S(1)} %copy-done.4, f32[21,8,512]{2,1,0:T(8,128)S(1)} %collective-permute-done.6.ra_ref, f32[21,8,512]{2,1,0:T(8,128)S(1)} %collective-permute-done.7.rb_ref), custom_call_target="tpu_custom_call" | custom-call | flops 143360000 | bytes 1048576 | tf_op jit(solution)/shard_map/pallas_call | solution.py:417
  126.3 1.0 copy-done.5
  127.3 1.1 copy-done.7
  128.4 0.0 all-to-all-done.recv_ref
  128.4 1.4 shard_map.54
  129.8 1.1 copy-done.2
  130.8 2.0 collective-permute-start.8
  132.8 1.2 collective-permute-start.9
  134.0 0.5 collective-permute-start.10
  134.5 0.0 collective-permute-done.8.ra_ref
  134.5 10.3 %collective-permute-done.9.rb_ref = f32[26,8,512]{2,1,0:T(8,128)S(1)} collective-permute-done((f32[26,8,512]{2,1,0:T(8,128)S(1)}, f32[26,8,512]{2,1,0:T(8,128)S(1)}, u32[]{:S(2)}, u32[]{:S(2)}) %collective-permute-start.9) | collective-permute-done | bytes 426016 | tf_op jit(solution)/shard_map/ppermute | solution.py:647
  144.8 0.3 collective-permute-done.10.pc_ref
  145.0 1.3 copy-done.8
  146.3 14.6 %shard_map.55 = (f32[12,32,512]{2,1,0:T(8,128)}, f32[12,48,512]{2,1,0:T(8,128)S(1)}, f32[12,48,512]{2,1,0:T(8,128)S(1)}, f32[3,40,512]{2,1,0:T(8,128)S(1)}, f32[3,40,512]{2,1,0:T(8,128)S(1)}) custom-call(s32[6]{0:T(128)S(1)} %stack.46.place_ref, f32[20,32,512]{2,1,0:T(8,128)} %copy-done.2, f32[26,8,512]{2,1,0:T(8,128)S(1)} %collective-permute-done.8.ra_ref, ...), custom_call_target="tpu_custom_call" | custom-call | flops 32768000 | bytes 1048576 | tf_op jit(solution)/shard_map/pallas_call | solution.py:417
  161.0 3.7 %collective-permute-start.11 = (f32[3,40,512]{2,1,0:T(8,128)S(1)}, f32[3,40,512]{2,1,0:T(8,128)S(1)}, u32[]{:S(2)}, u32[]{:S(2)}) collective-permute-start(f32[3,40,512]{2,1,0:T(8,128)S(1)} %get-tuple-element.67), channel_id=1, source_target_pairs={{0,4},{4,0},{8,12},{12,8},{16,20},{20,16},{24,28},{28,24},{32,36},... | collective-permute-start | bytes 737288 | tf_op jit(solution)/shard_map/ppermute | solution.py:661
  164.6 0.0 collective-permute-start.12
  164.6 13.7 %shard_map.56 = (f32[12,40,512]{2,1,0:T(8,128)S(1)}, f32[12,40,512]{2,1,0:T(8,128)S(1)}) custom-call(f32[12,48,512]{2,1,0:T(8,128)S(1)} %get-tuple-element.66.phi_ref), custom_call_target="tpu_custom_call" | custom-call | flops 49152000 | bytes 1048576 | tf_op jit(solution)/shard_map/pallas_call | solution.py:417
  178.3 0.0 collective-permute-done.11.ra_ref
  178.4 0.0 collective-permute-done.12.rb_ref
  178.4 5.9 %shard_map.57 = (f32[12,40,512]{2,1,0:T(8,128)S(1)}, f32[3,32,512]{2,1,0:T(8,128)S(1)}, f32[3,32,512]{2,1,0:T(8,128)S(1)}) custom-call(s32[6]{0:T(128)S(1)} %stack.46.place_ref, f32[12,48,512]{2,1,0:T(8,128)S(1)} %get-tuple-element.66.phi_ref, f32[3,40,512]{2,1,0:T(8,128)S(1)} %collective-permute-done.11.ra_ref, ...), custom_call_target="tpu_custom_call" | custom-call | flops 20480000 | bytes 1048576 | tf_op jit(solution)/shard_map/pallas_call | solution.py:417
  184.3 0.0 copy-start.9
  184.3 4.4 %collective-permute-start.13 = (f32[3,32,512]{2,1,0:T(8,128)S(1)}, f32[3,32,512]{2,1,0:T(8,128)S(1)}, u32[]{:S(2)}, u32[]{:S(2)}) collective-permute-start(f32[3,32,512]{2,1,0:T(8,128)S(1)} %get-tuple-element.73), channel_id=1, source_target_pairs={{0,4},{4,0},{8,12},{12,8},{16,20},{20,16},{24,28},{28,24},{32,36},... | collective-permute-start | bytes 589832 | tf_op jit(solution)/shard_map/ppermute | solution.py:671
  188.8 3.5 %collective-permute-start.14 = (f32[3,32,512]{2,1,0:T(8,128)S(1)}, f32[3,32,512]{2,1,0:T(8,128)S(1)}, u32[]{:S(2)}, u32[]{:S(2)}) collective-permute-start(f32[3,32,512]{2,1,0:T(8,128)S(1)} %get-tuple-element.74), channel_id=1, source_target_pairs={{4,8},{8,4},{12,16},{16,12},{20,24},{24,20},{28,32},{32,28},{36,40... | collective-permute-start | bytes 589832 | tf_op jit(solution)/shard_map/ppermute | solution.py:672
  192.3 12.6 %shard_map.58 = (f32[12,32,512]{2,1,0:T(8,128)S(1)}, f32[12,32,512]{2,1,0:T(8,128)S(1)}) custom-call(f32[12,40,512]{2,1,0:T(8,128)S(1)} %get-tuple-element.72.phi_ref), custom_call_target="tpu_custom_call" | custom-call | flops 49152000 | bytes 1048576 | tf_op jit(solution)/shard_map/pallas_call | solution.py:417
  204.9 0.0 collective-permute-done.13.ra_ref
  204.9 0.0 collective-permute-done.14.rb_ref
  204.9 5.4 %shard_map.59 = f32[12,32,512]{2,1,0:T(8,128)} custom-call(s32[6]{0:T(128)S(1)} %stack.46.place_ref, f32[12,40,512]{2,1,0:T(8,128)S(1)} %get-tuple-element.72.phi_ref, f32[3,32,512]{2,1,0:T(8,128)S(1)} %collective-permute-done.13.ra_ref, f32[3,32,512]{2,1,0:T(8,128)S(1)} %collective-permute-done.14.rb_ref, f32[12,32,512]{2,1,0:T(8,128)S(1)} %get-tuple-element.75.gp_ref, ...), custom_call_target="tpu_custom_call" | custom-call | flops 20480000 | bytes 1048576 | tf_op jit(solution)/shard_map/pallas_call | solution.py:417
  (34 shorter events, 0.3 us)
Async XLA Ops:
  0.6 4.6 %copy-start.1 = (f32[12,32,512]{2,1,0:T(8,128)S(1)}, f32[12,32,512]{2,1,0:T(8,128)}, u32[]{:S(2)}) copy-start(f32[12,32,512]{2,1,0:T(8,128)} %ls_ref.1) | copy-start | bytes 2359300
  3.9 9.5 %collective-permute-start.1 = (f32[3,3,2,16,384]{4,3,2,1,0:T(8,128)S(1)}, f32[3,3,2,16,384]{4,3,2,1,0:T(8,128)S(1)}, u32[]{:S(2)}, u32[]{:S(2)}) collective-permute-start(f32[3,3,2,16,384]{4,3,2,1,0:T(8,128)S(1)} %pad_maximum_fusion.1), channel_id=1, source_target_pairs={{1,0},{2,1},{3,2},{5,4},{6,5},{7,6},{9,8},{10,9},{11,10},{13,12},{... | collective-permute-start | bytes 1327112 | tf_op jit(solution)/shard_map/ppermute | solution.py:765
  5.2 19.1 %collective-permute-start.4 = (f32[3,32,512]{2,1,0:T(8,128)S(1)}, f32[3,32,512]{2,1,0:T(8,128)S(1)}, u32[]{:S(2)}, u32[]{:S(2)}) collective-permute-start(f32[3,32,512]{2,1,0:T(8,128)S(1)} %get-tuple-element.81), channel_id=1, source_target_pairs={{4,8},{8,4},{12,16},{16,12},{20,24},{24,20},{28,32},{32,28},{36,40... | collective-permute-start | bytes 589832 | tf_op jit(solution)/shard_map/ppermute | solution.py:781
  8.5 15.9 %collective-permute-start.3 = (f32[3,32,512]{2,1,0:T(8,128)S(1)}, f32[3,32,512]{2,1,0:T(8,128)S(1)}, u32[]{:S(2)}, u32[]{:S(2)}) collective-permute-start(f32[3,32,512]{2,1,0:T(8,128)S(1)} %get-tuple-element.82), channel_id=1, source_target_pairs={{0,4},{4,0},{8,12},{12,8},{16,20},{20,16},{24,28},{28,24},{32,36},... | collective-permute-start | bytes 589832 | tf_op jit(solution)/shard_map/ppermute | solution.py:780
  9.8 3.6 %collective-permute-start = (f32[3,3,16,384]{3,2,1,0:T(8,128)S(1)}, f32[3,3,16,384]{3,2,1,0:T(8,128)S(1)}, u32[]{:S(2)}, u32[]{:S(2)}) collective-permute-start(f32[3,3,16,384]{3,2,1,0:T(8,128)S(1)} %bitcast.25), channel_id=1, source_target_pairs={{0,1},{1,2},{2,3},{4,5},{5,6},{6,7},{8,9},{9,10},{10,11},{12,13},{... | collective-permute-start | bytes 663560 | tf_op jit(solution)/shard_map/ppermute | solution.py:764
  13.4 10.9 %collective-permute-start.2 = (f32[28,3,384]{2,1,0:T(4,128)S(1)}, f32[28,3,384]{2,1,0:T(4,128)S(1)}, u32[]{:S(2)}, u32[]{:S(2)}) collective-permute-start(f32[28,3,384]{2,1,0:T(4,128)S(1)} %pad_maximum_fusion.3), channel_id=1, source_target_pairs={{0,124},{4,0},{8,4},{12,8},{16,12},{20,16},{24,20},{28,24},{32,28}... | collective-permute-start | bytes 387080 | tf_op jit(solution)/shard_map/ppermute | solution.py:773
  24.3 0.7 copy-start.15
  25.0 38.3 %collective-permute-start.5 = (f32[3,3,3,32,384]{4,3,2,1,0:T(8,128)}, f32[3,3,3,32,384]{4,3,2,1,0:T(8,128)S(1)}, u32[]{:S(2)}, u32[]{:S(2)}) collective-permute-start(f32[3,3,3,32,384]{4,3,2,1,0:T(8,128)} %slice.42), channel_id=1, source_target_pairs={{0,124},{4,0},{8,4},{12,8},{16,12},{20,16},{24,20},{28,24},{32,28}... | collective-permute-start | bytes 3981320 | tf_op jit(solution)/shard_map/ppermute | solution.py:784
  59.5 1.9 copy-start
  61.4 1.8 copy-start.14
  62.2 1.1 copy-start.3
  63.2 8.6 %copy-start.10 = (f32[21,8,512]{2,1,0:T(8,128)}, f32[21,8,512]{2,1,0:T(8,128)S(1)}, u32[]{:S(2)}) copy-start(f32[21,8,512]{2,1,0:T(8,128)S(1)} %get-tuple-element.56) | copy-start | bytes 1032196
  63.2 8.6 %copy-start.12 = (f32[21,8,512]{2,1,0:T(8,128)}, f32[21,8,512]{2,1,0:T(8,128)S(1)}, u32[]{:S(2)}) copy-start(f32[21,8,512]{2,1,0:T(8,128)S(1)} %get-tuple-element.55) | copy-start | bytes 1032196
  71.8 8.0 %copy-start.13 = (f32[21,8,512]{2,1,0:T(8,128)S(1)}, f32[21,8,512]{2,1,0:T(8,128)}, u32[]{:S(2)}) copy-start(f32[21,8,512]{2,1,0:T(8,128)} %copy-done.12) | copy-start | bytes 1032196
  71.9 14.1 %copy-start.11 = (f32[21,8,512]{2,1,0:T(8,128)S(1)}, f32[21,8,512]{2,1,0:T(8,128)}, u32[]{:S(2)}) copy-start(f32[21,8,512]{2,1,0:T(8,128)} %copy-done.10) | copy-start | bytes 1032196
  71.9 31.9 %copy-start.4 = (f32[18,32,512]{2,1,0:T(8,128)S(1)}, f32[18,32,512]{2,1,0:T(8,128)}, u32[]{:S(2)}) copy-start(f32[18,32,512]{2,1,0:T(8,128)} %copy-done.3) | copy-start | bytes 3538948
  71.9 56.5 %all-to-all-start = ((f32[32,88,128]{2,1,0:T(8,128)}), f32[32,88,128]{2,1,0:T(8,128)S(1)}, u32[]{:S(2)}, u32[]{:S(2)}) async-start(f32[32,88,128]{2,1,0:T(8,128)} %bitcast.12), calls=%async_computation | async-start | bytes 2883584 | tf_op jit(solution)/shard_map/all_to_all | solution.py:793
  79.8 9.7 %collective-permute-start.6 = (f32[21,8,512]{2,1,0:T(8,128)S(1)}, f32[21,8,512]{2,1,0:T(8,128)S(1)}, u32[]{:S(2)}, u32[]{:S(2)}) collective-permute-start(f32[21,8,512]{2,1,0:T(8,128)S(1)} %copy-done.13), channel_id=1, source_target_pairs={{0,1},{1,0},{2,3},{3,2},{4,5},{5,4},{6,7},{7,6},{8,9},{9,8},{10,11... | collective-permute-start | bytes 1032200 | tf_op jit(solution)/shard_map/ppermute | solution.py:788
  85.9 17.8 %collective-permute-start.7 = (f32[21,8,512]{2,1,0:T(8,128)S(1)}, f32[21,8,512]{2,1,0:T(8,128)S(1)}, u32[]{:S(2)}, u32[]{:S(2)}) collective-permute-start(f32[21,8,512]{2,1,0:T(8,128)S(1)} %copy-done.11), channel_id=1, source_target_pairs={{1,2},{2,1},{3,0},{0,3},{5,6},{6,5},{7,4},{4,7},{9,10},{10,9},{11,... | collective-permute-start | bytes 1032200 | tf_op jit(solution)/shard_map/ppermute | solution.py:789
  126.3 1.1 copy-start.5
  127.3 1.1 copy-start.7
  128.4 16.7 %copy-start.6 = (f32[12,48,512]{2,1,0:T(8,128)S(1)}, f32[12,48,512]{2,1,0:T(8,128)}, u32[]{:S(2)}) copy-start(f32[12,48,512]{2,1,0:T(8,128)} %copy-done.5) | copy-start | bytes 3538948
  129.8 1.1 copy-start.2
  130.8 3.6 %collective-permute-start.8 = (f32[26,8,512]{2,1,0:T(8,128)S(1)}, f32[26,8,512]{2,1,0:T(8,128)S(1)}, u32[]{:S(2)}, u32[]{:S(2)}) collective-permute-start(f32[26,8,512]{2,1,0:T(8,128)S(1)} %get-tuple-element.60), channel_id=1, source_target_pairs={{0,1},{1,0},{2,3},{3,2},{4,5},{5,4},{6,7},{7,6},{8,9},{9,8},{10,11... | collective-permute-start | bytes 1277960 | tf_op jit(solution)/shard_map/ppermute | solution.py:646
  132.8 11.9 %collective-permute-start.9 = (f32[26,8,512]{2,1,0:T(8,128)S(1)}, f32[26,8,512]{2,1,0:T(8,128)S(1)}, u32[]{:S(2)}, u32[]{:S(2)}) collective-permute-start(f32[26,8,512]{2,1,0:T(8,128)S(1)} %get-tuple-element.61), channel_id=1, source_target_pairs={{1,2},{2,1},{3,0},{0,3},{5,6},{6,5},{7,4},{4,7},{9,10},{10,9},{11,... | collective-permute-start | bytes 1277960 | tf_op jit(solution)/shard_map/ppermute | solution.py:647
  134.0 11.1 %collective-permute-start.10 = (f32[8,128]{1,0:T(8,128)S(1)}, f32[8,128]{1,0:T(8,128)S(1)}, u32[]{:S(2)}, u32[]{:S(2)}) collective-permute-start(f32[8,128]{1,0:T(8,128)S(1)} %get-tuple-element.62.po_ref), channel_id=1, source_target_pairs={{0,2},{1,3},{2,0},{3,1},{4,6},{5,7},{6,4},{7,5},{8,10},{9,11},{10,... | collective-permute-start | bytes 12296 | tf_op jit(solution)/shard_map/ppermute | solution.py:648
  145.0 1.3 copy-start.8
  161.0 17.4 %collective-permute-start.11 = (f32[3,40,512]{2,1,0:T(8,128)S(1)}, f32[3,40,512]{2,1,0:T(8,128)S(1)}, u32[]{:S(2)}, u32[]{:S(2)}) collective-permute-start(f32[3,40,512]{2,1,0:T(8,128)S(1)} %get-tuple-element.67), channel_id=1, source_target_pairs={{0,4},{4,0},{8,12},{12,8},{16,20},{20,16},{24,28},{28,24},{32,36},... | collective-permute-start | bytes 737288 | tf_op jit(solution)/shard_map/ppermute | solution.py:661
  164.6 13.7 %collective-permute-start.12 = (f32[3,40,512]{2,1,0:T(8,128)S(1)}, f32[3,40,512]{2,1,0:T(8,128)S(1)}, u32[]{:S(2)}, u32[]{:S(2)}) collective-permute-start(f32[3,40,512]{2,1,0:T(8,128)S(1)} %get-tuple-element.68), channel_id=1, source_target_pairs={{4,8},{8,4},{12,16},{16,12},{20,24},{24,20},{28,32},{32,28},{36,40... | collective-permute-start | bytes 737288 | tf_op jit(solution)/shard_map/ppermute | solution.py:662
  184.3 20.6 %copy-start.9 = (f32[12,32,512]{2,1,0:T(8,128)S(1)}, f32[12,32,512]{2,1,0:T(8,128)}, u32[]{:S(2)}) copy-start(f32[12,32,512]{2,1,0:T(8,128)} %get-tuple-element.39.speed_ref) | copy-start | bytes 2359300
  184.3 20.6 %collective-permute-start.13 = (f32[3,32,512]{2,1,0:T(8,128)S(1)}, f32[3,32,512]{2,1,0:T(8,128)S(1)}, u32[]{:S(2)}, u32[]{:S(2)}) collective-permute-start(f32[3,32,512]{2,1,0:T(8,128)S(1)} %get-tuple-element.73), channel_id=1, source_target_pairs={{0,4},{4,0},{8,12},{12,8},{16,20},{20,16},{24,28},{28,24},{32,36},... | collective-permute-start | bytes 589832 | tf_op jit(solution)/shard_map/ppermute | solution.py:671
  188.8 16.2 %collective-permute-start.14 = (f32[3,32,512]{2,1,0:T(8,128)S(1)}, f32[3,32,512]{2,1,0:T(8,128)S(1)}, u32[]{:S(2)}, u32[]{:S(2)}) collective-permute-start(f32[3,32,512]{2,1,0:T(8,128)S(1)} %get-tuple-element.74), channel_id=1, source_target_pairs={{4,8},{8,4},{12,16},{16,12},{20,24},{24,20},{28,32},{32,28},{36,40... | collective-permute-start | bytes 589832 | tf_op jit(solution)/shard_map/ppermute | solution.py:672

commit v5 on v4

--- a/solution.py
+++ b/solution.py
@@ -125,17 +125,21 @@
                 tail_ref[0, comp, which, k] = filt[comp, which, own_x - 3 + k]
 
 
-def outer_kernel(place_ref, tail_ref, xh_ref, ch_ref, inner_ref, solid_ref, msg_ref, plane, filt, energy, turned):
+def outer_kernel(place_ref, tail_ref, next_ref, inner_ref, solid_ref, msg_ref, plane, filt, energy, turned):
     load = pl.program_id(0)
-    rows, size_z = xh_ref.shape[3:5]
-    own_x, _, blocks = solid_ref.shape
+    own_x, rows, blocks = solid_ref.shape
+    size_z = next_ref.shape[1]
+    loads = 3
     inner = own_x - 3
     tiles = rows // 8
     keep = jnp.where(place_ref[2] == 1, 0.0, 1.0)
     for comp in range(3):
         for k in range(3):
-            edge = [ch_ref[0, comp, which, k : k + 1, :] for which in range(3)]
-            filter_plane(plane, filt, comp, k, xh_ref[0, comp, k], *edge)
+            layer = (load * 3 + comp) * 3 + k
+            corner = loads * 9 * rows + rows
+            edge = [next_ref[pl.ds(corner + (load * 3 + comp) * 9 + 3 * which + k, 1), :] for which in range(3)]
+            value = next_ref[pl.ds(pl.multiple_of(layer * rows, 8), rows), :]
+            filter_plane(plane, filt, comp, k, value, *edge)
 
     def density_at(slot, masked):
         def field(comp, which, span):
@@ -162,8 +166,12 @@
             stack = []
             for q in range(4):
                 x = 4 * g + q
-                solid = jnp.dot(solid_ref[x], spread, preferred_element_type=jnp.float32)
-                value = (inner_ref[x] if x < inner else energy[x - inner]) * (0.2 + 0.8 * solid)
+                if x < own_x - 1:
+                    solid = jnp.dot(solid_ref[x + 1].astype(jnp.float32), spread, preferred_element_type=jnp.float32)
+                    stiff = 0.2 + 0.8 * solid
+                else:
+                    stiff = next_ref[loads * 9 * rows : loads * 9 * rows + rows, :]
+                value = (inner_ref[x] if x < inner else energy[x - inner]) * stiff
                 stack.append(value)
                 for tile in range(tiles):
                     for b in range(size_z // 128):
@@ -219,10 +227,10 @@
     )(disp, yh)
 
 
-def strain_message(place, tail, xh, ch, inner, solid, parts):
-    loads, comps = xh.shape[:2]
+def strain_message(place, tail, beyond, inner, solid, parts):
+    loads, comps = tail.shape[:2]
     own_x, rows, blocks = solid.shape
-    size_z = xh.shape[4]
+    size_z = beyond.shape[1]
     return pl.pallas_call(
         outer_kernel,
         grid=(loads,),
@@ -230,8 +238,7 @@
         in_specs=[
             pl.BlockSpec(memory_space=pltpu.SMEM),
             load_block(comps, 3, 3, rows, size_z),
-            load_block(comps, 3, rows, size_z),
-            load_block(comps, 3, 3, size_z),
+            fixed_block(*beyond.shape),
             fixed_block(own_x - 3, rows, size_z),
             fixed_block(own_x, rows, blocks),
         ],
@@ -244,7 +251,7 @@
         ],
         compiler_params=pltpu.CompilerParams(vmem_limit_bytes=VMEM_LIMIT),
         cost_estimate=pl.CostEstimate(flops=10000 * 4096, bytes_accessed=1 << 20, transcendentals=0),
-    )(place, tail, xh, ch, inner, solid)
+    )(place, tail, beyond, inner, solid)
 
 
 def ring(axis, step):
@@ -766,29 +773,23 @@
         jnp.stack([displacement[:, :, :, 0], displacement[:, :, :, 1]], axis=2), "narrow", ring("narrow", -1)
     )
     yh = jnp.concatenate([low[:, :, None], high], axis=2)
-    blocks = material.shape[2]
-    corner = yh[:, :, :, :3].reshape(loads * comps * 3, 3, size_z)
-    first = material[0].astype(jnp.float32).reshape(-1)
-    first = jnp.pad(first, (0, 3 * size_z - first.size)).reshape(1, 3, size_z)
-    got = lax.ppermute(jnp.concatenate([corner, first], axis=0), "wide", backward)
-    ch = got[: loads * comps * 3].reshape(loads, comps, 3, 3, size_z)
-    beyond = got[loads * comps * 3].reshape(-1)[: rows * blocks].reshape(1, rows, blocks)
-    solid = jnp.concatenate([material[1:].astype(jnp.float32), beyond], axis=0)
-
     bounds = level_set[:3], level_set[own_z - 3 :]
     even = place[0] == 1
     la = lax.ppermute(jnp.where(even, bounds[1], bounds[0]), "wide", wfirst)
     lb = lax.ppermute(jnp.where(even, bounds[0], bounds[1]), "wide", wsecond)
 
-    layers, yh, ch, la, lb = lax.optimization_barrier((displacement[:, :, :3], yh, ch, la, lb))
-    xh = lax.ppermute(layers, "wide", backward)
+    stiff = 0.2 + 0.8 * jnp.repeat(material[0].astype(jnp.float32), BZ, axis=1)
+    layers, yh, la, lb = lax.optimization_barrier((displacement[:, :, :3], yh, la, lb))
+    flat = [layers.reshape(-1, size_z), stiff, yh[:, :, :, :3].reshape(-1, size_z)]
+    flat.append(jnp.zeros((-sum(f.shape[0] for f in flat) % 8, size_z), jnp.float32))
+    beyond = lax.ppermute(jnp.concatenate(flat, axis=0), "wide", backward)
     inner, tail = inner_strain(displacement, yh)
     la, lb, inner = lax.optimization_barrier((la, lb, inner))
     tall, ya, yb = stack_level(place, level_set, la, lb)
     ya = lax.ppermute(ya, "narrow", nfirst)
     yb = lax.ppermute(yb, "narrow", nsecond)
-    xh, tall = lax.optimization_barrier((xh, tall))
-    message = strain_message(place, tail, xh, ch, inner, solid, wide)
+    beyond, ya, yb = lax.optimization_barrier((beyond, ya, yb))
+    message = strain_message(place, tail, beyond, inner, material, wide)
     message, tall = lax.optimization_barrier((message, tall))
     recv = lax.all_to_all(message.reshape(wide, 88, 128), "wide", split_axis=0, concat_axis=0, tiled=True)
     ls, sp, sm = first_gradient(place, tall, ya, yb)

time: 211 us -> 195 us (0.924)
  starting transfers between devices: 54 us -> 39.8 us
  waiting for transfers between devices: 25.3 us -> 22.2 us
  other arithmetic: 2.58 us -> 4.75 us
    ppermute x2 -> x1, starting transfers between devices: 12.9 us -> 4.29 us  [per_device(): beyond = lax.ppermute(jnp.concatenate(flat, axis=0), 'wide', backward)]
    ppermute x1, waiting for transfers between devices: 14.2 us -> 8.5 us  [per_device(): yb = lax.ppermute(yb, 'narrow', nsecond)]
    ppermute x1, starting transfers between devices: 6.1 us -> 2.31 us  [per_device(): ya = lax.ppermute(ya, 'narrow', nfirst)]
    ppermute x1, waiting for transfers between devices: 0.01 us -> 3.63 us  [per_device(): la = lax.ppermute(jnp.where(even, bounds[1], bounds[0]), 'wide', wfirst)]
    slice x1 -> x2, local copies, waits for them, and re-layouts: 2.52 us -> 0.01 us  [per_device(): displacement[:, :, :3]]
    convert_element_type x2 -> x0, other arithmetic: 2.37 us -> none  [the longest x1 1.66 us: per_device(): solid = jnp.concatenate([material[1:].astype(jnp.float32), beyond], axis=0)]
    unnamed x34 -> x32, local copies, waits for them, and re-layouts: 8.86 us -> 11.2 us
    slice x4 -> x2, local copies, waits for them, and re-layouts: 4.79 us -> 3.16 us  [the longest x1 3.14 us: per_device(): low = lax.ppermute(displacement[:, :, :, -1], 'narrow', ring('narrow', 1))]
  transfers between devices with their start and end apart: 16 -> 15, of which waited for: 5 -> 4; matrix products, arithmetic and copies ran while one was open for 4% -> 2% of each run, Pallas kernels for 36% -> 39%
where the time goes in v5:
time: 195 us
  Pallas kernels  112 us (57%)
  starting transfers between devices  39.8 us (20%)
  waiting for transfers between devices  22.2 us (11%)
  local copies, waits for them, and re-layouts  15.4 us (8%)
  other arithmetic  4.75 us (2%)
    pallas_call x8, Pallas kernels, vmem_call(): pl.pallas_call(kernel, out_shape=tuple((jax.ShapeDtypeStruct(shape, jnp.f...  77.8 us
    pallas_call x1, Pallas kernels, inner_strain(): pl.pallas_call(inner_kernel, grid=(loads,), out_shape=(jax.ShapeDtypeStru...  25.3 us
    unnamed x32, local copies, waits for them, and re-layouts  11.2 us
    ppermute x1, waiting for transfers between devices, level_part(): rb = lax.ppermute(mb, 'narrow', nsecond)  9.33 us
    all_to_all x1, starting transfers between devices, per_device(): lax.all_to_all(message.reshape(wide, 88, 128), 'wide', split_axis=0, conc...  8.57 us
    ppermute x1, waiting for transfers between devices, per_device(): yb = lax.ppermute(yb, 'narrow', nsecond)  8.5 us
    pallas_call x1, Pallas kernels, strain_message(): pl.pallas_call(outer_kernel, grid=(loads,), out_shape=jax.ShapeDtypeStruc...  8.36 us
    ppermute x2, starting transfers between devices, level_part(): ga = lax.ppermute(sa, 'wide', wfirst)  7.24 us
  transfers between devices with their start and end apart: 15, of which 4 were waited for; matrix products, arithmetic and copies ran while one was open for 2% of the time, Pallas kernels for 39%

profile of v5, /device:TPU:2, one launch (start us, length us, event | category | flops | bytes accessed | tf_op | source)
XLA Modules:
  0.0 194.6 jit_solution(8132657834153990345)
XLA Ops:
  0.6 3.1 %fusion = (f32[3,3,16,1,384]{4,3,2,1,0:T(1,128)S(1)}, f32[3,3,16,1,384]{4,3,2,1,0:T(1,128)S(1)}, f32[3,3,16,1,384]{4,3,2,1,0:T(1,128)S(1)}) fusion(f32[3,3,16,32,384]{4,3,2,1,0:T(8,128)} %u_ref.1), kind=kLoop, calls=%fused_computation.11 | loop fusion | bytes 1327104 | tf_op jit(solution)/shard_map/slice | solution.py:771
  3.8 0.1 copy_bitcast_fusion
  3.8 0.1 pad_maximum_fusion.1
  3.9 1.3 collective-permute-start.1
  5.2 0.7 slice_select_fusion
  5.9 3.2 %collective-permute-start.3 = (f32[3,32,512]{2,1,0:T(8,128)}, f32[3,32,512]{2,1,0:T(8,128)S(1)}, u32[]{:S(2)}, u32[]{:S(2)}) collective-permute-start(f32[3,32,512]{2,1,0:T(8,128)} %get-tuple-element.81), channel_id=1, source_target_pairs={{4,8},{8,4},{12,16},{16,12},{20,24},{24,20},{28,32},{32,28},{36,40... | collective-permute-start | bytes 589832 | tf_op jit(solution)/shard_map/ppermute | solution.py:779
  9.1 1.3 collective-permute-start.2
  10.4 0.7 copy.21
  11.1 3.1 %collective-permute-start = (f32[3,3,16,384]{3,2,1,0:T(8,128)}, f32[3,3,16,384]{3,2,1,0:T(8,128)}, u32[]{:S(2)}, u32[]{:S(2)}) collective-permute-start(f32[3,3,16,384]{3,2,1,0:T(8,128)} %bitcast.22), channel_id=1, source_target_pairs={{0,1},{1,2},{2,3},{4,5},{5,6},{6,7},{8,9},{9,10},{10,11},{12,13},{... | collective-permute-start | bytes 663560 | tf_op jit(solution)/shard_map/ppermute | solution.py:771
  14.2 0.7 add_bitcast_fusion
  14.9 0.7 copy.13
  15.7 0.1 pad.3.clone
  15.7 0.0 collective-permute-done
  15.8 0.0 collective-permute-done.1
  15.8 1.1 pad_maximum_fusion.yh_ref
  16.9 0.0 collective-permute-done.3.rb_ref
  16.9 3.6 %collective-permute-done.2.ra_ref = f32[3,32,512]{2,1,0:T(8,128)S(1)} collective-permute-done((f32[3,32,512]{2,1,0:T(8,128)S(1)}, f32[3,32,512]{2,1,0:T(8,128)S(1)}, u32[]{:S(2)}, u32[]{:S(2)}) %collective-permute-start.2) | collective-permute-done | bytes 196640 | tf_op jit(solution)/shard_map/ppermute | solution.py:778
  20.5 0.1 reshape.24
  20.6 2.2 %maximum_maximum_fusion = f32[984,384]{1,0:T(8,128)} fusion(f32[81,384]{1,0:T(8,128)S(1)} %reshape.24, f32[32,384]{1,0:T(8,128)} %copy.13, f32[864,384]{1,0:T(8,128)S(1)} %bitcast.23, f32[984]{0:T(1024)S(1)} %pad.3.clone), kind=kLoop, calls=%fused_computation | loop fusion | flops 1133568 | bytes 3016032 | tf_op jit(solution)/shard_map/concatenate | solution.py:785
  22.8 4.3 %collective-permute-start.4 = (f32[984,384]{1,0:T(8,128)}, f32[984,384]{1,0:T(8,128)S(1)}, u32[]{:S(2)}, u32[]{:S(2)}) collective-permute-start(f32[984,384]{1,0:T(8,128)} %maximum_maximum_fusion), channel_id=1, source_target_pairs={{0,124},{4,0},{8,4},{12,8},{16,12},{20,16},{24,20},{28,24},{32,28}... | collective-permute-start | bytes 4534280 | tf_op jit(solution)/shard_map/ppermute | solution.py:785
  27.1 0.1 stack.46.place_ref
  27.2 25.3 %shard_map.50 = (f32[13,32,384]{2,1,0:T(8,128)S(1)}, f32[3,3,3,3,32,384]{5,4,3,2,1,0:T(8,128)S(1)}) custom-call(f32[3,3,16,32,384]{4,3,2,1,0:T(8,128)} %u_ref.1, f32[3,3,3,16,384]{4,3,2,1,0:T(8,128)S(1)} %pad_maximum_fusion.yh_ref), custom_call_target="tpu_custom_call" | custom-call | flops 163840000 | bytes 1048576 | tf_op jit(solution)/shard_map/pallas_call | solution.py:212
  52.5 1.9 copy-done
  54.4 0.8 copy-done.10
  55.2 1.6 shard_map.51
  56.8 1.0 copy-done.3
  57.9 2.3 %collective-permute-start.5 = (f32[21,8,512]{2,1,0:T(8,128)}, f32[21,8,512]{2,1,0:T(8,128)S(1)}, u32[]{:S(2)}, u32[]{:S(2)}) collective-permute-start(f32[21,8,512]{2,1,0:T(8,128)} %get-tuple-element.48), channel_id=1, source_target_pairs={{0,1},{1,0},{2,3},{3,2},{4,5},{5,4},{6,7},{7,6},{8,9},{9,8},{10,11... | collective-permute-start | bytes 1032200 | tf_op jit(solution)/shard_map/ppermute | solution.py:789
  60.2 2.2 %collective-permute-start.6 = (f32[21,8,512]{2,1,0:T(8,128)}, f32[21,8,512]{2,1,0:T(8,128)S(1)}, u32[]{:S(2)}, u32[]{:S(2)}) collective-permute-start(f32[21,8,512]{2,1,0:T(8,128)} %get-tuple-element.49), channel_id=1, source_target_pairs={{1,2},{2,1},{3,0},{0,3},{5,6},{6,5},{7,4},{4,7},{9,10},{10,9},{11,... | collective-permute-start | bytes 1032200 | tf_op jit(solution)/shard_map/ppermute | solution.py:790
  62.3 0.1 copy.14.solid_ref
  62.5 0.0 collective-permute-done.5.ra_ref
  62.5 8.5 %collective-permute-done.6.rb_ref = f32[21,8,512]{2,1,0:T(8,128)S(1)} collective-permute-done((f32[21,8,512]{2,1,0:T(8,128)}, f32[21,8,512]{2,1,0:T(8,128)S(1)}, u32[]{:S(2)}, u32[]{:S(2)}) %collective-permute-start.6) | collective-permute-done | bytes 344096 | tf_op jit(solution)/shard_map/ppermute | solution.py:790
  71.0 0.0 collective-permute-done.4.next_ref
  71.0 1.2 copy-done.11
  72.2 8.4 %shard_map.52 = f32[2816,128]{1,0:T(8,128)} custom-call(s32[6]{0:T(128)S(1)} %stack.46.place_ref, f32[3,3,3,3,32,384]{5,4,3,2,1,0:T(8,128)} %copy-done, f32[984,384]{1,0:T(8,128)S(1)} %collective-permute-done.4.next_ref, f32[13,32,384]{2,1,0:T(8,128)S(1)} %copy-done.11, s32[16,32,24]{2,1,0:T(8,128)S(1)} %copy.14.solid_ref), custom_call_target="tpu_custom_call" | custom-call | flops 40960000 | bytes 1048576 | tf_op jit(solution)/shard_map/pallas_call | solution.py:234
  80.6 8.6 %all-to-all-start = ((f32[32,88,128]{2,1,0:T(8,128)}), f32[32,88,128]{2,1,0:T(8,128)S(1)}, u32[]{:S(2)}, u32[]{:S(2)}) async-start(f32[32,88,128]{2,1,0:T(8,128)} %bitcast.13), calls=%async_computation | async-start | bytes 2883584 | tf_op jit(solution)/shard_map/all_to_all | solution.py:794
  89.1 0.0 copy-start.13
  89.2 1.0 copy-done.13
  90.1 22.5 %shard_map.53 = (f32[18,56,512]{2,1,0:T(8,128)}, f32[12,48,512]{2,1,0:T(8,128)S(1)}, f32[12,48,512]{2,1,0:T(8,128)S(1)}) custom-call(s32[6]{0:T(128)S(1)} %stack.46.place_ref, f32[18,32,512]{2,1,0:T(8,128)S(1)} %copy-done.4, f32[21,8,512]{2,1,0:T(8,128)S(1)} %collective-permute-done.5.ra_ref, f32[21,8,512]{2,1,0:T(8,128)S(1)} %copy-done.13), custom_call_target="tpu_custom_call" | custom-call | flops 143360000 | bytes 1048576 | tf_op jit(solution)/shard_map/pallas_call | solution.py:424
  112.7 1.0 copy-done.5
  113.7 1.1 copy-done.7
  114.8 0.0 all-to-all-done.recv_ref
  114.8 1.4 shard_map.54
  116.2 1.1 copy-done.2
  117.2 0.0 collective-permute-start.7
  117.2 0.7 collective-permute-start.8
  118.0 1.4 collective-permute-start.9
  119.4 0.0 collective-permute-done.7.ra_ref
  119.4 9.3 %collective-permute-done.8.rb_ref = f32[26,8,512]{2,1,0:T(8,128)S(1)} collective-permute-done((f32[26,8,512]{2,1,0:T(8,128)S(1)}, f32[26,8,512]{2,1,0:T(8,128)S(1)}, u32[]{:S(2)}, u32[]{:S(2)}) %collective-permute-start.8) | collective-permute-done | bytes 426016 | tf_op jit(solution)/shard_map/ppermute | solution.py:654
  128.7 0.7 collective-permute-done.9.pc_ref
  129.4 1.3 copy-done.8
  130.7 14.6 %shard_map.55 = (f32[12,32,512]{2,1,0:T(8,128)}, f32[12,48,512]{2,1,0:T(8,128)S(1)}, f32[12,48,512]{2,1,0:T(8,128)S(1)}, f32[3,40,512]{2,1,0:T(8,128)S(1)}, f32[3,40,512]{2,1,0:T(8,128)S(1)}) custom-call(s32[6]{0:T(128)S(1)} %stack.46.place_ref, f32[20,32,512]{2,1,0:T(8,128)} %copy-done.2, f32[26,8,512]{2,1,0:T(8,128)S(1)} %collective-permute-done.7.ra_ref, ...), custom_call_target="tpu_custom_call" | custom-call | flops 32768000 | bytes 1048576 | tf_op jit(solution)/shard_map/pallas_call | solution.py:424
  145.4 3.0 %collective-permute-start.10 = (f32[3,40,512]{2,1,0:T(8,128)S(1)}, f32[3,40,512]{2,1,0:T(8,128)S(1)}, u32[]{:S(2)}, u32[]{:S(2)}) collective-permute-start(f32[3,40,512]{2,1,0:T(8,128)S(1)} %get-tuple-element.67), channel_id=1, source_target_pairs={{0,4},{4,0},{8,12},{12,8},{16,20},{20,16},{24,28},{28,24},{32,36},... | collective-permute-start | bytes 737288 | tf_op jit(solution)/shard_map/ppermute | solution.py:668
  148.3 0.2 collective-permute-start.11
  148.6 13.7 %shard_map.56 = (f32[12,40,512]{2,1,0:T(8,128)S(1)}, f32[12,40,512]{2,1,0:T(8,128)S(1)}) custom-call(f32[12,48,512]{2,1,0:T(8,128)S(1)} %get-tuple-element.66.phi_ref), custom_call_target="tpu_custom_call" | custom-call | flops 49152000 | bytes 1048576 | tf_op jit(solution)/shard_map/pallas_call | solution.py:424
  162.3 0.0 collective-permute-done.10.ra_ref
  162.3 0.0 collective-permute-done.11.rb_ref
  162.3 5.9 %shard_map.57 = (f32[12,40,512]{2,1,0:T(8,128)S(1)}, f32[3,32,512]{2,1,0:T(8,128)S(1)}, f32[3,32,512]{2,1,0:T(8,128)S(1)}) custom-call(s32[6]{0:T(128)S(1)} %stack.46.place_ref, f32[12,48,512]{2,1,0:T(8,128)S(1)} %get-tuple-element.66.phi_ref, f32[3,40,512]{2,1,0:T(8,128)S(1)} %collective-permute-done.10.ra_ref, ...), custom_call_target="tpu_custom_call" | custom-call | flops 20480000 | bytes 1048576 | tf_op jit(solution)/shard_map/pallas_call | solution.py:424
  168.2 0.0 copy-start.9
  168.3 4.3 %collective-permute-start.12 = (f32[3,32,512]{2,1,0:T(8,128)S(1)}, f32[3,32,512]{2,1,0:T(8,128)S(1)}, u32[]{:S(2)}, u32[]{:S(2)}) collective-permute-start(f32[3,32,512]{2,1,0:T(8,128)S(1)} %get-tuple-element.73), channel_id=1, source_target_pairs={{0,4},{4,0},{8,12},{12,8},{16,20},{20,16},{24,28},{28,24},{32,36},... | collective-permute-start | bytes 589832 | tf_op jit(solution)/shard_map/ppermute | solution.py:678
  172.5 4.0 %collective-permute-start.13 = (f32[3,32,512]{2,1,0:T(8,128)S(1)}, f32[3,32,512]{2,1,0:T(8,128)S(1)}, u32[]{:S(2)}, u32[]{:S(2)}) collective-permute-start(f32[3,32,512]{2,1,0:T(8,128)S(1)} %get-tuple-element.74), channel_id=1, source_target_pairs={{4,8},{8,4},{12,16},{16,12},{20,24},{24,20},{28,32},{32,28},{36,40... | collective-permute-start | bytes 589832 | tf_op jit(solution)/shard_map/ppermute | solution.py:679
  176.5 12.6 %shard_map.58 = (f32[12,32,512]{2,1,0:T(8,128)S(1)}, f32[12,32,512]{2,1,0:T(8,128)S(1)}) custom-call(f32[12,40,512]{2,1,0:T(8,128)S(1)} %get-tuple-element.72.phi_ref), custom_call_target="tpu_custom_call" | custom-call | flops 49152000 | bytes 1048576 | tf_op jit(solution)/shard_map/pallas_call | solution.py:424
  189.1 0.0 collective-permute-done.12.ra_ref
  189.2 0.0 collective-permute-done.13.rb_ref
  189.2 5.4 %shard_map.59 = f32[12,32,512]{2,1,0:T(8,128)} custom-call(s32[6]{0:T(128)S(1)} %stack.46.place_ref, f32[12,40,512]{2,1,0:T(8,128)S(1)} %get-tuple-element.72.phi_ref, f32[3,32,512]{2,1,0:T(8,128)S(1)} %collective-permute-done.12.ra_ref, f32[3,32,512]{2,1,0:T(8,128)S(1)} %collective-permute-done.13.rb_ref, f32[12,32,512]{2,1,0:T(8,128)S(1)} %get-tuple-element.75.gp_ref, ...), custom_call_target="tpu_custom_call" | custom-call | flops 20480000 | bytes 1048576 | tf_op jit(solution)/shard_map/pallas_call | solution.py:424
  (26 shorter events, 0.1 us)
Async XLA Ops:
  0.6 4.6 %copy-start.1 = (f32[12,32,512]{2,1,0:T(8,128)S(1)}, f32[12,32,512]{2,1,0:T(8,128)}, u32[]{:S(2)}) copy-start(f32[12,32,512]{2,1,0:T(8,128)} %ls_ref.1) | copy-start | bytes 2359300
  3.9 11.9 %collective-permute-start.1 = (f32[3,3,2,16,384]{4,3,2,1,0:T(8,128)S(1)}, f32[3,3,2,16,384]{4,3,2,1,0:T(8,128)}, u32[]{:S(2)}, u32[]{:S(2)}) collective-permute-start(f32[3,3,2,16,384]{4,3,2,1,0:T(8,128)S(1)} %pad_maximum_fusion.1), channel_id=1, source_target_pairs={{1,0},{2,1},{3,2},{5,4},{6,5},{7,6},{9,8},{10,9},{11,10},{13,12},{... | collective-permute-start | bytes 1327112 | tf_op jit(solution)/shard_map/ppermute | solution.py:772
  5.9 11.0 %collective-permute-start.3 = (f32[3,32,512]{2,1,0:T(8,128)}, f32[3,32,512]{2,1,0:T(8,128)S(1)}, u32[]{:S(2)}, u32[]{:S(2)}) collective-permute-start(f32[3,32,512]{2,1,0:T(8,128)} %get-tuple-element.81), channel_id=1, source_target_pairs={{4,8},{8,4},{12,16},{16,12},{20,24},{24,20},{28,32},{32,28},{36,40... | collective-permute-start | bytes 589832 | tf_op jit(solution)/shard_map/ppermute | solution.py:779
  9.1 11.4 %collective-permute-start.2 = (f32[3,32,512]{2,1,0:T(8,128)S(1)}, f32[3,32,512]{2,1,0:T(8,128)S(1)}, u32[]{:S(2)}, u32[]{:S(2)}) collective-permute-start(f32[3,32,512]{2,1,0:T(8,128)S(1)} %get-tuple-element.82), channel_id=1, source_target_pairs={{0,4},{4,0},{8,12},{12,8},{16,20},{20,16},{24,28},{28,24},{32,36},... | collective-permute-start | bytes 589832 | tf_op jit(solution)/shard_map/ppermute | solution.py:778
  11.1 4.7 %collective-permute-start = (f32[3,3,16,384]{3,2,1,0:T(8,128)}, f32[3,3,16,384]{3,2,1,0:T(8,128)}, u32[]{:S(2)}, u32[]{:S(2)}) collective-permute-start(f32[3,3,16,384]{3,2,1,0:T(8,128)} %bitcast.22), channel_id=1, source_target_pairs={{0,1},{1,2},{2,3},{4,5},{5,6},{6,7},{8,9},{9,10},{10,11},{12,13},{... | collective-permute-start | bytes 663560 | tf_op jit(solution)/shard_map/ppermute | solution.py:771
  14.9 5.7 %slice-start = ((f32[3,3,16,32,384]{4,3,2,1,0:T(8,128)}), f32[3,3,3,32,384]{4,3,2,1,0:T(8,128)S(1)}, s32[]{:S(2)}) async-start(f32[3,3,16,32,384]{4,3,2,1,0:T(8,128)} %u_ref.1), calls=%async_computation.1 | async-start | bytes 2654208 | tf_op jit(solution)/shard_map/slice | solution.py:782
  22.8 48.2 %collective-permute-start.4 = (f32[984,384]{1,0:T(8,128)}, f32[984,384]{1,0:T(8,128)S(1)}, u32[]{:S(2)}, u32[]{:S(2)}) collective-permute-start(f32[984,384]{1,0:T(8,128)} %maximum_maximum_fusion), channel_id=1, source_target_pairs={{0,124},{4,0},{8,4},{12,8},{16,12},{20,16},{24,20},{28,24},{32,28}... | collective-permute-start | bytes 4534280 | tf_op jit(solution)/shard_map/ppermute | solution.py:785
  27.2 35.2 %copy-start.14 = (s32[16,32,24]{1,2,0:T(8,128)S(1)}, s32[16,32,24]{1,2,0:T(8,128)}, u32[]{:S(2)}) copy-start(s32[16,32,24]{1,2,0:T(8,128)} %param.4) | copy-start | bytes 147460
  52.5 1.9 copy-start
  54.4 0.8 copy-start.10
  56.8 1.0 copy-start.3
  57.9 4.6 %collective-permute-start.5 = (f32[21,8,512]{2,1,0:T(8,128)}, f32[21,8,512]{2,1,0:T(8,128)S(1)}, u32[]{:S(2)}, u32[]{:S(2)}) collective-permute-start(f32[21,8,512]{2,1,0:T(8,128)} %get-tuple-element.48), channel_id=1, source_target_pairs={{0,1},{1,0},{2,3},{3,2},{4,5},{5,4},{6,7},{7,6},{8,9},{9,8},{10,11... | collective-permute-start | bytes 1032200 | tf_op jit(solution)/shard_map/ppermute | solution.py:789
  60.2 10.8 %collective-permute-start.6 = (f32[21,8,512]{2,1,0:T(8,128)}, f32[21,8,512]{2,1,0:T(8,128)S(1)}, u32[]{:S(2)}, u32[]{:S(2)}) collective-permute-start(f32[21,8,512]{2,1,0:T(8,128)} %get-tuple-element.49), channel_id=1, source_target_pairs={{1,2},{2,1},{3,0},{0,3},{5,6},{6,5},{7,4},{4,7},{9,10},{10,9},{11,... | collective-permute-start | bytes 1032200 | tf_op jit(solution)/shard_map/ppermute | solution.py:790
  71.0 9.6 %copy-start.12 = (f32[21,8,512]{2,1,0:T(8,128)}, f32[21,8,512]{2,1,0:T(8,128)S(1)}, u32[]{:S(2)}) copy-start(f32[21,8,512]{2,1,0:T(8,128)S(1)} %collective-permute-done.6.rb_ref) | copy-start | bytes 1032196
  71.0 1.2 copy-start.11
  80.6 8.6 %copy-start.4 = (f32[18,32,512]{2,1,0:T(8,128)S(1)}, f32[18,32,512]{2,1,0:T(8,128)}, u32[]{:S(2)}) copy-start(f32[18,32,512]{2,1,0:T(8,128)} %copy-done.3) | copy-start | bytes 3538948
  80.6 34.2 %all-to-all-start = ((f32[32,88,128]{2,1,0:T(8,128)}), f32[32,88,128]{2,1,0:T(8,128)S(1)}, u32[]{:S(2)}, u32[]{:S(2)}) async-start(f32[32,88,128]{2,1,0:T(8,128)} %bitcast.13), calls=%async_computation | async-start | bytes 2883584 | tf_op jit(solution)/shard_map/all_to_all | solution.py:794
  89.1 1.0 copy-start.13
  112.6 1.1 copy-start.5
  113.7 1.1 copy-start.7
  114.8 14.7 %copy-start.6 = (f32[12,48,512]{2,1,0:T(8,128)S(1)}, f32[12,48,512]{2,1,0:T(8,128)}, u32[]{:S(2)}) copy-start(f32[12,48,512]{2,1,0:T(8,128)} %copy-done.5) | copy-start | bytes 3538948
  116.2 1.1 copy-start.2
  117.2 2.1 %collective-permute-start.7 = (f32[26,8,512]{2,1,0:T(8,128)S(1)}, f32[26,8,512]{2,1,0:T(8,128)S(1)}, u32[]{:S(2)}, u32[]{:S(2)}) collective-permute-start(f32[26,8,512]{2,1,0:T(8,128)S(1)} %get-tuple-element.60), channel_id=1, source_target_pairs={{0,1},{1,0},{2,3},{3,2},{4,5},{5,4},{6,7},{7,6},{8,9},{9,8},{10,11... | collective-permute-start | bytes 1277960 | tf_op jit(solution)/shard_map/ppermute | solution.py:653
  117.2 11.5 %collective-permute-start.8 = (f32[26,8,512]{2,1,0:T(8,128)S(1)}, f32[26,8,512]{2,1,0:T(8,128)S(1)}, u32[]{:S(2)}, u32[]{:S(2)}) collective-permute-start(f32[26,8,512]{2,1,0:T(8,128)S(1)} %get-tuple-element.61), channel_id=1, source_target_pairs={{1,2},{2,1},{3,0},{0,3},{5,6},{6,5},{7,4},{4,7},{9,10},{10,9},{11,... | collective-permute-start | bytes 1277960 | tf_op jit(solution)/shard_map/ppermute | solution.py:654
  118.0 11.5 %collective-permute-start.9 = (f32[8,128]{1,0:T(8,128)S(1)}, f32[8,128]{1,0:T(8,128)S(1)}, u32[]{:S(2)}, u32[]{:S(2)}) collective-permute-start(f32[8,128]{1,0:T(8,128)S(1)} %get-tuple-element.62.po_ref), channel_id=1, source_target_pairs={{0,2},{1,3},{2,0},{3,1},{4,6},{5,7},{6,4},{7,5},{8,10},{9,11},{10,... | collective-permute-start | bytes 12296 | tf_op jit(solution)/shard_map/ppermute | solution.py:655
  129.4 1.3 copy-start.8
  145.4 16.9 %collective-permute-start.10 = (f32[3,40,512]{2,1,0:T(8,128)S(1)}, f32[3,40,512]{2,1,0:T(8,128)S(1)}, u32[]{:S(2)}, u32[]{:S(2)}) collective-permute-start(f32[3,40,512]{2,1,0:T(8,128)S(1)} %get-tuple-element.67), channel_id=1, source_target_pairs={{0,4},{4,0},{8,12},{12,8},{16,20},{20,16},{24,28},{28,24},{32,36},... | collective-permute-start | bytes 737288 | tf_op jit(solution)/shard_map/ppermute | solution.py:668
  148.3 14.0 %collective-permute-start.11 = (f32[3,40,512]{2,1,0:T(8,128)S(1)}, f32[3,40,512]{2,1,0:T(8,128)S(1)}, u32[]{:S(2)}, u32[]{:S(2)}) collective-permute-start(f32[3,40,512]{2,1,0:T(8,128)S(1)} %get-tuple-element.68), channel_id=1, source_target_pairs={{4,8},{8,4},{12,16},{16,12},{20,24},{24,20},{28,32},{32,28},{36,40... | collective-permute-start | bytes 737288 | tf_op jit(solution)/shard_map/ppermute | solution.py:669
  168.2 20.9 %copy-start.9 = (f32[12,32,512]{2,1,0:T(8,128)S(1)}, f32[12,32,512]{2,1,0:T(8,128)}, u32[]{:S(2)}) copy-start(f32[12,32,512]{2,1,0:T(8,128)} %get-tuple-element.39.speed_ref) | copy-start | bytes 2359300
  168.3 20.9 %collective-permute-start.12 = (f32[3,32,512]{2,1,0:T(8,128)S(1)}, f32[3,32,512]{2,1,0:T(8,128)S(1)}, u32[]{:S(2)}, u32[]{:S(2)}) collective-permute-start(f32[3,32,512]{2,1,0:T(8,128)S(1)} %get-tuple-element.73), channel_id=1, source_target_pairs={{0,4},{4,0},{8,12},{12,8},{16,20},{20,16},{24,28},{28,24},{32,36},... | collective-permute-start | bytes 589832 | tf_op jit(solution)/shard_map/ppermute | solution.py:678
  172.5 16.6 %collective-permute-start.13 = (f32[3,32,512]{2,1,0:T(8,128)S(1)}, f32[3,32,512]{2,1,0:T(8,128)S(1)}, u32[]{:S(2)}, u32[]{:S(2)}) collective-permute-start(f32[3,32,512]{2,1,0:T(8,128)S(1)} %get-tuple-element.74), channel_id=1, source_target_pairs={{4,8},{8,4},{12,16},{16,12},{20,24},{24,20},{28,32},{32,28},{36,40... | collective-permute-start | bytes 589832 | tf_op jit(solution)/shard_map/ppermute | solution.py:679

commit v6 on v5

--- a/solution.py
+++ b/solution.py
@@ -18,7 +18,6 @@
 YE = 10
 Y1 = 6
 Y2 = 3
-VMEM_LIMIT = 48 * 1024 * 1024
 
 
 def lane_shifts(value):
@@ -49,22 +48,25 @@
     return (d - a) + 5.0 * (c - b)
 
 
-def filter_plane(plane, filt, comp, layer, value, low, high0, high1):
-    rows = value.shape[0]
-    plane[8 : 8 + rows, :] = value
-    plane[7:8, :] = low
-    plane[8 + rows : 9 + rows, :] = high0
-    plane[9 + rows : 10 + rows, :] = high1
-    for tile in range(rows // 8):
-        base = 8 + 8 * tile
-        a = plane[base - 1 : base + 7, :]
-        b = plane[base : base + 8, :]
-        c = plane[base + 1 : base + 9, :]
-        d = plane[base + 2 : base + 10, :]
+def filter_plane(filt, comp, layer, get_rows, tiles, low, high0, high1):
+    tile_rows = [get_rows(t) for t in range(tiles)]
+    row = lax.broadcasted_iota(jnp.int32, tile_rows[0].shape, 0)
+    down = [pltpu.roll(v, 1, 0) for v in tile_rows]
+    up = [pltpu.roll(v, 7, 0) for v in tile_rows]
+    up2 = [pltpu.roll(v, 6, 0) for v in tile_rows]
+    for t in range(tiles):
+        b = tile_rows[t]
+        a = jnp.where(row == 0, down[t - 1] if t else low, down[t])
+        if t + 1 < tiles:
+            c = jnp.where(row == 7, up[t + 1], up[t])
+            d = jnp.where(row >= 6, up2[t + 1], up2[t])
+        else:
+            c = jnp.where(row == 7, high0, up[t])
+            d = jnp.where(row == 6, high0, jnp.where(row == 7, high1, up2[t]))
         val_y = val4(a, b, c, d)
         der_y = der4(a, b, c, d)
         before, after, after2 = lane_shifts(val_y)
-        span = pl.ds(8 * tile, 8)
+        span = pl.ds(8 * t, 8)
         filt[comp, 0, layer, span, :] = val4(before, val_y, after, after2)
         filt[comp, 2, layer, span, :] = der4(before, val_y, after, after2)
         before, after, after2 = lane_shifts(der_y)
@@ -102,13 +104,14 @@
     return finish
 
 
-def inner_kernel(u_ref, yh_ref, energy_ref, tail_ref, plane, filt):
+def inner_kernel(u_ref, yh_ref, energy_ref, tail_ref, filt):
     own_x, rows = u_ref.shape[2:4]
 
     def own_layer(layer, carry):
         for comp in range(3):
             edge = [yh_ref[0, comp, k, pl.ds(layer, 1), :] for k in range(3)]
-            filter_plane(plane, filt, comp, layer, u_ref[0, comp, layer], *edge)
+            get_rows = lambda t: u_ref[0, comp, layer, 8 * t : 8 * t + 8, :]
+            filter_plane(filt, comp, layer, get_rows, rows // 8, *edge)
         return carry
 
     lax.fori_loop(0, own_x, own_layer, 0)
@@ -125,7 +128,7 @@
                 tail_ref[0, comp, which, k] = filt[comp, which, own_x - 3 + k]
 
 
-def outer_kernel(place_ref, tail_ref, next_ref, inner_ref, solid_ref, msg_ref, plane, filt, energy, turned):
+def outer_kernel(place_ref, tail_ref, next_ref, inner_ref, solid_ref, msg_ref, filt, energy, turned):
     load = pl.program_id(0)
     own_x, rows, blocks = solid_ref.shape
     size_z = next_ref.shape[1]
@@ -138,8 +141,8 @@
             layer = (load * 3 + comp) * 3 + k
             corner = loads * 9 * rows + rows
             edge = [next_ref[pl.ds(corner + (load * 3 + comp) * 9 + 3 * which + k, 1), :] for which in range(3)]
-            value = next_ref[pl.ds(pl.multiple_of(layer * rows, 8), rows), :]
-            filter_plane(plane, filt, comp, k, value, *edge)
+            get_rows = lambda t: next_ref[pl.ds(pl.multiple_of(layer * rows + 8 * t, 8), 8), :]
+            filter_plane(filt, comp, k, get_rows, tiles, *edge)
 
     def density_at(slot, masked):
         def field(comp, which, span):
@@ -219,10 +222,9 @@
         in_specs=[load_block(comps, own_x, rows, size_z), load_block(comps, 3, own_x, size_z)],
         out_specs=(fixed_block(own_x - 3, rows, size_z), load_block(comps, 3, 3, rows, size_z)),
         scratch_shapes=[
-            pltpu.VMEM((rows + 16, size_z), jnp.float32),
             pltpu.VMEM((3, 3, own_x, rows, size_z), jnp.float32),
         ],
-        compiler_params=pltpu.CompilerParams(vmem_limit_bytes=VMEM_LIMIT),
+        compiler_params=pltpu.CompilerParams(vmem_limit_bytes=48 << 20),
         cost_estimate=pl.CostEstimate(flops=40000 * 4096, bytes_accessed=1 << 20, transcendentals=0),
     )(disp, yh)
 
@@ -244,12 +246,11 @@
         ],
         out_specs=fixed_block(parts * 88, 128),
         scratch_shapes=[
-            pltpu.VMEM((rows + 16, size_z), jnp.float32),
             pltpu.VMEM((3, 3, 3, rows, size_z), jnp.float32),
             pltpu.VMEM((3, rows, size_z), jnp.float32),
             pltpu.VMEM((own_x // 4, size_z + 16, 128), jnp.float32),
         ],
-        compiler_params=pltpu.CompilerParams(vmem_limit_bytes=VMEM_LIMIT),
+        compiler_params=pltpu.CompilerParams(vmem_limit_bytes=48 << 20),
         cost_estimate=pl.CostEstimate(flops=10000 * 4096, bytes_accessed=1 << 20, transcendentals=0),
     )(place, tail, beyond, inner, solid)
 
@@ -315,33 +316,39 @@
     return godunov(pltpu.roll(minus, 1, 1)[:, :size], plus[:, :size])
 
 
-def y_cells(ref, layer, row):
-    p = [ref[layer, row + k : row + k + 8, :] for k in range(6)]
-    d = [p[k + 1] - p[k] for k in range(5)]
-    e = [d[k + 1] - d[k] for k in range(4)]
-    return weno_cell(d[2], *e)
-
-
-def xy_stage(phi_ref, offset, layer0, layers, gp_ref, gm_ref, exact=False):
-    rows = gp_ref.shape[1]
-    tiles = rows // 8
+def next_rows(tiles, step, count):
+    row = lax.broadcasted_iota(jnp.int32, tiles[0].shape, 0)
+    turned = [pltpu.roll(v, 8 - step, 0) for v in tiles]
+    last = len(tiles) - 1
+    return [jnp.where(row < 8 - step, turned[t], turned[min(t + 1, last)]) for t in range(count)]
+
+
+def y_stage(phi_ref, layer, span, gp_ref, gm_ref, z, exact):
+    tiles = gp_ref.shape[1] // 8
+    cells = tiles + 1 if exact else tiles
+    count = min(cells + 1, phi_ref.shape[1] // 8)
+    phi = [phi_ref[layer, 8 * t : 8 * t + 8, span] for t in range(count)]
+    d = [n - p for n, p in zip(next_rows(phi, 1, count), phi)]
+    e = [n - p for n, p in zip(next_rows(d, 1, count), d)]
+    d2 = next_rows(d, 2, cells)
+    e1, e2, e3 = (next_rows(e, k, cells) for k in (1, 2, 3))
+    sides = [weno_cell(d2[t], e[t], e1[t], e2[t], e3[t]) for t in range(cells)]
+    plus = next_rows([p for _, p in sides], 1, tiles)
+    for t in range(tiles):
+        rows = slice(8 * t, 8 * t + 8)
+        gp_ref[z, rows, span], gm_ref[z, rows, span] = godunov(sides[t][0], plus[t])
+
+
+def xy_stage(phi_ref, layer0, layers, gp_ref, gm_ref, exact=False):
+    _, rows, lanes = gp_ref.shape
 
     def layer_step(z, carry):
-        cells = [y_cells(phi_ref, z + layer0, 8 * t + offset - 3) for t in range(tiles)]
-        turned = [pltpu.roll(c[1], 7, 0) for c in cells]
-        if exact:
-            start = min(rows + offset - 3, phi_ref.shape[1] - 13)
-            extra = y_cells(phi_ref, z + layer0, start)[1]
-            turned.append(pltpu.roll(extra, 7 - (rows + offset - 3 - start), 0))
-        else:
-            turned.append(turned[-1])
-        row = lax.broadcasted_iota(jnp.int32, turned[0].shape, 0)
-        for t in range(tiles):
-            plus = jnp.where(row == 7, turned[t + 1], turned[t])
-            yp, ym = godunov(cells[t][0], plus)
-            xp, xm = x_terms(phi_ref[z + layer0, 8 * t + offset : 8 * t + offset + 8, :])
-            gp_ref[z, 8 * t : 8 * t + 8, :] = xp + yp
-            gm_ref[z, 8 * t : 8 * t + 8, :] = xm + ym
+        for block in range(lanes // 128):
+            y_stage(phi_ref, z + layer0, slice(128 * block, 128 * block + 128), gp_ref, gm_ref, z, exact)
+        for t in range(rows // 8):
+            xp, xm = x_terms(phi_ref[z + layer0, 8 * t + 3 : 8 * t + 11, :])
+            gp_ref[z, 8 * t : 8 * t + 8, :] += xp
+            gm_ref[z, 8 * t : 8 * t + 8, :] += xm
         return carry
 
     lax.fori_loop(0, layers, layer_step, 0)
@@ -365,7 +372,7 @@
     lax.fori_loop(0, lanes // 128, lane_step, 0)
 
 
-def first_gradient_kernel(place_ref, tall_ref, ra_ref, rb_ref, ls_ref, sp_ref, sm_ref):
+def first_gradient_kernel(place_ref, tall_ref, ra_ref, rb_ref, ls_ref, sp_ref, sm_ref, near):
     layers, rows, lanes = sp_ref.shape
     depth, own, _ = tall_ref.shape
     ones = jnp.ones((8, lanes), jnp.float32)
@@ -402,8 +409,16 @@
         below(ra_ref)
         above(rb_ref)
 
-    offset = YE - Y1
-    xy_stage(ls_ref, offset, 3, layers, sp_ref, sm_ref)
+    skip = YE - Y1 - 3
+
+    def move(z, carry):
+        near[z, 0 : near.shape[1] - 8, :] = ls_ref[z, skip : skip + near.shape[1] - 8, :]
+        near[z, near.shape[1] - 8 :, :] = ls_ref[z, near.shape[1] - 8 :, :]
+        near[z, near.shape[1] - 8 : near.shape[1] - skip, :] = ls_ref[z, near.shape[1] - 8 + skip :, :]
+        return carry
+
+    lax.fori_loop(0, depth, move, 0)
+    xy_stage(near, 3, layers, sp_ref, sm_ref)
 
     def finish(z, t, span, gp, gm):
         where = pl.ds(8 * t, 8)
@@ -412,11 +427,11 @@
         sm_ref[z, where, span] = scale * jnp.sqrt(sm_ref[z, where, span] + gm)
 
     z_stage(
-        lambda z, t, span: ls_ref[z + 3, 8 * t + offset : 8 * t + offset + 8, span], layers, rows, lanes, finish
-    )
-
-
-def vmem_call(kernel, outs, args, scratch=(), cycles=0):
+        lambda z, t, span: near[z + 3, 8 * t + 3 : 8 * t + 11, span], layers, rows, lanes, finish
+    )
+
+
+def vmem_call(kernel, outs, args, scratch=(), cycles=0, limit=8):
     specs = []
     for arg in args:
         space = pltpu.SMEM if arg.dtype == jnp.int32 else pltpu.VMEM
@@ -427,7 +442,7 @@
         in_specs=specs,
         out_specs=tuple(pl.BlockSpec(memory_space=pltpu.VMEM) for _ in outs),
         scratch_shapes=[pltpu.VMEM(shape, jnp.float32) for shape in scratch],
-        compiler_params=pltpu.CompilerParams(vmem_limit_bytes=VMEM_LIMIT),
+        compiler_params=pltpu.CompilerParams(vmem_limit_bytes=limit << 20),
         cost_estimate=pl.CostEstimate(flops=cycles * 4096, bytes_accessed=1 << 20, transcendentals=0),
     )(*args)
 
@@ -507,12 +522,18 @@
         source, target = (one, two) if step % 2 == 0 else (two, one)
 
         def extend(z, carry):
-            for t in range(tall // 8):
+            count = tall // 8
+            tiles = [source[z, 8 * t : 8 * t + 8, :] for t in range(count + 2)]
+            row = lax.broadcasted_iota(jnp.int32, tiles[0].shape, 0)
+            lane = lax.broadcasted_iota(jnp.int32, tiles[0].shape, 1)
+            down = [pltpu.roll(v, 1, 0) for v in tiles[:-1]]
+            up = [pltpu.roll(v, 7, 0) for v in tiles[1:]]
+            for t in range(count):
                 at = margin + 8 * t
-                centre = source[z, at : at + 8, :]
-                lane = lax.broadcasted_iota(jnp.int32, centre.shape, 1)
+                centre = tiles[t + 1]
                 total = source[z - 1, at : at + 8, :] + source[z + 1, at : at + 8, :]
-                total = total + (source[z, at - 1 : at + 7, :] + source[z, at + 1 : at + 9, :])
+                total = total + jnp.where(row == 0, down[t], down[t + 1])
+                total = total + jnp.where(row == 7, up[t + 1], up[t])
                 total = total + jnp.where(lane == 0, 0.0, pltpu.roll(centre, 1, 1))
                 total = total + jnp.where(lane == lanes - 1, 0.0, pltpu.roll(centre, lanes - 1, 1))
                 span = slice(8 * t, 8 * t + 8)
@@ -565,17 +586,17 @@
         edges[3:6] = jnp.ones((3,) + tuple(edges.shape[1:]), jnp.float32)
 
 
-def plane_kernel(offset, exact, phi_ref, gp_ref, gm_ref):
-    xy_stage(phi_ref, offset, 0, gp_ref.shape[0], gp_ref, gm_ref, exact)
+def plane_kernel(exact, phi_ref, gp_ref, gm_ref):
+    xy_stage(phi_ref, 0, gp_ref.shape[0], gp_ref, gm_ref, exact)
 
 
 def finish_kernel(
-    offset, rows, place_ref, phi_ref, ra_ref, rb_ref, gp_ref, gm_ref, speed_ref, *rest
+    rows, place_ref, phi_ref, ra_ref, rb_ref, gp_ref, gm_ref, speed_ref, *rest
 ):
     out_ref, edges = rest[0], rest[-1]
     layers, count, lanes = out_ref.shape
     base = Y2 if count > rows else 0
-    speed_offset = offset if count > rows else 0
+    speed_offset = 3 if count > rows else 0
     take_edges(place_ref, ra_ref, rb_ref, edges)
 
     def get_phi(z, t, span):
@@ -583,7 +604,7 @@
             return edges[z + 3, 8 * t : 8 * t + 8, span]
         if z >= layers:
             return edges[z - layers + 3, 8 * t : 8 * t + 8, span]
-        return phi_ref[z, 8 * t + offset : 8 * t + offset + 8, span]
+        return phi_ref[z, 8 * t + 3 : 8 * t + 11, span]
 
     def finish(z, t, span, gp, gm):
         where = pl.ds(8 * t, 8)
@@ -604,8 +625,8 @@
     first, second = [], []
     for i in range(0, count, 2):
         first += [(i, i + 1), (i + 1, i)]
-        j = (i + 2) % count
-        second += [(i + 1, j), (j, i + 1)]
+        if i + 2 < count:
+            second += [(i + 1, i + 2), (i + 2, i + 1)]
     return first, second
 
 
@@ -650,10 +671,12 @@
     wfirst, wsecond = swaps("wide")
     count = lax.axis_size("narrow")
     across = [(i, (i + count // 2) % count) for i in range(count)]
+    mirror = [(i, count - 1 - i) for i in range(count)]
     ra = lax.ppermute(ma, "narrow", nfirst)
     rb = lax.ppermute(mb, "narrow", nsecond)
     pc = lax.ppermute(wide_peak, "narrow", across)
-    pa, pb = ra[-1, :, :128], rb[-1, :, :128]
+    pb = lax.ppermute(wide_peak, "narrow", mirror)
+    pa = ra[-1, :, :128]
     tall = ls.shape[1]
     rows1 = -(-(rows + 2 * Y1) // 8) * 8
     rows2 = -(-(rows + 2 * Y2) // 8) * 8
@@ -664,12 +687,13 @@
         (place, tile, ra, rb, pa, pb, pc, wide_peak, ls, sp, sm),
         [(depth, tall + 16, lanes)] * 2 + [(depth, tall, lanes)] * 2,
         8000,
+        16,
     )
     ga = lax.ppermute(sa, "wide", wfirst)
     gb = lax.ppermute(sb, "wide", wsecond)
-    gp, gm = vmem_call(functools.partial(plane_kernel, Y1 - Y2, False), [(layers, rows2, lanes)] * 2, (phi,), (), 12000)
+    gp, gm = vmem_call(functools.partial(plane_kernel, False), [(layers, rows2, lanes)] * 2, (phi,), (), 12000)
     phi, sa, sb = vmem_call(
-        functools.partial(finish_kernel, Y1 - Y2, rows),
+        functools.partial(finish_kernel, rows),
         [(layers, rows2, lanes), (3, rows, lanes), (3, rows, lanes)],
         (place, phi, ga, gb, gp, gm, speed6),
         [(6, rows2, lanes)],
@@ -677,9 +701,9 @@
     )
     ga = lax.ppermute(sa, "wide", wfirst)
     gb = lax.ppermute(sb, "wide", wsecond)
-    gp, gm = vmem_call(functools.partial(plane_kernel, Y2, True), [(layers, rows, lanes)] * 2, (phi,), (), 12000)
+    gp, gm = vmem_call(functools.partial(plane_kernel, True), [(layers, rows, lanes)] * 2, (phi,), (), 12000)
     (phi,) = vmem_call(
-        functools.partial(finish_kernel, Y2, rows),
+        functools.partial(finish_kernel, rows),
         [(layers, rows, lanes)],
         (place, phi, ga, gb, gp, gm, speed),
         [(6, rows, lanes)],
@@ -693,7 +717,8 @@
     rows1 = -(-(rows + 2 * Y1) // 8) * 8
     total = -(-(rows + 2 * YE) // 8) * 8
     return vmem_call(
-        first_gradient_kernel, [(depth, total, lanes)] + [(depth - 6, rows1, lanes)] * 2, (place, tall, ra, rb), (), 35000
+        first_gradient_kernel, [(depth, total, lanes)] + [(depth - 6, rows1, lanes)] * 2, (place, tall, ra, rb),
+        [(depth, total, lanes)], 35000
     )
 
 

time: 195 us -> 176 us (0.903)
  Pallas kernels: 112 us -> 89.9 us
  starting transfers between devices: 39.8 us -> 48 us
  waiting for transfers between devices: 22.2 us -> 15.2 us
    pallas_call x8, Pallas kernels: 77.8 us -> 60 us  [vmem_call(): pl.pallas_call(kernel, out_shape=tuple((jax.ShapeDtypeStruct(shape, jnp.f...]
    ppermute x1, waiting for transfers between devices: 9.33 us -> 0.01 us  [level_part(): rb = lax.ppermute(mb, 'narrow', nsecond)]
    ppermute x1, waiting for transfers between devices: 8.5 us -> 0.01 us  [per_device(): yb = lax.ppermute(yb, 'narrow', nsecond)]
    all_to_all x1, starting transfers between devices: 8.57 us -> 15.8 us  [per_device(): lax.all_to_all(message.reshape(wide, 88, 128), 'wide', split_axis=0, conc...]
    ppermute x2, starting transfers between devices: 4.22 us -> 10.2 us  [level_part(): gb = lax.ppermute(sb, 'wide', wsecond)]
    ppermute x1, waiting for transfers between devices: 0.73 us -> 6.08 us  [level_part(): pc = lax.ppermute(wide_peak, 'narrow', across)]
    ppermute x2, starting transfers between devices: 7.24 us -> 3.06 us  [level_part(): ga = lax.ppermute(sa, 'wide', wfirst)]
    ppermute x1, waiting for transfers between devices: 0.01 us -> 4.17 us  [per_device(): beyond = lax.ppermute(jnp.concatenate(flat, axis=0), 'wide', backward)]
  transfers between devices with their start and end apart: 15 -> 16, of which waited for: 4 -> 5; matrix products, arithmetic and copies ran while one was open for 2% -> 3% of each run, Pallas kernels for 39% -> 32%
where the time goes in v6:
time: 176 us; the launch traced here: 175 us
  Pallas kernels  89.9 us (51%)
  starting transfers between devices  48 us (27%)
  local copies, waits for them, and re-layouts  16.5 us (9%)
  waiting for transfers between devices  15.2 us (9%)
  other arithmetic  4.75 us (3%)
    pallas_call x8, Pallas kernels, vmem_call(): pl.pallas_call(kernel, out_shape=tuple((jax.ShapeDtypeStruct(shape, jnp.f...  60 us
    pallas_call x1, Pallas kernels, inner_strain(): pl.pallas_call(inner_kernel, grid=(loads,), out_shape=(jax.ShapeDtypeStru...  22.2 us
    all_to_all x1, starting transfers between devices, per_device(): lax.all_to_all(message.reshape(wide, 88, 128), 'wide', split_axis=0, conc...  15.8 us
    unnamed x32, local copies, waits for them, and re-layouts  12.3 us
    ppermute x2, starting transfers between devices, level_part(): gb = lax.ppermute(sb, 'wide', wsecond)  10.2 us
    pallas_call x1, Pallas kernels, strain_message(): pl.pallas_call(outer_kernel, grid=(loads,), out_shape=jax.ShapeDtypeStruc...  7.68 us
    ppermute x1, waiting for transfers between devices, level_part(): pc = lax.ppermute(wide_peak, 'narrow', across)  6.08 us
    ppermute x1, starting transfers between devices, per_device(): lb = lax.ppermute(jnp.where(even, bounds[0], bounds[1]), 'wide', wsecond)  5.06 us
  transfers between devices with their start and end apart: 16, of which 5 were waited for; matrix products, arithmetic and copies ran while one was open for 3% of the time, Pallas kernels for 32%

profile of v6, /device:TPU:2, one launch (start us, length us, event | category | flops | bytes accessed | tf_op | source)
XLA Modules:
  0.0 175.3 jit_solution(14923536101887674447)
XLA Ops:
  0.6 3.1 %fusion = (f32[3,3,16,1,384]{4,3,2,1,0:T(1,128)S(1)}, f32[3,3,16,1,384]{4,3,2,1,0:T(1,128)S(1)}, f32[3,3,16,1,384]{4,3,2,1,0:T(1,128)S(1)}) fusion(f32[3,3,16,32,384]{4,3,2,1,0:T(8,128)} %u_ref.1), kind=kLoop, calls=%fused_computation.10 | loop fusion | bytes 1327104 | tf_op jit(solution)/shard_map/slice | solution.py:796
  3.8 0.1 copy_bitcast_fusion
  3.8 0.1 pad_maximum_fusion.1
  3.9 1.3 collective-permute-start.1
  5.2 0.7 slice_select_fusion
  5.9 5.1 %collective-permute-start.3 = (f32[3,32,512]{2,1,0:T(8,128)}, f32[3,32,512]{2,1,0:T(8,128)S(1)}, u32[]{:S(2)}, u32[]{:S(2)}) collective-permute-start(f32[3,32,512]{2,1,0:T(8,128)} %get-tuple-element.81), channel_id=1, source_target_pairs={{4,8},{8,4},{12,16},{16,12},{20,24},{24,20},{28,32},{32,28},{36,40... | collective-permute-start | bytes 589832 | tf_op jit(solution)/shard_map/ppermute | solution.py:804
  11.0 1.4 collective-permute-start.2
  12.4 0.7 copy.21
  13.1 3.2 %collective-permute-start = (f32[3,3,16,384]{3,2,1,0:T(8,128)}, f32[3,3,16,384]{3,2,1,0:T(8,128)}, u32[]{:S(2)}, u32[]{:S(2)}) collective-permute-start(f32[3,3,16,384]{3,2,1,0:T(8,128)} %bitcast.20), channel_id=1, source_target_pairs={{0,1},{1,2},{2,3},{4,5},{5,6},{6,7},{8,9},{9,10},{10,11},{12,13},{... | collective-permute-start | bytes 663560 | tf_op jit(solution)/shard_map/ppermute | solution.py:796
  16.2 0.7 add_bitcast_fusion
  16.9 0.7 copy.13
  17.7 0.1 pad.3.clone
  17.7 0.0 collective-permute-done
  17.7 0.0 collective-permute-done.1
  17.7 1.1 pad_maximum_fusion.yh_ref
  18.9 0.0 collective-permute-done.3.rb_ref
  18.9 3.5 %collective-permute-done.2.ra_ref = f32[3,32,512]{2,1,0:T(8,128)S(1)} collective-permute-done((f32[3,32,512]{2,1,0:T(8,128)S(1)}, f32[3,32,512]{2,1,0:T(8,128)S(1)}, u32[]{:S(2)}, u32[]{:S(2)}) %collective-permute-start.2) | collective-permute-done | bytes 196640 | tf_op jit(solution)/shard_map/ppermute | solution.py:803
  22.4 0.1 reshape.24
  22.5 2.2 %maximum_maximum_fusion = f32[984,384]{1,0:T(8,128)} fusion(f32[81,384]{1,0:T(8,128)S(1)} %reshape.24, f32[32,384]{1,0:T(8,128)} %copy.13, f32[864,384]{1,0:T(8,128)S(1)} %bitcast.21, f32[984]{0:T(1024)S(1)} %pad.3.clone), kind=kLoop, calls=%fused_computation | loop fusion | flops 1133568 | bytes 3016032 | tf_op jit(solution)/shard_map/concatenate | solution.py:810
  24.7 3.2 %collective-permute-start.4 = (f32[984,384]{1,0:T(8,128)}, f32[984,384]{1,0:T(8,128)S(1)}, u32[]{:S(2)}, u32[]{:S(2)}) collective-permute-start(f32[984,384]{1,0:T(8,128)} %maximum_maximum_fusion), channel_id=1, source_target_pairs={{0,124},{4,0},{8,4},{12,8},{16,12},{20,16},{24,20},{28,24},{32,28}... | collective-permute-start | bytes 4534280 | tf_op jit(solution)/shard_map/ppermute | solution.py:810
  27.8 0.1 stack.46.place_ref
  27.9 22.2 %shard_map.50 = (f32[13,32,384]{2,1,0:T(8,128)S(1)}, f32[3,3,3,3,32,384]{5,4,3,2,1,0:T(8,128)S(1)}) custom-call(f32[3,3,16,32,384]{4,3,2,1,0:T(8,128)} %u_ref.1, f32[3,3,3,16,384]{4,3,2,1,0:T(8,128)S(1)} %pad_maximum_fusion.yh_ref), custom_call_target="tpu_custom_call" | custom-call | flops 163840000 | bytes 1048576 | tf_op jit(solution)/shard_map/pallas_call | solution.py:215
  50.2 1.9 %copy-done = f32[3,3,3,3,32,384]{5,4,3,2,1,0:T(8,128)} copy-done((f32[3,3,3,3,32,384]{5,4,3,2,1,0:T(8,128)}, f32[3,3,3,3,32,384]{5,4,3,2,1,0:T(8,128)S(1)}, u32[]{:S(2)}) %copy-start) | copy-done | bytes 3981336
  52.1 1.6 shard_map.51
  53.7 1.0 copy-done.2
  54.7 0.0 collective-permute-start.5
  54.7 0.7 collective-permute-start.6
  55.4 1.1 copy.14.solid_ref
  56.5 0.1 collective-permute-done.5.ra_ref
  56.6 0.0 collective-permute-done.6.rb_ref
  56.6 4.2 %collective-permute-done.4.next_ref = f32[984,384]{1,0:T(8,128)S(1)} collective-permute-done((f32[984,384]{1,0:T(8,128)}, f32[984,384]{1,0:T(8,128)S(1)}, u32[]{:S(2)}, u32[]{:S(2)}) %collective-permute-start.4) | collective-permute-done | bytes 1511456 | tf_op jit(solution)/shard_map/ppermute | solution.py:810
  60.8 1.1 copy-done.10
  61.8 7.7 %shard_map.52 = f32[2816,128]{1,0:T(8,128)} custom-call(s32[6]{0:T(128)S(1)} %stack.46.place_ref, f32[3,3,3,3,32,384]{5,4,3,2,1,0:T(8,128)} %copy-done, f32[984,384]{1,0:T(8,128)S(1)} %collective-permute-done.4.next_ref, f32[13,32,384]{2,1,0:T(8,128)S(1)} %copy-done.10, s32[16,32,24]{2,1,0:T(8,128)S(1)} %copy.14.solid_ref), custom_call_target="tpu_custom_call" | custom-call | flops 40960000 | bytes 1048576 | tf_op jit(solution)/shard_map/pallas_call | solution.py:236
  69.5 15.8 %all-to-all-start = ((f32[32,88,128]{2,1,0:T(8,128)}), f32[32,88,128]{2,1,0:T(8,128)S(1)}, u32[]{:S(2)}, u32[]{:S(2)}) async-start(f32[32,88,128]{2,1,0:T(8,128)} %bitcast.13), calls=%async_computation | async-start | bytes 2883584 | tf_op jit(solution)/shard_map/all_to_all | solution.py:819
  85.4 1.3 copy-done.3
  86.6 1.0 copy-done.12
  87.6 1.0 copy-done.14
  88.6 16.5 %shard_map.53 = (f32[18,56,512]{2,1,0:T(8,128)S(1)}, f32[12,48,512]{2,1,0:T(8,128)S(1)}, f32[12,48,512]{2,1,0:T(8,128)S(1)}) custom-call(s32[6]{0:T(128)S(1)} %stack.46.place_ref, f32[18,32,512]{2,1,0:T(8,128)S(1)} %copy-done.3, f32[21,8,512]{2,1,0:T(8,128)S(1)} %copy-done.12, f32[21,8,512]{2,1,0:T(8,128)S(1)} %copy-done.14), custom_call_target="tpu_custom_call" | custom-call | flops 143360000 | bytes 1048576 | tf_op jit(solution)/shard_map/pallas_call | solution.py:439
  105.1 1.0 copy-done.4
  106.2 1.0 copy-done.6
  107.2 1.3 all-to-all-done.recv_ref
  108.4 1.4 shard_map.54
  109.8 0.1 collective-permute-start.7
  109.9 0.7 collective-permute-start.8
  110.6 3.4 %collective-permute-start.10 = (f32[8,128]{1,0:T(8,128)S(1)}, f32[8,128]{1,0:T(8,128)S(1)}, u32[]{:S(2)}, u32[]{:S(2)}) collective-permute-start(f32[8,128]{1,0:T(8,128)S(1)} %get-tuple-element.62.po_ref), channel_id=1, source_target_pairs={{0,2},{1,3},{2,0},{3,1},{4,6},{5,7},{6,4},{7,5},{8,10},{9,11},{10,... | collective-permute-start | bytes 12296 | tf_op jit(solution)/shard_map/ppermute | solution.py:677
  114.0 0.0 collective-permute-start.9
  114.0 0.0 collective-permute-done.7.ra_ref
  114.1 6.1 %collective-permute-done.10.pc_ref = f32[8,128]{1,0:T(8,128)S(1)} collective-permute-done((f32[8,128]{1,0:T(8,128)S(1)}, f32[8,128]{1,0:T(8,128)S(1)}, u32[]{:S(2)}, u32[]{:S(2)}) %collective-permute-start.10) | collective-permute-done | bytes 4128 | tf_op jit(solution)/shard_map/ppermute | solution.py:677
  120.1 0.0 collective-permute-done.9.pb_ref
  120.1 0.0 collective-permute-done.8.rb_ref
  120.2 1.3 copy-done.7
  121.4 13.2 %shard_map.55 = (f32[12,32,512]{2,1,0:T(8,128)}, f32[12,48,512]{2,1,0:T(8,128)S(1)}, f32[12,48,512]{2,1,0:T(8,128)S(1)}, f32[3,40,512]{2,1,0:T(8,128)S(1)}, f32[3,40,512]{2,1,0:T(8,128)S(1)}) custom-call(s32[6]{0:T(128)S(1)} %stack.46.place_ref, f32[20,32,512]{2,1,0:T(8,128)S(1)} %get-tuple-element.59.tile_ref, ...), custom_call_target="tpu_custom_call" | custom-call | flops 32768000 | bytes 1048576 | tf_op jit(solution)/shard_map/pallas_call | solution.py:439
  134.6 1.8 collective-permute-start.11
  136.3 5.1 %collective-permute-start.12 = (f32[3,40,512]{2,1,0:T(8,128)S(1)}, f32[3,40,512]{2,1,0:T(8,128)S(1)}, u32[]{:S(2)}, u32[]{:S(2)}) collective-permute-start(f32[3,40,512]{2,1,0:T(8,128)S(1)} %get-tuple-element.68), channel_id=1, source_target_pairs={{4,8},{8,4},{12,16},{16,12},{20,24},{24,20},{28,32},{32,28},{36,40... | collective-permute-start | bytes 737288 | tf_op jit(solution)/shard_map/ppermute | solution.py:693
  141.4 8.4 %shard_map.56 = (f32[12,40,512]{2,1,0:T(8,128)S(1)}, f32[12,40,512]{2,1,0:T(8,128)S(1)}) custom-call(f32[12,48,512]{2,1,0:T(8,128)S(1)} %get-tuple-element.66.phi_ref), custom_call_target="tpu_custom_call" | custom-call | flops 49152000 | bytes 1048576 | tf_op jit(solution)/shard_map/pallas_call | solution.py:439
  149.8 0.0 collective-permute-done.11.ra_ref
  149.8 5.9 %shard_map.57 = (f32[12,40,512]{2,1,0:T(8,128)S(1)}, f32[3,32,512]{2,1,0:T(8,128)S(1)}, f32[3,32,512]{2,1,0:T(8,128)S(1)}) custom-call(s32[6]{0:T(128)S(1)} %stack.46.place_ref, f32[12,48,512]{2,1,0:T(8,128)S(1)} %get-tuple-element.66.phi_ref, f32[3,40,512]{2,1,0:T(8,128)S(1)} %collective-permute-done.11.ra_ref, ...), custom_call_target="tpu_custom_call" | custom-call | flops 20480000 | bytes 1048576 | tf_op jit(solution)/shard_map/pallas_call | solution.py:439
  155.8 0.0 copy-start.8
  155.8 1.3 collective-permute-start.13
  157.1 5.1 %collective-permute-start.14 = (f32[3,32,512]{2,1,0:T(8,128)S(1)}, f32[3,32,512]{2,1,0:T(8,128)S(1)}, u32[]{:S(2)}, u32[]{:S(2)}) collective-permute-start(f32[3,32,512]{2,1,0:T(8,128)S(1)} %get-tuple-element.74), channel_id=1, source_target_pairs={{4,8},{8,4},{12,16},{16,12},{20,24},{24,20},{28,32},{32,28},{36,40... | collective-permute-start | bytes 589832 | tf_op jit(solution)/shard_map/ppermute | solution.py:703
  162.2 7.6 %shard_map.58 = (f32[12,32,512]{2,1,0:T(8,128)S(1)}, f32[12,32,512]{2,1,0:T(8,128)S(1)}) custom-call(f32[12,40,512]{2,1,0:T(8,128)S(1)} %get-tuple-element.72.phi_ref), custom_call_target="tpu_custom_call" | custom-call | flops 49152000 | bytes 1048576 | tf_op jit(solution)/shard_map/pallas_call | solution.py:439
  169.8 0.0 collective-permute-done.13.ra_ref
  169.8 0.0 collective-permute-done.14.rb_ref
  169.9 5.4 %shard_map.59 = f32[12,32,512]{2,1,0:T(8,128)} custom-call(s32[6]{0:T(128)S(1)} %stack.46.place_ref, f32[12,40,512]{2,1,0:T(8,128)S(1)} %get-tuple-element.72.phi_ref, f32[3,32,512]{2,1,0:T(8,128)S(1)} %collective-permute-done.13.ra_ref, f32[3,32,512]{2,1,0:T(8,128)S(1)} %collective-permute-done.14.rb_ref, f32[12,32,512]{2,1,0:T(8,128)S(1)} %get-tuple-element.75.gp_ref, ...), custom_call_target="tpu_custom_call" | custom-call | flops 20480000 | bytes 1048576 | tf_op jit(solution)/shard_map/pallas_call | solution.py:439
  (27 shorter events, 0.1 us)
Async XLA Ops:
  0.6 4.6 %copy-start.1 = (f32[12,32,512]{2,1,0:T(8,128)S(1)}, f32[12,32,512]{2,1,0:T(8,128)}, u32[]{:S(2)}) copy-start(f32[12,32,512]{2,1,0:T(8,128)} %ls_ref.1) | copy-start | bytes 2359300
  3.9 13.9 %collective-permute-start.1 = (f32[3,3,2,16,384]{4,3,2,1,0:T(8,128)S(1)}, f32[3,3,2,16,384]{4,3,2,1,0:T(8,128)}, u32[]{:S(2)}, u32[]{:S(2)}) collective-permute-start(f32[3,3,2,16,384]{4,3,2,1,0:T(8,128)S(1)} %pad_maximum_fusion.1), channel_id=1, source_target_pairs={{1,0},{2,1},{3,2},{5,4},{6,5},{7,6},{9,8},{10,9},{11,10},{13,12},{... | collective-permute-start | bytes 1327112 | tf_op jit(solution)/shard_map/ppermute | solution.py:797
  5.9 13.0 %collective-permute-start.3 = (f32[3,32,512]{2,1,0:T(8,128)}, f32[3,32,512]{2,1,0:T(8,128)S(1)}, u32[]{:S(2)}, u32[]{:S(2)}) collective-permute-start(f32[3,32,512]{2,1,0:T(8,128)} %get-tuple-element.81), channel_id=1, source_target_pairs={{4,8},{8,4},{12,16},{16,12},{20,24},{24,20},{28,32},{32,28},{36,40... | collective-permute-start | bytes 589832 | tf_op jit(solution)/shard_map/ppermute | solution.py:804
  11.0 11.4 %collective-permute-start.2 = (f32[3,32,512]{2,1,0:T(8,128)S(1)}, f32[3,32,512]{2,1,0:T(8,128)S(1)}, u32[]{:S(2)}, u32[]{:S(2)}) collective-permute-start(f32[3,32,512]{2,1,0:T(8,128)S(1)} %get-tuple-element.82), channel_id=1, source_target_pairs={{0,4},{4,0},{8,12},{12,8},{16,20},{20,16},{24,28},{28,24},{32,36},... | collective-permute-start | bytes 589832 | tf_op jit(solution)/shard_map/ppermute | solution.py:803
  13.1 4.7 %collective-permute-start = (f32[3,3,16,384]{3,2,1,0:T(8,128)}, f32[3,3,16,384]{3,2,1,0:T(8,128)}, u32[]{:S(2)}, u32[]{:S(2)}) collective-permute-start(f32[3,3,16,384]{3,2,1,0:T(8,128)} %bitcast.20), channel_id=1, source_target_pairs={{0,1},{1,2},{2,3},{4,5},{5,6},{6,7},{8,9},{9,10},{10,11},{12,13},{... | collective-permute-start | bytes 663560 | tf_op jit(solution)/shard_map/ppermute | solution.py:796
  16.9 5.6 %slice-start = ((f32[3,3,16,32,384]{4,3,2,1,0:T(8,128)}), f32[3,3,3,32,384]{4,3,2,1,0:T(8,128)S(1)}, s32[]{:S(2)}) async-start(f32[3,3,16,32,384]{4,3,2,1,0:T(8,128)} %u_ref.1), calls=%async_computation.1 | async-start | bytes 2654208 | tf_op jit(solution)/shard_map/slice | solution.py:807
  24.7 36.1 %collective-permute-start.4 = (f32[984,384]{1,0:T(8,128)}, f32[984,384]{1,0:T(8,128)S(1)}, u32[]{:S(2)}, u32[]{:S(2)}) collective-permute-start(f32[984,384]{1,0:T(8,128)} %maximum_maximum_fusion), channel_id=1, source_target_pairs={{0,124},{4,0},{8,4},{12,8},{16,12},{20,16},{24,20},{28,24},{32,28}... | collective-permute-start | bytes 4534280 | tf_op jit(solution)/shard_map/ppermute | solution.py:810
  50.2 1.9 %copy-start = (f32[3,3,3,3,32,384]{5,4,3,2,1,0:T(8,128)}, f32[3,3,3,3,32,384]{5,4,3,2,1,0:T(8,128)S(1)}, u32[]{:S(2)}) copy-start(f32[3,3,3,3,32,384]{5,4,3,2,1,0:T(8,128)S(1)} %get-tuple-element.41.tail_ref) | copy-start | bytes 11943940
  52.1 2.7 %copy-start.9 = (f32[13,32,384]{2,1,0:T(8,128)}, f32[13,32,384]{2,1,0:T(8,128)S(1)}, u32[]{:S(2)}) copy-start(f32[13,32,384]{2,1,0:T(8,128)S(1)} %get-tuple-element.51.inner_ref) | copy-start | bytes 1916932
  53.7 1.0 copy-start.2
  54.7 1.9 %collective-permute-start.5 = (f32[21,8,512]{2,1,0:T(8,128)}, f32[21,8,512]{2,1,0:T(8,128)S(1)}, u32[]{:S(2)}, u32[]{:S(2)}) collective-permute-start(f32[21,8,512]{2,1,0:T(8,128)} %get-tuple-element.48), channel_id=1, source_target_pairs={{0,1},{1,0},{2,3},{3,2},{4,5},{5,4},{6,7},{7,6},{8,9},{9,8},{10,11... | collective-permute-start | bytes 1032200 | tf_op jit(solution)/shard_map/ppermute | solution.py:814
  54.7 1.9 %collective-permute-start.6 = (f32[21,8,512]{2,1,0:T(8,128)}, f32[21,8,512]{2,1,0:T(8,128)S(1)}, u32[]{:S(2)}, u32[]{:S(2)}) collective-permute-start(f32[21,8,512]{2,1,0:T(8,128)} %get-tuple-element.49), channel_id=1, source_target_pairs={{1,2},{2,1},{5,6},{6,5},{9,10},{10,9},{13,14},{14,13},{17,18},{18,... | collective-permute-start | bytes 1032200 | tf_op jit(solution)/shard_map/ppermute | solution.py:815
  56.6 12.9 %copy-start.11 = (f32[21,8,512]{2,1,0:T(8,128)}, f32[21,8,512]{2,1,0:T(8,128)S(1)}, u32[]{:S(2)}) copy-start(f32[21,8,512]{2,1,0:T(8,128)S(1)} %collective-permute-done.5.ra_ref) | copy-start | bytes 1032196
  56.6 12.9 %copy-start.13 = (f32[21,8,512]{2,1,0:T(8,128)}, f32[21,8,512]{2,1,0:T(8,128)S(1)}, u32[]{:S(2)}) copy-start(f32[21,8,512]{2,1,0:T(8,128)S(1)} %collective-permute-done.6.rb_ref) | copy-start | bytes 1032196
  60.8 1.1 copy-start.10
  69.5 38.9 %all-to-all-start = ((f32[32,88,128]{2,1,0:T(8,128)}), f32[32,88,128]{2,1,0:T(8,128)S(1)}, u32[]{:S(2)}, u32[]{:S(2)}) async-start(f32[32,88,128]{2,1,0:T(8,128)} %bitcast.13), calls=%async_computation | async-start | bytes 2883584 | tf_op jit(solution)/shard_map/all_to_all | solution.py:819
  85.4 1.3 copy-start.3
  86.6 1.0 copy-start.12
  87.6 1.0 copy-start.14
  105.1 1.0 copy-start.4
  106.2 1.0 copy-start.6
  108.4 11.7 %copy-start.5 = (f32[12,48,512]{2,1,0:T(8,128)S(1)}, f32[12,48,512]{2,1,0:T(8,128)}, u32[]{:S(2)}) copy-start(f32[12,48,512]{2,1,0:T(8,128)} %copy-done.4) | copy-start | bytes 3538948
  109.8 4.2 %collective-permute-start.7 = (f32[26,8,512]{2,1,0:T(8,128)S(1)}, f32[26,8,512]{2,1,0:T(8,128)S(1)}, u32[]{:S(2)}, u32[]{:S(2)}) collective-permute-start(f32[26,8,512]{2,1,0:T(8,128)S(1)} %get-tuple-element.60), channel_id=1, source_target_pairs={{0,1},{1,0},{2,3},{3,2},{4,5},{5,4},{6,7},{7,6},{8,9},{9,8},{10,11... | collective-permute-start | bytes 1277960 | tf_op jit(solution)/shard_map/ppermute | solution.py:675
  109.9 10.2 %collective-permute-start.8 = (f32[26,8,512]{2,1,0:T(8,128)S(1)}, f32[26,8,512]{2,1,0:T(8,128)S(1)}, u32[]{:S(2)}, u32[]{:S(2)}) collective-permute-start(f32[26,8,512]{2,1,0:T(8,128)S(1)} %get-tuple-element.61), channel_id=1, source_target_pairs={{1,2},{2,1},{5,6},{6,5},{9,10},{10,9},{13,14},{14,13},{17,18},{18,... | collective-permute-start | bytes 1277960 | tf_op jit(solution)/shard_map/ppermute | solution.py:676
  110.6 9.5 %collective-permute-start.10 = (f32[8,128]{1,0:T(8,128)S(1)}, f32[8,128]{1,0:T(8,128)S(1)}, u32[]{:S(2)}, u32[]{:S(2)}) collective-permute-start(f32[8,128]{1,0:T(8,128)S(1)} %get-tuple-element.62.po_ref), channel_id=1, source_target_pairs={{0,2},{1,3},{2,0},{3,1},{4,6},{5,7},{6,4},{7,5},{8,10},{9,11},{10,... | collective-permute-start | bytes 12296 | tf_op jit(solution)/shard_map/ppermute | solution.py:677
  114.0 6.1 %collective-permute-start.9 = (f32[8,128]{1,0:T(8,128)S(1)}, f32[8,128]{1,0:T(8,128)S(1)}, u32[]{:S(2)}, u32[]{:S(2)}) collective-permute-start(f32[8,128]{1,0:T(8,128)S(1)} %get-tuple-element.62.po_ref), channel_id=1, source_target_pairs={{0,3},{1,2},{2,1},{3,0},{4,7},{5,6},{6,5},{7,4},{8,11},{9,10},{10,... | collective-permute-start | bytes 12296 | tf_op jit(solution)/shard_map/ppermute | solution.py:678
  120.1 1.3 copy-start.7
  134.6 15.2 %collective-permute-start.11 = (f32[3,40,512]{2,1,0:T(8,128)S(1)}, f32[3,40,512]{2,1,0:T(8,128)S(1)}, u32[]{:S(2)}, u32[]{:S(2)}) collective-permute-start(f32[3,40,512]{2,1,0:T(8,128)S(1)} %get-tuple-element.67), channel_id=1, source_target_pairs={{0,4},{4,0},{8,12},{12,8},{16,20},{20,16},{24,28},{28,24},{32,36},... | collective-permute-start | bytes 737288 | tf_op jit(solution)/shard_map/ppermute | solution.py:692
  136.3 13.5 %collective-permute-start.12 = (f32[3,40,512]{2,1,0:T(8,128)S(1)}, f32[3,40,512]{2,1,0:T(8,128)S(1)}, u32[]{:S(2)}, u32[]{:S(2)}) collective-permute-start(f32[3,40,512]{2,1,0:T(8,128)S(1)} %get-tuple-element.68), channel_id=1, source_target_pairs={{4,8},{8,4},{12,16},{16,12},{20,24},{24,20},{28,32},{32,28},{36,40... | collective-permute-start | bytes 737288 | tf_op jit(solution)/shard_map/ppermute | solution.py:693
  155.8 14.1 %copy-start.8 = (f32[12,32,512]{2,1,0:T(8,128)S(1)}, f32[12,32,512]{2,1,0:T(8,128)}, u32[]{:S(2)}) copy-start(f32[12,32,512]{2,1,0:T(8,128)} %get-tuple-element.39.speed_ref) | copy-start | bytes 2359300
  155.8 14.0 %collective-permute-start.13 = (f32[3,32,512]{2,1,0:T(8,128)S(1)}, f32[3,32,512]{2,1,0:T(8,128)S(1)}, u32[]{:S(2)}, u32[]{:S(2)}) collective-permute-start(f32[3,32,512]{2,1,0:T(8,128)S(1)} %get-tuple-element.73), channel_id=1, source_target_pairs={{0,4},{4,0},{8,12},{12,8},{16,20},{20,16},{24,28},{28,24},{32,36},... | collective-permute-start | bytes 589832 | tf_op jit(solution)/shard_map/ppermute | solution.py:702
  157.1 12.7 %collective-permute-start.14 = (f32[3,32,512]{2,1,0:T(8,128)S(1)}, f32[3,32,512]{2,1,0:T(8,128)S(1)}, u32[]{:S(2)}, u32[]{:S(2)}) collective-permute-start(f32[3,32,512]{2,1,0:T(8,128)S(1)} %get-tuple-element.74), channel_id=1, source_target_pairs={{4,8},{8,4},{12,16},{16,12},{20,24},{24,20},{28,32},{32,28},{36,40... | collective-permute-start | bytes 589832 | tf_op jit(solution)/shard_map/ppermute | solution.py:703

commit v7 on v6

--- a/solution.py
+++ b/solution.py
@@ -15,7 +15,7 @@
 TIME_STEP = 0.3
 HALO = EXT_PASSES
 GRAD_SCALE = 1.0 / (8.0 * 48.0 * 48.0)
-YE = 10
+YE = 9
 Y1 = 6
 Y2 = 3
 
@@ -323,7 +323,7 @@
     return [jnp.where(row < 8 - step, turned[t], turned[min(t + 1, last)]) for t in range(count)]
 
 
-def y_stage(phi_ref, layer, span, gp_ref, gm_ref, z, exact):
+def y_stage(phi_ref, layer, span, gp_ref, gm_ref, mid_ref, z, exact):
     tiles = gp_ref.shape[1] // 8
     cells = tiles + 1 if exact else tiles
     count = min(cells + 1, phi_ref.shape[1] // 8)
@@ -334,19 +334,21 @@
     e1, e2, e3 = (next_rows(e, k, cells) for k in (1, 2, 3))
     sides = [weno_cell(d2[t], e[t], e1[t], e2[t], e3[t]) for t in range(cells)]
     plus = next_rows([p for _, p in sides], 1, tiles)
+    mid = next_rows(phi, 3, tiles)
     for t in range(tiles):
         rows = slice(8 * t, 8 * t + 8)
         gp_ref[z, rows, span], gm_ref[z, rows, span] = godunov(sides[t][0], plus[t])
-
-
-def xy_stage(phi_ref, layer0, layers, gp_ref, gm_ref, exact=False):
+        mid_ref[z, rows, span] = mid[t]
+
+
+def xy_stage(phi_ref, layer0, layers, gp_ref, gm_ref, mid_ref, exact=False):
     _, rows, lanes = gp_ref.shape
 
     def layer_step(z, carry):
         for block in range(lanes // 128):
-            y_stage(phi_ref, z + layer0, slice(128 * block, 128 * block + 128), gp_ref, gm_ref, z, exact)
+            y_stage(phi_ref, z + layer0, slice(128 * block, 128 * block + 128), gp_ref, gm_ref, mid_ref, z, exact)
         for t in range(rows // 8):
-            xp, xm = x_terms(phi_ref[z + layer0, 8 * t + 3 : 8 * t + 11, :])
+            xp, xm = x_terms(mid_ref[z, 8 * t : 8 * t + 8, :])
             gp_ref[z, 8 * t : 8 * t + 8, :] += xp
             gm_ref[z, 8 * t : 8 * t + 8, :] += xm
         return carry
@@ -365,14 +367,23 @@
             for cell in range(layers + 1):
                 minus, plus = weno_cell(d[cell + 2], e[cell], e[cell + 1], e[cell + 2], e[cell + 3])
                 if before is not None:
-                    finish(cell - 1, t, span, *godunov(before, plus))
+                    finish(cell - 1, t, span, p[cell + 2], *godunov(before, plus))
                 before = minus
         return carry
 
     lax.fori_loop(0, lanes // 128, lane_step, 0)
 
 
-def first_gradient_kernel(place_ref, tall_ref, ra_ref, rb_ref, ls_ref, sp_ref, sm_ref, near):
+def layer_rows(mid_ref, edges, z, t, span):
+    layers = mid_ref.shape[0]
+    if z < 0:
+        return edges[z + 3, 8 * t : 8 * t + 8, span]
+    if z >= layers:
+        return edges[z - layers + 3, 8 * t : 8 * t + 8, span]
+    return mid_ref[z, 8 * t : 8 * t + 8, span]
+
+
+def first_gradient_kernel(place_ref, tall_ref, ra_ref, rb_ref, ls_ref, sp_ref, sm_ref, mid_ref, edges):
     layers, rows, lanes = sp_ref.shape
     depth, own, _ = tall_ref.shape
     ones = jnp.ones((8, lanes), jnp.float32)
@@ -409,25 +420,21 @@
         below(ra_ref)
         above(rb_ref)
 
-    skip = YE - Y1 - 3
-
-    def move(z, carry):
-        near[z, 0 : near.shape[1] - 8, :] = ls_ref[z, skip : skip + near.shape[1] - 8, :]
-        near[z, near.shape[1] - 8 :, :] = ls_ref[z, near.shape[1] - 8 :, :]
-        near[z, near.shape[1] - 8 : near.shape[1] - skip, :] = ls_ref[z, near.shape[1] - 8 + skip :, :]
-        return carry
-
-    lax.fori_loop(0, depth, move, 0)
-    xy_stage(near, 3, layers, sp_ref, sm_ref)
-
-    def finish(z, t, span, gp, gm):
+    for k in range(6):
+        layer = k if k < 3 else depth - 6 + k
+        tiles = [ls_ref[layer, 8 * t : 8 * t + 8, :] for t in range(rows // 8 + 1)]
+        for t, value in enumerate(next_rows(tiles, 3, rows // 8)):
+            edges[k, 8 * t : 8 * t + 8, :] = value
+    xy_stage(ls_ref, 3, layers, sp_ref, sm_ref, mid_ref)
+
+    def finish(z, t, span, phi, gp, gm):
         where = pl.ds(8 * t, 8)
         scale = TIME_STEP / 6.0
         sp_ref[z, where, span] = scale * jnp.sqrt(sp_ref[z, where, span] + gp)
         sm_ref[z, where, span] = scale * jnp.sqrt(sm_ref[z, where, span] + gm)
 
     z_stage(
-        lambda z, t, span: near[z + 3, 8 * t + 3 : 8 * t + 11, span], layers, rows, lanes, finish
+        lambda z, t, span: layer_rows(mid_ref, edges, z, t, span), layers, rows, lanes, finish
     )
 
 
@@ -463,8 +470,8 @@
 
 
 def extend_kernel(
-    place_ref, tile_ref, ra_ref, rb_ref, pa_ref, pb_ref, pc_ref, po_ref, ls_ref, sp_ref, sm_ref,
-    speed_ref, speed6_ref, phi_ref, ma_ref, mb_ref, one, two, keep, pull,
+    place_ref, tile_ref, ra_ref, rb_ref, pa_ref, pb_ref, pc_ref, po_ref, ls_ref, sp_ref, sm_ref, mid_ref,
+    speed_ref, speed3_ref, phi_ref, ma_ref, mb_ref, one, two, keep, pull,
 ):
     depth, rows, lanes = tile_ref.shape
     layers = depth - 2 * HALO
@@ -500,24 +507,27 @@
         below(ra_ref)
         above(rb_ref)
 
+    def inside(z, first_row):
+        outside = ((z < HALO) & (place_ref[1] == 1)) | ((z >= depth - HALO) & (place_ref[2] == 1))
+        return y_inside(place_ref, YE, first_row, (8, lanes), rows) & jnp.logical_not(outside)
+
     def normalise(z, carry):
-        outside = ((z < HALO) & (place_ref[1] == 1)) | ((z >= depth - HALO) & (place_ref[2] == 1))
+        for t in range(-1, tall // 8):
+            at = slice(margin + 8 * t, margin + 8 * t + 8)
+            one[z, at, :] = jnp.where(inside(z, 8 * t), one[z, at, :] * scale - 0.5, 0.0)
+        return carry
+
+    def weigh(z, carry):
         for t in range(tall // 8):
-            at = slice(margin + 8 * t, margin + 8 * t + 8)
-            ok = y_inside(place_ref, YE, 8 * t, (8, lanes), rows) & jnp.logical_not(outside)
-            velocity = jnp.where(ok, one[z, at, :] * scale - 0.5, 0.0)
-            one[z, at, :] = velocity
-
-            @pl.when((z >= 1) & (z < depth - 1))
-            def _():
-                ls = ls_ref[z - 1, 8 * t : 8 * t + 8, :]
-                weight = 1.0 / (1.0 + 4.0 * ls * ls)
-                keep[z, 8 * t : 8 * t + 8, :] = weight * velocity
-                pull[z, 8 * t : 8 * t + 8, :] = jnp.where(ok, (1.0 - weight) * (1.0 / 6.0), 0.0)
-
+            span = slice(8 * t, 8 * t + 8)
+            ls = ls_ref[z - 1, span, :]
+            weight = newton_reciprocal(1.0 + 4.0 * ls * ls)
+            keep[z, span, :] = weight * one[z, margin + 8 * t : margin + 8 * t + 8, :]
+            pull[z, span, :] = jnp.where(inside(z, 8 * t), (1.0 - weight) * (1.0 / 6.0), 0.0)
         return carry
 
     lax.fori_loop(0, depth, normalise, 0)
+    lax.fori_loop(1, depth - 1, weigh, 0)
     for step in range(EXT_PASSES):
         source, target = (one, two) if step % 2 == 0 else (two, one)
 
@@ -545,15 +555,19 @@
     final = one if EXT_PASSES % 2 == 0 else two
 
     def march(z, carry):
-        speed_ref[z] = final[z + HALO, base : base + rows, :]
-        shift = YE - Y1
-        for t in range(speed6_ref.shape[1] // 8):
+        count = tall // 8
+        tiles = [final[z + HALO, margin + 8 * t : margin + 8 * t + 8, :] for t in range(count)]
+        moved = next_rows(tiles, YE - Y1, count - 1)
+        for t in range(count - 1):
             span = slice(8 * t, 8 * t + 8)
-            speed = final[z + HALO, margin + shift + 8 * t : margin + shift + 8 * t + 8, :]
-            speed6_ref[z, span, :] = speed
+            speed = moved[t]
             change = jnp.maximum(speed, 0.0) * sp_ref[z, span, :] + jnp.minimum(speed, 0.0) * sm_ref[z, span, :]
-            phi = ls_ref[z + 3, shift + 8 * t : shift + 8 * t + 8, :] - change
+            phi = mid_ref[z, span, :] - change
             phi_ref[z, span, :] = jnp.where(y_inside(place_ref, Y1, 8 * t, phi.shape, rows), phi, 1.0)
+        for t, value in enumerate(next_rows(tiles, YE - Y2, speed3_ref.shape[1] // 8)):
+            speed3_ref[z, 8 * t : 8 * t + 8, :] = value
+        for t, value in enumerate(next_rows(tiles[1:], YE - 8, rows // 8)):
+            speed_ref[z, 8 * t : 8 * t + 8, :] = value
         return carry
 
     lax.fori_loop(0, layers, march, 0)
@@ -586,8 +600,8 @@
         edges[3:6] = jnp.ones((3,) + tuple(edges.shape[1:]), jnp.float32)
 
 
-def plane_kernel(exact, phi_ref, gp_ref, gm_ref):
-    xy_stage(phi_ref, 0, gp_ref.shape[0], gp_ref, gm_ref, exact)
+def plane_kernel(exact, phi_ref, gp_ref, gm_ref, mid_ref):
+    xy_stage(phi_ref, 0, gp_ref.shape[0], gp_ref, gm_ref, mid_ref, exact)
 
 
 def finish_kernel(
@@ -596,21 +610,14 @@
     out_ref, edges = rest[0], rest[-1]
     layers, count, lanes = out_ref.shape
     base = Y2 if count > rows else 0
-    speed_offset = 3 if count > rows else 0
     take_edges(place_ref, ra_ref, rb_ref, edges)
-
-    def get_phi(z, t, span):
-        if z < 0:
-            return edges[z + 3, 8 * t : 8 * t + 8, span]
-        if z >= layers:
-            return edges[z - layers + 3, 8 * t : 8 * t + 8, span]
-        return phi_ref[z, 8 * t + 3 : 8 * t + 11, span]
-
-    def finish(z, t, span, gp, gm):
+    get_phi = functools.partial(layer_rows, phi_ref, edges)
+
+    def finish(z, t, span, phi, gp, gm):
         where = pl.ds(8 * t, 8)
-        speed = speed_ref[z, 8 * t + speed_offset : 8 * t + speed_offset + 8, span]
+        speed = speed_ref[z, where, span]
         total = jnp.where(speed > 0.0, gp_ref[z, where, span] + gp, gm_ref[z, where, span] + gm)
-        phi = get_phi(z, t, span) - (TIME_STEP / 6.0) * speed * jnp.sqrt(total)
+        phi = phi - (TIME_STEP / 6.0) * speed * jnp.sqrt(total)
         if count > rows:
             phi = jnp.where(y_inside(place_ref, base, 8 * t, phi.shape, rows), phi, 1.0)
         out_ref[z, where, span] = phi
@@ -665,7 +672,7 @@
         upper(mb_ref)
 
 
-def level_part(place, tile, ma, mb, wide_peak, level_set, ls, sp, sm):
+def level_part(place, tile, ma, mb, wide_peak, level_set, ls, sp, sm, mid):
     layers, rows, lanes = level_set.shape
     nfirst, nsecond = swaps("narrow")
     wfirst, wsecond = swaps("wide")
@@ -681,31 +688,31 @@
     rows1 = -(-(rows + 2 * Y1) // 8) * 8
     rows2 = -(-(rows + 2 * Y2) // 8) * 8
     depth = layers + 2 * HALO
-    speed, speed6, phi, sa, sb = vmem_call(
+    speed, speed3, phi, sa, sb = vmem_call(
         extend_kernel,
-        [(layers, rows, lanes), (layers, rows1, lanes), (layers, rows1, lanes), (3, rows2, lanes), (3, rows2, lanes)],
-        (place, tile, ra, rb, pa, pb, pc, wide_peak, ls, sp, sm),
+        [(layers, rows, lanes), (layers, rows2, lanes), (layers, rows1, lanes), (3, rows2, lanes), (3, rows2, lanes)],
+        (place, tile, ra, rb, pa, pb, pc, wide_peak, ls, sp, sm, mid),
         [(depth, tall + 16, lanes)] * 2 + [(depth, tall, lanes)] * 2,
         8000,
         16,
     )
     ga = lax.ppermute(sa, "wide", wfirst)
     gb = lax.ppermute(sb, "wide", wsecond)
-    gp, gm = vmem_call(functools.partial(plane_kernel, False), [(layers, rows2, lanes)] * 2, (phi,), (), 12000)
+    gp, gm, mid = vmem_call(functools.partial(plane_kernel, False), [(layers, rows2, lanes)] * 3, (phi,), (), 12000)
     phi, sa, sb = vmem_call(
         functools.partial(finish_kernel, rows),
         [(layers, rows2, lanes), (3, rows, lanes), (3, rows, lanes)],
-        (place, phi, ga, gb, gp, gm, speed6),
+        (place, mid, ga, gb, gp, gm, speed3),
         [(6, rows2, lanes)],
         5000,
     )
     ga = lax.ppermute(sa, "wide", wfirst)
     gb = lax.ppermute(sb, "wide", wsecond)
-    gp, gm = vmem_call(functools.partial(plane_kernel, True), [(layers, rows, lanes)] * 2, (phi,), (), 12000)
+    gp, gm, mid = vmem_call(functools.partial(plane_kernel, True), [(layers, rows, lanes)] * 3, (phi,), (), 12000)
     (phi,) = vmem_call(
         functools.partial(finish_kernel, rows),
         [(layers, rows, lanes)],
-        (place, phi, ga, gb, gp, gm, speed),
+        (place, mid, ga, gb, gp, gm, speed),
         [(6, rows, lanes)],
         5000,
     )
@@ -717,8 +724,8 @@
     rows1 = -(-(rows + 2 * Y1) // 8) * 8
     total = -(-(rows + 2 * YE) // 8) * 8
     return vmem_call(
-        first_gradient_kernel, [(depth, total, lanes)] + [(depth - 6, rows1, lanes)] * 2, (place, tall, ra, rb),
-        [(depth, total, lanes)], 35000
+        first_gradient_kernel, [(depth, total, lanes)] + [(depth - 6, rows1, lanes)] * 3, (place, tall, ra, rb),
+        [(6, rows1, lanes)], 35000
     )
 
 
@@ -817,10 +824,10 @@
     message = strain_message(place, tail, beyond, inner, material, wide)
     message, tall = lax.optimization_barrier((message, tall))
     recv = lax.all_to_all(message.reshape(wide, 88, 128), "wide", split_axis=0, concat_axis=0, tiled=True)
-    ls, sp, sm = first_gradient(place, tall, ya, yb)
+    ls, sp, sm, mid = first_gradient(place, tall, ya, yb)
     recv, sp = lax.optimization_barrier((recv, sp))
     tile, wide_peak, ma, mb = unpack(place, recv, own_z, rows)
-    return level_part(place, tile, ma, mb, wide_peak, level_set, ls, sp, sm)
+    return level_part(place, tile, ma, mb, wide_peak, level_set, ls, sp, sm, mid)
 
 
 def solution(mesh):

time: 176 us -> 172 us (0.977)
  Pallas kernels: 89.9 us -> 81.1 us
  local copies, waits for them, and re-layouts: 16.5 us -> 18.8 us
  waiting for transfers between devices: 15.2 us -> 17.2 us
    pallas_call x8, Pallas kernels: 60 us -> 51.1 us  [vmem_call(): pl.pallas_call(kernel, out_shape=tuple((jax.ShapeDtypeStruct(shape, jnp.f...]
    unnamed x32 -> x36, local copies, waits for them, and re-layouts: 12.3 us -> 14.6 us
    ppermute x2, starting transfers between devices: 10.2 us -> 12.3 us  [level_part(): gb = lax.ppermute(sb, 'wide', wsecond)]
    ppermute x2, starting transfers between devices: 3.06 us -> 0.98 us  [level_part(): ga = lax.ppermute(sa, 'wide', wfirst)]
    all_to_all x1, waiting for transfers between devices: 1.26 us -> 3.31 us  [per_device(): lax.all_to_all(message.reshape(wide, 88, 128), 'wide', split_axis=0, conc...]
  transfers between devices with their start and end apart: 16 -> 16, of which waited for: 5 -> 5; matrix products, arithmetic and copies ran while one was open for 3% -> 3% of each run, Pallas kernels for 32% -> 31%
where the time goes in v7:
time: 172 us; the launch traced here: 171 us
  Pallas kernels  81.1 us (47%)
  starting transfers between devices  48 us (28%)
  local copies, waits for them, and re-layouts  18.8 us (11%)
  waiting for transfers between devices  17.2 us (10%)
  other arithmetic  4.74 us (3%)
    pallas_call x8, Pallas kernels, vmem_call(): pl.pallas_call(kernel, out_shape=tuple((jax.ShapeDtypeStruct(shape, jnp.f...  51.1 us
    pallas_call x1, Pallas kernels, inner_strain(): pl.pallas_call(inner_kernel, grid=(loads,), out_shape=(jax.ShapeDtypeStru...  22.2 us
    all_to_all x1, starting transfers between devices, per_device(): lax.all_to_all(message.reshape(wide, 88, 128), 'wide', split_axis=0, conc...  15.8 us
    unnamed x36, local copies, waits for them, and re-layouts  14.6 us
    ppermute x2, starting transfers between devices, level_part(): gb = lax.ppermute(sb, 'wide', wsecond)  12.3 us
    pallas_call x1, Pallas kernels, strain_message(): pl.pallas_call(outer_kernel, grid=(loads,), out_shape=jax.ShapeDtypeStruc...  7.68 us
    ppermute x1, waiting for transfers between devices, level_part(): pc = lax.ppermute(wide_peak, 'narrow', across)  6.08 us
    ppermute x1, starting transfers between devices, per_device(): lb = lax.ppermute(jnp.where(even, bounds[0], bounds[1]), 'wide', wsecond)  5.06 us
  transfers between devices with their start and end apart: 16, of which 5 were waited for; matrix products, arithmetic and copies ran while one was open for 3% of the time, Pallas kernels for 31%

profile of v7, /device:TPU:2, one launch (start us, length us, event | category | flops | bytes accessed | tf_op | source)
XLA Modules:
  0.0 170.8 jit_solution(2219304420545480092)
XLA Ops:
  0.6 3.1 %fusion = (f32[3,3,16,1,384]{4,3,2,1,0:T(1,128)S(1)}, f32[3,3,16,1,384]{4,3,2,1,0:T(1,128)S(1)}, f32[3,3,16,1,384]{4,3,2,1,0:T(1,128)S(1)}) fusion(f32[3,3,16,32,384]{4,3,2,1,0:T(8,128)} %u_ref.1), kind=kLoop, calls=%fused_computation.10 | loop fusion | bytes 1327104 | tf_op jit(solution)/shard_map/slice | solution.py:803
  3.8 0.1 copy_bitcast_fusion
  3.8 0.1 pad_maximum_fusion.1
  3.9 1.3 collective-permute-start.1
  5.2 0.7 slice_select_fusion
  5.9 5.1 %collective-permute-start.3 = (f32[3,32,512]{2,1,0:T(8,128)}, f32[3,32,512]{2,1,0:T(8,128)S(1)}, u32[]{:S(2)}, u32[]{:S(2)}) collective-permute-start(f32[3,32,512]{2,1,0:T(8,128)} %get-tuple-element.87), channel_id=1, source_target_pairs={{4,8},{8,4},{12,16},{16,12},{20,24},{24,20},{28,32},{32,28},{36,40... | collective-permute-start | bytes 589832 | tf_op jit(solution)/shard_map/ppermute | solution.py:811
  11.0 1.4 collective-permute-start.2
  12.4 0.7 copy.21
  13.1 3.2 %collective-permute-start = (f32[3,3,16,384]{3,2,1,0:T(8,128)}, f32[3,3,16,384]{3,2,1,0:T(8,128)}, u32[]{:S(2)}, u32[]{:S(2)}) collective-permute-start(f32[3,3,16,384]{3,2,1,0:T(8,128)} %bitcast.20), channel_id=1, source_target_pairs={{0,1},{1,2},{2,3},{4,5},{5,6},{6,7},{8,9},{9,10},{10,11},{12,13},{... | collective-permute-start | bytes 663560 | tf_op jit(solution)/shard_map/ppermute | solution.py:803
  16.2 0.7 add_bitcast_fusion
  16.9 0.7 copy.13
  17.7 0.1 pad.3.clone
  17.7 0.0 collective-permute-done
  17.8 0.0 collective-permute-done.1
  17.8 1.1 pad_maximum_fusion.yh_ref
  18.9 0.0 collective-permute-done.3.rb_ref
  18.9 3.5 %collective-permute-done.2.ra_ref = f32[3,32,512]{2,1,0:T(8,128)S(1)} collective-permute-done((f32[3,32,512]{2,1,0:T(8,128)S(1)}, f32[3,32,512]{2,1,0:T(8,128)S(1)}, u32[]{:S(2)}, u32[]{:S(2)}) %collective-permute-start.2) | collective-permute-done | bytes 196640 | tf_op jit(solution)/shard_map/ppermute | solution.py:810
  22.4 0.1 reshape.24
  22.5 2.2 %maximum_maximum_fusion = f32[984,384]{1,0:T(8,128)} fusion(f32[81,384]{1,0:T(8,128)S(1)} %reshape.24, f32[32,384]{1,0:T(8,128)} %copy.13, f32[864,384]{1,0:T(8,128)S(1)} %bitcast.21, f32[984]{0:T(1024)S(1)} %pad.3.clone), kind=kLoop, calls=%fused_computation | loop fusion | flops 1133568 | bytes 3016032 | tf_op jit(solution)/shard_map/concatenate | solution.py:817
  24.7 3.2 %collective-permute-start.4 = (f32[984,384]{1,0:T(8,128)}, f32[984,384]{1,0:T(8,128)S(1)}, u32[]{:S(2)}, u32[]{:S(2)}) collective-permute-start(f32[984,384]{1,0:T(8,128)} %maximum_maximum_fusion), channel_id=1, source_target_pairs={{0,124},{4,0},{8,4},{12,8},{16,12},{20,16},{24,20},{28,24},{32,28}... | collective-permute-start | bytes 4534280 | tf_op jit(solution)/shard_map/ppermute | solution.py:817
  27.8 0.1 stack.46.place_ref
  27.9 22.2 %shard_map.50 = (f32[13,32,384]{2,1,0:T(8,128)S(1)}, f32[3,3,3,3,32,384]{5,4,3,2,1,0:T(8,128)S(1)}) custom-call(f32[3,3,16,32,384]{4,3,2,1,0:T(8,128)} %u_ref.1, f32[3,3,3,16,384]{4,3,2,1,0:T(8,128)S(1)} %pad_maximum_fusion.yh_ref), custom_call_target="tpu_custom_call" | custom-call | flops 163840000 | bytes 1048576 | tf_op jit(solution)/shard_map/pallas_call | solution.py:215
  50.2 1.9 %copy-done = f32[3,3,3,3,32,384]{5,4,3,2,1,0:T(8,128)} copy-done((f32[3,3,3,3,32,384]{5,4,3,2,1,0:T(8,128)}, f32[3,3,3,3,32,384]{5,4,3,2,1,0:T(8,128)S(1)}, u32[]{:S(2)}) %copy-start) | copy-done | bytes 3981336
  52.0 1.6 shard_map.51
  53.7 1.0 copy-done.2
  54.7 0.0 collective-permute-start.5
  54.7 0.7 collective-permute-start.6
  55.4 1.1 copy.14.solid_ref
  56.4 0.1 collective-permute-done.5.ra_ref
  56.6 0.0 collective-permute-done.6.rb_ref
  56.6 4.2 %collective-permute-done.4.next_ref = f32[984,384]{1,0:T(8,128)S(1)} collective-permute-done((f32[984,384]{1,0:T(8,128)}, f32[984,384]{1,0:T(8,128)S(1)}, u32[]{:S(2)}, u32[]{:S(2)}) %collective-permute-start.4) | collective-permute-done | bytes 1511456 | tf_op jit(solution)/shard_map/ppermute | solution.py:817
  60.7 1.1 copy-done.12
  61.8 7.7 %shard_map.52 = f32[2816,128]{1,0:T(8,128)} custom-call(s32[6]{0:T(128)S(1)} %stack.46.place_ref, f32[3,3,3,3,32,384]{5,4,3,2,1,0:T(8,128)} %copy-done, f32[984,384]{1,0:T(8,128)S(1)} %collective-permute-done.4.next_ref, f32[13,32,384]{2,1,0:T(8,128)S(1)} %copy-done.12, s32[16,32,24]{2,1,0:T(8,128)S(1)} %copy.14.solid_ref), custom_call_target="tpu_custom_call" | custom-call | flops 40960000 | bytes 1048576 | tf_op jit(solution)/shard_map/pallas_call | solution.py:236
  69.5 15.8 %all-to-all-start = ((f32[32,88,128]{2,1,0:T(8,128)}), f32[32,88,128]{2,1,0:T(8,128)S(1)}, u32[]{:S(2)}, u32[]{:S(2)}) async-start(f32[32,88,128]{2,1,0:T(8,128)} %bitcast.13), calls=%async_computation | async-start | bytes 2883584 | tf_op jit(solution)/shard_map/all_to_all | solution.py:826
  85.3 1.3 copy-done.3
  86.6 1.0 copy-done.14
  87.6 1.0 copy-done.16
  88.6 13.4 %shard_map.53 = (f32[18,56,512]{2,1,0:T(8,128)S(1)}, f32[12,48,512]{2,1,0:T(8,128)S(1)}, f32[12,48,512]{2,1,0:T(8,128)S(1)}, f32[12,48,512]{2,1,0:T(8,128)S(1)}) custom-call(s32[6]{0:T(128)S(1)} %stack.46.place_ref, f32[18,32,512]{2,1,0:T(8,128)S(1)} %copy-done.3, f32[21,8,512]{2,1,0:T(8,128)S(1)} %copy-done.14, f32[21,8,512]{2,1,0:T(8,128)S(1)} %copy-done.16), custom_call_target="tpu_custom_call" | custom-call | flops 143360000 | bytes 1048576 | tf_op jit(solution)/shard_map/pallas_call | solution.py:446
  102.0 1.0 copy-done.4
  103.1 1.0 copy-done.6
  104.1 1.0 copy-done.8
  105.1 3.3 %all-to-all-done.recv_ref = f32[32,88,128]{2,1,0:T(8,128)S(1)} async-done(((f32[32,88,128]{2,1,0:T(8,128)}), f32[32,88,128]{2,1,0:T(8,128)S(1)}, u32[]{:S(2)}, u32[]{:S(2)}) %all-to-all-start) | async-done | bytes 1441824 | tf_op jit(solution)/shard_map/all_to_all | solution.py:826
  108.4 1.4 shard_map.54
  109.8 0.1 collective-permute-start.7
  109.9 0.7 collective-permute-start.8
  110.6 3.4 %collective-permute-start.10 = (f32[8,128]{1,0:T(8,128)S(1)}, f32[8,128]{1,0:T(8,128)S(1)}, u32[]{:S(2)}, u32[]{:S(2)}) collective-permute-start(f32[8,128]{1,0:T(8,128)S(1)} %get-tuple-element.65.po_ref), channel_id=1, source_target_pairs={{0,2},{1,3},{2,0},{3,1},{4,6},{5,7},{6,4},{7,5},{8,10},{9,11},{10,... | collective-permute-start | bytes 12296 | tf_op jit(solution)/shard_map/ppermute | solution.py:684
  114.0 6.1 %collective-permute-done.10.pc_ref = f32[8,128]{1,0:T(8,128)S(1)} collective-permute-done((f32[8,128]{1,0:T(8,128)S(1)}, f32[8,128]{1,0:T(8,128)S(1)}, u32[]{:S(2)}, u32[]{:S(2)}) %collective-permute-start.10) | collective-permute-done | bytes 4128 | tf_op jit(solution)/shard_map/ppermute | solution.py:684
  120.1 0.0 collective-permute-done.9.pb_ref
  120.1 0.0 collective-permute-done.8.rb_ref
  120.1 1.3 copy-done.7
  121.4 1.3 copy-done.9
  122.7 12.1 %shard_map.55 = (f32[12,32,512]{2,1,0:T(8,128)}, f32[12,40,512]{2,1,0:T(8,128)S(1)}, f32[12,48,512]{2,1,0:T(8,128)S(1)}, f32[3,40,512]{2,1,0:T(8,128)S(1)}, f32[3,40,512]{2,1,0:T(8,128)S(1)}) custom-call(s32[6]{0:T(128)S(1)} %stack.46.place_ref, f32[20,32,512]{2,1,0:T(8,128)S(1)} %get-tuple-element.62.tile_ref, ...), custom_call_target="tpu_custom_call" | custom-call | flops 32768000 | bytes 1048576 | tf_op jit(solution)/shard_map/pallas_call | solution.py:446
  134.8 0.8 collective-permute-start.11
  135.5 6.2 %collective-permute-start.12 = (f32[3,40,512]{2,1,0:T(8,128)S(1)}, f32[3,40,512]{2,1,0:T(8,128)S(1)}, u32[]{:S(2)}, u32[]{:S(2)}) collective-permute-start(f32[3,40,512]{2,1,0:T(8,128)S(1)} %get-tuple-element.73), channel_id=1, source_target_pairs={{4,8},{8,4},{12,16},{16,12},{20,24},{24,20},{28,32},{32,28},{36,40... | collective-permute-start | bytes 737288 | tf_op jit(solution)/shard_map/ppermute | solution.py:700
  141.8 8.3 %shard_map.56 = (f32[12,40,512]{2,1,0:T(8,128)S(1)}, f32[12,40,512]{2,1,0:T(8,128)S(1)}, f32[12,40,512]{2,1,0:T(8,128)S(1)}) custom-call(f32[12,48,512]{2,1,0:T(8,128)S(1)} %get-tuple-element.70.phi_ref), custom_call_target="tpu_custom_call" | custom-call | flops 49152000 | bytes 1048576 | tf_op jit(solution)/shard_map/pallas_call | solution.py:446
  150.2 0.0 collective-permute-done.12.rb_ref
  150.2 3.2 %shard_map.57 = (f32[12,40,512]{2,1,0:T(8,128)S(1)}, f32[3,32,512]{2,1,0:T(8,128)S(1)}, f32[3,32,512]{2,1,0:T(8,128)S(1)}) custom-call(s32[6]{0:T(128)S(1)} %stack.46.place_ref, f32[12,40,512]{2,1,0:T(8,128)S(1)} %get-tuple-element.71.phi_ref, f32[3,40,512]{2,1,0:T(8,128)S(1)} %collective-permute-done.11.ra_ref, ...), custom_call_target="tpu_custom_call" | custom-call | flops 20480000 | bytes 1048576 | tf_op jit(solution)/shard_map/pallas_call | solution.py:446
  153.4 0.0 copy-start.10
  153.4 0.2 collective-permute-start.13
  153.6 6.1 %collective-permute-start.14 = (f32[3,32,512]{2,1,0:T(8,128)S(1)}, f32[3,32,512]{2,1,0:T(8,128)S(1)}, u32[]{:S(2)}, u32[]{:S(2)}) collective-permute-start(f32[3,32,512]{2,1,0:T(8,128)S(1)} %get-tuple-element.80), channel_id=1, source_target_pairs={{4,8},{8,4},{12,16},{16,12},{20,24},{24,20},{28,32},{32,28},{36,40... | collective-permute-start | bytes 589832 | tf_op jit(solution)/shard_map/ppermute | solution.py:710
  159.7 7.6 %shard_map.58 = (f32[12,32,512]{2,1,0:T(8,128)S(1)}, f32[12,32,512]{2,1,0:T(8,128)S(1)}, f32[12,32,512]{2,1,0:T(8,128)S(1)}) custom-call(f32[12,40,512]{2,1,0:T(8,128)S(1)} %get-tuple-element.77.phi_ref), custom_call_target="tpu_custom_call" | custom-call | flops 49152000 | bytes 1048576 | tf_op jit(solution)/shard_map/pallas_call | solution.py:446
  167.2 0.0 collective-permute-done.13.ra_ref
  167.3 0.0 collective-permute-done.14.rb_ref
  167.3 3.5 %shard_map.59 = f32[12,32,512]{2,1,0:T(8,128)} custom-call(s32[6]{0:T(128)S(1)} %stack.46.place_ref, f32[12,32,512]{2,1,0:T(8,128)S(1)} %get-tuple-element.78.phi_ref, f32[3,32,512]{2,1,0:T(8,128)S(1)} %collective-permute-done.13.ra_ref, f32[3,32,512]{2,1,0:T(8,128)S(1)} %collective-permute-done.14.rb_ref, f32[12,32,512]{2,1,0:T(8,128)S(1)} %get-tuple-element.81.gp_ref, ...), custom_call_target="tpu_custom_call" | custom-call | flops 20480000 | bytes 1048576 | tf_op jit(solution)/shard_map/pallas_call | solution.py:446
  (31 shorter events, 0.1 us)
Async XLA Ops:
  0.6 4.6 %copy-start.1 = (f32[12,32,512]{2,1,0:T(8,128)S(1)}, f32[12,32,512]{2,1,0:T(8,128)}, u32[]{:S(2)}) copy-start(f32[12,32,512]{2,1,0:T(8,128)} %ls_ref.1) | copy-start | bytes 2359300
  3.9 13.9 %collective-permute-start.1 = (f32[3,3,2,16,384]{4,3,2,1,0:T(8,128)S(1)}, f32[3,3,2,16,384]{4,3,2,1,0:T(8,128)}, u32[]{:S(2)}, u32[]{:S(2)}) collective-permute-start(f32[3,3,2,16,384]{4,3,2,1,0:T(8,128)S(1)} %pad_maximum_fusion.1), channel_id=1, source_target_pairs={{1,0},{2,1},{3,2},{5,4},{6,5},{7,6},{9,8},{10,9},{11,10},{13,12},{... | collective-permute-start | bytes 1327112 | tf_op jit(solution)/shard_map/ppermute | solution.py:804
  5.9 13.0 %collective-permute-start.3 = (f32[3,32,512]{2,1,0:T(8,128)}, f32[3,32,512]{2,1,0:T(8,128)S(1)}, u32[]{:S(2)}, u32[]{:S(2)}) collective-permute-start(f32[3,32,512]{2,1,0:T(8,128)} %get-tuple-element.87), channel_id=1, source_target_pairs={{4,8},{8,4},{12,16},{16,12},{20,24},{24,20},{28,32},{32,28},{36,40... | collective-permute-start | bytes 589832 | tf_op jit(solution)/shard_map/ppermute | solution.py:811
  11.0 11.4 %collective-permute-start.2 = (f32[3,32,512]{2,1,0:T(8,128)S(1)}, f32[3,32,512]{2,1,0:T(8,128)S(1)}, u32[]{:S(2)}, u32[]{:S(2)}) collective-permute-start(f32[3,32,512]{2,1,0:T(8,128)S(1)} %get-tuple-element.88), channel_id=1, source_target_pairs={{0,4},{4,0},{8,12},{12,8},{16,20},{20,16},{24,28},{28,24},{32,36},... | collective-permute-start | bytes 589832 | tf_op jit(solution)/shard_map/ppermute | solution.py:810
  13.1 4.7 %collective-permute-start = (f32[3,3,16,384]{3,2,1,0:T(8,128)}, f32[3,3,16,384]{3,2,1,0:T(8,128)}, u32[]{:S(2)}, u32[]{:S(2)}) collective-permute-start(f32[3,3,16,384]{3,2,1,0:T(8,128)} %bitcast.20), channel_id=1, source_target_pairs={{0,1},{1,2},{2,3},{4,5},{5,6},{6,7},{8,9},{9,10},{10,11},{12,13},{... | collective-permute-start | bytes 663560 | tf_op jit(solution)/shard_map/ppermute | solution.py:803
  16.9 5.6 %slice-start = ((f32[3,3,16,32,384]{4,3,2,1,0:T(8,128)}), f32[3,3,3,32,384]{4,3,2,1,0:T(8,128)S(1)}, s32[]{:S(2)}) async-start(f32[3,3,16,32,384]{4,3,2,1,0:T(8,128)} %u_ref.1), calls=%async_computation.1 | async-start | bytes 2654208 | tf_op jit(solution)/shard_map/slice | solution.py:814
  24.7 36.1 %collective-permute-start.4 = (f32[984,384]{1,0:T(8,128)}, f32[984,384]{1,0:T(8,128)S(1)}, u32[]{:S(2)}, u32[]{:S(2)}) collective-permute-start(f32[984,384]{1,0:T(8,128)} %maximum_maximum_fusion), channel_id=1, source_target_pairs={{0,124},{4,0},{8,4},{12,8},{16,12},{20,16},{24,20},{28,24},{32,28}... | collective-permute-start | bytes 4534280 | tf_op jit(solution)/shard_map/ppermute | solution.py:817
  50.2 1.9 %copy-start = (f32[3,3,3,3,32,384]{5,4,3,2,1,0:T(8,128)}, f32[3,3,3,3,32,384]{5,4,3,2,1,0:T(8,128)S(1)}, u32[]{:S(2)}) copy-start(f32[3,3,3,3,32,384]{5,4,3,2,1,0:T(8,128)S(1)} %get-tuple-element.44.tail_ref) | copy-start | bytes 11943940
  52.0 2.7 %copy-start.11 = (f32[13,32,384]{2,1,0:T(8,128)}, f32[13,32,384]{2,1,0:T(8,128)S(1)}, u32[]{:S(2)}) copy-start(f32[13,32,384]{2,1,0:T(8,128)S(1)} %get-tuple-element.54.inner_ref) | copy-start | bytes 1916932
  53.7 1.0 copy-start.2
  54.7 1.9 %collective-permute-start.5 = (f32[21,8,512]{2,1,0:T(8,128)}, f32[21,8,512]{2,1,0:T(8,128)S(1)}, u32[]{:S(2)}, u32[]{:S(2)}) collective-permute-start(f32[21,8,512]{2,1,0:T(8,128)} %get-tuple-element.51), channel_id=1, source_target_pairs={{0,1},{1,0},{2,3},{3,2},{4,5},{5,4},{6,7},{7,6},{8,9},{9,8},{10,11... | collective-permute-start | bytes 1032200 | tf_op jit(solution)/shard_map/ppermute | solution.py:821
  54.7 1.9 %collective-permute-start.6 = (f32[21,8,512]{2,1,0:T(8,128)}, f32[21,8,512]{2,1,0:T(8,128)S(1)}, u32[]{:S(2)}, u32[]{:S(2)}) collective-permute-start(f32[21,8,512]{2,1,0:T(8,128)} %get-tuple-element.52), channel_id=1, source_target_pairs={{1,2},{2,1},{5,6},{6,5},{9,10},{10,9},{13,14},{14,13},{17,18},{18,... | collective-permute-start | bytes 1032200 | tf_op jit(solution)/shard_map/ppermute | solution.py:822
  56.6 13.0 %copy-start.13 = (f32[21,8,512]{2,1,0:T(8,128)}, f32[21,8,512]{2,1,0:T(8,128)S(1)}, u32[]{:S(2)}) copy-start(f32[21,8,512]{2,1,0:T(8,128)S(1)} %collective-permute-done.5.ra_ref) | copy-start | bytes 1032196
  56.6 12.9 %copy-start.15 = (f32[21,8,512]{2,1,0:T(8,128)}, f32[21,8,512]{2,1,0:T(8,128)S(1)}, u32[]{:S(2)}) copy-start(f32[21,8,512]{2,1,0:T(8,128)S(1)} %collective-permute-done.6.rb_ref) | copy-start | bytes 1032196
  60.7 1.1 copy-start.12
  69.5 38.9 %all-to-all-start = ((f32[32,88,128]{2,1,0:T(8,128)}), f32[32,88,128]{2,1,0:T(8,128)S(1)}, u32[]{:S(2)}, u32[]{:S(2)}) async-start(f32[32,88,128]{2,1,0:T(8,128)} %bitcast.13), calls=%async_computation | async-start | bytes 2883584 | tf_op jit(solution)/shard_map/all_to_all | solution.py:826
  85.3 1.3 copy-start.3
  86.6 1.0 copy-start.14
  87.6 1.0 copy-start.16
  102.0 1.0 copy-start.4
  103.1 1.0 copy-start.6
  104.1 1.0 copy-start.8
  108.4 11.7 %copy-start.5 = (f32[12,48,512]{2,1,0:T(8,128)S(1)}, f32[12,48,512]{2,1,0:T(8,128)}, u32[]{:S(2)}) copy-start(f32[12,48,512]{2,1,0:T(8,128)} %copy-done.4) | copy-start | bytes 3538948
  109.8 4.2 %collective-permute-start.7 = (f32[26,8,512]{2,1,0:T(8,128)S(1)}, f32[26,8,512]{2,1,0:T(8,128)S(1)}, u32[]{:S(2)}, u32[]{:S(2)}) collective-permute-start(f32[26,8,512]{2,1,0:T(8,128)S(1)} %get-tuple-element.63), channel_id=1, source_target_pairs={{0,1},{1,0},{2,3},{3,2},{4,5},{5,4},{6,7},{7,6},{8,9},{9,8},{10,11... | collective-permute-start | bytes 1277960 | tf_op jit(solution)/shard_map/ppermute | solution.py:682
  109.9 10.2 %collective-permute-start.8 = (f32[26,8,512]{2,1,0:T(8,128)S(1)}, f32[26,8,512]{2,1,0:T(8,128)S(1)}, u32[]{:S(2)}, u32[]{:S(2)}) collective-permute-start(f32[26,8,512]{2,1,0:T(8,128)S(1)} %get-tuple-element.64), channel_id=1, source_target_pairs={{1,2},{2,1},{5,6},{6,5},{9,10},{10,9},{13,14},{14,13},{17,18},{18,... | collective-permute-start | bytes 1277960 | tf_op jit(solution)/shard_map/ppermute | solution.py:683
  110.6 9.5 %collective-permute-start.10 = (f32[8,128]{1,0:T(8,128)S(1)}, f32[8,128]{1,0:T(8,128)S(1)}, u32[]{:S(2)}, u32[]{:S(2)}) collective-permute-start(f32[8,128]{1,0:T(8,128)S(1)} %get-tuple-element.65.po_ref), channel_id=1, source_target_pairs={{0,2},{1,3},{2,0},{3,1},{4,6},{5,7},{6,4},{7,5},{8,10},{9,11},{10,... | collective-permute-start | bytes 12296 | tf_op jit(solution)/shard_map/ppermute | solution.py:684
  114.0 6.1 %collective-permute-start.9 = (f32[8,128]{1,0:T(8,128)S(1)}, f32[8,128]{1,0:T(8,128)S(1)}, u32[]{:S(2)}, u32[]{:S(2)}) collective-permute-start(f32[8,128]{1,0:T(8,128)S(1)} %get-tuple-element.65.po_ref), channel_id=1, source_target_pairs={{0,3},{1,2},{2,1},{3,0},{4,7},{5,6},{6,5},{7,4},{8,11},{9,10},{10,... | collective-permute-start | bytes 12296 | tf_op jit(solution)/shard_map/ppermute | solution.py:685
  120.1 1.3 copy-start.7
  121.4 1.3 copy-start.9
  134.8 15.4 %collective-permute-start.11 = (f32[3,40,512]{2,1,0:T(8,128)S(1)}, f32[3,40,512]{2,1,0:T(8,128)S(1)}, u32[]{:S(2)}, u32[]{:S(2)}) collective-permute-start(f32[3,40,512]{2,1,0:T(8,128)S(1)} %get-tuple-element.72), channel_id=1, source_target_pairs={{0,4},{4,0},{8,12},{12,8},{16,20},{20,16},{24,28},{28,24},{32,36},... | collective-permute-start | bytes 737288 | tf_op jit(solution)/shard_map/ppermute | solution.py:699
  135.5 14.6 %collective-permute-start.12 = (f32[3,40,512]{2,1,0:T(8,128)S(1)}, f32[3,40,512]{2,1,0:T(8,128)S(1)}, u32[]{:S(2)}, u32[]{:S(2)}) collective-permute-start(f32[3,40,512]{2,1,0:T(8,128)S(1)} %get-tuple-element.73), channel_id=1, source_target_pairs={{4,8},{8,4},{12,16},{16,12},{20,24},{24,20},{28,32},{32,28},{36,40... | collective-permute-start | bytes 737288 | tf_op jit(solution)/shard_map/ppermute | solution.py:700
  153.4 13.9 %copy-start.10 = (f32[12,32,512]{2,1,0:T(8,128)S(1)}, f32[12,32,512]{2,1,0:T(8,128)}, u32[]{:S(2)}) copy-start(f32[12,32,512]{2,1,0:T(8,128)} %get-tuple-element.42.speed_ref) | copy-start | bytes 2359300
  153.4 13.9 %collective-permute-start.13 = (f32[3,32,512]{2,1,0:T(8,128)S(1)}, f32[3,32,512]{2,1,0:T(8,128)S(1)}, u32[]{:S(2)}, u32[]{:S(2)}) collective-permute-start(f32[3,32,512]{2,1,0:T(8,128)S(1)} %get-tuple-element.79), channel_id=1, source_target_pairs={{0,4},{4,0},{8,12},{12,8},{16,20},{20,16},{24,28},{28,24},{32,36},... | collective-permute-start | bytes 589832 | tf_op jit(solution)/shard_map/ppermute | solution.py:709
  153.6 13.7 %collective-permute-start.14 = (f32[3,32,512]{2,1,0:T(8,128)S(1)}, f32[3,32,512]{2,1,0:T(8,128)S(1)}, u32[]{:S(2)}, u32[]{:S(2)}) collective-permute-start(f32[3,32,512]{2,1,0:T(8,128)S(1)} %get-tuple-element.80), channel_id=1, source_target_pairs={{4,8},{8,4},{12,16},{16,12},{20,24},{24,20},{28,32},{32,28},{36,40... | collective-permute-start | bytes 589832 | tf_op jit(solution)/shard_map/ppermute | solution.py:710

commit v8 on v7

--- a/solution.py
+++ b/solution.py
@@ -383,8 +383,10 @@
     return mid_ref[z, 8 * t : 8 * t + 8, span]
 
 
-def first_gradient_kernel(place_ref, tall_ref, ra_ref, rb_ref, ls_ref, sp_ref, sm_ref, mid_ref, edges):
-    layers, rows, lanes = sp_ref.shape
+def first_gradient_kernel(place_ref, tall_ref, ra_ref, rb_ref, ls_ref, step_ref, edges):
+    layers = step_ref.shape[0] // 3
+    sp_ref, sm_ref, mid_ref = (step_ref.at[pl.ds(k * layers, layers)] for k in range(3))
+    _, rows, lanes = step_ref.shape
     depth, own, _ = tall_ref.shape
     ones = jnp.ones((8, lanes), jnp.float32)
 
@@ -470,11 +472,12 @@
 
 
 def extend_kernel(
-    place_ref, tile_ref, ra_ref, rb_ref, pa_ref, pb_ref, pc_ref, po_ref, ls_ref, sp_ref, sm_ref, mid_ref,
+    place_ref, tile_ref, ra_ref, rb_ref, pa_ref, pb_ref, pc_ref, po_ref, ls_ref, step_ref,
     speed_ref, speed3_ref, phi_ref, ma_ref, mb_ref, one, two, keep, pull,
 ):
     depth, rows, lanes = tile_ref.shape
     layers = depth - 2 * HALO
+    sp_ref, sm_ref, mid_ref = (step_ref.at[pl.ds(k * layers, layers)] for k in range(3))
     tall = ls_ref.shape[1]
     margin = 8
     base = margin + YE
@@ -528,11 +531,12 @@
 
     lax.fori_loop(0, depth, normalise, 0)
     lax.fori_loop(1, depth - 1, weigh, 0)
+    rows_of = [-(-(YE + rows + YE - k) // 8) * 8 for k in range(EXT_PASSES)]
     for step in range(EXT_PASSES):
         source, target = (one, two) if step % 2 == 0 else (two, one)
 
         def extend(z, carry):
-            count = tall // 8
+            count = rows_of[step] // 8
             tiles = [source[z, 8 * t : 8 * t + 8, :] for t in range(count + 2)]
             row = lax.broadcasted_iota(jnp.int32, tiles[0].shape, 0)
             lane = lax.broadcasted_iota(jnp.int32, tiles[0].shape, 1)
@@ -672,7 +676,7 @@
         upper(mb_ref)
 
 
-def level_part(place, tile, ma, mb, wide_peak, level_set, ls, sp, sm, mid):
+def level_part(place, tile, ma, mb, wide_peak, level_set, ls, step):
     layers, rows, lanes = level_set.shape
     nfirst, nsecond = swaps("narrow")
     wfirst, wsecond = swaps("wide")
@@ -691,7 +695,7 @@
     speed, speed3, phi, sa, sb = vmem_call(
         extend_kernel,
         [(layers, rows, lanes), (layers, rows2, lanes), (layers, rows1, lanes), (3, rows2, lanes), (3, rows2, lanes)],
-        (place, tile, ra, rb, pa, pb, pc, wide_peak, ls, sp, sm, mid),
+        (place, tile, ra, rb, pa, pb, pc, wide_peak, ls, step),
         [(depth, tall + 16, lanes)] * 2 + [(depth, tall, lanes)] * 2,
         8000,
         16,
@@ -724,7 +728,7 @@
     rows1 = -(-(rows + 2 * Y1) // 8) * 8
     total = -(-(rows + 2 * YE) // 8) * 8
     return vmem_call(
-        first_gradient_kernel, [(depth, total, lanes)] + [(depth - 6, rows1, lanes)] * 3, (place, tall, ra, rb),
+        first_gradient_kernel, [(depth, total, lanes), (3 * (depth - 6), rows1, lanes)], (place, tall, ra, rb),
         [(6, rows1, lanes)], 35000
     )
 
@@ -824,10 +828,10 @@
     message = strain_message(place, tail, beyond, inner, material, wide)
     message, tall = lax.optimization_barrier((message, tall))
     recv = lax.all_to_all(message.reshape(wide, 88, 128), "wide", split_axis=0, concat_axis=0, tiled=True)
-    ls, sp, sm, mid = first_gradient(place, tall, ya, yb)
-    recv, sp = lax.optimization_barrier((recv, sp))
+    ls, step = first_gradient(place, tall, ya, yb)
+    recv, step = lax.optimization_barrier((recv, step))
     tile, wide_peak, ma, mb = unpack(place, recv, own_z, rows)
-    return level_part(place, tile, ma, mb, wide_peak, level_set, ls, sp, sm, mid)
+    return level_part(place, tile, ma, mb, wide_peak, level_set, ls, step)
 
 
 def solution(mesh):

time: 172 us -> 171 us (level)
  local copies, waits for them, and re-layouts: 18.8 us -> 16.9 us
    unnamed x36 -> x28, local copies, waits for them, and re-layouts: 14.6 us -> 12.7 us
where the time goes in v8:
time: 171 us; the launch traced here: 170 us
  Pallas kernels  80.8 us (47%)
  starting transfers between devices  48 us (28%)
  waiting for transfers between devices  18.6 us (11%)
  local copies, waits for them, and re-layouts  16.9 us (10%)
  other arithmetic  4.74 us (3%)
    pallas_call x8, Pallas kernels, vmem_call(): pl.pallas_call(kernel, out_shape=tuple((jax.ShapeDtypeStruct(shape, jnp.f...  50.9 us
    pallas_call x1, Pallas kernels, inner_strain(): pl.pallas_call(inner_kernel, grid=(loads,), out_shape=(jax.ShapeDtypeStru...  22.2 us
    all_to_all x1, starting transfers between devices, per_device(): lax.all_to_all(message.reshape(wide, 88, 128), 'wide', split_axis=0, conc...  15.8 us
    unnamed x28, local copies, waits for them, and re-layouts  12.7 us
    ppermute x2, starting transfers between devices, level_part(): gb = lax.ppermute(sb, 'wide', wsecond)  12.4 us
    pallas_call x1, Pallas kernels, strain_message(): pl.pallas_call(outer_kernel, grid=(loads,), out_shape=jax.ShapeDtypeStruc...  7.69 us
    ppermute x1, waiting for transfers between devices, level_part(): pc = lax.ppermute(wide_peak, 'narrow', across)  6.08 us
    ppermute x1, starting transfers between devices, per_device(): lb = lax.ppermute(jnp.where(even, bounds[0], bounds[1]), 'wide', wsecond)  5.06 us
  transfers between devices with their start and end apart: 16, of which 5 were waited for; matrix products, arithmetic and copies ran while one was open for 3% of the time, Pallas kernels for 31%

profile of v8, /device:TPU:2, one launch (start us, length us, event | category | flops | bytes accessed | tf_op | source)
XLA Modules:
  0.0 170.0 jit_solution(9600950295667962364)
XLA Ops:
  0.6 3.1 %fusion = (f32[3,3,16,1,384]{4,3,2,1,0:T(1,128)S(1)}, f32[3,3,16,1,384]{4,3,2,1,0:T(1,128)S(1)}, f32[3,3,16,1,384]{4,3,2,1,0:T(1,128)S(1)}) fusion(f32[3,3,16,32,384]{4,3,2,1,0:T(8,128)} %u_ref.1), kind=kLoop, calls=%fused_computation.10 | loop fusion | bytes 1327104 | tf_op jit(solution)/shard_map/slice | solution.py:807
  3.8 0.1 copy_bitcast_fusion
  3.8 0.1 pad_maximum_fusion.1
  3.9 1.3 collective-permute-start.1
  5.2 0.7 slice_select_fusion
  5.9 5.1 %collective-permute-start.3 = (f32[3,32,512]{2,1,0:T(8,128)}, f32[3,32,512]{2,1,0:T(8,128)S(1)}, u32[]{:S(2)}, u32[]{:S(2)}) collective-permute-start(f32[3,32,512]{2,1,0:T(8,128)} %get-tuple-element.83), channel_id=1, source_target_pairs={{4,8},{8,4},{12,16},{16,12},{20,24},{24,20},{28,32},{32,28},{36,40... | collective-permute-start | bytes 589832 | tf_op jit(solution)/shard_map/ppermute | solution.py:815
  11.0 1.4 collective-permute-start.2
  12.4 0.7 copy.21
  13.1 3.1 %collective-permute-start = (f32[3,3,16,384]{3,2,1,0:T(8,128)}, f32[3,3,16,384]{3,2,1,0:T(8,128)}, u32[]{:S(2)}, u32[]{:S(2)}) collective-permute-start(f32[3,3,16,384]{3,2,1,0:T(8,128)} %bitcast.20), channel_id=1, source_target_pairs={{0,1},{1,2},{2,3},{4,5},{5,6},{6,7},{8,9},{9,10},{10,11},{12,13},{... | collective-permute-start | bytes 663560 | tf_op jit(solution)/shard_map/ppermute | solution.py:807
  16.2 0.7 add_bitcast_fusion
  16.9 0.7 copy.13
  17.7 0.1 pad.3.clone
  17.7 0.0 collective-permute-done
  17.7 0.0 collective-permute-done.1
  17.7 1.1 pad_maximum_fusion.yh_ref
  18.9 0.0 collective-permute-done.3.rb_ref
  18.9 3.5 %collective-permute-done.2.ra_ref = f32[3,32,512]{2,1,0:T(8,128)S(1)} collective-permute-done((f32[3,32,512]{2,1,0:T(8,128)S(1)}, f32[3,32,512]{2,1,0:T(8,128)S(1)}, u32[]{:S(2)}, u32[]{:S(2)}) %collective-permute-start.2) | collective-permute-done | bytes 196640 | tf_op jit(solution)/shard_map/ppermute | solution.py:814
  22.4 0.1 reshape.24
  22.5 2.2 %maximum_maximum_fusion = f32[984,384]{1,0:T(8,128)} fusion(f32[81,384]{1,0:T(8,128)S(1)} %reshape.24, f32[32,384]{1,0:T(8,128)} %copy.13, f32[864,384]{1,0:T(8,128)S(1)} %bitcast.21, f32[984]{0:T(1024)S(1)} %pad.3.clone), kind=kLoop, calls=%fused_computation | loop fusion | flops 1133568 | bytes 3016032 | tf_op jit(solution)/shard_map/concatenate | solution.py:821
  24.7 3.2 %collective-permute-start.4 = (f32[984,384]{1,0:T(8,128)}, f32[984,384]{1,0:T(8,128)S(1)}, u32[]{:S(2)}, u32[]{:S(2)}) collective-permute-start(f32[984,384]{1,0:T(8,128)} %maximum_maximum_fusion), channel_id=1, source_target_pairs={{0,124},{4,0},{8,4},{12,8},{16,12},{20,16},{24,20},{28,24},{32,28}... | collective-permute-start | bytes 4534280 | tf_op jit(solution)/shard_map/ppermute | solution.py:821
  27.8 0.1 stack.46.place_ref
  27.9 22.2 %shard_map.50 = (f32[13,32,384]{2,1,0:T(8,128)S(1)}, f32[3,3,3,3,32,384]{5,4,3,2,1,0:T(8,128)S(1)}) custom-call(f32[3,3,16,32,384]{4,3,2,1,0:T(8,128)} %u_ref.1, f32[3,3,3,16,384]{4,3,2,1,0:T(8,128)S(1)} %pad_maximum_fusion.yh_ref), custom_call_target="tpu_custom_call" | custom-call | flops 163840000 | bytes 1048576 | tf_op jit(solution)/shard_map/pallas_call | solution.py:215
  50.2 1.9 %copy-done = f32[3,3,3,3,32,384]{5,4,3,2,1,0:T(8,128)} copy-done((f32[3,3,3,3,32,384]{5,4,3,2,1,0:T(8,128)}, f32[3,3,3,3,32,384]{5,4,3,2,1,0:T(8,128)S(1)}, u32[]{:S(2)}) %copy-start) | copy-done | bytes 3981336
  52.1 1.6 shard_map.51
  53.7 1.0 copy-done.4
  54.7 0.0 collective-permute-start.5
  54.7 0.7 collective-permute-start.6
  55.4 1.1 copy.14.solid_ref
  56.5 0.1 collective-permute-done.5.ra_ref
  56.6 0.0 collective-permute-done.6.rb_ref
  56.6 4.2 %collective-permute-done.4.next_ref = f32[984,384]{1,0:T(8,128)S(1)} collective-permute-done((f32[984,384]{1,0:T(8,128)}, f32[984,384]{1,0:T(8,128)S(1)}, u32[]{:S(2)}, u32[]{:S(2)}) %collective-permute-start.4) | collective-permute-done | bytes 1511456 | tf_op jit(solution)/shard_map/ppermute | solution.py:821
  60.7 1.1 copy-done.8
  61.8 7.7 %shard_map.52 = f32[2816,128]{1,0:T(8,128)} custom-call(s32[6]{0:T(128)S(1)} %stack.46.place_ref, f32[3,3,3,3,32,384]{5,4,3,2,1,0:T(8,128)} %copy-done, f32[984,384]{1,0:T(8,128)S(1)} %collective-permute-done.4.next_ref, f32[13,32,384]{2,1,0:T(8,128)S(1)} %copy-done.8, s32[16,32,24]{2,1,0:T(8,128)S(1)} %copy.14.solid_ref), custom_call_target="tpu_custom_call" | custom-call | flops 40960000 | bytes 1048576 | tf_op jit(solution)/shard_map/pallas_call | solution.py:236
  69.5 15.8 %all-to-all-start = ((f32[32,88,128]{2,1,0:T(8,128)}), f32[32,88,128]{2,1,0:T(8,128)S(1)}, u32[]{:S(2)}, u32[]{:S(2)}) async-start(f32[32,88,128]{2,1,0:T(8,128)} %bitcast.13), calls=%async_computation | async-start | bytes 2883584 | tf_op jit(solution)/shard_map/all_to_all | solution.py:830
  85.4 1.3 copy-done.5
  86.6 1.0 copy-done.10
  87.6 1.0 copy-done.12
  88.6 13.4 %shard_map.53 = (f32[18,56,512]{2,1,0:T(8,128)S(1)}, f32[36,48,512]{2,1,0:T(8,128)S(1)}) custom-call(s32[6]{0:T(128)S(1)} %stack.46.place_ref, f32[18,32,512]{2,1,0:T(8,128)S(1)} %copy-done.5, f32[21,8,512]{2,1,0:T(8,128)S(1)} %copy-done.10, f32[21,8,512]{2,1,0:T(8,128)S(1)} %copy-done.12), custom_call_target="tpu_custom_call" | custom-call | flops 143360000 | bytes 1048576 | tf_op jit(solution)/shard_map/pallas_call | solution.py:448
  102.0 1.7 %copy-done.1 = f32[36,48,512]{2,1,0:T(8,128)} copy-done((f32[36,48,512]{2,1,0:T(8,128)}, f32[36,48,512]{2,1,0:T(8,128)S(1)}, u32[]{:S(2)}) %copy-start.1) | copy-done | bytes 3538968
  103.8 4.7 %all-to-all-done.recv_ref = f32[32,88,128]{2,1,0:T(8,128)S(1)} async-done(((f32[32,88,128]{2,1,0:T(8,128)}), f32[32,88,128]{2,1,0:T(8,128)S(1)}, u32[]{:S(2)}, u32[]{:S(2)}) %all-to-all-start) | async-done | bytes 1441824 | tf_op jit(solution)/shard_map/all_to_all | solution.py:830
  108.4 1.4 shard_map.54
  109.8 0.1 collective-permute-start.7
  109.9 0.7 collective-permute-start.8
  110.6 3.4 %collective-permute-start.10 = (f32[8,128]{1,0:T(8,128)S(1)}, f32[8,128]{1,0:T(8,128)S(1)}, u32[]{:S(2)}, u32[]{:S(2)}) collective-permute-start(f32[8,128]{1,0:T(8,128)S(1)} %get-tuple-element.63.po_ref), channel_id=1, source_target_pairs={{0,2},{1,3},{2,0},{3,1},{4,6},{5,7},{6,4},{7,5},{8,10},{9,11},{10,... | collective-permute-start | bytes 12296 | tf_op jit(solution)/shard_map/ppermute | solution.py:688
  114.0 0.0 collective-permute-start.9
  114.0 0.0 collective-permute-done.7.ra_ref
  114.1 6.1 %collective-permute-done.10.pc_ref = f32[8,128]{1,0:T(8,128)S(1)} collective-permute-done((f32[8,128]{1,0:T(8,128)S(1)}, f32[8,128]{1,0:T(8,128)S(1)}, u32[]{:S(2)}, u32[]{:S(2)}) %collective-permute-start.10) | collective-permute-done | bytes 4128 | tf_op jit(solution)/shard_map/ppermute | solution.py:688
  120.1 0.0 collective-permute-done.9.pb_ref
  120.1 0.0 collective-permute-done.8.rb_ref
  120.1 2.0 %copy-done.2 = f32[36,48,512]{2,1,0:T(8,128)S(1)} copy-done((f32[36,48,512]{2,1,0:T(8,128)S(1)}, f32[36,48,512]{2,1,0:T(8,128)}, u32[]{:S(2)}) %copy-start.2) | copy-done | bytes 3538968
  122.1 11.8 %shard_map.55 = (f32[12,32,512]{2,1,0:T(8,128)}, f32[12,40,512]{2,1,0:T(8,128)S(1)}, f32[12,48,512]{2,1,0:T(8,128)S(1)}, f32[3,40,512]{2,1,0:T(8,128)S(1)}, f32[3,40,512]{2,1,0:T(8,128)S(1)}) custom-call(s32[6]{0:T(128)S(1)} %stack.46.place_ref, f32[20,32,512]{2,1,0:T(8,128)S(1)} %get-tuple-element.60.tile_ref, ...), custom_call_target="tpu_custom_call" | custom-call | flops 32768000 | bytes 1048576 | tf_op jit(solution)/shard_map/pallas_call | solution.py:448
  133.9 0.8 collective-permute-start.11
  134.7 6.3 %collective-permute-start.12 = (f32[3,40,512]{2,1,0:T(8,128)S(1)}, f32[3,40,512]{2,1,0:T(8,128)S(1)}, u32[]{:S(2)}, u32[]{:S(2)}) collective-permute-start(f32[3,40,512]{2,1,0:T(8,128)S(1)} %get-tuple-element.69), channel_id=1, source_target_pairs={{4,8},{8,4},{12,16},{16,12},{20,24},{24,20},{28,32},{32,28},{36,40... | collective-permute-start | bytes 737288 | tf_op jit(solution)/shard_map/ppermute | solution.py:704
  141.0 8.3 %shard_map.56 = (f32[12,40,512]{2,1,0:T(8,128)S(1)}, f32[12,40,512]{2,1,0:T(8,128)S(1)}, f32[12,40,512]{2,1,0:T(8,128)S(1)}) custom-call(f32[12,48,512]{2,1,0:T(8,128)S(1)} %get-tuple-element.66.phi_ref), custom_call_target="tpu_custom_call" | custom-call | flops 49152000 | bytes 1048576 | tf_op jit(solution)/shard_map/pallas_call | solution.py:448
  149.3 0.0 collective-permute-done.11.ra_ref
  149.4 0.0 collective-permute-done.12.rb_ref
  149.4 3.2 %shard_map.57 = (f32[12,40,512]{2,1,0:T(8,128)S(1)}, f32[3,32,512]{2,1,0:T(8,128)S(1)}, f32[3,32,512]{2,1,0:T(8,128)S(1)}) custom-call(s32[6]{0:T(128)S(1)} %stack.46.place_ref, f32[12,40,512]{2,1,0:T(8,128)S(1)} %get-tuple-element.67.phi_ref, f32[3,40,512]{2,1,0:T(8,128)S(1)} %collective-permute-done.11.ra_ref, ...), custom_call_target="tpu_custom_call" | custom-call | flops 20480000 | bytes 1048576 | tf_op jit(solution)/shard_map/pallas_call | solution.py:448
  152.6 0.0 copy-start.6
  152.6 0.2 collective-permute-start.13
  152.8 6.1 %collective-permute-start.14 = (f32[3,32,512]{2,1,0:T(8,128)S(1)}, f32[3,32,512]{2,1,0:T(8,128)S(1)}, u32[]{:S(2)}, u32[]{:S(2)}) collective-permute-start(f32[3,32,512]{2,1,0:T(8,128)S(1)} %get-tuple-element.76), channel_id=1, source_target_pairs={{4,8},{8,4},{12,16},{16,12},{20,24},{24,20},{28,32},{32,28},{36,40... | collective-permute-start | bytes 589832 | tf_op jit(solution)/shard_map/ppermute | solution.py:714
  158.9 7.6 %shard_map.58 = (f32[12,32,512]{2,1,0:T(8,128)S(1)}, f32[12,32,512]{2,1,0:T(8,128)S(1)}, f32[12,32,512]{2,1,0:T(8,128)S(1)}) custom-call(f32[12,40,512]{2,1,0:T(8,128)S(1)} %get-tuple-element.73.phi_ref), custom_call_target="tpu_custom_call" | custom-call | flops 49152000 | bytes 1048576 | tf_op jit(solution)/shard_map/pallas_call | solution.py:448
  166.4 0.0 collective-permute-done.13.ra_ref
  166.5 0.0 collective-permute-done.14.rb_ref
  166.5 3.5 %shard_map.59 = f32[12,32,512]{2,1,0:T(8,128)} custom-call(s32[6]{0:T(128)S(1)} %stack.46.place_ref, f32[12,32,512]{2,1,0:T(8,128)S(1)} %get-tuple-element.74.phi_ref, f32[3,32,512]{2,1,0:T(8,128)S(1)} %collective-permute-done.13.ra_ref, f32[3,32,512]{2,1,0:T(8,128)S(1)} %collective-permute-done.14.rb_ref, f32[12,32,512]{2,1,0:T(8,128)S(1)} %get-tuple-element.77.gp_ref, ...), custom_call_target="tpu_custom_call" | custom-call | flops 20480000 | bytes 1048576 | tf_op jit(solution)/shard_map/pallas_call | solution.py:448
  (23 shorter events, 0.1 us)
Async XLA Ops:
  0.6 4.6 %copy-start.3 = (f32[12,32,512]{2,1,0:T(8,128)S(1)}, f32[12,32,512]{2,1,0:T(8,128)}, u32[]{:S(2)}) copy-start(f32[12,32,512]{2,1,0:T(8,128)} %ls_ref.1) | copy-start | bytes 2359300
  3.9 13.9 %collective-permute-start.1 = (f32[3,3,2,16,384]{4,3,2,1,0:T(8,128)S(1)}, f32[3,3,2,16,384]{4,3,2,1,0:T(8,128)}, u32[]{:S(2)}, u32[]{:S(2)}) collective-permute-start(f32[3,3,2,16,384]{4,3,2,1,0:T(8,128)S(1)} %pad_maximum_fusion.1), channel_id=1, source_target_pairs={{1,0},{2,1},{3,2},{5,4},{6,5},{7,6},{9,8},{10,9},{11,10},{13,12},{... | collective-permute-start | bytes 1327112 | tf_op jit(solution)/shard_map/ppermute | solution.py:808
  5.9 13.0 %collective-permute-start.3 = (f32[3,32,512]{2,1,0:T(8,128)}, f32[3,32,512]{2,1,0:T(8,128)S(1)}, u32[]{:S(2)}, u32[]{:S(2)}) collective-permute-start(f32[3,32,512]{2,1,0:T(8,128)} %get-tuple-element.83), channel_id=1, source_target_pairs={{4,8},{8,4},{12,16},{16,12},{20,24},{24,20},{28,32},{32,28},{36,40... | collective-permute-start | bytes 589832 | tf_op jit(solution)/shard_map/ppermute | solution.py:815
  11.0 11.4 %collective-permute-start.2 = (f32[3,32,512]{2,1,0:T(8,128)S(1)}, f32[3,32,512]{2,1,0:T(8,128)S(1)}, u32[]{:S(2)}, u32[]{:S(2)}) collective-permute-start(f32[3,32,512]{2,1,0:T(8,128)S(1)} %get-tuple-element.84), channel_id=1, source_target_pairs={{0,4},{4,0},{8,12},{12,8},{16,20},{20,16},{24,28},{28,24},{32,36},... | collective-permute-start | bytes 589832 | tf_op jit(solution)/shard_map/ppermute | solution.py:814
  13.1 4.7 %collective-permute-start = (f32[3,3,16,384]{3,2,1,0:T(8,128)}, f32[3,3,16,384]{3,2,1,0:T(8,128)}, u32[]{:S(2)}, u32[]{:S(2)}) collective-permute-start(f32[3,3,16,384]{3,2,1,0:T(8,128)} %bitcast.20), channel_id=1, source_target_pairs={{0,1},{1,2},{2,3},{4,5},{5,6},{6,7},{8,9},{9,10},{10,11},{12,13},{... | collective-permute-start | bytes 663560 | tf_op jit(solution)/shard_map/ppermute | solution.py:807
  16.9 5.6 %slice-start = ((f32[3,3,16,32,384]{4,3,2,1,0:T(8,128)}), f32[3,3,3,32,384]{4,3,2,1,0:T(8,128)S(1)}, s32[]{:S(2)}) async-start(f32[3,3,16,32,384]{4,3,2,1,0:T(8,128)} %u_ref.1), calls=%async_computation.1 | async-start | bytes 2654208 | tf_op jit(solution)/shard_map/slice | solution.py:818
  24.7 36.1 %collective-permute-start.4 = (f32[984,384]{1,0:T(8,128)}, f32[984,384]{1,0:T(8,128)S(1)}, u32[]{:S(2)}, u32[]{:S(2)}) collective-permute-start(f32[984,384]{1,0:T(8,128)} %maximum_maximum_fusion), channel_id=1, source_target_pairs={{0,124},{4,0},{8,4},{12,8},{16,12},{20,16},{24,20},{28,24},{32,28}... | collective-permute-start | bytes 4534280 | tf_op jit(solution)/shard_map/ppermute | solution.py:821
  50.2 1.9 %copy-start = (f32[3,3,3,3,32,384]{5,4,3,2,1,0:T(8,128)}, f32[3,3,3,3,32,384]{5,4,3,2,1,0:T(8,128)S(1)}, u32[]{:S(2)}) copy-start(f32[3,3,3,3,32,384]{5,4,3,2,1,0:T(8,128)S(1)} %get-tuple-element.42.tail_ref) | copy-start | bytes 11943940
  52.1 2.7 %copy-start.7 = (f32[13,32,384]{2,1,0:T(8,128)}, f32[13,32,384]{2,1,0:T(8,128)S(1)}, u32[]{:S(2)}) copy-start(f32[13,32,384]{2,1,0:T(8,128)S(1)} %get-tuple-element.52.inner_ref) | copy-start | bytes 1916932
  53.7 1.0 copy-start.4
  54.7 1.9 %collective-permute-start.5 = (f32[21,8,512]{2,1,0:T(8,128)}, f32[21,8,512]{2,1,0:T(8,128)S(1)}, u32[]{:S(2)}, u32[]{:S(2)}) collective-permute-start(f32[21,8,512]{2,1,0:T(8,128)} %get-tuple-element.49), channel_id=1, source_target_pairs={{0,1},{1,0},{2,3},{3,2},{4,5},{5,4},{6,7},{7,6},{8,9},{9,8},{10,11... | collective-permute-start | bytes 1032200 | tf_op jit(solution)/shard_map/ppermute | solution.py:825
  54.7 1.9 %collective-permute-start.6 = (f32[21,8,512]{2,1,0:T(8,128)}, f32[21,8,512]{2,1,0:T(8,128)S(1)}, u32[]{:S(2)}, u32[]{:S(2)}) collective-permute-start(f32[21,8,512]{2,1,0:T(8,128)} %get-tuple-element.50), channel_id=1, source_target_pairs={{1,2},{2,1},{5,6},{6,5},{9,10},{10,9},{13,14},{14,13},{17,18},{18,... | collective-permute-start | bytes 1032200 | tf_op jit(solution)/shard_map/ppermute | solution.py:826
  56.6 13.0 %copy-start.9 = (f32[21,8,512]{2,1,0:T(8,128)}, f32[21,8,512]{2,1,0:T(8,128)S(1)}, u32[]{:S(2)}) copy-start(f32[21,8,512]{2,1,0:T(8,128)S(1)} %collective-permute-done.5.ra_ref) | copy-start | bytes 1032196
  56.6 12.9 %copy-start.11 = (f32[21,8,512]{2,1,0:T(8,128)}, f32[21,8,512]{2,1,0:T(8,128)S(1)}, u32[]{:S(2)}) copy-start(f32[21,8,512]{2,1,0:T(8,128)S(1)} %collective-permute-done.6.rb_ref) | copy-start | bytes 1032196
  60.7 1.1 copy-start.8
  69.5 38.9 %all-to-all-start = ((f32[32,88,128]{2,1,0:T(8,128)}), f32[32,88,128]{2,1,0:T(8,128)S(1)}, u32[]{:S(2)}, u32[]{:S(2)}) async-start(f32[32,88,128]{2,1,0:T(8,128)} %bitcast.13), calls=%async_computation | async-start | bytes 2883584 | tf_op jit(solution)/shard_map/all_to_all | solution.py:830
  85.4 1.3 copy-start.5
  86.6 1.0 copy-start.10
  87.6 1.0 copy-start.12
  102.0 1.7 %copy-start.1 = (f32[36,48,512]{2,1,0:T(8,128)}, f32[36,48,512]{2,1,0:T(8,128)S(1)}, u32[]{:S(2)}) copy-start(f32[36,48,512]{2,1,0:T(8,128)S(1)} %get-tuple-element.65.step_ref) | copy-start | bytes 10616836
  109.8 4.2 %collective-permute-start.7 = (f32[26,8,512]{2,1,0:T(8,128)S(1)}, f32[26,8,512]{2,1,0:T(8,128)S(1)}, u32[]{:S(2)}, u32[]{:S(2)}) collective-permute-start(f32[26,8,512]{2,1,0:T(8,128)S(1)} %get-tuple-element.61), channel_id=1, source_target_pairs={{0,1},{1,0},{2,3},{3,2},{4,5},{5,4},{6,7},{7,6},{8,9},{9,8},{10,11... | collective-permute-start | bytes 1277960 | tf_op jit(solution)/shard_map/ppermute | solution.py:686
  109.9 10.2 %collective-permute-start.8 = (f32[26,8,512]{2,1,0:T(8,128)S(1)}, f32[26,8,512]{2,1,0:T(8,128)S(1)}, u32[]{:S(2)}, u32[]{:S(2)}) collective-permute-start(f32[26,8,512]{2,1,0:T(8,128)S(1)} %get-tuple-element.62), channel_id=1, source_target_pairs={{1,2},{2,1},{5,6},{6,5},{9,10},{10,9},{13,14},{14,13},{17,18},{18,... | collective-permute-start | bytes 1277960 | tf_op jit(solution)/shard_map/ppermute | solution.py:687
  110.6 9.5 %collective-permute-start.10 = (f32[8,128]{1,0:T(8,128)S(1)}, f32[8,128]{1,0:T(8,128)S(1)}, u32[]{:S(2)}, u32[]{:S(2)}) collective-permute-start(f32[8,128]{1,0:T(8,128)S(1)} %get-tuple-element.63.po_ref), channel_id=1, source_target_pairs={{0,2},{1,3},{2,0},{3,1},{4,6},{5,7},{6,4},{7,5},{8,10},{9,11},{10,... | collective-permute-start | bytes 12296 | tf_op jit(solution)/shard_map/ppermute | solution.py:688
  114.0 6.1 %collective-permute-start.9 = (f32[8,128]{1,0:T(8,128)S(1)}, f32[8,128]{1,0:T(8,128)S(1)}, u32[]{:S(2)}, u32[]{:S(2)}) collective-permute-start(f32[8,128]{1,0:T(8,128)S(1)} %get-tuple-element.63.po_ref), channel_id=1, source_target_pairs={{0,3},{1,2},{2,1},{3,0},{4,7},{5,6},{6,5},{7,4},{8,11},{9,10},{10,... | collective-permute-start | bytes 12296 | tf_op jit(solution)/shard_map/ppermute | solution.py:689
  120.1 2.0 %copy-start.2 = (f32[36,48,512]{2,1,0:T(8,128)S(1)}, f32[36,48,512]{2,1,0:T(8,128)}, u32[]{:S(2)}) copy-start(f32[36,48,512]{2,1,0:T(8,128)} %copy-done.1) | copy-start | bytes 10616836
  133.9 15.4 %collective-permute-start.11 = (f32[3,40,512]{2,1,0:T(8,128)S(1)}, f32[3,40,512]{2,1,0:T(8,128)S(1)}, u32[]{:S(2)}, u32[]{:S(2)}) collective-permute-start(f32[3,40,512]{2,1,0:T(8,128)S(1)} %get-tuple-element.68), channel_id=1, source_target_pairs={{0,4},{4,0},{8,12},{12,8},{16,20},{20,16},{24,28},{28,24},{32,36},... | collective-permute-start | bytes 737288 | tf_op jit(solution)/shard_map/ppermute | solution.py:703
  134.7 14.6 %collective-permute-start.12 = (f32[3,40,512]{2,1,0:T(8,128)S(1)}, f32[3,40,512]{2,1,0:T(8,128)S(1)}, u32[]{:S(2)}, u32[]{:S(2)}) collective-permute-start(f32[3,40,512]{2,1,0:T(8,128)S(1)} %get-tuple-element.69), channel_id=1, source_target_pairs={{4,8},{8,4},{12,16},{16,12},{20,24},{24,20},{28,32},{32,28},{36,40... | collective-permute-start | bytes 737288 | tf_op jit(solution)/shard_map/ppermute | solution.py:704
  152.6 13.9 %copy-start.6 = (f32[12,32,512]{2,1,0:T(8,128)S(1)}, f32[12,32,512]{2,1,0:T(8,128)}, u32[]{:S(2)}) copy-start(f32[12,32,512]{2,1,0:T(8,128)} %get-tuple-element.40.speed_ref) | copy-start | bytes 2359300
  152.6 13.9 %collective-permute-start.13 = (f32[3,32,512]{2,1,0:T(8,128)S(1)}, f32[3,32,512]{2,1,0:T(8,128)S(1)}, u32[]{:S(2)}, u32[]{:S(2)}) collective-permute-start(f32[3,32,512]{2,1,0:T(8,128)S(1)} %get-tuple-element.75), channel_id=1, source_target_pairs={{0,4},{4,0},{8,12},{12,8},{16,20},{20,16},{24,28},{28,24},{32,36},... | collective-permute-start | bytes 589832 | tf_op jit(solution)/shard_map/ppermute | solution.py:713
  152.8 13.7 %collective-permute-start.14 = (f32[3,32,512]{2,1,0:T(8,128)S(1)}, f32[3,32,512]{2,1,0:T(8,128)S(1)}, u32[]{:S(2)}, u32[]{:S(2)}) collective-permute-start(f32[3,32,512]{2,1,0:T(8,128)S(1)} %get-tuple-element.76), channel_id=1, source_target_pairs={{4,8},{8,4},{12,16},{16,12},{20,24},{24,20},{28,32},{32,28},{36,40... | collective-permute-start | bytes 589832 | tf_op jit(solution)/shard_map/ppermute | solution.py:714

commit v9 on v8

--- a/solution.py
+++ b/solution.py
@@ -128,11 +128,17 @@
                 tail_ref[0, comp, which, k] = filt[comp, which, own_x - 3 + k]
 
 
-def outer_kernel(place_ref, tail_ref, next_ref, inner_ref, solid_ref, msg_ref, filt, energy, turned):
+def outer_kernel(place_ref, tail_ref, part_ref, rest_ref, inner_ref, solid_ref, msg_ref, filt, energy, turned, next_ref):
     load = pl.program_id(0)
     own_x, rows, blocks = solid_ref.shape
-    size_z = next_ref.shape[1]
+    size_z = rest_ref.shape[1]
     loads = 3
+
+    @pl.when(load == 0)
+    def _():
+        next_ref[0 : part_ref.shape[0], :] = part_ref[...]
+        next_ref[part_ref.shape[0] :, :] = rest_ref[...]
+
     inner = own_x - 3
     tiles = rows // 8
     keep = jnp.where(place_ref[2] == 1, 0.0, 1.0)
@@ -229,7 +235,7 @@
     )(disp, yh)
 
 
-def strain_message(place, tail, beyond, inner, solid, parts):
+def strain_message(place, tail, part, beyond, inner, solid, parts):
     loads, comps = tail.shape[:2]
     own_x, rows, blocks = solid.shape
     size_z = beyond.shape[1]
@@ -240,6 +246,7 @@
         in_specs=[
             pl.BlockSpec(memory_space=pltpu.SMEM),
             load_block(comps, 3, 3, rows, size_z),
+            fixed_block(*part.shape),
             fixed_block(*beyond.shape),
             fixed_block(own_x - 3, rows, size_z),
             fixed_block(own_x, rows, blocks),
@@ -249,10 +256,11 @@
             pltpu.VMEM((3, 3, 3, rows, size_z), jnp.float32),
             pltpu.VMEM((3, rows, size_z), jnp.float32),
             pltpu.VMEM((own_x // 4, size_z + 16, 128), jnp.float32),
+            pltpu.VMEM((part.shape[0] + beyond.shape[0], size_z), jnp.float32),
         ],
         compiler_params=pltpu.CompilerParams(vmem_limit_bytes=48 << 20),
         cost_estimate=pl.CostEstimate(flops=10000 * 4096, bytes_accessed=1 << 20, transcendentals=0),
-    )(place, tail, beyond, inner, solid)
+    )(place, tail, part, beyond, inner, solid)
 
 
 def ring(axis, step):
@@ -440,17 +448,17 @@
     )
 
 
-def vmem_call(kernel, outs, args, scratch=(), cycles=0, limit=8):
+def vmem_call(kernel, outs, args, scratch=(), cycles=0, limit=8, fetched=()):
     specs = []
-    for arg in args:
-        space = pltpu.SMEM if arg.dtype == jnp.int32 else pltpu.VMEM
+    for k, arg in enumerate(args):
+        space = pltpu.SMEM if arg.dtype == jnp.int32 else pltpu.HBM if k in fetched else pltpu.VMEM
         specs.append(pl.BlockSpec(memory_space=space))
     return pl.pallas_call(
         kernel,
         out_shape=tuple(jax.ShapeDtypeStruct(shape, jnp.float32) for shape in outs),
         in_specs=specs,
         out_specs=tuple(pl.BlockSpec(memory_space=pltpu.VMEM) for _ in outs),
-        scratch_shapes=[pltpu.VMEM(shape, jnp.float32) for shape in scratch],
+        scratch_shapes=[pltpu.VMEM(shape, jnp.float32) for shape in scratch] + [pltpu.SemaphoreType.DMA] * len(fetched),
         compiler_params=pltpu.CompilerParams(vmem_limit_bytes=limit << 20),
         cost_estimate=pl.CostEstimate(flops=cycles * 4096, bytes_accessed=1 << 20, transcendentals=0),
     )(*args)
@@ -473,11 +481,13 @@
 
 def extend_kernel(
     place_ref, tile_ref, ra_ref, rb_ref, pa_ref, pb_ref, pc_ref, po_ref, ls_ref, step_ref,
-    speed_ref, speed3_ref, phi_ref, ma_ref, mb_ref, one, two, keep, pull,
+    speed_ref, speed3_ref, phi_ref, ma_ref, mb_ref, one, two, keep, pull, step_buf, sem,
 ):
     depth, rows, lanes = tile_ref.shape
     layers = depth - 2 * HALO
-    sp_ref, sm_ref, mid_ref = (step_ref.at[pl.ds(k * layers, layers)] for k in range(3))
+    fetch = pltpu.make_async_copy(step_ref, step_buf, sem)
+    fetch.start()
+    sp_ref, sm_ref, mid_ref = (step_buf.at[pl.ds(k * layers, layers)] for k in range(3))
     tall = ls_ref.shape[1]
     margin = 8
     base = margin + YE
@@ -557,6 +567,7 @@
         lax.fori_loop(step + 1, depth - 1 - step, extend, 0)
 
     final = one if EXT_PASSES % 2 == 0 else two
+    fetch.wait()
 
     def march(z, carry):
         count = tall // 8
@@ -696,9 +707,10 @@
         extend_kernel,
         [(layers, rows, lanes), (layers, rows2, lanes), (layers, rows1, lanes), (3, rows2, lanes), (3, rows2, lanes)],
         (place, tile, ra, rb, pa, pb, pc, wide_peak, ls, step),
-        [(depth, tall + 16, lanes)] * 2 + [(depth, tall, lanes)] * 2,
+        [(depth, tall + 16, lanes)] * 2 + [(depth, tall, lanes)] * 2 + [step.shape],
         8000,
-        16,
+        20,
+        (9,),
     )
     ga = lax.ppermute(sa, "wide", wfirst)
     gb = lax.ppermute(sb, "wide", wsecond)
@@ -804,6 +816,7 @@
     wfirst, wsecond = swaps("wide")
     nfirst, nsecond = swaps("narrow")
 
+    part = lax.ppermute(displacement[0, :, :3].reshape(-1, size_z), "wide", backward)
     low = lax.ppermute(displacement[:, :, :, -1], "narrow", ring("narrow", 1))
     high = lax.ppermute(
         jnp.stack([displacement[:, :, :, 0], displacement[:, :, :, 1]], axis=2), "narrow", ring("narrow", -1)
@@ -815,7 +828,7 @@
     lb = lax.ppermute(jnp.where(even, bounds[0], bounds[1]), "wide", wsecond)
 
     stiff = 0.2 + 0.8 * jnp.repeat(material[0].astype(jnp.float32), BZ, axis=1)
-    layers, yh, la, lb = lax.optimization_barrier((displacement[:, :, :3], yh, la, lb))
+    layers, yh, la, lb, part = lax.optimization_barrier((displacement[1:, :, :3], yh, la, lb, part))
     flat = [layers.reshape(-1, size_z), stiff, yh[:, :, :, :3].reshape(-1, size_z)]
     flat.append(jnp.zeros((-sum(f.shape[0] for f in flat) % 8, size_z), jnp.float32))
     beyond = lax.ppermute(jnp.concatenate(flat, axis=0), "wide", backward)
@@ -825,7 +838,7 @@
     ya = lax.ppermute(ya, "narrow", nfirst)
     yb = lax.ppermute(yb, "narrow", nsecond)
     beyond, ya, yb = lax.optimization_barrier((beyond, ya, yb))
-    message = strain_message(place, tail, beyond, inner, material, wide)
+    message = strain_message(place, tail, part, beyond, inner, material, wide)
     message, tall = lax.optimization_barrier((message, tall))
     recv = lax.all_to_all(message.reshape(wide, 88, 128), "wide", split_axis=0, concat_axis=0, tiled=True)
     ls, step = first_gradient(place, tall, ya, yb)

time: 171 us -> 172 us (level)
  waiting for transfers between devices: 18.6 us -> 9.86 us
  starting transfers between devices: 48 us -> 53.5 us
  local copies, waits for them, and re-layouts: 16.9 us -> 20.1 us
    all_to_all x1, starting transfers between devices: 15.8 us -> 7.2 us  [per_device(): lax.all_to_all(message.reshape(wide, 88, 128), 'wide', split_axis=0, conc...]
    ppermute x1, starting transfers between devices: 0.09 us -> 8.63 us  [level_part(): ra = lax.ppermute(ma, 'narrow', nfirst)]
    ppermute x2, starting transfers between devices: 12.4 us -> 4.13 us  [level_part(): gb = lax.ppermute(sb, 'wide', wsecond)]
    ppermute x2, starting transfers between devices: 0.98 us -> 6.66 us  [level_part(): ga = lax.ppermute(sa, 'wide', wfirst)]
    all_to_all x1, waiting for transfers between devices: 4.67 us -> 0.01 us  [per_device(): lax.all_to_all(message.reshape(wide, 88, 128), 'wide', split_axis=0, conc...]
    ppermute x1, waiting for transfers between devices: 4.16 us -> 0.01 us  [per_device(): beyond = lax.ppermute(jnp.concatenate(flat, axis=0), 'wide', backward)]
    ppermute x1, starting transfers between devices: 0.01 us -> 3.51 us  [per_device(): ya = lax.ppermute(ya, 'narrow', nfirst)]
    ppermute x0 -> x1, starting transfers between devices: none -> 3.17 us  [per_device(): lax.ppermute(displacement[0, :, :3].reshape(-1, size_z), 'wide', backward)]
  transfers between devices with their start and end apart: 16 -> 17, of which waited for: 5 -> 5; matrix products, arithmetic and copies ran while one was open for 3% -> 5% of each run, Pallas kernels for 31% -> 31%
where the time goes in v9:
time: 172 us; the launch traced here: 169 us
  Pallas kernels  81.3 us (47%)
  starting transfers between devices  53.5 us (31%)
  local copies, waits for them, and re-layouts  20.1 us (12%)
  waiting for transfers between devices  9.86 us (6%)
  other arithmetic  3.88 us (2%)
    pallas_call x8, Pallas kernels, vmem_call(): pl.pallas_call(kernel, out_shape=tuple((jax.ShapeDtypeStruct(shape, jnp.f...  51.2 us
    pallas_call x1, Pallas kernels, inner_strain(): pl.pallas_call(inner_kernel, grid=(loads,), out_shape=(jax.ShapeDtypeStru...  22.2 us
    unnamed x28, local copies, waits for them, and re-layouts  13.6 us
    ppermute x1, starting transfers between devices, level_part(): ra = lax.ppermute(ma, 'narrow', nfirst)  8.63 us
    pallas_call x1, Pallas kernels, strain_message(): pl.pallas_call(outer_kernel, grid=(loads,), out_shape=jax.ShapeDtypeStruc...  7.81 us
    all_to_all x1, starting transfers between devices, per_device(): lax.all_to_all(message.reshape(wide, 88, 128), 'wide', split_axis=0, conc...  7.2 us
    ppermute x2, starting transfers between devices, level_part(): ga = lax.ppermute(sa, 'wide', wfirst)  6.66 us
    ppermute x1, waiting for transfers between devices, level_part(): pc = lax.ppermute(wide_peak, 'narrow', across)  4.67 us
  transfers between devices with their start and end apart: 17, of which 5 were waited for; matrix products, arithmetic and copies ran while one was open for 5% of the time, Pallas kernels for 31%

profile of v9, /device:TPU:2, one launch (start us, length us, event | category | flops | bytes accessed | tf_op | source)
XLA Modules:
  0.0 169.5 jit_solution(5647822450842091702)
XLA Ops:
  0.6 1.8 %slice.36 = f32[1,3,3,32,384]{4,3,2,1,0:T(8,128)} slice(f32[3,3,16,32,384]{4,3,2,1,0:T(8,128)} %u_ref.1), slice={[0:1], [0:3], [0:3], [0:32], [0:384]} | slice | bytes 884736 | tf_op jit(solution)/shard_map/slice | solution.py:819
  2.4 3.2 %collective-permute-start.4 = (f32[288,384]{1,0:T(8,128)}, f32[288,384]{1,0:T(8,128)S(1)}, u32[]{:S(2)}, u32[]{:S(2)}) collective-permute-start(f32[288,384]{1,0:T(8,128)} %bitcast.10), channel_id=1, source_target_pairs={{0,124},{4,0},{8,4},{12,8},{16,12},{20,16},{24,20},{28,24},{32,28}... | collective-permute-start | bytes 1327112 | tf_op jit(solution)/shard_map/ppermute | solution.py:819
  5.6 3.1 %fusion = (f32[3,3,16,1,384]{4,3,2,1,0:T(1,128)S(1)}, f32[3,3,16,1,384]{4,3,2,1,0:T(1,128)S(1)}, f32[3,3,16,1,384]{4,3,2,1,0:T(1,128)S(1)}) fusion(f32[3,3,16,32,384]{4,3,2,1,0:T(8,128)} %u_ref.1), kind=kLoop, calls=%fused_computation.10 | loop fusion | bytes 1327104 | tf_op jit(solution)/shard_map/slice | solution.py:820
  8.7 0.0 copy-start.3
  8.7 0.1 copy_bitcast_fusion
  8.7 0.1 pad_maximum_fusion.1
  8.8 1.4 collective-permute-start.1
  10.2 0.8 slice_select_fusion
  11.1 2.1 %collective-permute-start.3 = (f32[3,32,512]{2,1,0:T(8,128)}, f32[3,32,512]{2,1,0:T(8,128)S(1)}, u32[]{:S(2)}, u32[]{:S(2)}) collective-permute-start(f32[3,32,512]{2,1,0:T(8,128)} %get-tuple-element.85), channel_id=1, source_target_pairs={{4,8},{8,4},{12,16},{16,12},{20,24},{24,20},{28,32},{32,28},{36,40... | collective-permute-start | bytes 589832 | tf_op jit(solution)/shard_map/ppermute | solution.py:828
  13.2 4.3 %collective-permute-start.2 = (f32[3,32,512]{2,1,0:T(8,128)}, f32[3,32,512]{2,1,0:T(8,128)S(1)}, u32[]{:S(2)}, u32[]{:S(2)}) collective-permute-start(f32[3,32,512]{2,1,0:T(8,128)} %get-tuple-element.86), channel_id=1, source_target_pairs={{0,4},{4,0},{8,12},{12,8},{16,20},{20,16},{24,28},{28,24},{32,36},... | collective-permute-start | bytes 589832 | tf_op jit(solution)/shard_map/ppermute | solution.py:827
  17.5 0.7 copy.21
  18.2 3.2 %collective-permute-start = (f32[3,3,16,384]{3,2,1,0:T(8,128)}, f32[3,3,16,384]{3,2,1,0:T(8,128)}, u32[]{:S(2)}, u32[]{:S(2)}) collective-permute-start(f32[3,3,16,384]{3,2,1,0:T(8,128)} %bitcast.21), channel_id=1, source_target_pairs={{0,1},{1,2},{2,3},{4,5},{5,6},{6,7},{8,9},{9,10},{10,11},{12,13},{... | collective-permute-start | bytes 663560 | tf_op jit(solution)/shard_map/ppermute | solution.py:820
  21.3 0.7 add_bitcast_fusion
  22.1 1.2 slice.30
  23.3 0.1 copy.13
  23.4 0.1 pad.3.clone
  23.5 1.1 pad_maximum_fusion.yh_ref
  24.6 2.9 %collective-permute-done.2.ra_ref = f32[3,32,512]{2,1,0:T(8,128)S(1)} collective-permute-done((f32[3,32,512]{2,1,0:T(8,128)}, f32[3,32,512]{2,1,0:T(8,128)S(1)}, u32[]{:S(2)}, u32[]{:S(2)}) %collective-permute-start.2) | collective-permute-done | bytes 196640 | tf_op jit(solution)/shard_map/ppermute | solution.py:827
  27.6 0.1 reshape.24
  27.6 0.7 copy-done.7
  28.3 1.2 maximum_maximum_fusion
  29.5 3.1 %collective-permute-start.5 = (f32[696,384]{1,0:T(8,128)}, f32[696,384]{1,0:T(8,128)S(1)}, u32[]{:S(2)}, u32[]{:S(2)}) collective-permute-start(f32[696,384]{1,0:T(8,128)} %maximum_maximum_fusion), channel_id=1, source_target_pairs={{0,124},{4,0},{8,4},{12,8},{16,12},{20,16},{24,20},{28,24},{32,28}... | collective-permute-start | bytes 3207176 | tf_op jit(solution)/shard_map/ppermute | solution.py:834
  32.6 0.1 stack.46.place_ref
  32.7 22.2 %shard_map.50 = (f32[13,32,384]{2,1,0:T(8,128)S(1)}, f32[3,3,3,3,32,384]{5,4,3,2,1,0:T(8,128)S(1)}) custom-call(f32[3,3,16,32,384]{4,3,2,1,0:T(8,128)} %u_ref.1, f32[3,3,3,16,384]{4,3,2,1,0:T(8,128)S(1)} %pad_maximum_fusion.yh_ref), custom_call_target="tpu_custom_call" | custom-call | flops 163840000 | bytes 1048576 | tf_op jit(solution)/shard_map/pallas_call | solution.py:221
  54.9 1.9 %copy-done = f32[3,3,3,3,32,384]{5,4,3,2,1,0:T(8,128)} copy-done((f32[3,3,3,3,32,384]{5,4,3,2,1,0:T(8,128)}, f32[3,3,3,3,32,384]{5,4,3,2,1,0:T(8,128)S(1)}, u32[]{:S(2)}) %copy-start) | copy-done | bytes 3981336
  56.8 1.6 shard_map.51
  58.4 1.1 copy-done.4
  59.5 3.5 %collective-permute-start.6 = (f32[21,8,512]{2,1,0:T(8,128)}, f32[21,8,512]{2,1,0:T(8,128)S(1)}, u32[]{:S(2)}, u32[]{:S(2)}) collective-permute-start(f32[21,8,512]{2,1,0:T(8,128)} %get-tuple-element.51), channel_id=1, source_target_pairs={{0,1},{1,0},{2,3},{3,2},{4,5},{5,4},{6,7},{7,6},{8,9},{9,8},{10,11... | collective-permute-start | bytes 1032200 | tf_op jit(solution)/shard_map/ppermute | solution.py:838
  63.0 0.7 collective-permute-start.7
  63.7 1.1 copy.14.solid_ref
  64.8 0.0 collective-permute-done.6.ra_ref
  64.8 0.0 copy-start.9
  64.8 0.0 copy-start.8
  64.8 1.2 copy-done.8
  66.1 7.8 %shard_map.52 = f32[2816,128]{1,0:T(8,128)} custom-call(s32[6]{0:T(128)S(1)} %stack.46.place_ref, f32[3,3,3,3,32,384]{5,4,3,2,1,0:T(8,128)} %copy-done, f32[288,384]{1,0:T(8,128)S(1)} %copy-done.8, f32[696,384]{1,0:T(8,128)S(1)} %collective-permute-done.5.rest_ref, f32[13,32,384]{2,1,0:T(8,128)S(1)} %get-tuple-element.54.inner_ref, ...), custom_call_target="tpu_custom_call" | custom-call | flops 40960000 | bytes 1048576 | tf_op jit(solution)/shard_map/pallas_call | solution.py:242
  73.9 7.2 %all-to-all-start = ((f32[32,88,128]{2,1,0:T(8,128)}), f32[32,88,128]{2,1,0:T(8,128)S(1)}, u32[]{:S(2)}, u32[]{:S(2)}) async-start(f32[32,88,128]{2,1,0:T(8,128)} %bitcast.14), calls=%async_computation | async-start | bytes 2883584 | tf_op jit(solution)/shard_map/all_to_all | solution.py:843
  81.1 1.3 copy-done.5
  82.3 1.0 copy-done.10
  83.3 1.0 copy-done.12
  84.3 13.4 %shard_map.53 = (f32[18,56,512]{2,1,0:T(8,128)S(1)}, f32[36,48,512]{2,1,0:T(8,128)S(1)}) custom-call(s32[6]{0:T(128)S(1)} %stack.46.place_ref, f32[18,32,512]{2,1,0:T(8,128)S(1)} %copy-done.5, f32[21,8,512]{2,1,0:T(8,128)S(1)} %copy-done.10, f32[21,8,512]{2,1,0:T(8,128)S(1)} %copy-done.12), custom_call_target="tpu_custom_call" | custom-call | flops 143360000 | bytes 1048576 | tf_op jit(solution)/shard_map/pallas_call | solution.py:456
  97.8 1.7 %copy-done.1 = f32[36,48,512]{2,1,0:T(8,128)} copy-done((f32[36,48,512]{2,1,0:T(8,128)}, f32[36,48,512]{2,1,0:T(8,128)S(1)}, u32[]{:S(2)}) %copy-start.1) | copy-done | bytes 3538968
  99.5 0.0 all-to-all-done.recv_ref
  99.5 1.4 shard_map.54
  100.9 8.6 %collective-permute-start.8 = (f32[26,8,512]{2,1,0:T(8,128)S(1)}, f32[26,8,512]{2,1,0:T(8,128)S(1)}, u32[]{:S(2)}, u32[]{:S(2)}) collective-permute-start(f32[26,8,512]{2,1,0:T(8,128)S(1)} %get-tuple-element.63), channel_id=1, source_target_pairs={{0,1},{1,0},{2,3},{3,2},{4,5},{5,4},{6,7},{7,6},{8,9},{9,8},{10,11... | collective-permute-start | bytes 1277960 | tf_op jit(solution)/shard_map/ppermute | solution.py:697
  109.5 0.7 collective-permute-start.9
  110.2 3.2 %collective-permute-start.11 = (f32[8,128]{1,0:T(8,128)S(1)}, f32[8,128]{1,0:T(8,128)S(1)}, u32[]{:S(2)}, u32[]{:S(2)}) collective-permute-start(f32[8,128]{1,0:T(8,128)S(1)} %get-tuple-element.65.po_ref), channel_id=1, source_target_pairs={{0,2},{1,3},{2,0},{3,1},{4,6},{5,7},{6,4},{7,5},{8,10},{9,11},{10,... | collective-permute-start | bytes 12296 | tf_op jit(solution)/shard_map/ppermute | solution.py:699
  113.4 1.5 collective-permute-start.10
  114.9 4.7 %collective-permute-done.11.pc_ref = f32[8,128]{1,0:T(8,128)S(1)} collective-permute-done((f32[8,128]{1,0:T(8,128)S(1)}, f32[8,128]{1,0:T(8,128)S(1)}, u32[]{:S(2)}, u32[]{:S(2)}) %collective-permute-start.11) | collective-permute-done | bytes 4128 | tf_op jit(solution)/shard_map/ppermute | solution.py:699
  119.6 0.0 collective-permute-done.10.pb_ref
  119.6 0.0 collective-permute-done.9.rb_ref
  119.6 2.0 %copy-done.2 = f32[36,48,512]{2,1,0:T(8,128)S(1)} copy-done((f32[36,48,512]{2,1,0:T(8,128)S(1)}, f32[36,48,512]{2,1,0:T(8,128)}, u32[]{:S(2)}) %copy-start.2) | copy-done | bytes 3538968
  121.6 12.2 %shard_map.55 = (f32[12,32,512]{2,1,0:T(8,128)}, f32[12,40,512]{2,1,0:T(8,128)S(1)}, f32[12,48,512]{2,1,0:T(8,128)S(1)}, f32[3,40,512]{2,1,0:T(8,128)S(1)}, f32[3,40,512]{2,1,0:T(8,128)S(1)}) custom-call(s32[6]{0:T(128)S(1)} %stack.46.place_ref, f32[20,32,512]{2,1,0:T(8,128)S(1)} %get-tuple-element.62.tile_ref, ...), custom_call_target="tpu_custom_call" | custom-call | flops 32768000 | bytes 1048576 | tf_op jit(solution)/shard_map/pallas_call | solution.py:456
  133.7 3.7 %collective-permute-start.12 = (f32[3,40,512]{2,1,0:T(8,128)S(1)}, f32[3,40,512]{2,1,0:T(8,128)S(1)}, u32[]{:S(2)}, u32[]{:S(2)}) collective-permute-start(f32[3,40,512]{2,1,0:T(8,128)S(1)} %get-tuple-element.70), channel_id=1, source_target_pairs={{0,4},{4,0},{8,12},{12,8},{16,20},{20,16},{24,28},{28,24},{32,36},... | collective-permute-start | bytes 737288 | tf_op jit(solution)/shard_map/ppermute | solution.py:715
  137.4 2.1 %collective-permute-start.13 = (f32[3,40,512]{2,1,0:T(8,128)S(1)}, f32[3,40,512]{2,1,0:T(8,128)S(1)}, u32[]{:S(2)}, u32[]{:S(2)}) collective-permute-start(f32[3,40,512]{2,1,0:T(8,128)S(1)} %get-tuple-element.71), channel_id=1, source_target_pairs={{4,8},{8,4},{12,16},{16,12},{20,24},{24,20},{28,32},{32,28},{36,40... | collective-permute-start | bytes 737288 | tf_op jit(solution)/shard_map/ppermute | solution.py:716
  139.5 8.3 %shard_map.56 = (f32[12,40,512]{2,1,0:T(8,128)S(1)}, f32[12,40,512]{2,1,0:T(8,128)S(1)}, f32[12,40,512]{2,1,0:T(8,128)S(1)}) custom-call(f32[12,48,512]{2,1,0:T(8,128)S(1)} %get-tuple-element.68.phi_ref), custom_call_target="tpu_custom_call" | custom-call | flops 49152000 | bytes 1048576 | tf_op jit(solution)/shard_map/pallas_call | solution.py:456
  147.8 0.3 collective-permute-done.12.ra_ref
  148.2 1.2 collective-permute-done.13.rb_ref
  149.4 3.2 %shard_map.57 = (f32[12,40,512]{2,1,0:T(8,128)S(1)}, f32[3,32,512]{2,1,0:T(8,128)S(1)}, f32[3,32,512]{2,1,0:T(8,128)S(1)}) custom-call(s32[6]{0:T(128)S(1)} %stack.46.place_ref, f32[12,40,512]{2,1,0:T(8,128)S(1)} %get-tuple-element.69.phi_ref, f32[3,40,512]{2,1,0:T(8,128)S(1)} %collective-permute-done.12.ra_ref, ...), custom_call_target="tpu_custom_call" | custom-call | flops 20480000 | bytes 1048576 | tf_op jit(solution)/shard_map/pallas_call | solution.py:456
  152.6 0.0 copy-start.6
  152.6 3.0 %collective-permute-start.14 = (f32[3,32,512]{2,1,0:T(8,128)S(1)}, f32[3,32,512]{2,1,0:T(8,128)S(1)}, u32[]{:S(2)}, u32[]{:S(2)}) collective-permute-start(f32[3,32,512]{2,1,0:T(8,128)S(1)} %get-tuple-element.77), channel_id=1, source_target_pairs={{0,4},{4,0},{8,12},{12,8},{16,20},{20,16},{24,28},{28,24},{32,36},... | collective-permute-start | bytes 589832 | tf_op jit(solution)/shard_map/ppermute | solution.py:725
  155.6 2.0 %collective-permute-start.15 = (f32[3,32,512]{2,1,0:T(8,128)S(1)}, f32[3,32,512]{2,1,0:T(8,128)S(1)}, u32[]{:S(2)}, u32[]{:S(2)}) collective-permute-start(f32[3,32,512]{2,1,0:T(8,128)S(1)} %get-tuple-element.78), channel_id=1, source_target_pairs={{4,8},{8,4},{12,16},{16,12},{20,24},{24,20},{28,32},{32,28},{36,40... | collective-permute-start | bytes 589832 | tf_op jit(solution)/shard_map/ppermute | solution.py:726
  157.6 7.6 %shard_map.58 = (f32[12,32,512]{2,1,0:T(8,128)S(1)}, f32[12,32,512]{2,1,0:T(8,128)S(1)}, f32[12,32,512]{2,1,0:T(8,128)S(1)}) custom-call(f32[12,40,512]{2,1,0:T(8,128)S(1)} %get-tuple-element.75.phi_ref), custom_call_target="tpu_custom_call" | custom-call | flops 49152000 | bytes 1048576 | tf_op jit(solution)/shard_map/pallas_call | solution.py:456
  165.2 0.7 collective-permute-done.15.rb_ref
  166.0 3.5 %shard_map.59 = f32[12,32,512]{2,1,0:T(8,128)} custom-call(s32[6]{0:T(128)S(1)} %stack.46.place_ref, f32[12,32,512]{2,1,0:T(8,128)S(1)} %get-tuple-element.76.phi_ref, f32[3,32,512]{2,1,0:T(8,128)S(1)} %collective-permute-done.14.ra_ref, f32[3,32,512]{2,1,0:T(8,128)S(1)} %collective-permute-done.15.rb_ref, f32[12,32,512]{2,1,0:T(8,128)S(1)} %get-tuple-element.79.gp_ref, ...), custom_call_target="tpu_custom_call" | custom-call | flops 20480000 | bytes 1048576 | tf_op jit(solution)/shard_map/pallas_call | solution.py:456
  (25 shorter events, 0.1 us)
Async XLA Ops:
  2.4 25.1 %collective-permute-start.4 = (f32[288,384]{1,0:T(8,128)}, f32[288,384]{1,0:T(8,128)S(1)}, u32[]{:S(2)}, u32[]{:S(2)}) collective-permute-start(f32[288,384]{1,0:T(8,128)} %bitcast.10), channel_id=1, source_target_pairs={{0,124},{4,0},{8,4},{12,8},{16,12},{20,16},{24,20},{28,24},{32,28}... | collective-permute-start | bytes 1327112 | tf_op jit(solution)/shard_map/ppermute | solution.py:819
  8.7 1.6 copy-start.3
  8.8 14.7 %collective-permute-start.1 = (f32[3,3,2,16,384]{4,3,2,1,0:T(8,128)S(1)}, f32[3,3,2,16,384]{4,3,2,1,0:T(8,128)}, u32[]{:S(2)}, u32[]{:S(2)}) collective-permute-start(f32[3,3,2,16,384]{4,3,2,1,0:T(8,128)S(1)} %pad_maximum_fusion.1), channel_id=1, source_target_pairs={{1,0},{2,1},{3,2},{5,4},{6,5},{7,6},{9,8},{10,9},{11,10},{13,12},{... | collective-permute-start | bytes 1327112 | tf_op jit(solution)/shard_map/ppermute | solution.py:821
  11.1 13.6 %collective-permute-start.3 = (f32[3,32,512]{2,1,0:T(8,128)}, f32[3,32,512]{2,1,0:T(8,128)S(1)}, u32[]{:S(2)}, u32[]{:S(2)}) collective-permute-start(f32[3,32,512]{2,1,0:T(8,128)} %get-tuple-element.85), channel_id=1, source_target_pairs={{4,8},{8,4},{12,16},{16,12},{20,24},{24,20},{28,32},{32,28},{36,40... | collective-permute-start | bytes 589832 | tf_op jit(solution)/shard_map/ppermute | solution.py:828
  13.2 14.3 %collective-permute-start.2 = (f32[3,32,512]{2,1,0:T(8,128)}, f32[3,32,512]{2,1,0:T(8,128)S(1)}, u32[]{:S(2)}, u32[]{:S(2)}) collective-permute-start(f32[3,32,512]{2,1,0:T(8,128)} %get-tuple-element.86), channel_id=1, source_target_pairs={{0,4},{4,0},{8,12},{12,8},{16,20},{20,16},{24,28},{28,24},{32,36},... | collective-permute-start | bytes 589832 | tf_op jit(solution)/shard_map/ppermute | solution.py:827
  18.2 5.3 %collective-permute-start = (f32[3,3,16,384]{3,2,1,0:T(8,128)}, f32[3,3,16,384]{3,2,1,0:T(8,128)}, u32[]{:S(2)}, u32[]{:S(2)}) collective-permute-start(f32[3,3,16,384]{3,2,1,0:T(8,128)} %bitcast.21), channel_id=1, source_target_pairs={{0,1},{1,2},{2,3},{4,5},{5,6},{6,7},{8,9},{9,10},{10,11},{12,13},{... | collective-permute-start | bytes 663560 | tf_op jit(solution)/shard_map/ppermute | solution.py:820
  27.5 0.8 copy-start.7
  29.5 35.3 %collective-permute-start.5 = (f32[696,384]{1,0:T(8,128)}, f32[696,384]{1,0:T(8,128)S(1)}, u32[]{:S(2)}, u32[]{:S(2)}) collective-permute-start(f32[696,384]{1,0:T(8,128)} %maximum_maximum_fusion), channel_id=1, source_target_pairs={{0,124},{4,0},{8,4},{12,8},{16,12},{20,16},{24,20},{28,24},{32,28}... | collective-permute-start | bytes 3207176 | tf_op jit(solution)/shard_map/ppermute | solution.py:834
  54.9 1.9 %copy-start = (f32[3,3,3,3,32,384]{5,4,3,2,1,0:T(8,128)}, f32[3,3,3,3,32,384]{5,4,3,2,1,0:T(8,128)S(1)}, u32[]{:S(2)}) copy-start(f32[3,3,3,3,32,384]{5,4,3,2,1,0:T(8,128)S(1)} %get-tuple-element.43.tail_ref) | copy-start | bytes 11943940
  58.4 1.1 copy-start.4
  59.5 5.3 %collective-permute-start.6 = (f32[21,8,512]{2,1,0:T(8,128)}, f32[21,8,512]{2,1,0:T(8,128)S(1)}, u32[]{:S(2)}, u32[]{:S(2)}) collective-permute-start(f32[21,8,512]{2,1,0:T(8,128)} %get-tuple-element.51), channel_id=1, source_target_pairs={{0,1},{1,0},{2,3},{3,2},{4,5},{5,4},{6,7},{7,6},{8,9},{9,8},{10,11... | collective-permute-start | bytes 1032200 | tf_op jit(solution)/shard_map/ppermute | solution.py:838
  63.0 1.8 %collective-permute-start.7 = (f32[21,8,512]{2,1,0:T(8,128)}, f32[21,8,512]{2,1,0:T(8,128)S(1)}, u32[]{:S(2)}, u32[]{:S(2)}) collective-permute-start(f32[21,8,512]{2,1,0:T(8,128)} %get-tuple-element.52), channel_id=1, source_target_pairs={{1,2},{2,1},{5,6},{6,5},{9,10},{10,9},{13,14},{14,13},{17,18},{18,... | collective-permute-start | bytes 1032200 | tf_op jit(solution)/shard_map/ppermute | solution.py:839
  64.8 9.1 %copy-start.9 = (f32[21,8,512]{2,1,0:T(8,128)}, f32[21,8,512]{2,1,0:T(8,128)S(1)}, u32[]{:S(2)}) copy-start(f32[21,8,512]{2,1,0:T(8,128)S(1)} %collective-permute-done.6.ra_ref) | copy-start | bytes 1032196
  64.8 9.1 %copy-start.11 = (f32[21,8,512]{2,1,0:T(8,128)}, f32[21,8,512]{2,1,0:T(8,128)S(1)}, u32[]{:S(2)}) copy-start(f32[21,8,512]{2,1,0:T(8,128)S(1)} %collective-permute-done.7.rb_ref) | copy-start | bytes 1032196
  64.8 1.2 copy-start.8
  73.9 25.6 %all-to-all-start = ((f32[32,88,128]{2,1,0:T(8,128)}), f32[32,88,128]{2,1,0:T(8,128)S(1)}, u32[]{:S(2)}, u32[]{:S(2)}) async-start(f32[32,88,128]{2,1,0:T(8,128)} %bitcast.14), calls=%async_computation | async-start | bytes 2883584 | tf_op jit(solution)/shard_map/all_to_all | solution.py:843
  81.1 1.3 copy-start.5
  82.3 1.0 copy-start.10
  83.3 1.0 copy-start.12
  97.8 1.7 %copy-start.1 = (f32[36,48,512]{2,1,0:T(8,128)}, f32[36,48,512]{2,1,0:T(8,128)S(1)}, u32[]{:S(2)}) copy-start(f32[36,48,512]{2,1,0:T(8,128)S(1)} %get-tuple-element.67.step_ref) | copy-start | bytes 10616836
  100.9 14.0 %collective-permute-start.8 = (f32[26,8,512]{2,1,0:T(8,128)S(1)}, f32[26,8,512]{2,1,0:T(8,128)S(1)}, u32[]{:S(2)}, u32[]{:S(2)}) collective-permute-start(f32[26,8,512]{2,1,0:T(8,128)S(1)} %get-tuple-element.63), channel_id=1, source_target_pairs={{0,1},{1,0},{2,3},{3,2},{4,5},{5,4},{6,7},{7,6},{8,9},{9,8},{10,11... | collective-permute-start | bytes 1277960 | tf_op jit(solution)/shard_map/ppermute | solution.py:697
  109.5 10.0 %collective-permute-start.9 = (f32[26,8,512]{2,1,0:T(8,128)S(1)}, f32[26,8,512]{2,1,0:T(8,128)S(1)}, u32[]{:S(2)}, u32[]{:S(2)}) collective-permute-start(f32[26,8,512]{2,1,0:T(8,128)S(1)} %get-tuple-element.64), channel_id=1, source_target_pairs={{1,2},{2,1},{5,6},{6,5},{9,10},{10,9},{13,14},{14,13},{17,18},{18,... | collective-permute-start | bytes 1277960 | tf_op jit(solution)/shard_map/ppermute | solution.py:698
  110.2 9.4 %collective-permute-start.11 = (f32[8,128]{1,0:T(8,128)S(1)}, f32[8,128]{1,0:T(8,128)S(1)}, u32[]{:S(2)}, u32[]{:S(2)}) collective-permute-start(f32[8,128]{1,0:T(8,128)S(1)} %get-tuple-element.65.po_ref), channel_id=1, source_target_pairs={{0,2},{1,3},{2,0},{3,1},{4,6},{5,7},{6,4},{7,5},{8,10},{9,11},{10,... | collective-permute-start | bytes 12296 | tf_op jit(solution)/shard_map/ppermute | solution.py:699
  113.4 6.1 %collective-permute-start.10 = (f32[8,128]{1,0:T(8,128)S(1)}, f32[8,128]{1,0:T(8,128)S(1)}, u32[]{:S(2)}, u32[]{:S(2)}) collective-permute-start(f32[8,128]{1,0:T(8,128)S(1)} %get-tuple-element.65.po_ref), channel_id=1, source_target_pairs={{0,3},{1,2},{2,1},{3,0},{4,7},{5,6},{6,5},{7,4},{8,11},{9,10},{10,... | collective-permute-start | bytes 12296 | tf_op jit(solution)/shard_map/ppermute | solution.py:700
  119.6 2.0 %copy-start.2 = (f32[36,48,512]{2,1,0:T(8,128)S(1)}, f32[36,48,512]{2,1,0:T(8,128)}, u32[]{:S(2)}) copy-start(f32[36,48,512]{2,1,0:T(8,128)} %copy-done.1) | copy-start | bytes 10616836
  133.7 14.4 %collective-permute-start.12 = (f32[3,40,512]{2,1,0:T(8,128)S(1)}, f32[3,40,512]{2,1,0:T(8,128)S(1)}, u32[]{:S(2)}, u32[]{:S(2)}) collective-permute-start(f32[3,40,512]{2,1,0:T(8,128)S(1)} %get-tuple-element.70), channel_id=1, source_target_pairs={{0,4},{4,0},{8,12},{12,8},{16,20},{20,16},{24,28},{28,24},{32,36},... | collective-permute-start | bytes 737288 | tf_op jit(solution)/shard_map/ppermute | solution.py:715
  137.4 12.0 %collective-permute-start.13 = (f32[3,40,512]{2,1,0:T(8,128)S(1)}, f32[3,40,512]{2,1,0:T(8,128)S(1)}, u32[]{:S(2)}, u32[]{:S(2)}) collective-permute-start(f32[3,40,512]{2,1,0:T(8,128)S(1)} %get-tuple-element.71), channel_id=1, source_target_pairs={{4,8},{8,4},{12,16},{16,12},{20,24},{24,20},{28,32},{32,28},{36,40... | collective-permute-start | bytes 737288 | tf_op jit(solution)/shard_map/ppermute | solution.py:716
  152.6 13.4 %copy-start.6 = (f32[12,32,512]{2,1,0:T(8,128)S(1)}, f32[12,32,512]{2,1,0:T(8,128)}, u32[]{:S(2)}) copy-start(f32[12,32,512]{2,1,0:T(8,128)} %get-tuple-element.41.speed_ref) | copy-start | bytes 2359300
  152.6 12.6 %collective-permute-start.14 = (f32[3,32,512]{2,1,0:T(8,128)S(1)}, f32[3,32,512]{2,1,0:T(8,128)S(1)}, u32[]{:S(2)}, u32[]{:S(2)}) collective-permute-start(f32[3,32,512]{2,1,0:T(8,128)S(1)} %get-tuple-element.77), channel_id=1, source_target_pairs={{0,4},{4,0},{8,12},{12,8},{16,20},{20,16},{24,28},{28,24},{32,36},... | collective-permute-start | bytes 589832 | tf_op jit(solution)/shard_map/ppermute | solution.py:725
  155.6 10.4 %collective-permute-start.15 = (f32[3,32,512]{2,1,0:T(8,128)S(1)}, f32[3,32,512]{2,1,0:T(8,128)S(1)}, u32[]{:S(2)}, u32[]{:S(2)}) collective-permute-start(f32[3,32,512]{2,1,0:T(8,128)S(1)} %get-tuple-element.78), channel_id=1, source_target_pairs={{4,8},{8,4},{12,16},{16,12},{20,24},{24,20},{28,32},{32,28},{36,40... | collective-permute-start | bytes 589832 | tf_op jit(solution)/shard_map/ppermute | solution.py:726

commit v10 on v8

--- a/solution.py
+++ b/solution.py
@@ -224,7 +224,7 @@
         scratch_shapes=[
             pltpu.VMEM((3, 3, own_x, rows, size_z), jnp.float32),
         ],
-        compiler_params=pltpu.CompilerParams(vmem_limit_bytes=48 << 20),
+        compiler_params=pltpu.CompilerParams(vmem_limit_bytes=54 << 20),
         cost_estimate=pl.CostEstimate(flops=40000 * 4096, bytes_accessed=1 << 20, transcendentals=0),
     )(disp, yh)
 

time: 171 us -> 169 us (0.988)
  local copies, waits for them, and re-layouts: 16.9 us -> 13.3 us
    unnamed x28, local copies, waits for them, and re-layouts: 12.7 us -> 9.09 us
  transfers between devices with their start and end apart: 16 -> 16, of which waited for: 5 -> 4; matrix products, arithmetic and copies ran while one was open for 3% -> 3% of each run, Pallas kernels for 31% -> 32%
where the time goes in v10:
time: 169 us; the launch traced here: 168 us
  Pallas kernels  82 us (49%)
  starting transfers between devices  47.8 us (28%)
  waiting for transfers between devices  20.2 us (12%)
  local copies, waits for them, and re-layouts  13.3 us (8%)
  other arithmetic  4.03 us (2%)
    pallas_call x8, Pallas kernels, vmem_call(): pl.pallas_call(kernel, out_shape=tuple((jax.ShapeDtypeStruct(shape, jnp.f...  50.8 us
    pallas_call x1, Pallas kernels, inner_strain(): pl.pallas_call(inner_kernel, grid=(loads,), out_shape=(jax.ShapeDtypeStru...  23.5 us
    all_to_all x1, starting transfers between devices, per_device(): lax.all_to_all(message.reshape(wide, 88, 128), 'wide', split_axis=0, conc...  15 us
    ppermute x2, starting transfers between devices, level_part(): gb = lax.ppermute(sb, 'wide', wsecond)  12.3 us
    unnamed x28, local copies, waits for them, and re-layouts  9.09 us
    pallas_call x1, Pallas kernels, strain_message(): pl.pallas_call(outer_kernel, grid=(loads,), out_shape=jax.ShapeDtypeStruc...  7.7 us
    ppermute x1, waiting for transfers between devices, level_part(): pc = lax.ppermute(wide_peak, 'narrow', across)  6.08 us
    ppermute x1, waiting for transfers between devices, per_device(): beyond = lax.ppermute(jnp.concatenate(flat, axis=0), 'wide', backward)  5.16 us
  transfers between devices with their start and end apart: 16, of which 4 were waited for; matrix products, arithmetic and copies ran while one was open for 3% of the time, Pallas kernels for 32%

profile of v10, /device:TPU:2, one launch (start us, length us, event | category | flops | bytes accessed | tf_op | source)
XLA Modules:
  0.0 168.3 jit_solution(15829603463640506525)
XLA Ops:
  0.6 3.1 %fusion = (f32[3,3,16,1,384]{4,3,2,1,0:T(1,128)S(1)}, f32[3,3,16,1,384]{4,3,2,1,0:T(1,128)S(1)}, f32[3,3,16,1,384]{4,3,2,1,0:T(1,128)S(1)}) fusion(f32[3,3,16,32,384]{4,3,2,1,0:T(8,128)} %u_ref.1), kind=kLoop, calls=%fused_computation.10 | loop fusion | bytes 1327104 | tf_op jit(solution)/shard_map/slice | solution.py:807
  3.8 0.1 copy_bitcast_fusion
  3.8 0.1 pad_maximum_fusion.1
  3.9 1.3 collective-permute-start.1
  5.2 0.0 copy-done.2
  5.2 0.8 slice_select_fusion
  6.0 5.1 %collective-permute-start.3 = (f32[3,32,512]{2,1,0:T(8,128)}, f32[3,32,512]{2,1,0:T(8,128)S(1)}, u32[]{:S(2)}, u32[]{:S(2)}) collective-permute-start(f32[3,32,512]{2,1,0:T(8,128)} %get-tuple-element.83), channel_id=1, source_target_pairs={{4,8},{8,4},{12,16},{16,12},{20,24},{24,20},{28,32},{32,28},{36,40... | collective-permute-start | bytes 589832 | tf_op jit(solution)/shard_map/ppermute | solution.py:815
  11.1 1.4 collective-permute-start.2
  12.5 3.2 %collective-permute-start = (f32[3,3,16,384]{3,2,1,0:T(8,128)S(1)}, f32[3,3,16,384]{3,2,1,0:T(8,128)}, u32[]{:S(2)}, u32[]{:S(2)}) collective-permute-start(f32[3,3,16,384]{3,2,1,0:T(8,128)S(1)} %bitcast.23), channel_id=1, source_target_pairs={{0,1},{1,2},{2,3},{4,5},{5,6},{6,7},{8,9},{9,10},{10,11},{12,13},{... | collective-permute-start | bytes 663560 | tf_op jit(solution)/shard_map/ppermute | solution.py:807
  15.6 0.7 add_bitcast_fusion
  16.3 0.7 copy.13
  17.1 0.1 pad.3.clone
  17.1 0.0 collective-permute-done
  17.2 0.0 collective-permute-done.1
  17.2 1.1 pad_maximum_fusion.yh_ref
  18.3 0.0 copy-start.11
  18.3 0.0 collective-permute-done.3.rb_ref
  18.3 4.2 %collective-permute-done.2.ra_ref = f32[3,32,512]{2,1,0:T(8,128)S(1)} collective-permute-done((f32[3,32,512]{2,1,0:T(8,128)}, f32[3,32,512]{2,1,0:T(8,128)S(1)}, u32[]{:S(2)}, u32[]{:S(2)}) %collective-permute-start.2) | collective-permute-done | bytes 196640 | tf_op jit(solution)/shard_map/ppermute | solution.py:814
  22.5 0.1 reshape.24
  22.6 1.4 maximum_maximum_fusion
  24.0 3.2 %collective-permute-start.4 = (f32[984,384]{1,0:T(8,128)}, f32[984,384]{1,0:T(8,128)S(1)}, u32[]{:S(2)}, u32[]{:S(2)}) collective-permute-start(f32[984,384]{1,0:T(8,128)} %maximum_maximum_fusion), channel_id=1, source_target_pairs={{0,124},{4,0},{8,4},{12,8},{16,12},{20,16},{24,20},{28,24},{32,28}... | collective-permute-start | bytes 4534280 | tf_op jit(solution)/shard_map/ppermute | solution.py:821
  27.1 0.1 stack.46.place_ref
  27.2 23.5 %shard_map.50 = (f32[13,32,384]{2,1,0:T(8,128)}, f32[3,3,3,3,32,384]{5,4,3,2,1,0:T(8,128)}) custom-call(f32[3,3,16,32,384]{4,3,2,1,0:T(8,128)} %u_ref.1, f32[3,3,3,16,384]{4,3,2,1,0:T(8,128)} %copy-done.11), custom_call_target="tpu_custom_call" | custom-call | flops 163840000 | bytes 1048576 | tf_op jit(solution)/shard_map/pallas_call | solution.py:215
  50.7 1.6 shard_map.51
  52.3 1.0 copy-done.3
  53.3 0.5 collective-permute-start.5
  53.8 0.7 collective-permute-start.6
  54.5 1.1 copy.14.solid_ref
  55.6 0.0 collective-permute-done.5.ra_ref
  55.6 0.0 copy-start.7
  55.6 0.0 collective-permute-done.6.rb_ref
  55.6 5.2 %collective-permute-done.4.next_ref = f32[984,384]{1,0:T(8,128)S(1)} collective-permute-done((f32[984,384]{1,0:T(8,128)}, f32[984,384]{1,0:T(8,128)S(1)}, u32[]{:S(2)}, u32[]{:S(2)}) %collective-permute-start.4) | collective-permute-done | bytes 1511456 | tf_op jit(solution)/shard_map/ppermute | solution.py:821
  60.8 7.7 %shard_map.52 = f32[2816,128]{1,0:T(8,128)} custom-call(s32[6]{0:T(128)S(1)} %stack.46.place_ref, f32[3,3,3,3,32,384]{5,4,3,2,1,0:T(8,128)} %get-tuple-element.42.tail_ref, f32[984,384]{1,0:T(8,128)S(1)} %collective-permute-done.4.next_ref, f32[13,32,384]{2,1,0:T(8,128)S(1)} %copy-done.6, s32[16,32,24]{2,1,0:T(8,128)S(1)} %copy.14.solid_ref), custom_call_target="tpu_custom_call" | custom-call | flops 40960000 | bytes 1048576 | tf_op jit(solution)/shard_map/pallas_call | solution.py:236
  68.5 15.0 %all-to-all-start = ((f32[32,88,128]{2,1,0:T(8,128)}), f32[32,88,128]{2,1,0:T(8,128)S(1)}, u32[]{:S(2)}, u32[]{:S(2)}) async-start(f32[32,88,128]{2,1,0:T(8,128)} %bitcast.13), calls=%async_computation | async-start | bytes 2883584 | tf_op jit(solution)/shard_map/all_to_all | solution.py:830
  83.5 1.3 copy-done.4
  84.8 1.0 copy-done.8
  85.7 1.0 copy-done.10
  86.7 13.4 %shard_map.53 = (f32[18,56,512]{2,1,0:T(8,128)S(1)}, f32[36,48,512]{2,1,0:T(8,128)S(1)}) custom-call(s32[6]{0:T(128)S(1)} %stack.46.place_ref, f32[18,32,512]{2,1,0:T(8,128)S(1)} %copy-done.4, f32[21,8,512]{2,1,0:T(8,128)S(1)} %copy-done.8, f32[21,8,512]{2,1,0:T(8,128)S(1)} %copy-done.10), custom_call_target="tpu_custom_call" | custom-call | flops 143360000 | bytes 1048576 | tf_op jit(solution)/shard_map/pallas_call | solution.py:448
  100.2 1.7 %copy-done = f32[36,48,512]{2,1,0:T(8,128)} copy-done((f32[36,48,512]{2,1,0:T(8,128)}, f32[36,48,512]{2,1,0:T(8,128)S(1)}, u32[]{:S(2)}) %copy-start) | copy-done | bytes 3538968
  101.9 4.8 %all-to-all-done.recv_ref = f32[32,88,128]{2,1,0:T(8,128)S(1)} async-done(((f32[32,88,128]{2,1,0:T(8,128)}), f32[32,88,128]{2,1,0:T(8,128)S(1)}, u32[]{:S(2)}, u32[]{:S(2)}) %all-to-all-start) | async-done | bytes 1441824 | tf_op jit(solution)/shard_map/all_to_all | solution.py:830
  106.7 1.4 shard_map.54
  108.1 0.1 collective-permute-start.7
  108.2 0.7 collective-permute-start.8
  108.9 3.4 %collective-permute-start.10 = (f32[8,128]{1,0:T(8,128)S(1)}, f32[8,128]{1,0:T(8,128)S(1)}, u32[]{:S(2)}, u32[]{:S(2)}) collective-permute-start(f32[8,128]{1,0:T(8,128)S(1)} %get-tuple-element.63.po_ref), channel_id=1, source_target_pairs={{0,2},{1,3},{2,0},{3,1},{4,6},{5,7},{6,4},{7,5},{8,10},{9,11},{10,... | collective-permute-start | bytes 12296 | tf_op jit(solution)/shard_map/ppermute | solution.py:688
  112.3 0.0 collective-permute-start.9
  112.3 0.0 collective-permute-done.7.ra_ref
  112.3 6.1 %collective-permute-done.10.pc_ref = f32[8,128]{1,0:T(8,128)S(1)} collective-permute-done((f32[8,128]{1,0:T(8,128)S(1)}, f32[8,128]{1,0:T(8,128)S(1)}, u32[]{:S(2)}, u32[]{:S(2)}) %collective-permute-start.10) | collective-permute-done | bytes 4128 | tf_op jit(solution)/shard_map/ppermute | solution.py:688
  118.4 0.0 collective-permute-done.9.pb_ref
  118.4 0.0 collective-permute-done.8.rb_ref
  118.4 2.0 %copy-done.1 = f32[36,48,512]{2,1,0:T(8,128)S(1)} copy-done((f32[36,48,512]{2,1,0:T(8,128)S(1)}, f32[36,48,512]{2,1,0:T(8,128)}, u32[]{:S(2)}) %copy-start.1) | copy-done | bytes 3538968
  120.4 11.8 %shard_map.55 = (f32[12,32,512]{2,1,0:T(8,128)}, f32[12,40,512]{2,1,0:T(8,128)S(1)}, f32[12,48,512]{2,1,0:T(8,128)S(1)}, f32[3,40,512]{2,1,0:T(8,128)S(1)}, f32[3,40,512]{2,1,0:T(8,128)S(1)}) custom-call(s32[6]{0:T(128)S(1)} %stack.46.place_ref, f32[20,32,512]{2,1,0:T(8,128)S(1)} %get-tuple-element.60.tile_ref, ...), custom_call_target="tpu_custom_call" | custom-call | flops 32768000 | bytes 1048576 | tf_op jit(solution)/shard_map/pallas_call | solution.py:448
  132.2 0.9 collective-permute-start.11
  133.1 6.2 %collective-permute-start.12 = (f32[3,40,512]{2,1,0:T(8,128)S(1)}, f32[3,40,512]{2,1,0:T(8,128)S(1)}, u32[]{:S(2)}, u32[]{:S(2)}) collective-permute-start(f32[3,40,512]{2,1,0:T(8,128)S(1)} %get-tuple-element.69), channel_id=1, source_target_pairs={{4,8},{8,4},{12,16},{16,12},{20,24},{24,20},{28,32},{32,28},{36,40... | collective-permute-start | bytes 737288 | tf_op jit(solution)/shard_map/ppermute | solution.py:704
  139.3 8.3 %shard_map.56 = (f32[12,40,512]{2,1,0:T(8,128)S(1)}, f32[12,40,512]{2,1,0:T(8,128)S(1)}, f32[12,40,512]{2,1,0:T(8,128)S(1)}) custom-call(f32[12,48,512]{2,1,0:T(8,128)S(1)} %get-tuple-element.66.phi_ref), custom_call_target="tpu_custom_call" | custom-call | flops 49152000 | bytes 1048576 | tf_op jit(solution)/shard_map/pallas_call | solution.py:448
  147.7 0.0 collective-permute-done.11.ra_ref
  147.7 0.0 collective-permute-done.12.rb_ref
  147.7 3.2 %shard_map.57 = (f32[12,40,512]{2,1,0:T(8,128)S(1)}, f32[3,32,512]{2,1,0:T(8,128)S(1)}, f32[3,32,512]{2,1,0:T(8,128)S(1)}) custom-call(s32[6]{0:T(128)S(1)} %stack.46.place_ref, f32[12,40,512]{2,1,0:T(8,128)S(1)} %get-tuple-element.67.phi_ref, f32[3,40,512]{2,1,0:T(8,128)S(1)} %collective-permute-done.11.ra_ref, ...), custom_call_target="tpu_custom_call" | custom-call | flops 20480000 | bytes 1048576 | tf_op jit(solution)/shard_map/pallas_call | solution.py:448
  150.9 0.0 copy-start.5
  150.9 0.2 collective-permute-start.13
  151.1 6.1 %collective-permute-start.14 = (f32[3,32,512]{2,1,0:T(8,128)S(1)}, f32[3,32,512]{2,1,0:T(8,128)S(1)}, u32[]{:S(2)}, u32[]{:S(2)}) collective-permute-start(f32[3,32,512]{2,1,0:T(8,128)S(1)} %get-tuple-element.76), channel_id=1, source_target_pairs={{4,8},{8,4},{12,16},{16,12},{20,24},{24,20},{28,32},{32,28},{36,40... | collective-permute-start | bytes 589832 | tf_op jit(solution)/shard_map/ppermute | solution.py:714
  157.2 7.6 %shard_map.58 = (f32[12,32,512]{2,1,0:T(8,128)S(1)}, f32[12,32,512]{2,1,0:T(8,128)S(1)}, f32[12,32,512]{2,1,0:T(8,128)S(1)}) custom-call(f32[12,40,512]{2,1,0:T(8,128)S(1)} %get-tuple-element.73.phi_ref), custom_call_target="tpu_custom_call" | custom-call | flops 49152000 | bytes 1048576 | tf_op jit(solution)/shard_map/pallas_call | solution.py:448
  164.8 0.0 collective-permute-done.13.ra_ref
  164.8 0.0 collective-permute-done.14.rb_ref
  164.8 3.5 %shard_map.59 = f32[12,32,512]{2,1,0:T(8,128)} custom-call(s32[6]{0:T(128)S(1)} %stack.46.place_ref, f32[12,32,512]{2,1,0:T(8,128)S(1)} %get-tuple-element.74.phi_ref, f32[3,32,512]{2,1,0:T(8,128)S(1)} %collective-permute-done.13.ra_ref, f32[3,32,512]{2,1,0:T(8,128)S(1)} %collective-permute-done.14.rb_ref, f32[12,32,512]{2,1,0:T(8,128)S(1)} %get-tuple-element.77.gp_ref, ...), custom_call_target="tpu_custom_call" | custom-call | flops 20480000 | bytes 1048576 | tf_op jit(solution)/shard_map/pallas_call | solution.py:448
  (23 shorter events, 0.1 us)
Async XLA Ops:
  0.6 4.6 %copy-start.2 = (f32[12,32,512]{2,1,0:T(8,128)S(1)}, f32[12,32,512]{2,1,0:T(8,128)}, u32[]{:S(2)}) copy-start(f32[12,32,512]{2,1,0:T(8,128)} %ls_ref.1) | copy-start | bytes 2359300
  3.9 13.3 %collective-permute-start.1 = (f32[3,3,2,16,384]{4,3,2,1,0:T(8,128)S(1)}, f32[3,3,2,16,384]{4,3,2,1,0:T(8,128)}, u32[]{:S(2)}, u32[]{:S(2)}) collective-permute-start(f32[3,3,2,16,384]{4,3,2,1,0:T(8,128)S(1)} %pad_maximum_fusion.1), channel_id=1, source_target_pairs={{1,0},{2,1},{3,2},{5,4},{6,5},{7,6},{9,8},{10,9},{11,10},{13,12},{... | collective-permute-start | bytes 1327112 | tf_op jit(solution)/shard_map/ppermute | solution.py:808
  6.0 12.3 %collective-permute-start.3 = (f32[3,32,512]{2,1,0:T(8,128)}, f32[3,32,512]{2,1,0:T(8,128)S(1)}, u32[]{:S(2)}, u32[]{:S(2)}) collective-permute-start(f32[3,32,512]{2,1,0:T(8,128)} %get-tuple-element.83), channel_id=1, source_target_pairs={{4,8},{8,4},{12,16},{16,12},{20,24},{24,20},{28,32},{32,28},{36,40... | collective-permute-start | bytes 589832 | tf_op jit(solution)/shard_map/ppermute | solution.py:815
  11.1 11.4 %collective-permute-start.2 = (f32[3,32,512]{2,1,0:T(8,128)}, f32[3,32,512]{2,1,0:T(8,128)S(1)}, u32[]{:S(2)}, u32[]{:S(2)}) collective-permute-start(f32[3,32,512]{2,1,0:T(8,128)} %get-tuple-element.84), channel_id=1, source_target_pairs={{0,4},{4,0},{8,12},{12,8},{16,20},{20,16},{24,28},{28,24},{32,36},... | collective-permute-start | bytes 589832 | tf_op jit(solution)/shard_map/ppermute | solution.py:814
  12.5 4.7 %collective-permute-start = (f32[3,3,16,384]{3,2,1,0:T(8,128)S(1)}, f32[3,3,16,384]{3,2,1,0:T(8,128)}, u32[]{:S(2)}, u32[]{:S(2)}) collective-permute-start(f32[3,3,16,384]{3,2,1,0:T(8,128)S(1)} %bitcast.23), channel_id=1, source_target_pairs={{0,1},{1,2},{2,3},{4,5},{5,6},{6,7},{8,9},{9,10},{10,11},{12,13},{... | collective-permute-start | bytes 663560 | tf_op jit(solution)/shard_map/ppermute | solution.py:807
  16.3 6.3 %slice-start = ((f32[3,3,16,32,384]{4,3,2,1,0:T(8,128)}), f32[3,3,3,32,384]{4,3,2,1,0:T(8,128)S(1)}, s32[]{:S(2)}) async-start(f32[3,3,16,32,384]{4,3,2,1,0:T(8,128)} %u_ref.1), calls=%async_computation.1 | async-start | bytes 2654208 | tf_op jit(solution)/shard_map/slice | solution.py:818
  17.2 5.5 %copy-start.12 = (f32[32,384]{1,0:T(8,128)S(1)}, f32[32,384]{1,0:T(8,128)}, u32[]{:S(2)}) copy-start(f32[32,384]{1,0:T(8,128)} %copy.13) | copy-start | bytes 147460
  18.3 4.3 %copy-start.11 = (f32[3,3,3,16,384]{4,3,2,1,0:T(8,128)}, f32[3,3,3,16,384]{4,3,2,1,0:T(8,128)S(1)}, u32[]{:S(2)}) copy-start(f32[3,3,3,16,384]{4,3,2,1,0:T(8,128)S(1)} %pad_maximum_fusion.yh_ref) | copy-start | bytes 1990660
  24.0 36.8 %collective-permute-start.4 = (f32[984,384]{1,0:T(8,128)}, f32[984,384]{1,0:T(8,128)S(1)}, u32[]{:S(2)}, u32[]{:S(2)}) collective-permute-start(f32[984,384]{1,0:T(8,128)} %maximum_maximum_fusion), channel_id=1, source_target_pairs={{0,124},{4,0},{8,4},{12,8},{16,12},{20,16},{24,20},{28,24},{32,28}... | collective-permute-start | bytes 4534280 | tf_op jit(solution)/shard_map/ppermute | solution.py:821
  50.7 10.1 %copy-start.6 = (f32[13,32,384]{2,1,0:T(8,128)S(1)}, f32[13,32,384]{2,1,0:T(8,128)}, u32[]{:S(2)}) copy-start(f32[13,32,384]{2,1,0:T(8,128)} %get-tuple-element.52.inner_ref) | copy-start | bytes 1916932
  52.3 1.0 copy-start.3
  53.3 2.3 %collective-permute-start.5 = (f32[21,8,512]{2,1,0:T(8,128)}, f32[21,8,512]{2,1,0:T(8,128)S(1)}, u32[]{:S(2)}, u32[]{:S(2)}) collective-permute-start(f32[21,8,512]{2,1,0:T(8,128)} %get-tuple-element.49), channel_id=1, source_target_pairs={{0,1},{1,0},{2,3},{3,2},{4,5},{5,4},{6,7},{7,6},{8,9},{9,8},{10,11... | collective-permute-start | bytes 1032200 | tf_op jit(solution)/shard_map/ppermute | solution.py:825
  53.8 1.8 %collective-permute-start.6 = (f32[21,8,512]{2,1,0:T(8,128)}, f32[21,8,512]{2,1,0:T(8,128)S(1)}, u32[]{:S(2)}, u32[]{:S(2)}) collective-permute-start(f32[21,8,512]{2,1,0:T(8,128)} %get-tuple-element.50), channel_id=1, source_target_pairs={{1,2},{2,1},{5,6},{6,5},{9,10},{10,9},{13,14},{14,13},{17,18},{18,... | collective-permute-start | bytes 1032200 | tf_op jit(solution)/shard_map/ppermute | solution.py:826
  55.6 12.9 %copy-start.7 = (f32[21,8,512]{2,1,0:T(8,128)}, f32[21,8,512]{2,1,0:T(8,128)S(1)}, u32[]{:S(2)}) copy-start(f32[21,8,512]{2,1,0:T(8,128)S(1)} %collective-permute-done.5.ra_ref) | copy-start | bytes 1032196
  55.6 12.9 %copy-start.9 = (f32[21,8,512]{2,1,0:T(8,128)}, f32[21,8,512]{2,1,0:T(8,128)S(1)}, u32[]{:S(2)}) copy-start(f32[21,8,512]{2,1,0:T(8,128)S(1)} %collective-permute-done.6.rb_ref) | copy-start | bytes 1032196
  68.5 38.2 %all-to-all-start = ((f32[32,88,128]{2,1,0:T(8,128)}), f32[32,88,128]{2,1,0:T(8,128)S(1)}, u32[]{:S(2)}, u32[]{:S(2)}) async-start(f32[32,88,128]{2,1,0:T(8,128)} %bitcast.13), calls=%async_computation | async-start | bytes 2883584 | tf_op jit(solution)/shard_map/all_to_all | solution.py:830
  83.5 1.3 copy-start.4
  84.8 1.0 copy-start.8
  85.7 1.0 copy-start.10
  100.2 1.7 %copy-start = (f32[36,48,512]{2,1,0:T(8,128)}, f32[36,48,512]{2,1,0:T(8,128)S(1)}, u32[]{:S(2)}) copy-start(f32[36,48,512]{2,1,0:T(8,128)S(1)} %get-tuple-element.65.step_ref) | copy-start | bytes 10616836
  108.1 4.2 %collective-permute-start.7 = (f32[26,8,512]{2,1,0:T(8,128)S(1)}, f32[26,8,512]{2,1,0:T(8,128)S(1)}, u32[]{:S(2)}, u32[]{:S(2)}) collective-permute-start(f32[26,8,512]{2,1,0:T(8,128)S(1)} %get-tuple-element.61), channel_id=1, source_target_pairs={{0,1},{1,0},{2,3},{3,2},{4,5},{5,4},{6,7},{7,6},{8,9},{9,8},{10,11... | collective-permute-start | bytes 1277960 | tf_op jit(solution)/shard_map/ppermute | solution.py:686
  108.2 10.2 %collective-permute-start.8 = (f32[26,8,512]{2,1,0:T(8,128)S(1)}, f32[26,8,512]{2,1,0:T(8,128)S(1)}, u32[]{:S(2)}, u32[]{:S(2)}) collective-permute-start(f32[26,8,512]{2,1,0:T(8,128)S(1)} %get-tuple-element.62), channel_id=1, source_target_pairs={{1,2},{2,1},{5,6},{6,5},{9,10},{10,9},{13,14},{14,13},{17,18},{18,... | collective-permute-start | bytes 1277960 | tf_op jit(solution)/shard_map/ppermute | solution.py:687
  108.9 9.5 %collective-permute-start.10 = (f32[8,128]{1,0:T(8,128)S(1)}, f32[8,128]{1,0:T(8,128)S(1)}, u32[]{:S(2)}, u32[]{:S(2)}) collective-permute-start(f32[8,128]{1,0:T(8,128)S(1)} %get-tuple-element.63.po_ref), channel_id=1, source_target_pairs={{0,2},{1,3},{2,0},{3,1},{4,6},{5,7},{6,4},{7,5},{8,10},{9,11},{10,... | collective-permute-start | bytes 12296 | tf_op jit(solution)/shard_map/ppermute | solution.py:688
  112.3 6.1 %collective-permute-start.9 = (f32[8,128]{1,0:T(8,128)S(1)}, f32[8,128]{1,0:T(8,128)S(1)}, u32[]{:S(2)}, u32[]{:S(2)}) collective-permute-start(f32[8,128]{1,0:T(8,128)S(1)} %get-tuple-element.63.po_ref), channel_id=1, source_target_pairs={{0,3},{1,2},{2,1},{3,0},{4,7},{5,6},{6,5},{7,4},{8,11},{9,10},{10,... | collective-permute-start | bytes 12296 | tf_op jit(solution)/shard_map/ppermute | solution.py:689
  118.4 2.0 %copy-start.1 = (f32[36,48,512]{2,1,0:T(8,128)S(1)}, f32[36,48,512]{2,1,0:T(8,128)}, u32[]{:S(2)}) copy-start(f32[36,48,512]{2,1,0:T(8,128)} %copy-done) | copy-start | bytes 10616836
  132.2 15.5 %collective-permute-start.11 = (f32[3,40,512]{2,1,0:T(8,128)S(1)}, f32[3,40,512]{2,1,0:T(8,128)S(1)}, u32[]{:S(2)}, u32[]{:S(2)}) collective-permute-start(f32[3,40,512]{2,1,0:T(8,128)S(1)} %get-tuple-element.68), channel_id=1, source_target_pairs={{0,4},{4,0},{8,12},{12,8},{16,20},{20,16},{24,28},{28,24},{32,36},... | collective-permute-start | bytes 737288 | tf_op jit(solution)/shard_map/ppermute | solution.py:703
  133.1 14.6 %collective-permute-start.12 = (f32[3,40,512]{2,1,0:T(8,128)S(1)}, f32[3,40,512]{2,1,0:T(8,128)S(1)}, u32[]{:S(2)}, u32[]{:S(2)}) collective-permute-start(f32[3,40,512]{2,1,0:T(8,128)S(1)} %get-tuple-element.69), channel_id=1, source_target_pairs={{4,8},{8,4},{12,16},{16,12},{20,24},{24,20},{28,32},{32,28},{36,40... | collective-permute-start | bytes 737288 | tf_op jit(solution)/shard_map/ppermute | solution.py:704
  150.9 13.9 %copy-start.5 = (f32[12,32,512]{2,1,0:T(8,128)S(1)}, f32[12,32,512]{2,1,0:T(8,128)}, u32[]{:S(2)}) copy-start(f32[12,32,512]{2,1,0:T(8,128)} %get-tuple-element.40.speed_ref) | copy-start | bytes 2359300
  150.9 13.9 %collective-permute-start.13 = (f32[3,32,512]{2,1,0:T(8,128)S(1)}, f32[3,32,512]{2,1,0:T(8,128)S(1)}, u32[]{:S(2)}, u32[]{:S(2)}) collective-permute-start(f32[3,32,512]{2,1,0:T(8,128)S(1)} %get-tuple-element.75), channel_id=1, source_target_pairs={{0,4},{4,0},{8,12},{12,8},{16,20},{20,16},{24,28},{28,24},{32,36},... | collective-permute-start | bytes 589832 | tf_op jit(solution)/shard_map/ppermute | solution.py:713
  151.1 13.7 %collective-permute-start.14 = (f32[3,32,512]{2,1,0:T(8,128)S(1)}, f32[3,32,512]{2,1,0:T(8,128)S(1)}, u32[]{:S(2)}, u32[]{:S(2)}) collective-permute-start(f32[3,32,512]{2,1,0:T(8,128)S(1)} %get-tuple-element.76), channel_id=1, source_target_pairs={{4,8},{8,4},{12,16},{16,12},{20,24},{24,20},{28,32},{32,28},{36,40... | collective-permute-start | bytes 589832 | tf_op jit(solution)/shard_map/ppermute | solution.py:714

commit v11 on v10

--- a/solution.py
+++ b/solution.py
@@ -729,7 +729,7 @@
     total = -(-(rows + 2 * YE) // 8) * 8
     return vmem_call(
         first_gradient_kernel, [(depth, total, lanes), (3 * (depth - 6), rows1, lanes)], (place, tall, ra, rb),
-        [(6, rows1, lanes)], 35000
+        [(6, rows1, lanes)], 35000, 54
     )
 
 

time: 169 us -> 170 us (level)
  local copies, waits for them, and re-layouts: 13.3 us -> 9.05 us
  waiting for transfers between devices: 20.2 us -> 23.4 us
  Pallas kernels: 82 us -> 84.6 us
    unnamed x28, local copies, waits for them, and re-layouts: 9.09 us -> 4.87 us
    pallas_call x8, Pallas kernels: 50.8 us -> 53.5 us  [vmem_call(): pl.pallas_call(kernel, out_shape=tuple((jax.ShapeDtypeStruct(shape, jnp.f...]
    all_to_all x1, waiting for transfers between devices: 4.79 us -> 7.1 us  [per_device(): lax.all_to_all(message.reshape(wide, 88, 128), 'wide', split_axis=0, conc...]
  transfers between devices with their start and end apart: 16 -> 16, of which waited for: 4 -> 5; matrix products, arithmetic and copies ran while one was open for 3% -> 2% of each run, Pallas kernels for 32% -> 34%
where the time goes in v11:
time: 170 us
  Pallas kernels  84.6 us (50%)
  starting transfers between devices  47.8 us (28%)
  waiting for transfers between devices  23.4 us (14%)
  local copies, waits for them, and re-layouts  9.05 us (5%)
  other arithmetic  4.03 us (2%)
    pallas_call x8, Pallas kernels, vmem_call(): pl.pallas_call(kernel, out_shape=tuple((jax.ShapeDtypeStruct(shape, jnp.f...  53.5 us
    pallas_call x1, Pallas kernels, inner_strain(): pl.pallas_call(inner_kernel, grid=(loads,), out_shape=(jax.ShapeDtypeStru...  23.5 us
    all_to_all x1, starting transfers between devices, per_device(): lax.all_to_all(message.reshape(wide, 88, 128), 'wide', split_axis=0, conc...  15 us
    ppermute x2, starting transfers between devices, level_part(): gb = lax.ppermute(sb, 'wide', wsecond)  12.3 us
    pallas_call x1, Pallas kernels, strain_message(): pl.pallas_call(outer_kernel, grid=(loads,), out_shape=jax.ShapeDtypeStruc...  7.65 us
    all_to_all x1, waiting for transfers between devices, per_device(): lax.all_to_all(message.reshape(wide, 88, 128), 'wide', split_axis=0, conc...  7.1 us
    ppermute x1, waiting for transfers between devices, level_part(): pc = lax.ppermute(wide_peak, 'narrow', across)  6.08 us
    ppermute x1, waiting for transfers between devices, per_device(): beyond = lax.ppermute(jnp.concatenate(flat, axis=0), 'wide', backward)  5.32 us
  transfers between devices with their start and end apart: 16, of which 5 were waited for; matrix products, arithmetic and copies ran while one was open for 2% of the time, Pallas kernels for 34%

profile of v11, /device:TPU:2, one launch (start us, length us, event | category | flops | bytes accessed | tf_op | source)
XLA Modules:
  0.0 169.9 jit_solution(11870070291336286372)
XLA Ops:
  0.6 0.0 copy-start.2
  0.6 3.1 %fusion = (f32[3,3,16,1,384]{4,3,2,1,0:T(1,128)S(1)}, f32[3,3,16,1,384]{4,3,2,1,0:T(1,128)S(1)}, f32[3,3,16,1,384]{4,3,2,1,0:T(1,128)S(1)}) fusion(f32[3,3,16,32,384]{4,3,2,1,0:T(8,128)} %u_ref.1), kind=kLoop, calls=%fused_computation.10 | loop fusion | bytes 1327104 | tf_op jit(solution)/shard_map/slice | solution.py:807
  3.8 0.1 copy_bitcast_fusion
  3.8 0.1 pad_maximum_fusion.1
  3.9 1.3 collective-permute-start.1
  5.2 0.0 copy-done.2
  5.2 0.8 slice_select_fusion
  6.0 5.1 %collective-permute-start.3 = (f32[3,32,512]{2,1,0:T(8,128)}, f32[3,32,512]{2,1,0:T(8,128)S(1)}, u32[]{:S(2)}, u32[]{:S(2)}) collective-permute-start(f32[3,32,512]{2,1,0:T(8,128)} %get-tuple-element.83), channel_id=1, source_target_pairs={{4,8},{8,4},{12,16},{16,12},{20,24},{24,20},{28,32},{32,28},{36,40... | collective-permute-start | bytes 589832 | tf_op jit(solution)/shard_map/ppermute | solution.py:815
  11.1 1.4 collective-permute-start.2
  12.5 3.2 %collective-permute-start = (f32[3,3,16,384]{3,2,1,0:T(8,128)S(1)}, f32[3,3,16,384]{3,2,1,0:T(8,128)}, u32[]{:S(2)}, u32[]{:S(2)}) collective-permute-start(f32[3,3,16,384]{3,2,1,0:T(8,128)S(1)} %bitcast.23), channel_id=1, source_target_pairs={{0,1},{1,2},{2,3},{4,5},{5,6},{6,7},{8,9},{9,10},{10,11},{12,13},{... | collective-permute-start | bytes 663560 | tf_op jit(solution)/shard_map/ppermute | solution.py:807
  15.6 0.7 add_bitcast_fusion
  16.3 0.7 copy.13
  17.1 0.1 pad.3.clone
  17.1 0.0 collective-permute-done
  17.2 0.0 collective-permute-done.1
  17.2 1.1 pad_maximum_fusion.yh_ref
  18.3 0.0 copy-start.8
  18.3 0.0 collective-permute-done.3.rb_ref
  18.3 4.2 %collective-permute-done.2.ra_ref = f32[3,32,512]{2,1,0:T(8,128)S(1)} collective-permute-done((f32[3,32,512]{2,1,0:T(8,128)}, f32[3,32,512]{2,1,0:T(8,128)S(1)}, u32[]{:S(2)}, u32[]{:S(2)}) %collective-permute-start.2) | collective-permute-done | bytes 196640 | tf_op jit(solution)/shard_map/ppermute | solution.py:814
  22.5 0.1 reshape.24
  22.6 0.0 copy-done.8
  22.6 0.0 slice-done
  22.6 0.0 copy-done.12
  22.6 1.4 maximum_maximum_fusion
  24.0 3.2 %collective-permute-start.4 = (f32[984,384]{1,0:T(8,128)}, f32[984,384]{1,0:T(8,128)S(1)}, u32[]{:S(2)}, u32[]{:S(2)}) collective-permute-start(f32[984,384]{1,0:T(8,128)} %maximum_maximum_fusion), channel_id=1, source_target_pairs={{0,124},{4,0},{8,4},{12,8},{16,12},{20,16},{24,20},{28,24},{32,28}... | collective-permute-start | bytes 4534280 | tf_op jit(solution)/shard_map/ppermute | solution.py:821
  27.1 0.1 stack.46.place_ref
  27.2 23.5 %shard_map.50 = (f32[13,32,384]{2,1,0:T(8,128)}, f32[3,3,3,3,32,384]{5,4,3,2,1,0:T(8,128)}) custom-call(f32[3,3,16,32,384]{4,3,2,1,0:T(8,128)} %u_ref.1, f32[3,3,3,16,384]{4,3,2,1,0:T(8,128)} %copy-done.8), custom_call_target="tpu_custom_call" | custom-call | flops 163840000 | bytes 1048576 | tf_op jit(solution)/shard_map/pallas_call | solution.py:215
  50.7 1.6 shard_map.51
  52.3 1.1 copy-done.3
  53.4 0.5 collective-permute-start.5
  54.0 0.7 collective-permute-start.6
  54.6 0.1 copy.14.solid_ref
  54.8 0.7 collective-permute-done.5.ra_ref
  55.5 0.0 collective-permute-done.6.rb_ref
  55.5 5.3 %collective-permute-done.4.next_ref = f32[984,384]{1,0:T(8,128)S(1)} collective-permute-done((f32[984,384]{1,0:T(8,128)}, f32[984,384]{1,0:T(8,128)S(1)}, u32[]{:S(2)}, u32[]{:S(2)}) %collective-permute-start.4) | collective-permute-done | bytes 1511456 | tf_op jit(solution)/shard_map/ppermute | solution.py:821
  60.8 7.7 %shard_map.52 = f32[2816,128]{1,0:T(8,128)} custom-call(s32[6]{0:T(128)S(1)} %stack.46.place_ref, f32[3,3,3,3,32,384]{5,4,3,2,1,0:T(8,128)} %get-tuple-element.42.tail_ref, f32[984,384]{1,0:T(8,128)S(1)} %collective-permute-done.4.next_ref, f32[13,32,384]{2,1,0:T(8,128)S(1)} %copy-done.5, s32[16,32,24]{2,1,0:T(8,128)S(1)} %copy.14.solid_ref), custom_call_target="tpu_custom_call" | custom-call | flops 40960000 | bytes 1048576 | tf_op jit(solution)/shard_map/pallas_call | solution.py:236
  68.4 15.0 %all-to-all-start = ((f32[32,88,128]{2,1,0:T(8,128)}), f32[32,88,128]{2,1,0:T(8,128)S(1)}, u32[]{:S(2)}, u32[]{:S(2)}) async-start(f32[32,88,128]{2,1,0:T(8,128)} %bitcast.13), calls=%async_computation | async-start | bytes 2883584 | tf_op jit(solution)/shard_map/all_to_all | solution.py:830
  83.5 16.1 %shard_map.53 = (f32[18,56,512]{2,1,0:T(8,128)}, f32[36,48,512]{2,1,0:T(8,128)}) custom-call(s32[6]{0:T(128)} %copy-done.6, f32[18,32,512]{2,1,0:T(8,128)} %copy-done.3, f32[21,8,512]{2,1,0:T(8,128)} %copy-done.9, f32[21,8,512]{2,1,0:T(8,128)} %copy-done.10), custom_call_target="tpu_custom_call" | custom-call | flops 143360000 | bytes 1048576 | tf_op jit(solution)/shard_map/pallas_call | solution.py:448
  99.6 7.1 %all-to-all-done.recv_ref = f32[32,88,128]{2,1,0:T(8,128)S(1)} async-done(((f32[32,88,128]{2,1,0:T(8,128)}), f32[32,88,128]{2,1,0:T(8,128)S(1)}, u32[]{:S(2)}, u32[]{:S(2)}) %all-to-all-start) | async-done | bytes 1441824 | tf_op jit(solution)/shard_map/all_to_all | solution.py:830
  106.7 1.4 shard_map.54
  108.1 0.1 collective-permute-start.7
  108.2 0.7 collective-permute-start.8
  108.8 3.4 %collective-permute-start.10 = (f32[8,128]{1,0:T(8,128)S(1)}, f32[8,128]{1,0:T(8,128)S(1)}, u32[]{:S(2)}, u32[]{:S(2)}) collective-permute-start(f32[8,128]{1,0:T(8,128)S(1)} %get-tuple-element.63.po_ref), channel_id=1, source_target_pairs={{0,2},{1,3},{2,0},{3,1},{4,6},{5,7},{6,4},{7,5},{8,10},{9,11},{10,... | collective-permute-start | bytes 12296 | tf_op jit(solution)/shard_map/ppermute | solution.py:688
  112.3 0.0 collective-permute-start.9
  112.3 0.0 collective-permute-done.7.ra_ref
  112.3 6.1 %collective-permute-done.10.pc_ref = f32[8,128]{1,0:T(8,128)S(1)} collective-permute-done((f32[8,128]{1,0:T(8,128)S(1)}, f32[8,128]{1,0:T(8,128)S(1)}, u32[]{:S(2)}, u32[]{:S(2)}) %collective-permute-start.10) | collective-permute-done | bytes 4128 | tf_op jit(solution)/shard_map/ppermute | solution.py:688
  118.4 0.0 collective-permute-done.9.pb_ref
  118.4 0.0 collective-permute-done.8.rb_ref
  118.4 2.0 %copy-done = f32[36,48,512]{2,1,0:T(8,128)S(1)} copy-done((f32[36,48,512]{2,1,0:T(8,128)S(1)}, f32[36,48,512]{2,1,0:T(8,128)}, u32[]{:S(2)}) %copy-start) | copy-done | bytes 3538968
  120.4 1.6 copy-done.1
  121.9 11.8 %shard_map.55 = (f32[12,32,512]{2,1,0:T(8,128)}, f32[12,40,512]{2,1,0:T(8,128)S(1)}, f32[12,48,512]{2,1,0:T(8,128)S(1)}, f32[3,40,512]{2,1,0:T(8,128)S(1)}, f32[3,40,512]{2,1,0:T(8,128)S(1)}) custom-call(s32[6]{0:T(128)S(1)} %copy-done.7, f32[20,32,512]{2,1,0:T(8,128)S(1)} %get-tuple-element.60.tile_ref, f32[26,8,512]{2,1,0:T(8,128)S(1)} %collective-permute-done.7.ra_ref, ...), custom_call_target="tpu_custom_call" | custom-call | flops 32768000 | bytes 1048576 | tf_op jit(solution)/shard_map/pallas_call | solution.py:448
  133.7 0.9 collective-permute-start.11
  134.6 6.2 %collective-permute-start.12 = (f32[3,40,512]{2,1,0:T(8,128)S(1)}, f32[3,40,512]{2,1,0:T(8,128)S(1)}, u32[]{:S(2)}, u32[]{:S(2)}) collective-permute-start(f32[3,40,512]{2,1,0:T(8,128)S(1)} %get-tuple-element.69), channel_id=1, source_target_pairs={{4,8},{8,4},{12,16},{16,12},{20,24},{24,20},{28,32},{32,28},{36,40... | collective-permute-start | bytes 737288 | tf_op jit(solution)/shard_map/ppermute | solution.py:704
  140.9 8.3 %shard_map.56 = (f32[12,40,512]{2,1,0:T(8,128)S(1)}, f32[12,40,512]{2,1,0:T(8,128)S(1)}, f32[12,40,512]{2,1,0:T(8,128)S(1)}) custom-call(f32[12,48,512]{2,1,0:T(8,128)S(1)} %get-tuple-element.66.phi_ref), custom_call_target="tpu_custom_call" | custom-call | flops 49152000 | bytes 1048576 | tf_op jit(solution)/shard_map/pallas_call | solution.py:448
  149.2 0.0 collective-permute-done.11.ra_ref
  149.2 0.0 collective-permute-done.12.rb_ref
  149.2 3.2 %shard_map.57 = (f32[12,40,512]{2,1,0:T(8,128)S(1)}, f32[3,32,512]{2,1,0:T(8,128)S(1)}, f32[3,32,512]{2,1,0:T(8,128)S(1)}) custom-call(s32[6]{0:T(128)S(1)} %copy-done.7, f32[12,40,512]{2,1,0:T(8,128)S(1)} %get-tuple-element.67.phi_ref, f32[3,40,512]{2,1,0:T(8,128)S(1)} %collective-permute-done.11.ra_ref, f32[3,40,512]{2,1,0:T(8,128)S(1)} %collective-permute-done.12.rb_ref, ...), custom_call_target="tpu_custom_call" | custom-call | flops 20480000 | bytes 1048576 | tf_op jit(solution)/shard_map/pallas_call | solution.py:448
  152.4 0.0 copy-start.4
  152.4 0.2 collective-permute-start.13
  152.6 6.1 %collective-permute-start.14 = (f32[3,32,512]{2,1,0:T(8,128)S(1)}, f32[3,32,512]{2,1,0:T(8,128)S(1)}, u32[]{:S(2)}, u32[]{:S(2)}) collective-permute-start(f32[3,32,512]{2,1,0:T(8,128)S(1)} %get-tuple-element.76), channel_id=1, source_target_pairs={{4,8},{8,4},{12,16},{16,12},{20,24},{24,20},{28,32},{32,28},{36,40... | collective-permute-start | bytes 589832 | tf_op jit(solution)/shard_map/ppermute | solution.py:714
  158.7 7.6 %shard_map.58 = (f32[12,32,512]{2,1,0:T(8,128)S(1)}, f32[12,32,512]{2,1,0:T(8,128)S(1)}, f32[12,32,512]{2,1,0:T(8,128)S(1)}) custom-call(f32[12,40,512]{2,1,0:T(8,128)S(1)} %get-tuple-element.73.phi_ref), custom_call_target="tpu_custom_call" | custom-call | flops 49152000 | bytes 1048576 | tf_op jit(solution)/shard_map/pallas_call | solution.py:448
  166.3 0.0 collective-permute-done.13.ra_ref
  166.3 0.0 collective-permute-done.14.rb_ref
  166.3 3.5 %shard_map.59 = f32[12,32,512]{2,1,0:T(8,128)} custom-call(s32[6]{0:T(128)S(1)} %copy-done.7, f32[12,32,512]{2,1,0:T(8,128)S(1)} %get-tuple-element.74.phi_ref, f32[3,32,512]{2,1,0:T(8,128)S(1)} %collective-permute-done.13.ra_ref, f32[3,32,512]{2,1,0:T(8,128)S(1)} %collective-permute-done.14.rb_ref, f32[12,32,512]{2,1,0:T(8,128)S(1)} %get-tuple-element.77.gp_ref, ...), custom_call_target="tpu_custom_call" | custom-call | flops 20480000 | bytes 1048576 | tf_op jit(solution)/shard_map/pallas_call | solution.py:448
  (23 shorter events, 0.1 us)
Async XLA Ops:
  0.6 4.6 %copy-start.2 = (f32[12,32,512]{2,1,0:T(8,128)S(1)}, f32[12,32,512]{2,1,0:T(8,128)}, u32[]{:S(2)}) copy-start(f32[12,32,512]{2,1,0:T(8,128)} %ls_ref.1) | copy-start | bytes 2359300
  3.9 13.3 %collective-permute-start.1 = (f32[3,3,2,16,384]{4,3,2,1,0:T(8,128)S(1)}, f32[3,3,2,16,384]{4,3,2,1,0:T(8,128)}, u32[]{:S(2)}, u32[]{:S(2)}) collective-permute-start(f32[3,3,2,16,384]{4,3,2,1,0:T(8,128)S(1)} %pad_maximum_fusion.1), channel_id=1, source_target_pairs={{1,0},{2,1},{3,2},{5,4},{6,5},{7,6},{9,8},{10,9},{11,10},{13,12},{... | collective-permute-start | bytes 1327112 | tf_op jit(solution)/shard_map/ppermute | solution.py:808
  6.0 12.3 %collective-permute-start.3 = (f32[3,32,512]{2,1,0:T(8,128)}, f32[3,32,512]{2,1,0:T(8,128)S(1)}, u32[]{:S(2)}, u32[]{:S(2)}) collective-permute-start(f32[3,32,512]{2,1,0:T(8,128)} %get-tuple-element.83), channel_id=1, source_target_pairs={{4,8},{8,4},{12,16},{16,12},{20,24},{24,20},{28,32},{32,28},{36,40... | collective-permute-start | bytes 589832 | tf_op jit(solution)/shard_map/ppermute | solution.py:815
  11.1 11.4 %collective-permute-start.2 = (f32[3,32,512]{2,1,0:T(8,128)}, f32[3,32,512]{2,1,0:T(8,128)S(1)}, u32[]{:S(2)}, u32[]{:S(2)}) collective-permute-start(f32[3,32,512]{2,1,0:T(8,128)} %get-tuple-element.84), channel_id=1, source_target_pairs={{0,4},{4,0},{8,12},{12,8},{16,20},{20,16},{24,28},{28,24},{32,36},... | collective-permute-start | bytes 589832 | tf_op jit(solution)/shard_map/ppermute | solution.py:814
  12.5 4.7 %collective-permute-start = (f32[3,3,16,384]{3,2,1,0:T(8,128)S(1)}, f32[3,3,16,384]{3,2,1,0:T(8,128)}, u32[]{:S(2)}, u32[]{:S(2)}) collective-permute-start(f32[3,3,16,384]{3,2,1,0:T(8,128)S(1)} %bitcast.23), channel_id=1, source_target_pairs={{0,1},{1,2},{2,3},{4,5},{5,6},{6,7},{8,9},{9,10},{10,11},{12,13},{... | collective-permute-start | bytes 663560 | tf_op jit(solution)/shard_map/ppermute | solution.py:807
  16.3 6.3 %slice-start = ((f32[3,3,16,32,384]{4,3,2,1,0:T(8,128)}), f32[3,3,3,32,384]{4,3,2,1,0:T(8,128)S(1)}, s32[]{:S(2)}) async-start(f32[3,3,16,32,384]{4,3,2,1,0:T(8,128)} %u_ref.1), calls=%async_computation.1 | async-start | bytes 2654208 | tf_op jit(solution)/shard_map/slice | solution.py:818
  17.2 5.5 %copy-start.12 = (f32[32,384]{1,0:T(8,128)S(1)}, f32[32,384]{1,0:T(8,128)}, u32[]{:S(2)}) copy-start(f32[32,384]{1,0:T(8,128)} %copy.13) | copy-start | bytes 147460
  18.3 4.3 %copy-start.8 = (f32[3,3,3,16,384]{4,3,2,1,0:T(8,128)}, f32[3,3,3,16,384]{4,3,2,1,0:T(8,128)S(1)}, u32[]{:S(2)}) copy-start(f32[3,3,3,16,384]{4,3,2,1,0:T(8,128)S(1)} %pad_maximum_fusion.yh_ref) | copy-start | bytes 1990660
  24.0 36.8 %collective-permute-start.4 = (f32[984,384]{1,0:T(8,128)}, f32[984,384]{1,0:T(8,128)S(1)}, u32[]{:S(2)}, u32[]{:S(2)}) collective-permute-start(f32[984,384]{1,0:T(8,128)} %maximum_maximum_fusion), channel_id=1, source_target_pairs={{0,124},{4,0},{8,4},{12,8},{16,12},{20,16},{24,20},{28,24},{32,28}... | collective-permute-start | bytes 4534280 | tf_op jit(solution)/shard_map/ppermute | solution.py:821
  27.2 33.6 %copy-start.6 = (s32[6]{0:T(128)}, s32[6]{0:T(128)S(1)}, u32[]{:S(2)}) copy-start(s32[6]{0:T(128)S(1)} %stack.46.place_ref) | copy-start | bytes 76
  27.2 27.4 %copy-start.11 = (s32[16,32,24]{1,2,0:T(8,128)S(1)}, s32[16,32,24]{1,2,0:T(8,128)}, u32[]{:S(2)}) copy-start(s32[16,32,24]{1,2,0:T(8,128)} %param.4) | copy-start | bytes 147460
  50.7 10.1 %copy-start.5 = (f32[13,32,384]{2,1,0:T(8,128)S(1)}, f32[13,32,384]{2,1,0:T(8,128)}, u32[]{:S(2)}) copy-start(f32[13,32,384]{2,1,0:T(8,128)} %get-tuple-element.52.inner_ref) | copy-start | bytes 1916932
  52.3 1.1 copy-start.3
  53.4 2.0 %collective-permute-start.5 = (f32[21,8,512]{2,1,0:T(8,128)}, f32[21,8,512]{2,1,0:T(8,128)S(1)}, u32[]{:S(2)}, u32[]{:S(2)}) collective-permute-start(f32[21,8,512]{2,1,0:T(8,128)} %get-tuple-element.49), channel_id=1, source_target_pairs={{0,1},{1,0},{2,3},{3,2},{4,5},{5,4},{6,7},{7,6},{8,9},{9,8},{10,11... | collective-permute-start | bytes 1032200 | tf_op jit(solution)/shard_map/ppermute | solution.py:825
  54.0 1.5 collective-permute-start.6
  55.4 13.0 %copy-start.9 = (f32[21,8,512]{2,1,0:T(8,128)}, f32[21,8,512]{2,1,0:T(8,128)S(1)}, u32[]{:S(2)}) copy-start(f32[21,8,512]{2,1,0:T(8,128)S(1)} %collective-permute-done.5.ra_ref) | copy-start | bytes 1032196
  55.5 13.0 %copy-start.10 = (f32[21,8,512]{2,1,0:T(8,128)}, f32[21,8,512]{2,1,0:T(8,128)S(1)}, u32[]{:S(2)}) copy-start(f32[21,8,512]{2,1,0:T(8,128)S(1)} %collective-permute-done.6.rb_ref) | copy-start | bytes 1032196
  68.4 38.2 %all-to-all-start = ((f32[32,88,128]{2,1,0:T(8,128)}), f32[32,88,128]{2,1,0:T(8,128)S(1)}, u32[]{:S(2)}, u32[]{:S(2)}) async-start(f32[32,88,128]{2,1,0:T(8,128)} %bitcast.13), calls=%async_computation | async-start | bytes 2883584 | tf_op jit(solution)/shard_map/all_to_all | solution.py:830
  83.4 23.2 %copy-start.7 = (s32[6]{0:T(128)S(1)}, s32[6]{0:T(128)}, u32[]{:S(2)}) copy-start(s32[6]{0:T(128)} %copy-done.6) | copy-start | bytes 76
  108.1 4.2 %collective-permute-start.7 = (f32[26,8,512]{2,1,0:T(8,128)S(1)}, f32[26,8,512]{2,1,0:T(8,128)S(1)}, u32[]{:S(2)}, u32[]{:S(2)}) collective-permute-start(f32[26,8,512]{2,1,0:T(8,128)S(1)} %get-tuple-element.61), channel_id=1, source_target_pairs={{0,1},{1,0},{2,3},{3,2},{4,5},{5,4},{6,7},{7,6},{8,9},{9,8},{10,11... | collective-permute-start | bytes 1277960 | tf_op jit(solution)/shard_map/ppermute | solution.py:686
  108.2 10.2 %collective-permute-start.8 = (f32[26,8,512]{2,1,0:T(8,128)S(1)}, f32[26,8,512]{2,1,0:T(8,128)S(1)}, u32[]{:S(2)}, u32[]{:S(2)}) collective-permute-start(f32[26,8,512]{2,1,0:T(8,128)S(1)} %get-tuple-element.62), channel_id=1, source_target_pairs={{1,2},{2,1},{5,6},{6,5},{9,10},{10,9},{13,14},{14,13},{17,18},{18,... | collective-permute-start | bytes 1277960 | tf_op jit(solution)/shard_map/ppermute | solution.py:687
  108.8 9.5 %collective-permute-start.10 = (f32[8,128]{1,0:T(8,128)S(1)}, f32[8,128]{1,0:T(8,128)S(1)}, u32[]{:S(2)}, u32[]{:S(2)}) collective-permute-start(f32[8,128]{1,0:T(8,128)S(1)} %get-tuple-element.63.po_ref), channel_id=1, source_target_pairs={{0,2},{1,3},{2,0},{3,1},{4,6},{5,7},{6,4},{7,5},{8,10},{9,11},{10,... | collective-permute-start | bytes 12296 | tf_op jit(solution)/shard_map/ppermute | solution.py:688
  112.3 6.1 %collective-permute-start.9 = (f32[8,128]{1,0:T(8,128)S(1)}, f32[8,128]{1,0:T(8,128)S(1)}, u32[]{:S(2)}, u32[]{:S(2)}) collective-permute-start(f32[8,128]{1,0:T(8,128)S(1)} %get-tuple-element.63.po_ref), channel_id=1, source_target_pairs={{0,3},{1,2},{2,1},{3,0},{4,7},{5,6},{6,5},{7,4},{8,11},{9,10},{10,... | collective-permute-start | bytes 12296 | tf_op jit(solution)/shard_map/ppermute | solution.py:689
  118.4 2.0 %copy-start = (f32[36,48,512]{2,1,0:T(8,128)S(1)}, f32[36,48,512]{2,1,0:T(8,128)}, u32[]{:S(2)}) copy-start(f32[36,48,512]{2,1,0:T(8,128)} %get-tuple-element.65.step_ref) | copy-start | bytes 10616836
  120.4 1.6 copy-start.1
  133.7 15.5 %collective-permute-start.11 = (f32[3,40,512]{2,1,0:T(8,128)S(1)}, f32[3,40,512]{2,1,0:T(8,128)S(1)}, u32[]{:S(2)}, u32[]{:S(2)}) collective-permute-start(f32[3,40,512]{2,1,0:T(8,128)S(1)} %get-tuple-element.68), channel_id=1, source_target_pairs={{0,4},{4,0},{8,12},{12,8},{16,20},{20,16},{24,28},{28,24},{32,36},... | collective-permute-start | bytes 737288 | tf_op jit(solution)/shard_map/ppermute | solution.py:703
  134.6 14.6 %collective-permute-start.12 = (f32[3,40,512]{2,1,0:T(8,128)S(1)}, f32[3,40,512]{2,1,0:T(8,128)S(1)}, u32[]{:S(2)}, u32[]{:S(2)}) collective-permute-start(f32[3,40,512]{2,1,0:T(8,128)S(1)} %get-tuple-element.69), channel_id=1, source_target_pairs={{4,8},{8,4},{12,16},{16,12},{20,24},{24,20},{28,32},{32,28},{36,40... | collective-permute-start | bytes 737288 | tf_op jit(solution)/shard_map/ppermute | solution.py:704
  152.4 13.9 %copy-start.4 = (f32[12,32,512]{2,1,0:T(8,128)S(1)}, f32[12,32,512]{2,1,0:T(8,128)}, u32[]{:S(2)}) copy-start(f32[12,32,512]{2,1,0:T(8,128)} %get-tuple-element.40.speed_ref) | copy-start | bytes 2359300
  152.4 13.9 %collective-permute-start.13 = (f32[3,32,512]{2,1,0:T(8,128)S(1)}, f32[3,32,512]{2,1,0:T(8,128)S(1)}, u32[]{:S(2)}, u32[]{:S(2)}) collective-permute-start(f32[3,32,512]{2,1,0:T(8,128)S(1)} %get-tuple-element.75), channel_id=1, source_target_pairs={{0,4},{4,0},{8,12},{12,8},{16,20},{20,16},{24,28},{28,24},{32,36},... | collective-permute-start | bytes 589832 | tf_op jit(solution)/shard_map/ppermute | solution.py:713
  152.6 13.7 %collective-permute-start.14 = (f32[3,32,512]{2,1,0:T(8,128)S(1)}, f32[3,32,512]{2,1,0:T(8,128)S(1)}, u32[]{:S(2)}, u32[]{:S(2)}) collective-permute-start(f32[3,32,512]{2,1,0:T(8,128)S(1)} %get-tuple-element.76), channel_id=1, source_target_pairs={{4,8},{8,4},{12,16},{16,12},{20,24},{24,20},{28,32},{32,28},{36,40... | collective-permute-start | bytes 589832 | tf_op jit(solution)/shard_map/ppermute | solution.py:714
